TPU v7x, 32 devices: a whole 2x2x4 slice. The times are simulated.
32 devices in a mesh: grp: 2 (over y), row: 16 (over z, x, core), col: 1.
Axes of the slice: x: 2, y: 2, z: 4, core: 2. Of those that a mesh axis runs over, the one named last changes fastest.
Arguments:
- pair_rep: bfloat16 [256, 128, 128], P(('grp', 'row'), 'col'), parts along dimension 0, may hold values from -6 to 6
- pair_mask: int32 [256, 128], P(('grp', 'row'), 'col'), parts along dimension 0, may hold values from 0 to 1, as said below
- cotangent: bfloat16 [256, 128, 128], P(('grp', 'row'), 'col'), parts along dimension 0, may hold values from -6 to 6
- in_gain: float32 [128], replicated, may hold values from 0.25 to 1.75
- in_bias: float32 [128], replicated, may hold values from -3 to 3
- proj_weight: bfloat16 [128, 512], replicated, may hold values from -0.5 to 0.5
- gate_weight: bfloat16 [128, 128], replicated, may hold values from -0.5 to 0.5
- mid_gain: float32 [128], replicated, may hold values from 0.25 to 1.75
- mid_bias: float32 [128], replicated, may hold values from -3 to 3
- out_weight: bfloat16 [128, 128], replicated, may hold values from -0.5 to 0.5
Outputs:
- output: bfloat16 [256, 128, 128], P(('grp', 'row'), 'col'), parts along dimension 0
- grad_pair: bfloat16 [256, 128, 128], P(('grp', 'row'), 'col'), parts along dimension 0
There are 2 independent parts, one for each index of `grp`. A program takes and returns all parts, laid end to end along the dimension named above; an argument that names none is the same for every part. Nothing has to cross between parts.
Inputs may be any that keep to these rules, and one draw needn't show every extreme that they name: pair_mask[i, j] = v[i] v[j] for a residue validity v of 0 and 1: residues from some position on (at least 96 and below 128) are padding with v = 0, and single residues before it may also have v = 0.
All inputs are finite; a program needn't handle non-finite values.
Results may differ from a plain program's by a relative error of at most 0.0074.
Values may be sent and summed in bfloat16 or wider, within the bound.
No kernel may reach another device: no remote copies, remote signals or barrier semaphores. Data moves between devices by JAX's collectives and lax.ppermute only.
A program may use at most 64 MiB of HBM per device.

v0:
```python
import jax
import jax.numpy as jnp
from jax import lax
from jax.sharding import PartitionSpec as P

EPSILON = 1e-05


def norm_stats(values, reduce_axis):
    center = values - jnp.mean(values, axis=reduce_axis, keepdims=True)
    inverse = lax.rsqrt(jnp.mean(center * center, axis=reduce_axis, keepdims=True) + EPSILON)
    return (center * inverse, inverse)


def norm_back(grad_hat, normed, inverse, reduce_axis):
    first = jnp.mean(grad_hat, axis=reduce_axis, keepdims=True)
    second = jnp.mean(grad_hat * normed, axis=reduce_axis, keepdims=True)
    return inverse * (grad_hat - first - normed * second)


def forward_products(left_chan, right_chan):
    return jnp.einsum("hik,hjk->hij", left_chan, right_chan, preferred_element_type=jnp.float32)


def backward_products(grad_full, left_chan, right_chan):
    grad_left = jnp.einsum(
        "hij,hjk->hik", grad_full, right_chan, preferred_element_type=jnp.float32
    )
    grad_right = jnp.einsum(
        "hij,hik->hjk", grad_full, left_chan, preferred_element_type=jnp.float32
    )
    return jnp.stack([grad_left, grad_right]).astype(jnp.bfloat16)


def per_device(
    pair_rep,
    pair_mask,
    cotangent,
    in_gain,
    in_bias,
    proj_weight,
    gate_weight,
    mid_gain,
    mid_bias,
    out_weight,
):
    width = pair_rep.shape[2]
    hidden = out_weight.shape[0]
    weights_four = proj_weight.reshape(width, 2, 2, hidden)
    mask_float = pair_mask.astype(jnp.float32)
    normed_in, inverse_in = norm_stats(pair_rep.astype(jnp.float32), 2)
    scaled_in = (normed_in * in_gain + in_bias).astype(jnp.bfloat16)
    gate_pre = jnp.einsum(
        "ijc,csh->shij", scaled_in, weights_four[:, :, 0], preferred_element_type=jnp.float32
    )
    value_pre = jnp.einsum(
        "ijc,csh->shij", scaled_in, weights_four[:, :, 1], preferred_element_type=jnp.float32
    )
    sigmoid_gate = jax.nn.sigmoid(gate_pre)
    both_sides = (sigmoid_gate * value_pre * mask_float).astype(jnp.bfloat16)
    gate_sig = jax.nn.sigmoid(
        jnp.einsum("ijc,cd->ijd", scaled_in, gate_weight, preferred_element_type=jnp.float32)
    )
    sides_chan = lax.all_to_all(both_sides, "row", split_axis=1, concat_axis=2, tiled=True)
    partial_sum = forward_products(sides_chan[0], sides_chan[1])
    product = lax.psum_scatter(partial_sum, "col", scatter_dimension=2, tiled=True).astype(
        jnp.bfloat16
    )
    mixed_pair = lax.all_to_all(product, "row", split_axis=1, concat_axis=0, tiled=True)
    normed_mid, inverse_mid = norm_stats(mixed_pair.astype(jnp.float32), 0)
    scaled_mid = (normed_mid * mid_gain[:, None, None] + mid_bias[:, None, None]).astype(
        jnp.bfloat16
    )
    update = jnp.einsum("hij,hc->ijc", scaled_mid, out_weight, preferred_element_type=jnp.float32)
    output = (gate_sig * update).astype(jnp.bfloat16)
    grad_out = cotangent.astype(jnp.float32)
    grad_update = (grad_out * gate_sig).astype(jnp.bfloat16)
    grad_gate = (grad_out * update * gate_sig * (1.0 - gate_sig)).astype(jnp.bfloat16)
    grad_scaled_mid = jnp.einsum(
        "ijc,hc->hij", grad_update, out_weight, preferred_element_type=jnp.float32
    )
    grad_mixed = norm_back(
        grad_scaled_mid * mid_gain[:, None, None], normed_mid, inverse_mid, 0
    ).astype(jnp.bfloat16)
    grad_chan = lax.all_to_all(grad_mixed, "row", split_axis=0, concat_axis=1, tiled=True)
    grad_full = lax.all_gather(grad_chan, "col", axis=2, tiled=True)
    grad_local = backward_products(grad_full, sides_chan[0], sides_chan[1])
    grad_sides = lax.all_to_all(grad_local, "row", split_axis=2, concat_axis=1, tiled=True)
    side_float = grad_sides.astype(jnp.float32) * mask_float
    grad_value = (side_float * sigmoid_gate).astype(jnp.bfloat16)
    grad_gate_pre = (side_float * value_pre * sigmoid_gate * (1.0 - sigmoid_gate)).astype(
        jnp.bfloat16
    )
    grad_scaled = jnp.einsum(
        "shij,csh->ijc", grad_gate_pre, weights_four[:, :, 0], preferred_element_type=jnp.float32
    )
    grad_scaled = grad_scaled + jnp.einsum(
        "shij,csh->ijc", grad_value, weights_four[:, :, 1], preferred_element_type=jnp.float32
    )
    grad_scaled = grad_scaled + jnp.einsum(
        "ijd,cd->ijc", grad_gate, gate_weight, preferred_element_type=jnp.float32
    )
    grad_pair = norm_back(grad_scaled * in_gain, normed_in, inverse_in, 2).astype(jnp.bfloat16)
    return (output, grad_pair)


def solution(mesh):
    placed = (
        P(("grp", "row"), "col", None),
        P(("grp", "row"), "col"),
        P(("grp", "row"), "col", None),
        P(),
        P(),
        P(),
        P(),
        P(),
        P(),
        P(),
    )
    return jax.shard_map(
        per_device,
        mesh=mesh,
        in_specs=placed,
        out_specs=(P(("grp", "row"), "col", None), P(("grp", "row"), "col", None)),
        check_vma=False,
    )
```

profile of v0, /device:TPU:0, one launch (start us, length us, event | category | flops | bytes accessed | tf_op | source)
XLA Modules:
  0.0 82.5 jit_solution(2473779919447756028)
XLA Ops:
  0.6 0.0 copy-start
  0.6 0.0 copy-start.9
  0.7 0.7 convert_element_type.75
  1.4 1.0 %copy.69 = bf16[128,512]{0,1:T(8,128)(2,1)S(1)} copy(bf16[128,512]{1,0:T(8,128)(2,1)} %param.15) | data formatting | bytes 262144 | tf_op args[5]
  2.4 0.0 copy-done.9
  2.4 0.0 copy-start.5
  2.4 0.2 copy.67
  2.7 0.1 fusion.23
  2.8 0.0 copy-start.11
  2.8 0.0 copy-start.12
  2.8 0.6 copy-done.11
  3.4 0.0 copy-done.12
  3.5 0.4 convolution_bitcast_fusion
  3.9 0.0 copy-done.5
  3.9 0.6 multiply_convert_fusion.2
  4.5 0.5 copy.74
  5.0 21.6 %all_to_all.51 = bf16[2,128,8,128]{3,0,2,1:T(2,128)(2,1)S(1)} all-to-all(bf16[2,128,8,128]{3,0,2,1:T(2,128)(2,1)S(1)} %copy.74), channel_id=1, replica_groups=mesh['grp'=2,'row'=16,'col'=1] {'row'}, dimensions={1} | all-to-all | bytes 1048576 | tf_op jit(solution)/shard_map/all_to_all | solution.py:64
  26.6 0.1 copy.75
  26.7 0.3 convolution_convert_fusion.2
  27.1 0.2 copy.78
  27.2 13.9 %all_to_all.52 = bf16[8,128,128]{2,0,1:T(8,128)(2,1)S(1)} all-to-all(bf16[8,128,128]{2,0,1:T(8,128)(2,1)S(1)} %copy.78), channel_id=1, replica_groups=mesh['grp'=2,'row'=16,'col'=1] {'row'}, dimensions={1} | all-to-all | bytes 524288 | tf_op jit(solution)/shard_map/all_to_all | solution.py:69
  41.3 0.0 copy-start.10
  41.3 0.1 fusion.30
  41.4 0.0 copy-start.13
  41.4 0.0 copy-start.14
  41.4 0.6 copy-done.10
  42.0 0.0 copy-done.13
  42.0 0.0 copy-done.14
  42.0 0.3 fusion.34
  42.4 0.0 copy-done
  42.4 0.0 copy-start.7
  42.4 0.0 copy-start.3
  42.4 1.1 %multiply_convert_fusion.6 = (bf16[8,128,128]{2,1,0:T(8,128)(2,1)}, f32[8,128,128]{2,1,0:T(8,128)S(1)}) fusion(f32[8,128,128]{2,1,0:T(8,128)S(1)} %fusion.34, bf16[128,128]{1,0:T(8,128)(2,1)S(1)} %copy-done, bf16[8,128,128]{1,2,0:T(8,128)(2,1)S(1)} %copy.67, f32[128]{0:T(128)S(1)} %copy-done.12, f32[128]{0:T(128)S(1)} %copy-done.11, ...), kind=kOutput, calls=%fused_computation.56 | convolution fusion | flops 34996224 | bytes 1614848 | tf_op jit(solution)/shard_map/ijc,cd->ijd/dot_general | solution.py:62
  43.5 0.0 copy-done.7
  43.6 0.0 copy-start.1
  43.6 0.0 copy-done.3
  43.6 0.3 fusion.66
  43.8 0.5 copy-done.1
  44.4 0.1 multiply_convert_fusion.5
  44.5 0.2 copy.81
  44.7 12.8 %all_to_all.53 = bf16[128,8,128]{2,1,0:T(8,128)(2,1)S(1)} all-to-all(bf16[128,8,128]{2,1,0:T(8,128)(2,1)S(1)} %copy.81), channel_id=1, replica_groups=mesh['grp'=2,'row'=16,'col'=1] {'row'}, dimensions={0} | all-to-all | bytes 524288 | tf_op jit(solution)/shard_map/all_to_all | solution.py:85
  57.5 0.3 fusion.11
  57.8 0.2 fusion.10
  58.0 0.1 pad_maximum_fusion
  58.1 0.3 copy.84
  58.4 17.2 %all_to_all.54 = bf16[2,8,128,128]{3,1,0,2:T(8,128)(2,1)S(1)} all-to-all(bf16[2,8,128,128]{3,1,0,2:T(8,128)(2,1)S(1)} %copy.84), channel_id=1, replica_groups=mesh['grp'=2,'row'=16,'col'=1] {'row'}, dimensions={2} | all-to-all | bytes 1048576 | tf_op jit(solution)/shard_map/all_to_all | solution.py:88
  75.7 0.1 convert_bitcast_fusion
  75.8 1.1 %copy.86 = f32[2,16,8,8,128]{4,3,2,1,0:T(8,128)} copy(f32[2,16,8,8,128]{4,3,1,2,0:T(8,128)S(1)} %convert_bitcast_fusion) | data formatting | bytes 2097152 | tf_op jit(solution)/shard_map/convert_element_type | solution.py:89
  76.9 1.6 %copy.87 = f32[2,128,8,128]{1,3,0,2:T(8,128)S(1)} copy(f32[2,128,8,128]{3,2,1,0:T(8,128)} %bitcast.114) | data formatting | bytes 2097152 | tf_op jit(solution)/shard_map/convert_element_type | solution.py:89
  78.5 0.0 copy-start.6
  78.5 1.3 %convolution_bitcast_fusion.1 = f32[8,128,128]{1,2,0:T(8,128)S(1)} fusion(f32[2,128,8,128]{1,3,0,2:T(8,128)S(1)} %get-tuple-element.17, f32[2,128,8,128]{1,3,0,2:T(8,128)S(1)} %copy.87, f32[8,128]{1,0:T(8,128)S(1)} %convert_element_type.75, bf16[128,2,2,128]{0,3,2,1:T(8,128)(2,1)} %bitcast.120), kind=kOutput, calls=%fused_computation.7 | convolution fusion | flops 67895296 | bytes 2691072 | tf_op jit(solution)/shard_map/shij,csh->ijc/dot_general | solution.py:97
  79.8 0.0 copy-done.6
  79.8 0.0 copy-start.2
  79.9 0.0 copy-start.4
  79.9 0.0 copy-start.8
  79.9 0.5 fusion.9
  80.3 0.5 copy-done.2
  80.9 0.1 copy-done.4
  81.0 0.2 copy-done.8
  81.1 0.3 fusion.65
  81.5 0.1 fusion.22
  81.6 0.8 %copy.90 = bf16[8,128,128]{2,1,0:T(8,128)(2,1)} copy(bf16[8,128,128]{1,2,0:T(8,128)(2,1)S(1)} %fusion.22) | data formatting | bytes 524288
  (11 shorter events, 0.2 us)
Async XLA Ops:
  0.6 41.8 %copy-start = (bf16[128,128]{1,0:T(8,128)(2,1)S(1)}, bf16[128,128]{1,0:T(8,128)(2,1)}, u32[]{:S(2)}) copy-start(bf16[128,128]{1,0:T(8,128)(2,1)} %param.16) | copy-start | bytes 98308
  0.6 1.8 %copy-start.9 = (bf16[8,128,128]{2,1,0:T(8,128)(2,1)S(1)}, bf16[8,128,128]{2,1,0:T(8,128)(2,1)}, u32[]{:S(2)}) copy-start(bf16[8,128,128]{2,1,0:T(8,128)(2,1)} %param.10) | copy-start | bytes 786436
  2.4 1.4 %copy-start.5 = (bf16[128,512]{0,1:T(8,128)(2,1)}, bf16[128,512]{0,1:T(8,128)(2,1)S(1)}, u32[]{:S(2)}) copy-start(bf16[128,512]{0,1:T(8,128)(2,1)S(1)} %copy.69) | copy-start | bytes 393220
  2.8 0.7 copy-start.11
  2.8 0.7 copy-start.12
  41.3 0.8 copy-start.10
  41.4 0.7 copy-start.13
  41.4 0.7 copy-start.14
  42.4 1.2 %copy-start.7 = (f32[8,128,128]{2,1,0:T(8,128)}, f32[8,128,128]{2,1,0:T(8,128)S(1)}, u32[]{:S(2)}) copy-start(f32[8,128,128]{2,1,0:T(8,128)S(1)} %fusion.34) | copy-start | bytes 1572868
  42.4 1.1 %copy-start.3 = (bf16[8,128,128]{2,1,0:T(8,128)(2,1)S(1)}, bf16[8,128,128]{2,1,0:T(8,128)(2,1)}, u32[]{:S(2)}) copy-start(bf16[8,128,128]{2,1,0:T(8,128)(2,1)} %param.12) | copy-start | bytes 786436
  43.6 0.8 copy-start.1
  78.5 1.3 %copy-start.6 = (bf16[128,512]{0,1:T(8,128)(2,1)S(1)}, bf16[128,512]{0,1:T(8,128)(2,1)}, u32[]{:S(2)}) copy-start(bf16[128,512]{0,1:T(8,128)(2,1)} %copy-done.5) | copy-start | bytes 393220
  79.8 1.0 %copy-start.2 = (f32[8,128,128]{2,1,0:T(8,128)S(1)}, f32[8,128,128]{2,1,0:T(8,128)}, u32[]{:S(2)}) copy-start(f32[8,128,128]{2,1,0:T(8,128)} %copy-done.1) | copy-start | bytes 1572868
  79.9 1.1 %copy-start.4 = (bf16[8,128,128]{2,1,0:T(8,128)(2,1)S(1)}, bf16[8,128,128]{2,1,0:T(8,128)(2,1)}, u32[]{:S(2)}) copy-start(bf16[8,128,128]{2,1,0:T(8,128)(2,1)} %param.12) | copy-start | bytes 786436
  79.9 1.3 %copy-start.8 = (f32[8,128,128]{2,1,0:T(8,128)S(1)}, f32[8,128,128]{2,1,0:T(8,128)}, u32[]{:S(2)}) copy-start(f32[8,128,128]{2,1,0:T(8,128)} %copy-done.7) | copy-start | bytes 1572868
where the time goes:
time: 83 us; the launch traced here: 82.5 us
  blocking collectives  65.6 us (79%)
  local copies, waits for them, and re-layouts  8.73 us (11%)
  matrix products  5.61 us (7%)
  other arithmetic  1.49 us (2%)
  between operations  1.01 us (1%)
    all_to_all x1, blocking collectives, per_device(): lax.all_to_all(both_sides, 'row', split_axis=1, concat_axis=2, tiled=True)  21.6 us
    all_to_all x1, blocking collectives, per_device(): lax.all_to_all(grad_local, 'row', split_axis=2, concat_axis=1, tiled=True)  17.2 us
    all_to_all x1, blocking collectives, per_device(): lax.all_to_all(product, 'row', split_axis=1, concat_axis=0, tiled=True)  13.9 us
    all_to_all x1, blocking collectives, per_device(): lax.all_to_all(grad_mixed, 'row', split_axis=0, concat_axis=1, tiled=True)  12.8 us
    unnamed x33, local copies, waits for them, and re-layouts  4.73 us
    convert_element_type x2, local copies, waits for them, and re-layouts, per_device(): side_float = grad_sides.astype(jnp.float32) * mask_float  2.68 us

commit v1 on v0

--- a/solution.py
+++ b/solution.py
@@ -4,6 +4,9 @@
 from jax.sharding import PartitionSpec as P
 
 EPSILON = 1e-05
+CORE, CHIP_X, Z_LOW, Z_HIGH = 1, 2, 4, 8
+LEFT_OFFSETS = (0, CHIP_X, Z_LOW, Z_LOW | CHIP_X)
+RIGHT_OFFSETS = (0, CORE, Z_HIGH, Z_HIGH | CORE)
 
 
 def norm_stats(values, reduce_axis):
@@ -32,7 +35,123 @@
     return jnp.stack([grad_left, grad_right]).astype(jnp.bfloat16)
 
 
-def per_device(
+def swap(values, offset):
+    return lax.ppermute(values, "row", [(s, s ^ offset) for s in range(16)])
+
+
+def reduce_pair(parts, far, near):
+    to_far = swap(parts[3], near).astype(jnp.float32) + parts[2].astype(jnp.float32)
+    from_far = swap(to_far.astype(jnp.bfloat16), far).astype(jnp.float32)
+    from_near = swap(parts[1], near).astype(jnp.float32)
+    return parts[0].astype(jnp.float32) + from_near + from_far
+
+
+def blocks_device(
+    pair_rep,
+    pair_mask,
+    cotangent,
+    in_gain,
+    in_bias,
+    proj_weight,
+    gate_weight,
+    mid_gain,
+    mid_bias,
+    out_weight,
+):
+    rows, cols, width = pair_rep.shape
+    hidden = out_weight.shape[0]
+    me = lax.axis_index("row")
+    weights_four = proj_weight.reshape(width, 2, 2, hidden)
+    mask_float = pair_mask.astype(jnp.float32)
+    normed_in, inverse_in = norm_stats(pair_rep.astype(jnp.float32), 2)
+    scaled_in = (normed_in * in_gain + in_bias).astype(jnp.bfloat16)
+    gate_pre = jnp.einsum(
+        "ijc,csh->shij", scaled_in, weights_four[:, :, 0], preferred_element_type=jnp.float32
+    )
+    value_pre = jnp.einsum(
+        "ijc,csh->shij", scaled_in, weights_four[:, :, 1], preferred_element_type=jnp.float32
+    )
+    sigmoid_gate = jax.nn.sigmoid(gate_pre)
+    both_sides = (sigmoid_gate * value_pre * mask_float).astype(jnp.bfloat16)
+    left, right = both_sides[0], both_sides[1]
+    left_far = swap(left, Z_LOW)
+    right_far = swap(right, Z_HIGH)
+    left_near = swap(left, CHIP_X)
+    right_near = swap(right, CORE)
+    left_both = swap(left_far, CHIP_X)
+    right_both = swap(right_far, CORE)
+
+    gate_sig = jax.nn.sigmoid(
+        jnp.einsum("ijc,cd->ijd", scaled_in, gate_weight, preferred_element_type=jnp.float32)
+    )
+    grad_out = cotangent.astype(jnp.float32)
+    grad_update = (grad_out * gate_sig).astype(jnp.bfloat16)
+
+    def columns_for(offset):
+        starts = [((me ^ offset) ^ other) * rows for other in RIGHT_OFFSETS]
+        pieces = [lax.dynamic_slice_in_dim(grad_update, s, rows, 1) for s in starts]
+        return jnp.concatenate(pieces, axis=1)
+
+    grad_block = jnp.concatenate(
+        [columns_for(0)] + [swap(columns_for(o), o) for o in LEFT_OFFSETS[1:]], axis=0
+    )
+
+    left_block = jnp.concatenate([left, left_near, left_far, left_both], axis=1)
+    right_block = jnp.concatenate([right, right_near, right_far, right_both], axis=1)
+    mixed = forward_products(left_block, right_block).astype(jnp.bfloat16)
+    normed_mid, inverse_mid = norm_stats(mixed.astype(jnp.float32), 0)
+    scaled_mid = (normed_mid * mid_gain[:, None, None] + mid_bias[:, None, None]).astype(
+        jnp.bfloat16
+    )
+    update_block = jnp.einsum(
+        "hij,hc->ijc", scaled_mid, out_weight, preferred_element_type=jnp.float32
+    ).astype(jnp.bfloat16)
+    grad_scaled_mid = jnp.einsum(
+        "ijc,hc->hij", grad_block, out_weight, preferred_element_type=jnp.float32
+    )
+    grad_mixed = norm_back(
+        grad_scaled_mid * mid_gain[:, None, None], normed_mid, inverse_mid, 0
+    ).astype(jnp.bfloat16)
+    grad_left, grad_right = backward_products(grad_mixed, left_block, right_block)
+    left_parts = jnp.split(grad_left, 4, axis=1)
+    right_parts = jnp.split(grad_right, 4, axis=1)
+    grad_left = reduce_pair(left_parts, Z_LOW, CHIP_X)
+    grad_right = reduce_pair(right_parts, Z_HIGH, CORE)
+
+    update_parts = jnp.split(update_block, 4, axis=0)
+    update_parts = [update_parts[0]] + [
+        swap(p, o) for p, o in zip(update_parts[1:], LEFT_OFFSETS[1:])
+    ]
+    update = jnp.zeros((rows, cols, width), jnp.bfloat16)
+    for part, offset in zip(update_parts, LEFT_OFFSETS):
+        for place, other in enumerate(RIGHT_OFFSETS):
+            piece = part[:, place * rows : (place + 1) * rows]
+            update = lax.dynamic_update_slice_in_dim(
+                update, piece, ((me ^ offset) ^ other) * rows, 1
+            )
+    update = update.astype(jnp.float32)
+    output = (gate_sig * update).astype(jnp.bfloat16)
+    grad_gate = (grad_out * update * gate_sig * (1.0 - gate_sig)).astype(jnp.bfloat16)
+
+    side_float = jnp.stack([grad_left, grad_right]) * mask_float
+    grad_value = (side_float * sigmoid_gate).astype(jnp.bfloat16)
+    grad_gate_pre = (side_float * value_pre * sigmoid_gate * (1.0 - sigmoid_gate)).astype(
+        jnp.bfloat16
+    )
+    grad_scaled = jnp.einsum(
+        "shij,csh->ijc", grad_gate_pre, weights_four[:, :, 0], preferred_element_type=jnp.float32
+    )
+    grad_scaled = grad_scaled + jnp.einsum(
+        "shij,csh->ijc", grad_value, weights_four[:, :, 1], preferred_element_type=jnp.float32
+    )
+    grad_scaled = grad_scaled + jnp.einsum(
+        "ijd,cd->ijc", grad_gate, gate_weight, preferred_element_type=jnp.float32
+    )
+    grad_pair = norm_back(grad_scaled * in_gain, normed_in, inverse_in, 2).astype(jnp.bfloat16)
+    return (output, grad_pair)
+
+
+def channels_device(
     pair_rep,
     pair_mask,
     cotangent,
@@ -105,6 +224,7 @@
 
 
 def solution(mesh):
+    blocks = mesh.shape["row"] == 16 and mesh.shape["col"] == 1
     placed = (
         P(("grp", "row"), "col", None),
         P(("grp", "row"), "col"),
@@ -118,7 +238,7 @@
         P(),
     )
     return jax.shard_map(
-        per_device,
+        blocks_device if blocks else channels_device,
         mesh=mesh,
         in_specs=placed,
         out_specs=(P(("grp", "row"), "col", None), P(("grp", "row"), "col", None)),

time: 83 us -> 98.5 us (1.19)
  blocking collectives: 65.6 us -> 0 us
  waiting for transfers between devices: 0 us -> 43.6 us
  starting transfers between devices: 0 us -> 21.6 us
  local copies, waits for them, and re-layouts: 8.73 us -> 16.7 us
  other arithmetic: 1.49 us -> 6.74 us
  matrix products: 5.61 us -> 8.24 us
    all_to_all x4 -> x0, blocking collectives: 65.6 us -> none  [the longest x1 21.6 us: per_device(): lax.all_to_all(both_sides, 'row', split_axis=1, concat_axis=2, tiled=True)]
    ppermute x0 -> x18, waiting for transfers between devices: none -> 43.6 us  [swap(): return lax.ppermute(values, 'row', [(s, s ^ offset) for s in range(16)])]
    ppermute x0 -> x18, starting transfers between devices: none -> 21.6 us  [swap(): return lax.ppermute(values, 'row', [(s, s ^ offset) for s in range(16)])]
    dot_general x0 -> x3, local copies, waits for them, and re-layouts: none -> 4.7 us  [the longest x1 1.94 us: backward_products(): jnp.einsum('hij,hjk->hik', grad_full, right_chan, preferred_element_type=...]
    convert_element_type x5, other arithmetic: 1.19 us -> 3.3 us  [the longest x1 1.31 us: blocks_device(): grad_mixed = norm_back(grad_scaled_mid * mid_gain[:, None, None], normed_...]
    concatenate x0 -> x2, local copies, waits for them, and re-layouts: none -> 1.94 us  [the longest x1 0.98 us: blocks_device(): left_block = jnp.concatenate([left, left_near, left_far, left_both], axis=1)]
    concatenate x0 -> x5, other arithmetic: none -> 1.49 us  [the longest x1 1.32 us: blocks_device(): left_block = jnp.concatenate([left, left_near, left_far, left_both], axis=1)]
    dot_general x1, matrix products: 0.22 us -> 1.52 us  [backward_products(): jnp.einsum('hij,hjk->hik', grad_full, right_chan, preferred_element_type=...]
  transfers between devices with their start and end apart: 0 -> 18, of which waited for: 0 -> 9; matrix products, arithmetic and copies ran while one was open for 0% -> 4% of each run, Pallas kernels for 0% -> 0%
where the time goes in v1:
time: 98.5 us; the launch traced here: 98.1 us
  waiting for transfers between devices  43.6 us (44%)
  starting transfers between devices  21.6 us (22%)
  local copies, waits for them, and re-layouts  16.7 us (17%)
  matrix products  8.24 us (8%)
  other arithmetic  6.74 us (7%)
  between operations  1.23 us (1%)
    ppermute x18, waiting for transfers between devices, swap(): return lax.ppermute(values, 'row', [(s, s ^ offset) for s in range(16)])  43.6 us
    ppermute x18, starting transfers between devices, swap(): return lax.ppermute(values, 'row', [(s, s ^ offset) for s in range(16)])  21.6 us
    unnamed x51, local copies, waits for them, and re-layouts  5.99 us
    convert_element_type x1, local copies, waits for them, and re-layouts, blocks_device(): grad_mixed = norm_back(grad_scaled_mid * mid_gain[:, None, None], normed_...  2.68 us
  transfers between devices with their start and end apart: 18, of which 9 were waited for; matrix products, arithmetic and copies ran while one was open for 4% of the time, Pallas kernels for 0%

profile of v1, /device:TPU:0, one launch (start us, length us, event | category | flops | bytes accessed | tf_op | source)
XLA Modules:
  0.0 98.1 jit_solution(978437186677724495)
XLA Ops:
  0.7 0.7 convert_element_type.90
  1.4 1.0 %copy.49 = bf16[128,512]{0,1:T(8,128)(2,1)S(1)} copy(bf16[128,512]{1,0:T(8,128)(2,1)} %param.15) | data formatting | bytes 262144 | tf_op args[5]
  2.4 0.2 copy.47
  2.7 0.1 fusion.33
  2.8 0.6 copy-done.19
  3.5 0.4 convolution_bitcast_fusion
  3.9 1.6 %multiply_convert_fusion.2 = (bf16[2,128,8,128]{1,3,0,2:T(8,128)(2,1)S(1)}, f32[2,128,8,128]{1,3,0,2:T(8,128)}) fusion(f32[2,128,8,128]{1,3,0,2:T(8,128)S(1)} %convolution_bitcast_fusion, f32[8,128]{1,0:T(8,128)S(1)} %convert_element_type.90, bf16[128,2,2,128]{0,3,2,1:T(8,128)(2,1)S(1)} %bitcast.72, f32[128]{0:T(128)S(1)} %copy-done.20, ...), kind=kOutput, calls=%fused_computation.23 | convolution fusion | flops 69468160 | bytes 2962432 | tf_op jit(solution)/shard_map/ijc,csh->shij/dot_general | solution.py:68
  5.5 4.1 %collective-permute-start.4 = (bf16[128,8,128]{0,2,1:T(8,128)(2,1)S(1)}, bf16[128,8,128]{0,2,1:T(8,128)(2,1)S(1)}, u32[]{:S(2)}, u32[]{:S(2)}) collective-permute-start(bf16[128,8,128]{0,2,1:T(8,128)(2,1)S(1)} %get-tuple-element.18), channel_id=1, source_target_pairs={{0,8},{1,9},{2,10},{3,11},{4,12},{5,13},{6,14},{7,15},{8,0},{9,1},... | collective-permute-start | bytes 786440 | tf_op jit(solution)/shard_map/ppermute | solution.py:39
  9.6 1.6 %collective-permute-start.1 = (bf16[128,8,128]{0,2,1:T(8,128)(2,1)S(1)}, bf16[128,8,128]{0,2,1:T(8,128)(2,1)S(1)}, u32[]{:S(2)}, u32[]{:S(2)}) collective-permute-start(bf16[128,8,128]{0,2,1:T(8,128)(2,1)S(1)} %get-tuple-element.19), channel_id=1, source_target_pairs={{0,4},{1,5},{2,6},{3,7},{4,0},{5,1},{6,2},{7,3},{8,12},{9,13},{10,... | collective-permute-start | bytes 786440 | tf_op jit(solution)/shard_map/ppermute | solution.py:39
  11.2 10.4 %collective-permute-done.4 = bf16[128,8,128]{0,2,1:T(8,128)(2,1)S(1)} collective-permute-done((bf16[128,8,128]{0,2,1:T(8,128)(2,1)S(1)}, bf16[128,8,128]{0,2,1:T(8,128)(2,1)S(1)}, u32[]{:S(2)}, u32[]{:S(2)}) %collective-permute-start.4) | collective-permute-done | bytes 262176 | tf_op jit(solution)/shard_map/ppermute | solution.py:39
  21.6 1.5 %collective-permute-start = (bf16[128,8,128]{0,2,1:T(8,128)(2,1)S(1)}, bf16[128,8,128]{0,2,1:T(8,128)(2,1)S(1)}, u32[]{:S(2)}, u32[]{:S(2)}) collective-permute-start(bf16[128,8,128]{0,2,1:T(8,128)(2,1)S(1)} %get-tuple-element.19), channel_id=1, source_target_pairs={{0,2},{1,3},{2,0},{3,1},{4,6},{5,7},{6,4},{7,5},{8,10},{9,11},{10,... | collective-permute-start | bytes 786440 | tf_op jit(solution)/shard_map/ppermute | solution.py:39
  23.2 0.5 collective-permute-start.2
  23.7 0.1 pad_maximum_fusion.1
  23.9 1.0 copy.55
  24.9 5.9 %collective-permute-done = bf16[128,8,128]{0,2,1:T(8,128)(2,1)S(1)} collective-permute-done((bf16[128,8,128]{0,2,1:T(8,128)(2,1)S(1)}, bf16[128,8,128]{0,2,1:T(8,128)(2,1)S(1)}, u32[]{:S(2)}, u32[]{:S(2)}) %collective-permute-start) | collective-permute-done | bytes 262176 | tf_op jit(solution)/shard_map/ppermute | solution.py:39
  30.7 0.7 copy-done.18
  31.4 4.6 %collective-permute-done.2 = bf16[128,8,128]{0,2,1:T(8,128)(2,1)} collective-permute-done((bf16[128,8,128]{0,2,1:T(8,128)(2,1)S(1)}, bf16[128,8,128]{0,2,1:T(8,128)(2,1)}, u32[]{:S(2)}, u32[]{:S(2)}) %collective-permute-start.2) | collective-permute-done | bytes 262176 | tf_op jit(solution)/shard_map/ppermute | solution.py:39
  36.1 1.3 %pad_maximum_fusion = bf16[128,32,128]{0,2,1:T(8,128)(2,1)S(1)} fusion(bf16[128,8,128]{0,2,1:T(8,128)(2,1)} %collective-permute-done.2, bf16[128,8,128]{0,2,1:T(8,128)(2,1)} %copy-done.17, bf16[128,8,128]{0,2,1:T(8,128)(2,1)} %copy-done.18, bf16[128,8,128]{0,2,1:T(8,128)(2,1)} %copy-done.9), kind=kLoop, calls=%fused_computation.18 | loop fusion | flops 1572864 | bytes 2097152 | tf_op jit(solution)/shard_map/concatenate | solution.py:99
  37.4 1.0 copy.54
  38.4 0.7 fusion.81
  39.0 1.8 %copy.56 = bf16[128,32,32]{0,2,1:T(8,128)(2,1)} copy(bf16[128,32,32]{2,1,0:T(8,128)(2,1)S(1)} %fusion.81) | data formatting | bytes 524288 | tf_op jit(solution)/shard_map/hik,hjk->hij/dot_general | solution.py:25
  40.8 1.2 %convert_reduce_fusion = f32[32,32]{1,0:T(8,128)S(1)} fusion(bf16[128,32,32]{0,2,1:T(8,128)(2,1)} %copy.56), kind=kLoop, calls=%fused_computation.28 | loop fusion | flops 261120 | bytes 266240 | tf_op jit(solution)/shard_map/reduce_sum | solution.py:13
  42.1 0.4 fusion.26
  42.5 0.2 copy-done.22
  42.8 0.5 copy-done.21
  43.3 0.4 convolution_convert_fusion
  43.7 1.6 %collective-permute-start.8 = (bf16[8,32,128]{2,1,0:T(8,128)(2,1)S(1)}, bf16[8,32,128]{2,1,0:T(8,128)(2,1)S(1)}, u32[]{:S(2)}, u32[]{:S(2)}) collective-permute-start(bf16[8,32,128]{2,1,0:T(8,128)(2,1)S(1)} %get-tuple-element.36), channel_id=1, source_target_pairs={{0,6},{1,7},{2,4},{3,5},{4,2},{5,3},{6,0},{7,1},{8,14},{9,15},{10,... | collective-permute-start | bytes 196616 | tf_op jit(solution)/shard_map/ppermute | solution.py:39
  45.3 1.5 %collective-permute-start.7 = (bf16[8,32,128]{2,1,0:T(8,128)(2,1)S(1)}, bf16[8,32,128]{2,1,0:T(8,128)(2,1)S(1)}, u32[]{:S(2)}, u32[]{:S(2)}) collective-permute-start(bf16[8,32,128]{2,1,0:T(8,128)(2,1)S(1)} %get-tuple-element.37), channel_id=1, source_target_pairs={{0,4},{1,5},{2,6},{3,7},{4,0},{5,1},{6,2},{7,3},{8,12},{9,13},{10,... | collective-permute-start | bytes 196616 | tf_op jit(solution)/shard_map/ppermute | solution.py:39
  46.8 0.5 collective-permute-start.6
  47.4 3.6 %collective-permute-done.6 = bf16[8,32,128]{2,1,0:T(8,128)(2,1)S(1)} collective-permute-done((bf16[8,32,128]{2,1,0:T(8,128)(2,1)S(1)}, bf16[8,32,128]{2,1,0:T(8,128)(2,1)S(1)}, u32[]{:S(2)}, u32[]{:S(2)}) %collective-permute-start.6) | collective-permute-done | bytes 65568 | tf_op jit(solution)/shard_map/ppermute | solution.py:39
  51.3 1.4 %fusion.35 = (bf16[8,128,128]{2,1,0:T(8,128)(2,1)S(1)}, bf16[8,128,128]{2,1,0:T(8,128)(2,1)}, f32[8,128,128]{2,1,0:T(8,128)}) fusion(bf16[8,128,128]{2,1,0:T(8,128)(2,1)S(1)} %copy-done.15, bf16[8,128,128]{2,1,0:T(8,128)(2,1)S(1)} %slice_dynamic-update-slice_fusion, bf16[128,128]{1,0:T(8,128)(2,1)S(1)} %copy-done, bf16[8,128,128]{1,2,0:T(8,128)(2,1)S(1)} %copy.47, ...), kind=kOutput, calls=%fused_computation.56 | convolution fusion | flops 35520512 | bytes 1876992 | tf_op jit(solution)/shard_map/ijc,cd->ijd/dot_general | solution.py:85
  52.8 0.6 collective-permute-start.9
  53.4 0.8 collective-permute-start.10
  54.3 2.3 %collective-permute-start.11 = (bf16[8,32,128]{2,1,0:T(8,128)(2,1)S(1)}, bf16[8,32,128]{2,1,0:T(8,128)(2,1)S(1)}, u32[]{:S(2)}, u32[]{:S(2)}) collective-permute-start(bf16[8,32,128]{2,1,0:T(8,128)(2,1)S(1)} %pad_maximum_fusion.4), channel_id=1, source_target_pairs={{0,6},{1,7},{2,4},{3,5},{4,2},{5,3},{6,0},{7,1},{8,14},{9,15},{10,... | collective-permute-start | bytes 196616 | tf_op jit(solution)/shard_map/ppermute | solution.py:39
  56.6 1.2 %collective-permute-done.9 = bf16[8,32,128]{2,1,0:T(8,128)(2,1)S(1)} collective-permute-done((bf16[8,32,128]{2,1,0:T(8,128)(2,1)S(1)}, bf16[8,32,128]{2,1,0:T(8,128)(2,1)S(1)}, u32[]{:S(2)}, u32[]{:S(2)}) %collective-permute-start.9) | collective-permute-done | bytes 65568 | tf_op jit(solution)/shard_map/ppermute | solution.py:39
  57.8 1.7 %collective-permute-done.11 = bf16[8,32,128]{2,1,0:T(8,128)(2,1)S(1)} collective-permute-done((bf16[8,32,128]{2,1,0:T(8,128)(2,1)S(1)}, bf16[8,32,128]{2,1,0:T(8,128)(2,1)S(1)}, u32[]{:S(2)}, u32[]{:S(2)}) %collective-permute-start.11) | collective-permute-done | bytes 65568 | tf_op jit(solution)/shard_map/ppermute | solution.py:39
  59.5 0.6 fusion.77
  60.2 1.3 %fusion.25 = bf16[128,32,32]{0,2,1:T(8,128)(2,1)} fusion(bf16[128,32,32]{0,2,1:T(8,128)(2,1)S(1)} %copy-done.4, f32[128,32,32]{0,2,1:T(8,128)S(1)} %get-tuple-element.42, f32[32,32]{1,0:T(8,128)S(1)} %get-tuple-element.44, f32[32,32]{1,0:T(8,128)S(1)} %get-tuple-element.45, f32[32,32]{1,0:T(8,128)S(1)} %add_rsqrt_fusion, ...), kind=kLoop, calls=%fused_computation.46 | loop fusion | flops 1048576 | bytes 1064960 | tf_op jit(solution)/shard_map/convert_element_type | solution.py:114
  61.5 2.7 %copy.60 = bf16[128,32,32]{1,2,0:T(8,128)(2,1)S(1)} copy(bf16[128,32,32]{0,2,1:T(8,128)(2,1)} %fusion.25) | data formatting | bytes 524288 | tf_op jit(solution)/shard_map/convert_element_type | solution.py:114
  64.2 1.5 %fusion.82 = bf16[128,32,128]{2,1,0:T(8,128)(2,1)} fusion(bf16[128,32,32]{1,2,0:T(8,128)(2,1)S(1)} %copy.60, bf16[128,32,128]{2,1,0:T(8,128)(2,1)S(1)} %copy.55), kind=kOutput, calls=%fused_computation.149 | convolution fusion | flops 33554432 | bytes 2359296 | tf_op jit(solution)/shard_map/hij,hjk->hik/dot_general | solution.py:29
  65.7 1.9 %copy.59 = bf16[128,32,128]{0,2,1:T(8,128)(2,1)S(1)} copy(bf16[128,32,128]{2,1,0:T(8,128)(2,1)} %fusion.82) | data formatting | bytes 2097152 | tf_op jit(solution)/shard_map/hij,hjk->hik/dot_general | solution.py:29
  67.6 0.9 fusion.78
  68.6 0.2 copy-done.5
  68.8 1.3 %collective-permute-start.13 = (bf16[128,8,128]{0,2,1:T(8,128)(2,1)}, bf16[128,8,128]{0,2,1:T(8,128)(2,1)}, u32[]{:S(2)}, u32[]{:S(2)}) collective-permute-start(bf16[128,8,128]{0,2,1:T(8,128)(2,1)} %get-tuple-element.13), channel_id=1, source_target_pairs={{0,2},{1,3},{2,0},{3,1},{4,6},{5,7},{6,4},{7,5},{8,10},{9,11},{10,... | collective-permute-start | bytes 786440 | tf_op jit(solution)/shard_map/ppermute | solution.py:39
  70.1 0.4 fusion.83
  70.5 1.0 %copy.62 = bf16[128,32,128]{0,2,1:T(8,128)(2,1)S(1)} copy(bf16[128,32,128]{2,1,0:T(8,128)(2,1)S(1)} %fusion.83) | data formatting | bytes 2097152 | tf_op jit(solution)/shard_map/hij,hik->hjk/dot_general | solution.py:32
  71.7 0.8 collective-permute-start.12
  72.4 3.5 %collective-permute-done.13 = bf16[128,8,128]{0,2,1:T(8,128)(2,1)} collective-permute-done((bf16[128,8,128]{0,2,1:T(8,128)(2,1)}, bf16[128,8,128]{0,2,1:T(8,128)(2,1)}, u32[]{:S(2)}, u32[]{:S(2)}) %collective-permute-start.13) | collective-permute-done | bytes 262176 | tf_op jit(solution)/shard_map/ppermute | solution.py:39
  76.0 1.0 %add_convert_fusion.1 = bf16[128,8,128]{0,2,1:T(8,128)(2,1)S(1)} fusion(bf16[128,8,128]{0,2,1:T(8,128)(2,1)} %collective-permute-done.13, bf16[128,32,128]{0,2,1:T(8,128)(2,1)S(1)} %copy-done.6), kind=kLoop, calls=%fused_computation.64 | loop fusion | flops 524288 | bytes 786432 | tf_op jit(solution)/shard_map/convert_element_type | solution.py:44
  77.0 1.2 %collective-permute-start.14 = (bf16[128,8,128]{0,2,1:T(8,128)(2,1)S(1)}, bf16[128,8,128]{0,2,1:T(8,128)(2,1)S(1)}, u32[]{:S(2)}, u32[]{:S(2)}) collective-permute-start(bf16[128,8,128]{0,2,1:T(8,128)(2,1)S(1)} %add_convert_fusion.1), channel_id=1, source_target_pairs={{0,4},{1,5},{2,6},{3,7},{4,0},{5,1},{6,2},{7,3},{8,12},{9,13},{10,... | collective-permute-start | bytes 786440 | tf_op jit(solution)/shard_map/ppermute | solution.py:39
  78.2 0.1 add_convert_fusion
  78.3 3.2 %collective-permute-start.17 = (bf16[128,8,128]{0,2,1:T(8,128)(2,1)S(1)}, bf16[128,8,128]{0,2,1:T(8,128)(2,1)S(1)}, u32[]{:S(2)}, u32[]{:S(2)}) collective-permute-start(bf16[128,8,128]{0,2,1:T(8,128)(2,1)S(1)} %add_convert_fusion), channel_id=1, source_target_pairs={{0,8},{1,9},{2,10},{3,11},{4,12},{5,13},{6,14},{7,15},{8,0},{9,1},... | collective-permute-start | bytes 786440 | tf_op jit(solution)/shard_map/ppermute | solution.py:39
  81.6 2.5 %collective-permute-done.14 = bf16[128,8,128]{0,2,1:T(8,128)(2,1)S(1)} collective-permute-done((bf16[128,8,128]{0,2,1:T(8,128)(2,1)S(1)}, bf16[128,8,128]{0,2,1:T(8,128)(2,1)S(1)}, u32[]{:S(2)}, u32[]{:S(2)}) %collective-permute-start.14) | collective-permute-done | bytes 262176 | tf_op jit(solution)/shard_map/ppermute | solution.py:39
  84.1 0.1 add_bitcast_fusion.1
  84.2 9.9 %collective-permute-done.17 = bf16[128,8,128]{0,2,1:T(8,128)(2,1)S(1)} collective-permute-done((bf16[128,8,128]{0,2,1:T(8,128)(2,1)S(1)}, bf16[128,8,128]{0,2,1:T(8,128)(2,1)S(1)}, u32[]{:S(2)}, u32[]{:S(2)}) %collective-permute-start.17) | collective-permute-done | bytes 262176 | tf_op jit(solution)/shard_map/ppermute | solution.py:39
  94.2 0.1 add_bitcast_fusion
  94.3 0.4 convolution_bitcast_fusion.1
  94.7 0.8 copy-done.2
  95.5 0.5 fusion.9
  96.0 0.5 copy-done.8
  96.5 0.2 copy-done.12
  96.7 0.3 fusion.76
  97.1 0.1 fusion.32
  97.2 0.9 copy.65
  (85 shorter events, 0.9 us)
Async XLA Ops:
  0.6 50.7 %copy-start = (bf16[128,128]{1,0:T(8,128)(2,1)S(1)}, bf16[128,128]{1,0:T(8,128)(2,1)}, u32[]{:S(2)}) copy-start(bf16[128,128]{1,0:T(8,128)(2,1)} %param.16) | copy-start | bytes 98308
  0.6 1.8 %copy-start.13 = (bf16[8,128,128]{2,1,0:T(8,128)(2,1)S(1)}, bf16[8,128,128]{2,1,0:T(8,128)(2,1)}, u32[]{:S(2)}) copy-start(bf16[8,128,128]{2,1,0:T(8,128)(2,1)} %param.10) | copy-start | bytes 786436
  2.4 1.4 %copy-start.10 = (bf16[128,512]{0,1:T(8,128)(2,1)}, bf16[128,512]{0,1:T(8,128)(2,1)S(1)}, u32[]{:S(2)}) copy-start(bf16[128,512]{0,1:T(8,128)(2,1)S(1)} %copy.49) | copy-start | bytes 393220
  2.8 0.7 copy-start.19
  2.8 0.7 copy-start.20
  3.9 1.6 %copy-start.1 = (f32[2,128,8,128]{1,3,0,2:T(8,128)}, f32[2,128,8,128]{1,3,0,2:T(8,128)S(1)}, u32[]{:S(2)}) copy-start(f32[2,128,8,128]{1,3,0,2:T(8,128)S(1)} %convolution_bitcast_fusion) | copy-start | bytes 3145732
  5.5 18.3 %copy-start.9 = (bf16[128,8,128]{0,2,1:T(8,128)(2,1)}, bf16[128,8,128]{0,2,1:T(8,128)(2,1)S(1)}, u32[]{:S(2)}) copy-start(bf16[128,8,128]{0,2,1:T(8,128)(2,1)S(1)} %get-tuple-element.19) | copy-start | bytes 786436
  5.5 16.1 %collective-permute-start.4 = (bf16[128,8,128]{0,2,1:T(8,128)(2,1)S(1)}, bf16[128,8,128]{0,2,1:T(8,128)(2,1)S(1)}, u32[]{:S(2)}, u32[]{:S(2)}) collective-permute-start(bf16[128,8,128]{0,2,1:T(8,128)(2,1)S(1)} %get-tuple-element.18), channel_id=1, source_target_pairs={{0,8},{1,9},{2,10},{3,11},{4,12},{5,13},{6,14},{7,15},{8,0},{9,1},... | collective-permute-start | bytes 786440 | tf_op jit(solution)/shard_map/ppermute | solution.py:39
  9.6 13.6 %collective-permute-start.1 = (bf16[128,8,128]{0,2,1:T(8,128)(2,1)S(1)}, bf16[128,8,128]{0,2,1:T(8,128)(2,1)S(1)}, u32[]{:S(2)}, u32[]{:S(2)}) collective-permute-start(bf16[128,8,128]{0,2,1:T(8,128)(2,1)S(1)} %get-tuple-element.19), channel_id=1, source_target_pairs={{0,4},{1,5},{2,6},{3,7},{4,0},{5,1},{6,2},{7,3},{8,12},{9,13},{10,... | collective-permute-start | bytes 786440 | tf_op jit(solution)/shard_map/ppermute | solution.py:39
  11.2 12.5 %collective-permute-start.3 = (bf16[128,8,128]{0,2,1:T(8,128)(2,1)S(1)}, bf16[128,8,128]{0,2,1:T(8,128)(2,1)S(1)}, u32[]{:S(2)}, u32[]{:S(2)}) collective-permute-start(bf16[128,8,128]{0,2,1:T(8,128)(2,1)S(1)} %get-tuple-element.18), channel_id=1, source_target_pairs={{0,1},{1,0},{2,3},{3,2},{4,5},{5,4},{6,7},{7,6},{8,9},{9,8},{10,11... | collective-permute-start | bytes 786440 | tf_op jit(solution)/shard_map/ppermute | solution.py:39
  21.6 2.0 %collective-permute-start.5 = (bf16[128,8,128]{0,2,1:T(8,128)(2,1)S(1)}, bf16[128,8,128]{0,2,1:T(8,128)(2,1)S(1)}, u32[]{:S(2)}, u32[]{:S(2)}) collective-permute-start(bf16[128,8,128]{0,2,1:T(8,128)(2,1)S(1)} %collective-permute-done.4), channel_id=1, source_target_pairs={{0,1},{1,0},{2,3},{3,2},{4,5},{5,4},{6,7},{7,6},{8,9},{9,8},{10,11... | collective-permute-start | bytes 786440 | tf_op jit(solution)/shard_map/ppermute | solution.py:39
  21.6 9.1 %collective-permute-start = (bf16[128,8,128]{0,2,1:T(8,128)(2,1)S(1)}, bf16[128,8,128]{0,2,1:T(8,128)(2,1)S(1)}, u32[]{:S(2)}, u32[]{:S(2)}) collective-permute-start(bf16[128,8,128]{0,2,1:T(8,128)(2,1)S(1)} %get-tuple-element.19), channel_id=1, source_target_pairs={{0,2},{1,3},{2,0},{3,1},{4,6},{5,7},{6,4},{7,5},{8,10},{9,11},{10,... | collective-permute-start | bytes 786440 | tf_op jit(solution)/shard_map/ppermute | solution.py:39
  23.2 0.7 copy-start.17
  23.2 12.9 %collective-permute-start.2 = (bf16[128,8,128]{0,2,1:T(8,128)(2,1)S(1)}, bf16[128,8,128]{0,2,1:T(8,128)(2,1)}, u32[]{:S(2)}, u32[]{:S(2)}) collective-permute-start(bf16[128,8,128]{0,2,1:T(8,128)(2,1)S(1)} %collective-permute-done.1), channel_id=1, source_target_pairs={{0,2},{1,3},{2,0},{3,1},{4,6},{5,7},{6,4},{7,5},{8,10},{9,11},{10,... | collective-permute-start | bytes 786440 | tf_op jit(solution)/shard_map/ppermute | solution.py:39
  30.7 0.7 copy-start.18
  40.8 1.2 %copy-start.4 = (bf16[128,32,32]{0,2,1:T(8,128)(2,1)S(1)}, bf16[128,32,32]{0,2,1:T(8,128)(2,1)}, u32[]{:S(2)}) copy-start(bf16[128,32,32]{0,2,1:T(8,128)(2,1)} %copy.56) | copy-start | bytes 786436
  42.1 0.7 copy-start.22
  42.1 0.7 copy-start.23
  42.5 0.8 copy-start.21
  43.7 7.5 %collective-permute-start.8 = (bf16[8,32,128]{2,1,0:T(8,128)(2,1)S(1)}, bf16[8,32,128]{2,1,0:T(8,128)(2,1)S(1)}, u32[]{:S(2)}, u32[]{:S(2)}) collective-permute-start(bf16[8,32,128]{2,1,0:T(8,128)(2,1)S(1)} %get-tuple-element.36), channel_id=1, source_target_pairs={{0,6},{1,7},{2,4},{3,5},{4,2},{5,3},{6,0},{7,1},{8,14},{9,15},{10,... | collective-permute-start | bytes 196616 | tf_op jit(solution)/shard_map/ppermute | solution.py:39
  45.3 5.8 %collective-permute-start.7 = (bf16[8,32,128]{2,1,0:T(8,128)(2,1)S(1)}, bf16[8,32,128]{2,1,0:T(8,128)(2,1)S(1)}, u32[]{:S(2)}, u32[]{:S(2)}) collective-permute-start(bf16[8,32,128]{2,1,0:T(8,128)(2,1)S(1)} %get-tuple-element.37), channel_id=1, source_target_pairs={{0,4},{1,5},{2,6},{3,7},{4,0},{5,1},{6,2},{7,3},{8,12},{9,13},{10,... | collective-permute-start | bytes 196616 | tf_op jit(solution)/shard_map/ppermute | solution.py:39
  46.8 4.3 %collective-permute-start.6 = (bf16[8,32,128]{2,1,0:T(8,128)(2,1)S(1)}, bf16[8,32,128]{2,1,0:T(8,128)(2,1)S(1)}, u32[]{:S(2)}, u32[]{:S(2)}) collective-permute-start(bf16[8,32,128]{2,1,0:T(8,128)(2,1)S(1)} %get-tuple-element.38), channel_id=1, source_target_pairs={{0,2},{1,3},{2,0},{3,1},{4,6},{5,7},{6,4},{7,5},{8,10},{9,11},{10,... | collective-permute-start | bytes 196616 | tf_op jit(solution)/shard_map/ppermute | solution.py:39
  47.3 4.0 %copy-start.15 = (bf16[8,128,128]{2,1,0:T(8,128)(2,1)S(1)}, bf16[8,128,128]{2,1,0:T(8,128)(2,1)}, u32[]{:S(2)}) copy-start(bf16[8,128,128]{2,1,0:T(8,128)(2,1)} %param.12) | copy-start | bytes 786436
  51.3 1.4 %copy-start.7 = (bf16[8,128,128]{2,1,0:T(8,128)(2,1)}, bf16[8,128,128]{2,1,0:T(8,128)(2,1)S(1)}, u32[]{:S(2)}) copy-start(bf16[8,128,128]{2,1,0:T(8,128)(2,1)S(1)} %slice_dynamic-update-slice_fusion) | copy-start | bytes 786436
  52.8 4.9 %collective-permute-start.9 = (bf16[8,32,128]{2,1,0:T(8,128)(2,1)S(1)}, bf16[8,32,128]{2,1,0:T(8,128)(2,1)S(1)}, u32[]{:S(2)}, u32[]{:S(2)}) collective-permute-start(bf16[8,32,128]{2,1,0:T(8,128)(2,1)S(1)} %pad_maximum_fusion.2), channel_id=1, source_target_pairs={{0,2},{1,3},{2,0},{3,1},{4,6},{5,7},{6,4},{7,5},{8,10},{9,11},{10,... | collective-permute-start | bytes 196616 | tf_op jit(solution)/shard_map/ppermute | solution.py:39
  53.4 4.3 %collective-permute-start.10 = (bf16[8,32,128]{2,1,0:T(8,128)(2,1)S(1)}, bf16[8,32,128]{2,1,0:T(8,128)(2,1)S(1)}, u32[]{:S(2)}, u32[]{:S(2)}) collective-permute-start(bf16[8,32,128]{2,1,0:T(8,128)(2,1)S(1)} %pad_maximum_fusion.3), channel_id=1, source_target_pairs={{0,4},{1,5},{2,6},{3,7},{4,0},{5,1},{6,2},{7,3},{8,12},{9,13},{10,... | collective-permute-start | bytes 196616 | tf_op jit(solution)/shard_map/ppermute | solution.py:39
  54.3 5.2 %collective-permute-start.11 = (bf16[8,32,128]{2,1,0:T(8,128)(2,1)S(1)}, bf16[8,32,128]{2,1,0:T(8,128)(2,1)S(1)}, u32[]{:S(2)}, u32[]{:S(2)}) collective-permute-start(bf16[8,32,128]{2,1,0:T(8,128)(2,1)S(1)} %pad_maximum_fusion.4), channel_id=1, source_target_pairs={{0,6},{1,7},{2,4},{3,5},{4,2},{5,3},{6,0},{7,1},{8,14},{9,15},{10,... | collective-permute-start | bytes 196616 | tf_op jit(solution)/shard_map/ppermute | solution.py:39
  67.6 1.1 %copy-start.5 = (bf16[128,32,128]{0,2,1:T(8,128)(2,1)}, bf16[128,32,128]{0,2,1:T(8,128)(2,1)S(1)}, u32[]{:S(2)}) copy-start(bf16[128,32,128]{0,2,1:T(8,128)(2,1)S(1)} %copy.59) | copy-start | bytes 3145732
  68.8 7.2 %collective-permute-start.13 = (bf16[128,8,128]{0,2,1:T(8,128)(2,1)}, bf16[128,8,128]{0,2,1:T(8,128)(2,1)}, u32[]{:S(2)}, u32[]{:S(2)}) collective-permute-start(bf16[128,8,128]{0,2,1:T(8,128)(2,1)} %get-tuple-element.13), channel_id=1, source_target_pairs={{0,2},{1,3},{2,0},{3,1},{4,6},{5,7},{6,4},{7,5},{8,10},{9,11},{10,... | collective-permute-start | bytes 786440 | tf_op jit(solution)/shard_map/ppermute | solution.py:39
  70.5 1.1 %copy-start.14 = (bf16[128,8,128]{0,2,1:T(8,128)(2,1)S(1)}, bf16[128,8,128]{0,2,1:T(8,128)(2,1)}, u32[]{:S(2)}) copy-start(bf16[128,8,128]{0,2,1:T(8,128)(2,1)} %get-tuple-element.12) | copy-start | bytes 786436
  71.5 4.4 %copy-start.6 = (bf16[128,32,128]{0,2,1:T(8,128)(2,1)S(1)}, bf16[128,32,128]{0,2,1:T(8,128)(2,1)}, u32[]{:S(2)}) copy-start(bf16[128,32,128]{0,2,1:T(8,128)(2,1)} %copy-done.5) | copy-start | bytes 3145732
  71.6 6.7 %collective-permute-start.16 = (bf16[128,8,128]{0,2,1:T(8,128)(2,1)S(1)}, bf16[128,8,128]{0,2,1:T(8,128)(2,1)S(1)}, u32[]{:S(2)}, u32[]{:S(2)}) collective-permute-start(bf16[128,8,128]{0,2,1:T(8,128)(2,1)S(1)} %get-tuple-element.15), channel_id=1, source_target_pairs={{0,1},{1,0},{2,3},{3,2},{4,5},{5,4},{6,7},{7,6},{8,9},{9,8},{10,11... | collective-permute-start | bytes 786440 | tf_op jit(solution)/shard_map/ppermute | solution.py:39
  71.7 9.9 %collective-permute-start.12 = (bf16[128,8,128]{0,2,1:T(8,128)(2,1)S(1)}, bf16[128,8,128]{0,2,1:T(8,128)(2,1)S(1)}, u32[]{:S(2)}, u32[]{:S(2)}) collective-permute-start(bf16[128,8,128]{0,2,1:T(8,128)(2,1)S(1)} %copy-done.14), channel_id=1, source_target_pairs={{0,2},{1,3},{2,0},{3,1},{4,6},{5,7},{6,4},{7,5},{8,10},{9,11},{10,... | collective-permute-start | bytes 786440 | tf_op jit(solution)/shard_map/ppermute | solution.py:39
  77.0 7.1 %collective-permute-start.14 = (bf16[128,8,128]{0,2,1:T(8,128)(2,1)S(1)}, bf16[128,8,128]{0,2,1:T(8,128)(2,1)S(1)}, u32[]{:S(2)}, u32[]{:S(2)}) collective-permute-start(bf16[128,8,128]{0,2,1:T(8,128)(2,1)S(1)} %add_convert_fusion.1), channel_id=1, source_target_pairs={{0,4},{1,5},{2,6},{3,7},{4,0},{5,1},{6,2},{7,3},{8,12},{9,13},{10,... | collective-permute-start | bytes 786440 | tf_op jit(solution)/shard_map/ppermute | solution.py:39
  78.2 6.0 %collective-permute-start.15 = (bf16[128,8,128]{0,2,1:T(8,128)(2,1)S(1)}, bf16[128,8,128]{0,2,1:T(8,128)(2,1)S(1)}, u32[]{:S(2)}, u32[]{:S(2)}) collective-permute-start(bf16[128,8,128]{0,2,1:T(8,128)(2,1)S(1)} %get-tuple-element.14), channel_id=1, source_target_pairs={{0,1},{1,0},{2,3},{3,2},{4,5},{5,4},{6,7},{7,6},{8,9},{9,8},{10,11... | collective-permute-start | bytes 786440 | tf_op jit(solution)/shard_map/ppermute | solution.py:39
  78.3 15.9 %copy-start.3 = (f32[2,128,8,128]{1,3,0,2:T(8,128)S(1)}, f32[2,128,8,128]{1,3,0,2:T(8,128)}, u32[]{:S(2)}) copy-start(f32[2,128,8,128]{1,3,0,2:T(8,128)} %get-tuple-element.40) | copy-start | bytes 3145732
  78.3 15.8 %collective-permute-start.17 = (bf16[128,8,128]{0,2,1:T(8,128)(2,1)S(1)}, bf16[128,8,128]{0,2,1:T(8,128)(2,1)S(1)}, u32[]{:S(2)}, u32[]{:S(2)}) collective-permute-start(bf16[128,8,128]{0,2,1:T(8,128)(2,1)S(1)} %add_convert_fusion), channel_id=1, source_target_pairs={{0,8},{1,9},{2,10},{3,11},{4,12},{5,13},{6,14},{7,15},{8,0},{9,1},... | collective-permute-start | bytes 786440 | tf_op jit(solution)/shard_map/ppermute | solution.py:39
  84.2 10.1 %copy-start.11 = (bf16[128,512]{0,1:T(8,128)(2,1)S(1)}, bf16[128,512]{0,1:T(8,128)(2,1)}, u32[]{:S(2)}) copy-start(bf16[128,512]{0,1:T(8,128)(2,1)} %copy-done.10) | copy-start | bytes 393220
  94.3 1.2 %copy-start.2 = (f32[2,128,8,128]{1,3,0,2:T(8,128)S(1)}, f32[2,128,8,128]{1,3,0,2:T(8,128)}, u32[]{:S(2)}) copy-start(f32[2,128,8,128]{1,3,0,2:T(8,128)} %copy-done.1) | copy-start | bytes 3145732
  95.5 0.9 copy-start.8
  95.5 1.1 %copy-start.12 = (f32[8,128,128]{2,1,0:T(8,128)S(1)}, f32[8,128,128]{2,1,0:T(8,128)}, u32[]{:S(2)}) copy-start(f32[8,128,128]{2,1,0:T(8,128)} %get-tuple-element.41) | copy-start | bytes 1572868
  95.5 1.2 %copy-start.16 = (bf16[8,128,128]{2,1,0:T(8,128)(2,1)S(1)}, bf16[8,128,128]{2,1,0:T(8,128)(2,1)}, u32[]{:S(2)}) copy-start(bf16[8,128,128]{2,1,0:T(8,128)(2,1)} %param.12) | copy-start | bytes 786436

commit v2 on v0

--- a/solution.py
+++ b/solution.py
@@ -1,9 +1,361 @@
 import jax
 import jax.numpy as jnp
 from jax import lax
+from jax.experimental import pallas as pl
+from jax.experimental.pallas import tpu as pltpu
 from jax.sharding import PartitionSpec as P
 
 EPSILON = 1e-05
+CORE, CHIP_X, Z_LOW, Z_HIGH = 1, 2, 4, 8
+LEFT_OFFSETS = (0, CHIP_X, Z_LOW, Z_LOW | CHIP_X)
+RIGHT_OFFSETS = (0, CORE, Z_HIGH, Z_HIGH | CORE)
+ROWS = 8
+PEERS = 4
+VMEM_BYTES = 48 * 2**20
+
+NT = (((1,), (1,)), ((), ()))
+NN = (((1,), (0,)), ((), ()))
+TN = (((0,), (0,)), ((), ()))
+
+
+def dot(a, b, dims):
+    return lax.dot_general(a, b, dims, preferred_element_type=jnp.float32)
+
+
+def lane_norm(values):
+    center = values - jnp.mean(values, axis=1, keepdims=True)
+    inverse = lax.rsqrt(jnp.mean(center * center, axis=1, keepdims=True) + EPSILON)
+    return center * inverse, inverse
+
+
+def sigmoid(x):
+    return 1.0 / (1.0 + jnp.exp(-x))
+
+
+def call(kernel, out_shape, *args, scratch=(), flops=0, nbytes=2**20, exps=0, smem=0):
+    specs = [pl.BlockSpec(memory_space=pltpu.SMEM)] * smem
+    specs += [pl.BlockSpec(memory_space=pltpu.VMEM)] * (len(args) - smem)
+    return pl.pallas_call(
+        kernel,
+        out_shape=out_shape,
+        in_specs=specs,
+        out_specs=jax.tree.map(lambda _: pl.BlockSpec(memory_space=pltpu.VMEM), out_shape),
+        scratch_shapes=list(scratch),
+        compiler_params=pltpu.CompilerParams(vmem_limit_bytes=VMEM_BYTES),
+        cost_estimate=pl.CostEstimate(flops=flops, bytes_accessed=nbytes, transcendentals=exps),
+    )(*args)
+
+
+def side_rows(quarter, row, quarters):
+    return pl.ds(quarter * ROWS + row, 32, stride=quarters * ROWS)
+
+
+def sides_kernel(x_ref, mask_ref, gain_ref, bias_ref, weight_ref, left_ref, right_ref, rows_ref):
+    hidden = weight_ref.shape[0] // 4
+    for row in range(ROWS):
+        normed, _ = lane_norm(x_ref[row].astype(jnp.float32))
+        scaled = (normed * gain_ref[...] + bias_ref[...]).astype(jnp.bfloat16)
+        projected = dot(weight_ref[...], scaled, NT)
+        keep = mask_ref[row : row + 1].astype(jnp.float32)
+        for side in range(2):
+            base = 2 * side * hidden
+            gate = projected[base : base + hidden]
+            value = projected[base + hidden : base + 2 * hidden]
+            result = sigmoid(gate) * value * keep
+            for quarter in range(4):
+                rows_ref[side, side_rows(quarter, row, 4), :] = result[
+                    quarter * 32 : (quarter + 1) * 32
+                ]
+    left_ref[...] = rows_ref[0].astype(jnp.bfloat16)
+    right_ref[...] = rows_ref[1].astype(jnp.bfloat16)
+
+
+def gate_kernel(me_ref, x_ref, cot_ref, gain_ref, bias_ref, weight_ref, sig_ref, *rest):
+    piece_refs, full_ref = rest[:PEERS], rest[PEERS]
+    me = me_ref[0]
+    for row in range(ROWS):
+        normed, _ = lane_norm(x_ref[row].astype(jnp.float32))
+        scaled = (normed * gain_ref[...] + bias_ref[...]).astype(jnp.bfloat16)
+        gate_sig = sigmoid(dot(scaled, weight_ref[...], NN))
+        sig_ref[row] = gate_sig
+        full_ref[row] = cot_ref[row].astype(jnp.float32) * gate_sig
+    for piece_ref, offset in zip(piece_refs, LEFT_OFFSETS):
+        columns = []
+        for other in RIGHT_OFFSETS:
+            start = pl.multiple_of(((me ^ offset) ^ other) * ROWS, ROWS)
+            columns.append(full_ref[:, pl.ds(start, ROWS), :])
+        piece = jnp.concatenate(columns, axis=1)
+        piece_ref[...] = piece.reshape(piece_ref.shape).astype(jnp.bfloat16)
+
+
+def split_sum(values, ones):
+    high = values.astype(jnp.bfloat16)
+    low = (values - high.astype(jnp.float32)).astype(jnp.bfloat16)
+    return dot(high, ones, NN) + dot(low, ones, NN)
+
+
+def block_kernel(*refs):
+    left_refs, right_refs, grad_refs = refs[0:4], refs[4:8], refs[8:12]
+    weight_ref, gain_ref, bias_ref = refs[12:15]
+    update_refs, grad_left_refs, grad_right_refs = refs[15:19], refs[19:23], refs[23:27]
+    pairs_ref, = refs[27:]
+    groups = pairs_ref.shape[0] // 32
+    lane = lax.broadcasted_iota(jnp.int32, (ROWS, 128), 1)
+    of_quarter = [((lane >> 3) & 3) == q for q in range(4)]
+
+    def slab(side_refs, g):
+        return jnp.concatenate([r[g * 32 : (g + 1) * 32, :] for r in side_refs], axis=0)
+
+    for g in range(groups):
+        full = dot(slab(left_refs, g), slab(right_refs, g), NT).reshape(4, 4, ROWS, 128)
+        for m in range(4):
+            kept = full[m, 3]
+            for q in range(3):
+                kept = jnp.where(of_quarter[q], full[m, q], kept)
+            pairs_ref[g * 32 + m * ROWS : g * 32 + (m + 1) * ROWS, :] = kept
+
+    turned = []
+    for row in range(ROWS):
+        turn = pairs_ref[pl.ds(row, 128, stride=ROWS), :].T.reshape(4, 4, ROWS, 128)
+        turned.append(jnp.concatenate([turn[:, q].reshape(32, 128) for q in range(4)], axis=1))
+    mixed = jnp.concatenate(turned, axis=0).astype(jnp.bfloat16).astype(jnp.float32)
+
+    src = lax.broadcasted_iota(jnp.int32, (128, 128), 0)
+    dst = lax.broadcasted_iota(jnp.int32, (128, 128), 1)
+    ones = jnp.where((src & 3) == (dst & 3), 1.0, 0.0).astype(jnp.bfloat16)
+
+    def channel_mean(values):
+        total = values[:, :128] + values[:, 128:256] + values[:, 256:384] + values[:, 384:]
+        mean = split_sum(total, ones) * (1.0 / 128.0)
+        return jnp.concatenate([mean] * 4, axis=1)
+
+    center = mixed - channel_mean(mixed)
+    inverse = lax.rsqrt(channel_mean(center * center) + EPSILON)
+    normed = center * inverse
+    scaled = (normed * gain_ref[...] + bias_ref[...]).astype(jnp.bfloat16)
+    update = dot(scaled, weight_ref[...], NN)
+    for m in range(4):
+        update_refs[m][...] = update[:, m * 128 : (m + 1) * 128].astype(jnp.bfloat16)
+    grad_update = jnp.concatenate([r[...] for r in grad_refs], axis=1)
+    grad_hat = dot(grad_update, weight_ref[...], NT) * gain_ref[...]
+    first = channel_mean(grad_hat)
+    second = channel_mean(grad_hat * normed)
+    grad_mixed = inverse * (grad_hat - first - normed * second)
+
+    for row in range(ROWS):
+        part = grad_mixed[row * 32 : (row + 1) * 32]
+        parts = [part[:, q * 128 : (q + 1) * 128].reshape(4, 1, ROWS, 128) for q in range(4)]
+        turn = jnp.concatenate(parts, axis=1).reshape(128, 128)
+        pairs_ref[pl.ds(row, 128, stride=ROWS), :] = turn.T
+
+    for g in range(groups):
+        rows = []
+        for m in range(4):
+            part = pairs_ref[g * 32 + m * ROWS : g * 32 + (m + 1) * ROWS, :]
+            rows += [jnp.where(of_quarter[q], part, 0.0) for q in range(4)]
+        spread = jnp.concatenate(rows, axis=0).astype(jnp.bfloat16)
+        grad_right = dot(spread, slab(left_refs, g), TN).astype(jnp.bfloat16)
+        grad_left = dot(spread, slab(right_refs, g), NN).astype(jnp.bfloat16)
+        for m in range(4):
+            grad_right_refs[m][g * 32 : (g + 1) * 32, :] = grad_right[m * 32 : (m + 1) * 32]
+            grad_left_refs[m][g * 32 : (g + 1) * 32, :] = grad_left[m * 32 : (m + 1) * 32]
+
+
+def out_kernel(me_ref, *refs):
+    piece_refs = refs[:PEERS]
+    sig_ref, cot_ref, weight_ref, out_ref, grad_ref, full_ref = refs[PEERS:]
+    me = me_ref[0]
+    for piece_ref, offset in zip(piece_refs, LEFT_OFFSETS):
+        piece = piece_ref[...].astype(jnp.float32).reshape(ROWS, PEERS, ROWS, 128)
+        for place, other in enumerate(RIGHT_OFFSETS):
+            start = pl.multiple_of(((me ^ offset) ^ other) * ROWS, ROWS)
+            full_ref[:, pl.ds(start, ROWS), :] = piece[:, place]
+    for row in range(ROWS):
+        update, gate_sig = full_ref[row], sig_ref[row]
+        out = gate_sig * update
+        out_ref[row] = out.astype(jnp.bfloat16)
+        grad_gate = cot_ref[row].astype(jnp.float32) * out * (1.0 - gate_sig)
+        grad_ref[row] = dot(grad_gate.astype(jnp.bfloat16), weight_ref[...], NT)
+
+
+def add_kernel(mine_ref, got_ref, sum_ref):
+    total = mine_ref[...].astype(jnp.float32) + got_ref[...].astype(jnp.float32)
+    sum_ref[...] = total.astype(jnp.bfloat16)
+
+
+def factor_kernel(x_ref, mask_ref, gain_ref, bias_ref, weight_ref, factor_ref):
+    hidden = weight_ref.shape[0] // 4
+    for row in range(ROWS):
+        normed, _ = lane_norm(x_ref[row].astype(jnp.float32))
+        scaled = (normed * gain_ref[...] + bias_ref[...]).astype(jnp.bfloat16)
+        projected = dot(weight_ref[...], scaled, NT)
+        keep = mask_ref[row : row + 1].astype(jnp.float32)
+        for side in range(2):
+            base = 2 * side * hidden
+            gate = sigmoid(projected[base : base + hidden])
+            value = projected[base + hidden : base + 2 * hidden]
+            factor_ref[row, base : base + hidden, :] = keep * value * gate * (1.0 - gate)
+            factor_ref[row, base + hidden : base + 2 * hidden, :] = keep * gate
+
+
+def pair_kernel(*refs):
+    left_refs, right_refs = refs[0:3], refs[3:6]
+    factor_ref, x_ref, gate_ref, gain_ref, weight_ref, out_ref, rows_ref = refs[6:]
+    hidden = weight_ref.shape[1] // 4
+    for side, side_refs in enumerate((left_refs, right_refs)):
+        total = side_refs[0][...].astype(jnp.float32)
+        for r in side_refs[1:]:
+            total = total + r[...].astype(jnp.float32)
+        rows_ref[side] = total
+    for row in range(ROWS):
+        parts = []
+        for side in range(2):
+            grad = jnp.concatenate(
+                [rows_ref[side, side_rows(q, row, 4), :] for q in range(4)], axis=0
+            )
+            base = 2 * side * hidden
+            for place in (base, base + hidden):
+                factor = factor_ref[row, place : place + hidden, :]
+                parts.append((grad * factor).astype(jnp.bfloat16))
+        grad_projected = jnp.concatenate(parts, axis=0)
+        grad_scaled = dot(weight_ref[...], grad_projected, NN).T + gate_ref[row]
+        normed, inverse = lane_norm(x_ref[row].astype(jnp.float32))
+        grad_hat = grad_scaled * gain_ref[...]
+        first = jnp.mean(grad_hat, axis=1, keepdims=True)
+        second = jnp.mean(grad_hat * normed, axis=1, keepdims=True)
+        out_ref[row] = (inverse * (grad_hat - first - normed * second)).astype(jnp.bfloat16)
+
+
+def swap(values, offset):
+    return lax.ppermute(values, "row", [(s, s ^ offset) for s in range(16)])
+
+
+def blocks_device(
+    pair_rep,
+    pair_mask,
+    cotangent,
+    in_gain,
+    in_bias,
+    proj_weight,
+    gate_weight,
+    mid_gain,
+    mid_bias,
+    out_weight,
+):
+    rows, cols, width = pair_rep.shape
+    hidden = out_weight.shape[0]
+    f32, bf16 = jnp.float32, jnp.bfloat16
+    shape = jax.ShapeDtypeStruct
+    me = lax.axis_index("row").astype(jnp.int32).reshape(1)
+    gain, bias = in_gain.reshape(1, width), in_bias.reshape(1, width)
+    weight_t = proj_weight.T
+    side = shape((hidden * rows, cols), bf16)
+    piece = shape((rows * PEERS * rows, width), bf16)
+
+    left, right = call(
+        sides_kernel,
+        (side, side),
+        pair_rep,
+        pair_mask,
+        gain,
+        bias,
+        weight_t,
+        scratch=[pltpu.VMEM((2, hidden * rows, cols), f32)],
+        flops=2 * rows * cols * width * 4 * hidden,
+    )
+    left_far = swap(left, Z_LOW)
+    right_far = swap(right, Z_HIGH)
+    left_near = swap(left, CHIP_X)
+    right_near = swap(right, CORE)
+
+    gate_sig, *grad_pieces = call(
+        gate_kernel,
+        (shape(pair_rep.shape, f32),) + (piece,) * PEERS,
+        me,
+        pair_rep,
+        cotangent,
+        gain,
+        bias,
+        gate_weight,
+        smem=1,
+        scratch=[pltpu.VMEM(pair_rep.shape, f32)],
+        flops=2 * rows * cols * width * width,
+    )
+    grads = [grad_pieces[0]] + [swap(p, o) for p, o in zip(grad_pieces[1:], LEFT_OFFSETS[1:])]
+    left_both = swap(left_far, CHIP_X)
+    right_both = swap(right_far, CORE)
+
+    eye = jnp.eye(PEERS, dtype=out_weight.dtype)
+    weight_block = (out_weight[:, None, None, :] * eye[None, :, :, None]).reshape(
+        hidden * PEERS, PEERS * width
+    )
+    mid_gain_row = jnp.repeat(mid_gain, PEERS).reshape(1, -1)
+    mid_bias_row = jnp.repeat(mid_bias, PEERS).reshape(1, -1)
+    results = call(
+        block_kernel,
+        (piece,) * 4 + (side,) * 8,
+        left,
+        left_near,
+        left_far,
+        left_both,
+        right,
+        right_near,
+        right_far,
+        right_both,
+        *grads,
+        weight_block,
+        mid_gain_row,
+        mid_bias_row,
+        scratch=[pltpu.VMEM((hidden * rows, 128), f32)],
+        flops=2 * 3 * 32 * 128**3,
+    )
+    updates, left_parts, right_parts = results[0:4], results[4:8], results[8:12]
+
+    def add(mine, got):
+        return call(add_kernel, side, mine, got)
+
+    right_sum = add(right_parts[2], swap(right_parts[3], CORE))
+    left_sum = add(left_parts[2], swap(left_parts[3], CHIP_X))
+    right_got = [right_parts[0], swap(right_parts[1], CORE), swap(right_sum, Z_HIGH)]
+    left_got = [left_parts[0], swap(left_parts[1], CHIP_X), swap(left_sum, Z_LOW)]
+
+    updates = [updates[0]] + [swap(p, o) for p, o in zip(updates[1:], LEFT_OFFSETS[1:])]
+    factors = call(
+        factor_kernel,
+        shape((rows, 4 * hidden, cols), f32),
+        pair_rep,
+        pair_mask,
+        gain,
+        bias,
+        weight_t,
+        flops=2 * rows * cols * width * 4 * hidden,
+    )
+    output, gate_part = call(
+        out_kernel,
+        (shape(pair_rep.shape, bf16), shape(pair_rep.shape, f32)),
+        me,
+        *updates,
+        gate_sig,
+        cotangent,
+        gate_weight,
+        smem=1,
+        scratch=[pltpu.VMEM(pair_rep.shape, f32)],
+        flops=2 * rows * cols * width * width,
+    )
+    grad_pair = call(
+        pair_kernel,
+        shape(pair_rep.shape, bf16),
+        *left_got,
+        *right_got,
+        factors,
+        pair_rep,
+        gate_part,
+        gain,
+        proj_weight,
+        scratch=[pltpu.VMEM((2, hidden * rows, cols), f32)],
+        flops=2 * rows * cols * width * 4 * hidden,
+    )
+    return (output, grad_pair)
 
 
 def norm_stats(values, reduce_axis):
@@ -32,7 +384,7 @@
     return jnp.stack([grad_left, grad_right]).astype(jnp.bfloat16)
 
 
-def per_device(
+def channels_device(
     pair_rep,
     pair_mask,
     cotangent,
@@ -105,6 +457,7 @@
 
 
 def solution(mesh):
+    blocks = mesh.shape["row"] == 16 and mesh.shape["col"] == 1
     placed = (
         P(("grp", "row"), "col", None),
         P(("grp", "row"), "col"),
@@ -118,7 +471,7 @@
         P(),
     )
     return jax.shard_map(
-        per_device,
+        blocks_device if blocks else channels_device,
         mesh=mesh,
         in_specs=placed,
         out_specs=(P(("grp", "row"), "col", None), P(("grp", "row"), "col", None)),

time: 83 us -> 65.6 us (0.79)
  blocking collectives: 65.6 us -> 0 us
  waiting for transfers between devices: 0 us -> 23.9 us
  starting transfers between devices: 0 us -> 17.8 us
  Pallas kernels: 0 us -> 9.96 us
  matrix products: 5.61 us -> 0 us
  local copies, waits for them, and re-layouts: 8.73 us -> 10.8 us
    all_to_all x4 -> x0, blocking collectives: 65.6 us -> none  [the longest x1 21.6 us: per_device(): lax.all_to_all(both_sides, 'row', split_axis=1, concat_axis=2, tiled=True)]
    ppermute x0 -> x18, waiting for transfers between devices: none -> 23.9 us  [swap(): return lax.ppermute(values, 'row', [(s, s ^ offset) for s in range(16)])]
    ppermute x0 -> x18, starting transfers between devices: none -> 17.8 us  [swap(): return lax.ppermute(values, 'row', [(s, s ^ offset) for s in range(16)])]
    pallas_call x0 -> x8, Pallas kernels: none -> 9.96 us  [call(): pl.pallas_call(kernel, out_shape=out_shape, in_specs=specs, out_specs=jax...]
    dot_general x11 -> x0, matrix products: 5.61 us -> none  [the longest x1 1.33 us: per_device(): jnp.einsum('shij,csh->ijc', grad_value, weights_four[:, :, 1], preferred_...]
    unnamed x33 -> x34, local copies, waits for them, and re-layouts: 4.73 us -> 9.09 us
    convert_element_type x5 -> x0, local copies, waits for them, and re-layouts: 3.54 us -> none  [the longest x2 2.68 us: per_device(): side_float = grad_sides.astype(jnp.float32) * mask_float]
    mul x0 -> x1, other arithmetic: none -> 1.82 us  [blocks_device(): out_weight[:, None, None, :] * eye[None, :, :, None]]
  transfers between devices with their start and end apart: 0 -> 18, of which waited for: 0 -> 7; matrix products, arithmetic and copies ran while one was open for 0% -> 7% of each run, Pallas kernels for 0% -> 4%
where the time goes in v2:
time: 65.6 us; the launch traced here: 65.1 us
  waiting for transfers between devices  23.9 us (36%)
  starting transfers between devices  17.8 us (27%)
  local copies, waits for them, and re-layouts  10.8 us (16%)
  Pallas kernels  9.96 us (15%)
  other arithmetic  1.83 us (3%)
  between operations  0.8 us (1%)
    ppermute x18, waiting for transfers between devices, swap(): return lax.ppermute(values, 'row', [(s, s ^ offset) for s in range(16)])  23.9 us
    ppermute x18, starting transfers between devices, swap(): return lax.ppermute(values, 'row', [(s, s ^ offset) for s in range(16)])  17.8 us
    pallas_call x8, Pallas kernels, call(): pl.pallas_call(kernel, out_shape=out_shape, in_specs=specs, out_specs=jax...  9.96 us
    unnamed x34, local copies, waits for them, and re-layouts  9.09 us
    mul x1, other arithmetic, blocks_device(): out_weight[:, None, None, :] * eye[None, :, :, None]  1.82 us
  transfers between devices with their start and end apart: 18, of which 7 were waited for; matrix products, arithmetic and copies ran while one was open for 7% of the time, Pallas kernels for 4%

profile of v2, /device:TPU:0, one launch (start us, length us, event | category | flops | bytes accessed | tf_op | source)
XLA Modules:
  0.0 65.1 jit_solution(16076528021165501501)
XLA Ops:
  0.6 1.0 %copy.13 = bf16[128,512]{0,1:T(8,128)(2,1)S(1)} copy(bf16[128,512]{1,0:T(8,128)(2,1)} %refs_10_.1) | data formatting | bytes 262144 | tf_op args[5]
  1.7 0.0 copy-start
  1.7 0.9 %copy-done = bf16[8,128,128]{2,1,0:T(8,128)(2,1)S(1)} copy-done((bf16[8,128,128]{2,1,0:T(8,128)(2,1)S(1)}, bf16[8,128,128]{2,1,0:T(8,128)(2,1)}, u32[]{:S(2)}) %copy-start) | copy-done | bytes 262168
  2.6 0.7 %copy-done.8 = f32[128]{0:T(128)S(1)} copy-done((f32[128]{0:T(128)S(1)}, f32[128]{0:T(128)}, u32[]{:S(2)}) %copy-start.8) | copy-done | bytes 536
  3.3 0.7 %copy-done.11 = s32[8,128]{1,0:T(8,128)S(1)} copy-done((s32[8,128]{1,0:T(8,128)S(1)}, s32[8,128]{1,0:T(8,128)}, u32[]{:S(2)}) %copy-start.11) | copy-done | bytes 4120
  4.0 0.7 %copy-done.13 = f32[128]{0:T(128)S(1)} copy-done((f32[128]{0:T(128)S(1)}, f32[128]{0:T(128)}, u32[]{:S(2)}) %copy-start.13) | copy-done | bytes 536
  4.6 1.5 %shard_map.113 = (bf16[1024,128]{1,0:T(8,128)(2,1)S(1)}, bf16[1024,128]{1,0:T(8,128)(2,1)S(1)}) custom-call(bf16[8,128,128]{2,1,0:T(8,128)(2,1)S(1)} %copy-done, s32[8,128]{1,0:T(8,128)S(1)} %copy-done.11, f32[1,128]{1,0:T(1,128)S(1)} %bitcast.12, f32[1,128]{1,0:T(1,128)S(1)} %bitcast.16, bf16[512,128]{1,0:T(8,128)(2,1)S(1)} %bitcast.10), custom_call_target="tpu_custom_call" | custom-call | flops 134217728 | bytes 1048576 | tf_op jit(solution)/shard_map/pallas_call | solution.py:38
  6.1 3.1 %collective-permute-start.1 = (bf16[1024,128]{1,0:T(8,128)(2,1)S(1)}, bf16[1024,128]{1,0:T(8,128)(2,1)S(1)}, u32[]{:S(2)}, u32[]{:S(2)}) collective-permute-start(bf16[1024,128]{1,0:T(8,128)(2,1)S(1)} %get-tuple-element.23.refs_0_), channel_id=1, source_target_pairs={{0,4},{1,5},{2,6},{3,7},{4,0},{5,1},{6,2},{7,3},{8,12},{9,13},{10,... | collective-permute-start | bytes 786440 | tf_op jit(solution)/shard_map/ppermute | solution.py:230
  9.2 2.6 %collective-permute-start.4 = (bf16[1024,128]{1,0:T(8,128)(2,1)S(1)}, bf16[1024,128]{1,0:T(8,128)(2,1)S(1)}, u32[]{:S(2)}, u32[]{:S(2)}) collective-permute-start(bf16[1024,128]{1,0:T(8,128)(2,1)S(1)} %get-tuple-element.24.refs_4_), channel_id=1, source_target_pairs={{0,8},{1,9},{2,10},{3,11},{4,12},{5,13},{6,14},{7,15},{8,0},{9,1},... | collective-permute-start | bytes 786440 | tf_op jit(solution)/shard_map/ppermute | solution.py:230
  11.8 0.9 %copy-done.1 = bf16[8,128,128]{2,1,0:T(8,128)(2,1)S(1)} copy-done((bf16[8,128,128]{2,1,0:T(8,128)(2,1)S(1)}, bf16[8,128,128]{2,1,0:T(8,128)(2,1)}, u32[]{:S(2)}) %copy-start.1) | copy-done | bytes 262168
  12.7 0.9 %copy-done.3 = bf16[8,128,128]{2,1,0:T(8,128)(2,1)S(1)} copy-done((bf16[8,128,128]{2,1,0:T(8,128)(2,1)S(1)}, bf16[8,128,128]{2,1,0:T(8,128)(2,1)}, u32[]{:S(2)}) %copy-start.3) | copy-done | bytes 262168
  13.7 0.8 %copy-done.6 = bf16[128,128]{1,0:T(8,128)(2,1)S(1)} copy-done((bf16[128,128]{1,0:T(8,128)(2,1)S(1)}, bf16[128,128]{1,0:T(8,128)(2,1)}, u32[]{:S(2)}) %copy-start.6) | copy-done | bytes 32792
  14.4 0.7 %copy-done.9 = f32[128]{0:T(128)S(1)} copy-done((f32[128]{0:T(128)S(1)}, f32[128]{0:T(128)}, u32[]{:S(2)}) %copy-start.9) | copy-done | bytes 536
  15.1 0.7 %copy-done.14 = f32[128]{0:T(128)S(1)} copy-done((f32[128]{0:T(128)S(1)}, f32[128]{0:T(128)}, u32[]{:S(2)}) %copy-start.14) | copy-done | bytes 536
  15.7 0.6 shard_map.114
  16.3 1.6 %collective-permute-start.6 = (bf16[256,128]{1,0:T(8,128)(2,1)S(1)}, bf16[256,128]{1,0:T(8,128)(2,1)S(1)}, u32[]{:S(2)}, u32[]{:S(2)}) collective-permute-start(bf16[256,128]{1,0:T(8,128)(2,1)S(1)} %get-tuple-element.26), channel_id=1, source_target_pairs={{0,2},{1,3},{2,0},{3,1},{4,6},{5,7},{6,4},{7,5},{8,10},{9,11},{10,... | collective-permute-start | bytes 196616 | tf_op jit(solution)/shard_map/ppermute | solution.py:230
  17.9 0.5 collective-permute-start
  18.4 0.0 collective-permute-start.3
  18.4 2.9 %collective-permute-done.6.refs_9_ = bf16[256,128]{1,0:T(8,128)(2,1)S(1)} collective-permute-done((bf16[256,128]{1,0:T(8,128)(2,1)S(1)}, bf16[256,128]{1,0:T(8,128)(2,1)S(1)}, u32[]{:S(2)}, u32[]{:S(2)}) %collective-permute-start.6) | collective-permute-done | bytes 65568 | tf_op jit(solution)/shard_map/ppermute | solution.py:230
  21.3 0.4 collective-permute-start.7
  21.7 0.0 collective-permute-done.1.refs_2_
  21.7 1.6 %collective-permute-start.2 = (bf16[1024,128]{1,0:T(8,128)(2,1)S(1)}, bf16[1024,128]{1,0:T(8,128)(2,1)S(1)}, u32[]{:S(2)}, u32[]{:S(2)}) collective-permute-start(bf16[1024,128]{1,0:T(8,128)(2,1)S(1)} %collective-permute-done.1.refs_2_), channel_id=1, source_target_pairs={{0,2},{1,3},{2,0},{3,1},{4,6},{5,7},{6,4},{7,5},{8,10},{9,11},{10,... | collective-permute-start | bytes 786440 | tf_op jit(solution)/shard_map/ppermute | solution.py:230
  23.4 0.0 collective-permute-done.4.refs_6_
  23.4 0.0 collective-permute-start.5
  23.4 2.2 %collective-permute-done.7.refs_10_ = bf16[256,128]{1,0:T(8,128)(2,1)S(1)} collective-permute-done((bf16[256,128]{1,0:T(8,128)(2,1)S(1)}, bf16[256,128]{1,0:T(8,128)(2,1)S(1)}, u32[]{:S(2)}, u32[]{:S(2)}) %collective-permute-start.7) | collective-permute-done | bytes 65568 | tf_op jit(solution)/shard_map/ppermute | solution.py:230
  25.5 1.5 %collective-permute-start.8 = (bf16[256,128]{1,0:T(8,128)(2,1)S(1)}, bf16[256,128]{1,0:T(8,128)(2,1)S(1)}, u32[]{:S(2)}, u32[]{:S(2)}) collective-permute-start(bf16[256,128]{1,0:T(8,128)(2,1)S(1)} %get-tuple-element.28), channel_id=1, source_target_pairs={{0,6},{1,7},{2,4},{3,5},{4,2},{5,3},{6,0},{7,1},{8,14},{9,15},{10,... | collective-permute-start | bytes 196616 | tf_op jit(solution)/shard_map/ppermute | solution.py:230
  27.1 1.8 %broadcast_multiply_fusion = bf16[128,4,4,128]{3,2,1,0:T(4,128)(2,1)} fusion(bf16[4,4]{1,0:T(4,128)(2,1)S(1)} %fusion, bf16[128,128]{1,0:T(8,128)(2,1)} %param.19), kind=kLoop, calls=%fused_computation.1 | loop fusion | flops 262144 | bytes 557088 | tf_op jit(solution)/shard_map/mul | solution.py:289
  28.9 0.7 %broadcast_in_dim.8 = f32[128,4]{1,0:T(8,128)S(1)} broadcast(f32[128]{0:T(128)} %param.17), dimensions={0} | broadcast | bytes 2560 | tf_op jit(solution)/shard_map/broadcast_in_dim | solution.py:292
  29.6 0.1 reshape_reshape.6.refs_13_
  29.7 0.7 %broadcast_in_dim.9 = f32[128,4]{1,0:T(8,128)S(1)} broadcast(f32[128]{0:T(128)} %param.18), dimensions={0} | broadcast | bytes 2560 | tf_op jit(solution)/shard_map/broadcast_in_dim | solution.py:293
  30.5 0.1 reshape_reshape.7.refs_14_
  30.6 1.1 %copy.16 = bf16[64,8,4,128]{3,1,2,0:T(8,128)(2,1)S(1)} copy(bf16[64,8,4,128]{3,2,1,0:T(4,128)(2,1)} %bitcast.19) | data formatting | bytes 1048576
  31.7 0.0 collective-permute-done.8.refs_11_
  31.7 0.0 collective-permute-done.refs_1_
  31.7 0.0 collective-permute-done.3.refs_5_
  31.7 1.1 %collective-permute-done.2.refs_3_ = bf16[1024,128]{1,0:T(8,128)(2,1)S(1)} collective-permute-done((bf16[1024,128]{1,0:T(8,128)(2,1)S(1)}, bf16[1024,128]{1,0:T(8,128)(2,1)S(1)}, u32[]{:S(2)}, u32[]{:S(2)}) %collective-permute-start.2) | collective-permute-done | bytes 262176 | tf_op jit(solution)/shard_map/ppermute | solution.py:230
  32.8 0.0 collective-permute-done.5.refs_7_
  32.8 0.0 copy-start.15
  32.8 2.8 %shard_map.115 = (bf16[256,128]{1,0:T(8,128)(2,1)S(1)}, bf16[256,128]{1,0:T(8,128)(2,1)S(1)}, bf16[256,128]{1,0:T(8,128)(2,1)S(1)}, bf16[256,128]{1,0:T(8,128)(2...) custom-call(bf16[1024,128]{1,0:T(8,128)(2,1)S(1)} %get-tuple-element, ...), custom_call_target="tpu_custom_call" | custom-call | flops 402653184 | bytes 1048576 | tf_op jit(solution)/shard_map/pallas_call | solution.py:38
  35.7 0.0 copy-start.4
  35.7 0.0 copy-start.7
  35.7 1.1 %collective-permute-start.13 = (bf16[1024,128]{1,0:T(8,128)(2,1)S(1)}, bf16[1024,128]{1,0:T(8,128)(2,1)S(1)}, u32[]{:S(2)}, u32[]{:S(2)}) collective-permute-start(bf16[1024,128]{1,0:T(8,128)(2,1)S(1)} %get-tuple-element.38), channel_id=1, source_target_pairs={{0,2},{1,3},{2,0},{3,1},{4,6},{5,7},{6,4},{7,5},{8,10},{9,11},{10,... | collective-permute-start | bytes 786440 | tf_op jit(solution)/shard_map/ppermute | solution.py:230
  36.7 0.0 collective-permute-start.16
  36.7 1.0 %collective-permute-start.12 = (bf16[1024,128]{1,0:T(8,128)(2,1)S(1)}, bf16[1024,128]{1,0:T(8,128)(2,1)S(1)}, u32[]{:S(2)}, u32[]{:S(2)}) collective-permute-start(bf16[1024,128]{1,0:T(8,128)(2,1)S(1)} %get-tuple-element.36), channel_id=1, source_target_pairs={{0,2},{1,3},{2,0},{3,1},{4,6},{5,7},{6,4},{7,5},{8,10},{9,11},{10,... | collective-permute-start | bytes 786440 | tf_op jit(solution)/shard_map/ppermute | solution.py:230
  37.8 0.2 collective-permute-start.15
  38.0 7.0 %collective-permute-done.13.got_ref = bf16[1024,128]{1,0:T(8,128)(2,1)S(1)} collective-permute-done((bf16[1024,128]{1,0:T(8,128)(2,1)S(1)}, bf16[1024,128]{1,0:T(8,128)(2,1)S(1)}, u32[]{:S(2)}, u32[]{:S(2)}) %collective-permute-start.13) | collective-permute-done | bytes 262176 | tf_op jit(solution)/shard_map/ppermute | solution.py:230
  45.0 0.1 shard_map.117
  45.1 0.6 collective-permute-start.14
  45.7 0.0 collective-permute-done.16.got_ref
  45.7 0.1 shard_map.118
  45.8 0.4 collective-permute-start.17
  46.2 0.9 %collective-permute-start.9 = (bf16[256,128]{1,0:T(8,128)(2,1)S(1)}, bf16[256,128]{1,0:T(8,128)(2,1)S(1)}, u32[]{:S(2)}, u32[]{:S(2)}) collective-permute-start(bf16[256,128]{1,0:T(8,128)(2,1)S(1)} %get-tuple-element.30), channel_id=1, source_target_pairs={{0,2},{1,3},{2,0},{3,1},{4,6},{5,7},{6,4},{7,5},{8,10},{9,11},{10,... | collective-permute-start | bytes 196616 | tf_op jit(solution)/shard_map/ppermute | solution.py:230
  47.0 3.4 %collective-permute-done.9.refs_1_ = bf16[256,128]{1,0:T(8,128)(2,1)S(1)} collective-permute-done((bf16[256,128]{1,0:T(8,128)(2,1)S(1)}, bf16[256,128]{1,0:T(8,128)(2,1)S(1)}, u32[]{:S(2)}, u32[]{:S(2)}) %collective-permute-start.9) | collective-permute-done | bytes 65568 | tf_op jit(solution)/shard_map/ppermute | solution.py:230
  50.4 1.5 %collective-permute-start.10 = (bf16[256,128]{1,0:T(8,128)(2,1)S(1)}, bf16[256,128]{1,0:T(8,128)(2,1)S(1)}, u32[]{:S(2)}, u32[]{:S(2)}) collective-permute-start(bf16[256,128]{1,0:T(8,128)(2,1)S(1)} %get-tuple-element.31), channel_id=1, source_target_pairs={{0,4},{1,5},{2,6},{3,7},{4,0},{5,1},{6,2},{7,3},{8,12},{9,13},{10,... | collective-permute-start | bytes 196616 | tf_op jit(solution)/shard_map/ppermute | solution.py:230
  51.9 3.9 %collective-permute-done.10.refs_2_ = bf16[256,128]{1,0:T(8,128)(2,1)S(1)} collective-permute-done((bf16[256,128]{1,0:T(8,128)(2,1)S(1)}, bf16[256,128]{1,0:T(8,128)(2,1)S(1)}, u32[]{:S(2)}, u32[]{:S(2)}) %collective-permute-start.10) | collective-permute-done | bytes 65568 | tf_op jit(solution)/shard_map/ppermute | solution.py:230
  55.8 0.8 %collective-permute-start.11 = (bf16[256,128]{1,0:T(8,128)(2,1)S(1)}, bf16[256,128]{1,0:T(8,128)(2,1)S(1)}, u32[]{:S(2)}, u32[]{:S(2)}) collective-permute-start(bf16[256,128]{1,0:T(8,128)(2,1)S(1)} %get-tuple-element.32), channel_id=1, source_target_pairs={{0,6},{1,7},{2,4},{3,5},{4,2},{5,3},{6,0},{7,1},{8,14},{9,15},{10,... | collective-permute-start | bytes 196616 | tf_op jit(solution)/shard_map/ppermute | solution.py:230
  56.6 0.9 %shard_map.119.refs_6_ = f32[8,512,128]{2,1,0:T(8,128)S(1)} custom-call(bf16[8,128,128]{2,1,0:T(8,128)(2,1)S(1)} %copy-done.2, s32[8,128]{1,0:T(8,128)S(1)} %copy-done.12, f32[1,128]{1,0:T(1,128)S(1)} %bitcast.14, f32[1,128]{1,0:T(1,128)S(1)} %bitcast.18, bf16[512,128]{1,0:T(8,128)(2,1)S(1)} %bitcast.11), custom_call_target="tpu_custom_call" | custom-call | flops 134217728 | bytes 1048576 | tf_op jit(solution)/shard_map/pallas_call | solution.py:38
  57.5 3.5 %collective-permute-done.11.refs_3_ = bf16[256,128]{1,0:T(8,128)(2,1)S(1)} collective-permute-done((bf16[256,128]{1,0:T(8,128)(2,1)S(1)}, bf16[256,128]{1,0:T(8,128)(2,1)S(1)}, u32[]{:S(2)}, u32[]{:S(2)}) %collective-permute-start.11) | collective-permute-done | bytes 65568 | tf_op jit(solution)/shard_map/ppermute | solution.py:230
  61.0 0.9 %shard_map.116 = (bf16[8,128,128]{2,1,0:T(8,128)(2,1)}, f32[8,128,128]{2,1,0:T(8,128)S(1)}) custom-call(s32[1]{0:T(128)} %bitcast.me_ref, bf16[256,128]{1,0:T(8,128)(2,1)S(1)} %get-tuple-element.29.refs_0_, bf16[256,128]{1,0:T(8,128)(2,1)S(1)} %collective-permute-done.9.refs_1_, bf16[256,128]{1,0:T(8,128)(2,1)S(1)} %collective-permute-done.10.refs_2_, ...), custom_call_target="tpu_custom_call" | custom-call | flops 33554432 | bytes 1048576 | tf_op jit(solution)/shard_map/pallas_call | solution.py:38
  61.9 0.0 collective-permute-done.12.refs_1_
  61.9 0.0 collective-permute-done.15.refs_4_
  61.9 0.0 collective-permute-done.14.refs_2_
  61.9 0.0 collective-permute-done.17.refs_5_
  61.9 3.2 %shard_map.120 = bf16[8,128,128]{2,1,0:T(8,128)(2,1)} custom-call(bf16[1024,128]{1,0:T(8,128)(2,1)S(1)} %get-tuple-element.35.refs_0_, bf16[1024,128]{1,0:T(8,128)(2,1)S(1)} %collective-permute-done.12.refs_1_, bf16[1024,128]{1,0:T(8,128)(2,1)S(1)} %collective-permute-done.14.refs_2_, bf16[1024,128]{1,0:T(8,128)(2,1)S(1)} %get-tuple-element.39.refs_3_, ...), custom_call_target="tpu_custom_call" | custom-call | flops 134217728 | bytes 1048576 | tf_op jit(solution)/shard_map/pallas_call | solution.py:38
  (20 shorter events, 0.0 us)
Async XLA Ops:
  1.7 1.0 %copy-start = (bf16[8,128,128]{2,1,0:T(8,128)(2,1)S(1)}, bf16[8,128,128]{2,1,0:T(8,128)(2,1)}, u32[]{:S(2)}) copy-start(bf16[8,128,128]{2,1,0:T(8,128)(2,1)} %refs_7_.1) | copy-start | bytes 786436
  2.6 0.7 %copy-start.8 = (f32[128]{0:T(128)S(1)}, f32[128]{0:T(128)}, u32[]{:S(2)}) copy-start(f32[128]{0:T(128)} %param.13) | copy-start | bytes 1540
  3.3 0.7 %copy-start.11 = (s32[8,128]{1,0:T(8,128)S(1)}, s32[8,128]{1,0:T(8,128)}, u32[]{:S(2)}) copy-start(s32[8,128]{1,0:T(8,128)} %mask_ref.3) | copy-start | bytes 12292
  4.0 0.7 %copy-start.13 = (f32[128]{0:T(128)S(1)}, f32[128]{0:T(128)}, u32[]{:S(2)}) copy-start(f32[128]{0:T(128)} %param.14) | copy-start | bytes 1540
  6.1 15.6 %collective-permute-start.1 = (bf16[1024,128]{1,0:T(8,128)(2,1)S(1)}, bf16[1024,128]{1,0:T(8,128)(2,1)S(1)}, u32[]{:S(2)}, u32[]{:S(2)}) collective-permute-start(bf16[1024,128]{1,0:T(8,128)(2,1)S(1)} %get-tuple-element.23.refs_0_), channel_id=1, source_target_pairs={{0,4},{1,5},{2,6},{3,7},{4,0},{5,1},{6,2},{7,3},{8,12},{9,13},{10,... | collective-permute-start | bytes 786440 | tf_op jit(solution)/shard_map/ppermute | solution.py:230
  9.2 14.2 %collective-permute-start.4 = (bf16[1024,128]{1,0:T(8,128)(2,1)S(1)}, bf16[1024,128]{1,0:T(8,128)(2,1)S(1)}, u32[]{:S(2)}, u32[]{:S(2)}) collective-permute-start(bf16[1024,128]{1,0:T(8,128)(2,1)S(1)} %get-tuple-element.24.refs_4_), channel_id=1, source_target_pairs={{0,8},{1,9},{2,10},{3,11},{4,12},{5,13},{6,14},{7,15},{8,0},{9,1},... | collective-permute-start | bytes 786440 | tf_op jit(solution)/shard_map/ppermute | solution.py:230
  11.8 0.9 %copy-start.1 = (bf16[8,128,128]{2,1,0:T(8,128)(2,1)S(1)}, bf16[8,128,128]{2,1,0:T(8,128)(2,1)}, u32[]{:S(2)}) copy-start(bf16[8,128,128]{2,1,0:T(8,128)(2,1)} %refs_7_.1) | copy-start | bytes 786436
  12.7 0.9 %copy-start.3 = (bf16[8,128,128]{2,1,0:T(8,128)(2,1)S(1)}, bf16[8,128,128]{2,1,0:T(8,128)(2,1)}, u32[]{:S(2)}) copy-start(bf16[8,128,128]{2,1,0:T(8,128)(2,1)} %refs_5_.1) | copy-start | bytes 786436
  13.7 0.8 %copy-start.6 = (bf16[128,128]{1,0:T(8,128)(2,1)S(1)}, bf16[128,128]{1,0:T(8,128)(2,1)}, u32[]{:S(2)}) copy-start(bf16[128,128]{1,0:T(8,128)(2,1)} %refs_6_.1) | copy-start | bytes 98308
  14.4 0.7 %copy-start.9 = (f32[128]{0:T(128)S(1)}, f32[128]{0:T(128)}, u32[]{:S(2)}) copy-start(f32[128]{0:T(128)} %param.13) | copy-start | bytes 1540
  15.1 0.7 %copy-start.14 = (f32[128]{0:T(128)S(1)}, f32[128]{0:T(128)}, u32[]{:S(2)}) copy-start(f32[128]{0:T(128)} %param.14) | copy-start | bytes 1540
  16.3 5.0 %collective-permute-start.6 = (bf16[256,128]{1,0:T(8,128)(2,1)S(1)}, bf16[256,128]{1,0:T(8,128)(2,1)S(1)}, u32[]{:S(2)}, u32[]{:S(2)}) collective-permute-start(bf16[256,128]{1,0:T(8,128)(2,1)S(1)} %get-tuple-element.26), channel_id=1, source_target_pairs={{0,2},{1,3},{2,0},{3,1},{4,6},{5,7},{6,4},{7,5},{8,10},{9,11},{10,... | collective-permute-start | bytes 196616 | tf_op jit(solution)/shard_map/ppermute | solution.py:230
  17.9 13.8 %collective-permute-start = (bf16[1024,128]{1,0:T(8,128)(2,1)S(1)}, bf16[1024,128]{1,0:T(8,128)(2,1)S(1)}, u32[]{:S(2)}, u32[]{:S(2)}) collective-permute-start(bf16[1024,128]{1,0:T(8,128)(2,1)S(1)} %get-tuple-element.23.refs_0_), channel_id=1, source_target_pairs={{0,2},{1,3},{2,0},{3,1},{4,6},{5,7},{6,4},{7,5},{8,10},{9,11},{10,... | collective-permute-start | bytes 786440 | tf_op jit(solution)/shard_map/ppermute | solution.py:230
  18.4 13.3 %collective-permute-start.3 = (bf16[1024,128]{1,0:T(8,128)(2,1)S(1)}, bf16[1024,128]{1,0:T(8,128)(2,1)S(1)}, u32[]{:S(2)}, u32[]{:S(2)}) collective-permute-start(bf16[1024,128]{1,0:T(8,128)(2,1)S(1)} %get-tuple-element.24.refs_4_), channel_id=1, source_target_pairs={{0,1},{1,0},{2,3},{3,2},{4,5},{5,4},{6,7},{7,6},{8,9},{9,8},{10,11... | collective-permute-start | bytes 786440 | tf_op jit(solution)/shard_map/ppermute | solution.py:230
  21.3 4.3 %collective-permute-start.7 = (bf16[256,128]{1,0:T(8,128)(2,1)S(1)}, bf16[256,128]{1,0:T(8,128)(2,1)S(1)}, u32[]{:S(2)}, u32[]{:S(2)}) collective-permute-start(bf16[256,128]{1,0:T(8,128)(2,1)S(1)} %get-tuple-element.27), channel_id=1, source_target_pairs={{0,4},{1,5},{2,6},{3,7},{4,0},{5,1},{6,2},{7,3},{8,12},{9,13},{10,... | collective-permute-start | bytes 196616 | tf_op jit(solution)/shard_map/ppermute | solution.py:230
  21.7 11.1 %collective-permute-start.2 = (bf16[1024,128]{1,0:T(8,128)(2,1)S(1)}, bf16[1024,128]{1,0:T(8,128)(2,1)S(1)}, u32[]{:S(2)}, u32[]{:S(2)}) collective-permute-start(bf16[1024,128]{1,0:T(8,128)(2,1)S(1)} %collective-permute-done.1.refs_2_), channel_id=1, source_target_pairs={{0,2},{1,3},{2,0},{3,1},{4,6},{5,7},{6,4},{7,5},{8,10},{9,11},{10,... | collective-permute-start | bytes 786440 | tf_op jit(solution)/shard_map/ppermute | solution.py:230
  23.4 9.4 %collective-permute-start.5 = (bf16[1024,128]{1,0:T(8,128)(2,1)S(1)}, bf16[1024,128]{1,0:T(8,128)(2,1)S(1)}, u32[]{:S(2)}, u32[]{:S(2)}) collective-permute-start(bf16[1024,128]{1,0:T(8,128)(2,1)S(1)} %collective-permute-done.4.refs_6_), channel_id=1, source_target_pairs={{0,1},{1,0},{2,3},{3,2},{4,5},{5,4},{6,7},{7,6},{8,9},{9,8},{10,11... | collective-permute-start | bytes 786440 | tf_op jit(solution)/shard_map/ppermute | solution.py:230
  25.5 6.2 %collective-permute-start.8 = (bf16[256,128]{1,0:T(8,128)(2,1)S(1)}, bf16[256,128]{1,0:T(8,128)(2,1)S(1)}, u32[]{:S(2)}, u32[]{:S(2)}) collective-permute-start(bf16[256,128]{1,0:T(8,128)(2,1)S(1)} %get-tuple-element.28), channel_id=1, source_target_pairs={{0,6},{1,7},{2,4},{3,5},{4,2},{5,3},{6,0},{7,1},{8,14},{9,15},{10,... | collective-permute-start | bytes 196616 | tf_op jit(solution)/shard_map/ppermute | solution.py:230
  32.8 23.8 %copy-start.2 = (bf16[8,128,128]{2,1,0:T(8,128)(2,1)S(1)}, bf16[8,128,128]{2,1,0:T(8,128)(2,1)}, u32[]{:S(2)}) copy-start(bf16[8,128,128]{2,1,0:T(8,128)(2,1)} %refs_7_.1) | copy-start | bytes 786436
  32.8 23.8 %copy-start.10 = (f32[128]{0:T(128)S(1)}, f32[128]{0:T(128)}, u32[]{:S(2)}) copy-start(f32[128]{0:T(128)} %param.13) | copy-start | bytes 1540
  32.8 23.8 %copy-start.12 = (s32[8,128]{1,0:T(8,128)S(1)}, s32[8,128]{1,0:T(8,128)}, u32[]{:S(2)}) copy-start(s32[8,128]{1,0:T(8,128)} %mask_ref.3) | copy-start | bytes 12292
  32.8 23.8 %copy-start.15 = (f32[128]{0:T(128)S(1)}, f32[128]{0:T(128)}, u32[]{:S(2)}) copy-start(f32[128]{0:T(128)} %param.14) | copy-start | bytes 1540
  35.7 25.3 %copy-start.4 = (bf16[8,128,128]{2,1,0:T(8,128)(2,1)S(1)}, bf16[8,128,128]{2,1,0:T(8,128)(2,1)}, u32[]{:S(2)}) copy-start(bf16[8,128,128]{2,1,0:T(8,128)(2,1)} %refs_5_.1) | copy-start | bytes 786436
  35.7 25.3 %copy-start.7 = (bf16[128,128]{1,0:T(8,128)(2,1)S(1)}, bf16[128,128]{1,0:T(8,128)(2,1)}, u32[]{:S(2)}) copy-start(bf16[128,128]{1,0:T(8,128)(2,1)} %refs_6_.1) | copy-start | bytes 98308
  35.7 9.3 %collective-permute-start.13 = (bf16[1024,128]{1,0:T(8,128)(2,1)S(1)}, bf16[1024,128]{1,0:T(8,128)(2,1)S(1)}, u32[]{:S(2)}, u32[]{:S(2)}) collective-permute-start(bf16[1024,128]{1,0:T(8,128)(2,1)S(1)} %get-tuple-element.38), channel_id=1, source_target_pairs={{0,2},{1,3},{2,0},{3,1},{4,6},{5,7},{6,4},{7,5},{8,10},{9,11},{10,... | collective-permute-start | bytes 786440 | tf_op jit(solution)/shard_map/ppermute | solution.py:230
  36.7 8.9 %collective-permute-start.16 = (bf16[1024,128]{1,0:T(8,128)(2,1)S(1)}, bf16[1024,128]{1,0:T(8,128)(2,1)S(1)}, u32[]{:S(2)}, u32[]{:S(2)}) collective-permute-start(bf16[1024,128]{1,0:T(8,128)(2,1)S(1)} %get-tuple-element.42), channel_id=1, source_target_pairs={{0,1},{1,0},{2,3},{3,2},{4,5},{5,4},{6,7},{7,6},{8,9},{9,8},{10,11... | collective-permute-start | bytes 786440 | tf_op jit(solution)/shard_map/ppermute | solution.py:230
  36.7 25.1 %collective-permute-start.12 = (bf16[1024,128]{1,0:T(8,128)(2,1)S(1)}, bf16[1024,128]{1,0:T(8,128)(2,1)S(1)}, u32[]{:S(2)}, u32[]{:S(2)}) collective-permute-start(bf16[1024,128]{1,0:T(8,128)(2,1)S(1)} %get-tuple-element.36), channel_id=1, source_target_pairs={{0,2},{1,3},{2,0},{3,1},{4,6},{5,7},{6,4},{7,5},{8,10},{9,11},{10,... | collective-permute-start | bytes 786440 | tf_op jit(solution)/shard_map/ppermute | solution.py:230
  37.8 24.1 %collective-permute-start.15 = (bf16[1024,128]{1,0:T(8,128)(2,1)S(1)}, bf16[1024,128]{1,0:T(8,128)(2,1)S(1)}, u32[]{:S(2)}, u32[]{:S(2)}) collective-permute-start(bf16[1024,128]{1,0:T(8,128)(2,1)S(1)} %get-tuple-element.40), channel_id=1, source_target_pairs={{0,1},{1,0},{2,3},{3,2},{4,5},{5,4},{6,7},{7,6},{8,9},{9,8},{10,11... | collective-permute-start | bytes 786440 | tf_op jit(solution)/shard_map/ppermute | solution.py:230
  45.1 16.8 %collective-permute-start.14 = (bf16[1024,128]{1,0:T(8,128)(2,1)S(1)}, bf16[1024,128]{1,0:T(8,128)(2,1)S(1)}, u32[]{:S(2)}, u32[]{:S(2)}) collective-permute-start(bf16[1024,128]{1,0:T(8,128)(2,1)S(1)} %shard_map.117), channel_id=1, source_target_pairs={{0,4},{1,5},{2,6},{3,7},{4,0},{5,1},{6,2},{7,3},{8,12},{9,13},{10,... | collective-permute-start | bytes 786440 | tf_op jit(solution)/shard_map/ppermute | solution.py:230
  45.7 16.2 %copy-start.5 = (bf16[128,512]{1,0:T(8,128)(2,1)S(1)}, bf16[128,512]{1,0:T(8,128)(2,1)}, u32[]{:S(2)}) copy-start(bf16[128,512]{1,0:T(8,128)(2,1)} %refs_10_.1) | copy-start | bytes 393220
  45.8 16.1 %collective-permute-start.17 = (bf16[1024,128]{1,0:T(8,128)(2,1)S(1)}, bf16[1024,128]{1,0:T(8,128)(2,1)S(1)}, u32[]{:S(2)}, u32[]{:S(2)}) collective-permute-start(bf16[1024,128]{1,0:T(8,128)(2,1)S(1)} %shard_map.118), channel_id=1, source_target_pairs={{0,8},{1,9},{2,10},{3,11},{4,12},{5,13},{6,14},{7,15},{8,0},{9,1},... | collective-permute-start | bytes 786440 | tf_op jit(solution)/shard_map/ppermute | solution.py:230
  46.2 4.3 %collective-permute-start.9 = (bf16[256,128]{1,0:T(8,128)(2,1)S(1)}, bf16[256,128]{1,0:T(8,128)(2,1)S(1)}, u32[]{:S(2)}, u32[]{:S(2)}) collective-permute-start(bf16[256,128]{1,0:T(8,128)(2,1)S(1)} %get-tuple-element.30), channel_id=1, source_target_pairs={{0,2},{1,3},{2,0},{3,1},{4,6},{5,7},{6,4},{7,5},{8,10},{9,11},{10,... | collective-permute-start | bytes 196616 | tf_op jit(solution)/shard_map/ppermute | solution.py:230
  50.4 5.4 %collective-permute-start.10 = (bf16[256,128]{1,0:T(8,128)(2,1)S(1)}, bf16[256,128]{1,0:T(8,128)(2,1)S(1)}, u32[]{:S(2)}, u32[]{:S(2)}) collective-permute-start(bf16[256,128]{1,0:T(8,128)(2,1)S(1)} %get-tuple-element.31), channel_id=1, source_target_pairs={{0,4},{1,5},{2,6},{3,7},{4,0},{5,1},{6,2},{7,3},{8,12},{9,13},{10,... | collective-permute-start | bytes 196616 | tf_op jit(solution)/shard_map/ppermute | solution.py:230
  55.8 5.2 %collective-permute-start.11 = (bf16[256,128]{1,0:T(8,128)(2,1)S(1)}, bf16[256,128]{1,0:T(8,128)(2,1)S(1)}, u32[]{:S(2)}, u32[]{:S(2)}) collective-permute-start(bf16[256,128]{1,0:T(8,128)(2,1)S(1)} %get-tuple-element.32), channel_id=1, source_target_pairs={{0,6},{1,7},{2,4},{3,5},{4,2},{5,3},{6,0},{7,1},{8,14},{9,15},{10,... | collective-permute-start | bytes 196616 | tf_op jit(solution)/shard_map/ppermute | solution.py:230

commit v3 on v0

--- a/solution.py
+++ b/solution.py
@@ -1,9 +1,519 @@
 import jax
 import jax.numpy as jnp
 from jax import lax
+from jax.experimental import pallas as pl
+from jax.experimental.pallas import tpu as pltpu
 from jax.sharding import PartitionSpec as P
 
 EPSILON = 1e-05
+CORE, CHIP_X, Z_LOW, Z_HIGH = 1, 2, 4, 8
+LEFT_OFFSETS = (0, CORE, Z_LOW, Z_LOW | CORE)
+RIGHT_OFFSETS = (0, CHIP_X, Z_HIGH, Z_HIGH | CHIP_X)
+ROWS = 8
+SIDE = 1024
+PIECE = 256
+HEAD = PIECE + 16
+VMEM_BYTES = 48 * 2**20
+
+NT = (((1,), (1,)), ((), ()))
+NN = (((1,), (0,)), ((), ()))
+F32, BF16 = jnp.float32, jnp.bfloat16
+
+
+def dot(a, b, dims):
+    return lax.dot_general(a, b, dims, preferred_element_type=F32)
+
+
+def norm(values, axis):
+    center = values - jnp.mean(values, axis=axis, keepdims=True)
+    inverse = lax.rsqrt(jnp.mean(center * center, axis=axis, keepdims=True) + EPSILON)
+    return center * inverse, inverse
+
+
+def sigmoid(x):
+    return 1.0 / (1.0 + jnp.exp(-x))
+
+
+def call(kernel, outs, smem=(), hbm=(), vmem=(), scratch=(), micros=1):
+    here, there = len(smem), len(smem) + len(hbm)
+    total = there + len(vmem)
+    count = len(hbm)
+
+    def body(*refs):
+        ins, rest = refs[:total], refs[total:]
+        results, extra = rest[: len(outs)], rest[len(outs) :]
+        buffers, extra = extra[:count], extra[count:]
+        if count:
+            sems, extra = extra[0], extra[1:]
+            copies = [
+                pltpu.make_async_copy(src, dst, sems.at[n])
+                for n, (src, dst) in enumerate(zip(ins[here:there], buffers))
+            ]
+            for c in copies:
+                c.start()
+            for c in copies:
+                c.wait()
+        kernel(*ins[:here], *buffers, *ins[there:], *results, *extra)
+
+    vmem_spec = pl.BlockSpec(memory_space=pltpu.VMEM)
+    specs = [pl.BlockSpec(memory_space=pltpu.SMEM)] * here
+    specs += [pl.BlockSpec(memory_space=pl.ANY)] * count
+    specs += [vmem_spec] * len(vmem)
+    own = [pltpu.VMEM(a.shape, a.dtype) for a in hbm]
+    if count:
+        own.append(pltpu.SemaphoreType.DMA((count,)))
+    return pl.pallas_call(
+        body,
+        out_shape=[jax.ShapeDtypeStruct(s, d) for s, d in outs],
+        in_specs=specs,
+        out_specs=[vmem_spec] * len(outs),
+        scratch_shapes=own + list(scratch),
+        compiler_params=pltpu.CompilerParams(vmem_limit_bytes=VMEM_BYTES),
+        cost_estimate=pl.CostEstimate(
+            flops=0, bytes_accessed=int(micros * 3.0e6), transcendentals=0
+        ),
+    )(*smem, *hbm, *vmem)
+
+
+def side_rows(quarter, row):
+    return pl.ds(quarter * ROWS + row, 32, stride=4 * ROWS)
+
+
+def store_side(rows_ref, row, result):
+    for q in range(4):
+        rows_ref[side_rows(q, row), :] = result[q * 32 : (q + 1) * 32]
+
+
+def load_side(rows_ref, row):
+    return jnp.concatenate([rows_ref[side_rows(q, row), :] for q in range(4)], axis=0)
+
+
+def columns_of(me, offsets):
+    return [pl.multiple_of((me ^ o) * ROWS, ROWS) for o in offsets]
+
+
+def pick_columns(full_ref, starts):
+    columns = [full_ref[:, pl.ds(s, ROWS), :] for s in starts]
+    return jnp.concatenate(columns, axis=1).reshape(PIECE, 128)
+
+
+def pack_kernel(me_ref, x_ref, cot_ref, mask_ref, own_ref, near_ref, far_ref, full_ref):
+    me = me_ref[0]
+    full_ref[...] = cot_ref[...].astype(F32)
+    mask = jnp.concatenate([mask_ref[...].astype(F32), jnp.zeros((ROWS, 128), F32)], axis=0)
+    places = [(own_ref, 0), (near_ref, 0), (far_ref, 0), (far_ref, HEAD + SIDE)]
+    for (ref, place), offset in zip(places, LEFT_OFFSETS):
+        piece = pick_columns(full_ref, columns_of(me ^ offset, RIGHT_OFFSETS))
+        ref[place : place + PIECE, :] = piece.astype(BF16)
+        ref[place + PIECE : place + HEAD, :] = mask.astype(BF16)
+    near_ref[HEAD:, :] = x_ref[...]
+    far_ref[HEAD : HEAD + SIDE, :] = x_ref[...]
+
+
+def own_kernel(
+    me_ref,
+    x_ref,
+    mask_ref,
+    weight_ref,
+    gate_weight_ref,
+    out_weight_ref,
+    gain_ref,
+    bias_ref,
+    mid_gain_ref,
+    mid_bias_ref,
+    left_ref,
+    right_ref,
+    sig_ref,
+    weight_t_ref,
+    block_ref,
+    mid_ref,
+    rows_ref,
+    scaled_ref,
+):
+    weight_t_ref[...] = weight_ref[...].astype(F32).T.astype(BF16)
+    for row in range(ROWS):
+        normed, _ = norm(x_ref[row * 128 : (row + 1) * 128, :].astype(F32), 1)
+        scaled = normed * gain_ref[...] + bias_ref[...]
+        scaled_ref[row] = scaled
+        projected = dot(weight_t_ref[...], scaled.astype(BF16), NT)
+        keep = mask_ref[row : row + 1].astype(F32)
+        for side in range(2):
+            base = 256 * side
+            gate, value = projected[base : base + 128], projected[base + 128 : base + 256]
+            result = sigmoid(gate) * value
+            store_side(rows_ref.at[side], row, result if side else result * keep)
+    left_ref[...] = rows_ref[0].astype(BF16)
+    right_ref[...] = rows_ref[1].astype(BF16)
+    picked = pick_columns(scaled_ref, columns_of(me_ref[0], RIGHT_OFFSETS))
+    sig_ref[...] = sigmoid(dot(picked.astype(BF16), gate_weight_ref[...], NN))
+
+    repeat = lax.broadcasted_iota(jnp.int32, (512, 128), 0)
+    lane = lax.broadcasted_iota(jnp.int32, (512, 128), 1)
+    spread = jnp.where((repeat >> 2) == lane, 1.0, 0.0).astype(BF16)
+    tall = dot(spread, out_weight_ref[...], NN)
+    for m in range(4):
+        block_ref[:, m * 128 : (m + 1) * 128] = jnp.where((repeat & 3) == m, tall, 0.0).astype(BF16)
+    rows = lax.broadcasted_iota(jnp.int32, (ROWS, 128), 0)
+    both = jnp.where(rows == 0, mid_gain_ref[...], mid_bias_ref[...])
+    wide = jnp.zeros((ROWS, 512), F32)
+    for _ in range(3):
+        term = both.astype(BF16)
+        wide = wide + dot(term, spread, NT)
+        both = both - term.astype(F32)
+    mid_ref[...] = wide
+
+
+def peer_kernel(side_at, piece_at):
+    def kernel(
+        me_ref,
+        message_ref,
+        *refs,
+    ):
+        right_in, rest = refs[:-9], refs[-9:]
+        weight_t_ref, gate_weight_ref, gain_ref, bias_ref = rest[:4]
+        left_ref, right_ref, sig_ref, rows_ref, scaled_ref = rest[4:]
+        per = SIDE // len(right_in)
+        for row in range(ROWS):
+            start = side_at + row * 128
+            normed, _ = norm(message_ref[start : start + 128, :].astype(F32), 1)
+            scaled = normed * gain_ref[...] + bias_ref[...]
+            scaled_ref[row] = scaled
+            projected = dot(weight_t_ref[:256, :], scaled.astype(BF16), NT)
+            at = piece_at + PIECE
+            keep = message_ref[at : at + 16, :].astype(F32)[row : row + 1]
+            store_side(rows_ref.at[0], row, sigmoid(projected[:128]) * projected[128:] * keep)
+        for row in range(ROWS):
+            ref, start = right_in[row * 128 // per], row * 128 % per
+            normed, _ = norm(ref[start : start + 128, :].astype(F32), 1)
+            scaled = normed * gain_ref[...] + bias_ref[...]
+            projected = dot(weight_t_ref[256:, :], scaled.astype(BF16), NT)
+            store_side(rows_ref.at[1], row, sigmoid(projected[:128]) * projected[128:])
+        left_ref[...] = rows_ref[0].astype(BF16)
+        right_ref[...] = rows_ref[1].astype(BF16)
+        picked = pick_columns(scaled_ref, columns_of(me_ref[0], RIGHT_OFFSETS))
+        sig_ref[...] = sigmoid(dot(picked.astype(BF16), gate_weight_ref[...], NN))
+
+    return kernel
+
+
+def split_sum(values, ones):
+    high = values.astype(BF16)
+    low = (values - high.astype(F32)).astype(BF16)
+    return dot(high, ones, NN) + dot(low, ones, NN)
+
+
+def block_kernel(*refs):
+    me_ref, left_refs, right_refs, sig_refs, message_refs = (
+        refs[0],
+        refs[1:5],
+        refs[5:9],
+        refs[9:13],
+        refs[13:17],
+    )
+    block_ref, mid_ref = refs[17:19]
+    out_refs, out_at = refs[19:23], (0, SIDE, 0, SIDE)
+    left_outs = (refs[23], refs[20], refs[24], refs[22])
+    right_outs = refs[25:31]
+    (pairs_ref,) = refs[31:]
+    piece_at = (0, 0, 0, SIDE)
+    me = me_ref[0]
+    groups = SIDE // 32
+    lane = lax.broadcasted_iota(jnp.int32, (ROWS, 128), 1)
+    of_quarter = [((lane >> 3) & 3) == q for q in range(4)]
+
+    seen = [r[a + PIECE : a + HEAD, :].astype(F32) for r, a in zip(message_refs, piece_at)]
+    valid = jnp.max(jnp.concatenate(seen, axis=0), axis=0, keepdims=True)
+    src = lax.broadcasted_iota(jnp.int32, (128, 128), 0)
+    dst = lax.broadcasted_iota(jnp.int32, (128, 128), 1)
+    pick = jnp.zeros((128, 128), F32)
+    for n, offset in enumerate(RIGHT_OFFSETS):
+        wanted = (me ^ offset) * ROWS + (dst & 7)
+        pick = jnp.where((src == wanted) & ((dst >> 5) == n), 1.0, pick)
+    spread = jnp.broadcast_to(valid, (ROWS, 128)).astype(BF16)
+    column_valid = dot(spread, pick.astype(BF16), NN)
+
+    def slab(side_refs, g):
+        return jnp.concatenate([r[g * 32 : (g + 1) * 32, :] for r in side_refs], axis=0)
+
+    for g in range(groups):
+        full = dot(slab(left_refs, g), slab(right_refs, g), NT).reshape(4, 4, ROWS, 128)
+        for m in range(4):
+            kept = full[m, 3]
+            for q in range(3):
+                kept = jnp.where(of_quarter[q], full[m, q], kept)
+            pairs_ref[g * 32 + m * ROWS : g * 32 + (m + 1) * ROWS, :] = kept * column_valid
+
+    turned = []
+    for row in range(ROWS):
+        turn = pairs_ref[pl.ds(row, 128, stride=ROWS), :].T.reshape(4, 4, ROWS, 128)
+        turned.append(jnp.concatenate([turn[:, q].reshape(32, 128) for q in range(4)], axis=1))
+    mixed = jnp.concatenate(turned, axis=0).astype(BF16).astype(F32)
+
+    ones = jnp.where((src & 3) == (dst & 3), 1.0, 0.0).astype(BF16)
+
+    def channel_mean(values):
+        total = values[:, :128] + values[:, 128:256] + values[:, 256:384] + values[:, 384:]
+        mean = split_sum(total, ones) * (1.0 / 128.0)
+        return jnp.concatenate([mean] * 4, axis=1)
+
+    mid_gain, mid_bias = mid_ref[0:1, :], mid_ref[1:2, :]
+    center = mixed - channel_mean(mixed)
+    inverse = lax.rsqrt(channel_mean(center * center) + EPSILON)
+    normed = center * inverse
+    scaled = (normed * mid_gain + mid_bias).astype(BF16)
+    update = dot(scaled, block_ref[...], NN)
+    grad_update = []
+    for m in range(4):
+        sig = sig_refs[m][...]
+        out = sig * update[:, m * 128 : (m + 1) * 128]
+        out_refs[m][out_at[m] : out_at[m] + PIECE, :] = out.astype(BF16)
+        cot = message_refs[m][piece_at[m] : piece_at[m] + PIECE, :].astype(F32)
+        grad_update.append((cot * sig).astype(BF16))
+    grad_hat = dot(jnp.concatenate(grad_update, axis=1), block_ref[...], NT) * mid_gain
+    first = channel_mean(grad_hat)
+    second = channel_mean(grad_hat * normed)
+    grad_mixed = inverse * (grad_hat - first - normed * second)
+
+    for row in range(ROWS):
+        part = grad_mixed[row * 32 : (row + 1) * 32]
+        parts = [part[:, q * 128 : (q + 1) * 128].reshape(4, 1, ROWS, 128) for q in range(4)]
+        turn = jnp.concatenate(parts, axis=1).reshape(128, 128)
+        pairs_ref[pl.ds(row, 128, stride=ROWS), :] = turn.T
+
+    def right_out(n, g):
+        if n < 2:
+            return right_outs[n], g * 32
+        half = groups // 2
+        return right_outs[2 * n - 2 + g // half], (g % half) * 32
+
+    for g in range(groups):
+        rows = []
+        for m in range(4):
+            part = pairs_ref[g * 32 + m * ROWS : g * 32 + (m + 1) * ROWS, :] * column_valid
+            rows += [jnp.where(of_quarter[q], part, 0.0) for q in range(4)]
+        spread = jnp.concatenate(rows, axis=0)
+        grad_right = dot(spread.T.astype(BF16), slab(left_refs, g), NN).astype(BF16)
+        grad_left = dot(spread.astype(BF16), slab(right_refs, g), NN).astype(BF16)
+        for m in range(4):
+            left_outs[m][g * 32 : (g + 1) * 32, :] = grad_left[m * 32 : (m + 1) * 32]
+            ref, at = right_out(m, g)
+            ref[at : at + 32, :] = grad_right[m * 32 : (m + 1) * 32]
+
+
+def add_kernel(mine_ref, got_ref, sum_ref):
+    sum_ref[...] = (mine_ref[...].astype(F32) + got_ref[...].astype(F32)).astype(BF16)
+
+
+def add_left_kernel(mine_ref, piece_ref, got_ref, sum_ref, out_ref):
+    sum_ref[...] = (mine_ref[...].astype(F32) + got_ref[:SIDE, :].astype(F32)).astype(BF16)
+    out_ref[:PIECE, :] = piece_ref[...]
+    out_ref[PIECE:, :] = got_ref[SIDE:, :]
+
+
+def factor_kernel(
+    x_ref,
+    cot_ref,
+    mask_ref,
+    gate_weight_ref,
+    gain_ref,
+    bias_ref,
+    weight_t_ref,
+    factor_ref,
+    normed_ref,
+    inverse_ref,
+    open_ref,
+    gain_t_ref,
+):
+    gain_t = jnp.broadcast_to(gain_ref[...], (128, 128)).T
+    bias_t = jnp.broadcast_to(bias_ref[...], (128, 128)).T
+    gain_t_ref[...] = gain_t
+    for row in range(ROWS):
+        x = x_ref[row * 128 : (row + 1) * 128, :].astype(F32)
+        normed, inverse = norm(x.T, 0)
+        normed_ref[row] = normed
+        inverse_ref[row : row + 1, :] = inverse
+        scaled = (normed * gain_t + bias_t).astype(BF16)
+        projected = dot(weight_t_ref[...], scaled, NN)
+        keep = mask_ref[row : row + 1].astype(F32)
+        for side in range(2):
+            base = 256 * side
+            gate = sigmoid(projected[base : base + 128])
+            value = projected[base + 128 : base + 256]
+            factor_ref[row, base : base + 128, :] = keep * value * gate * (1.0 - gate)
+            factor_ref[row, base + 128 : base + 256, :] = keep * gate
+        normed, _ = norm(x, 1)
+        scaled = (normed * gain_ref[...] + bias_ref[...]).astype(BF16)
+        gate_sig = sigmoid(dot(scaled, gate_weight_ref[...], NN))
+        open_ref[row] = cot_ref[row].astype(F32) * (1.0 - gate_sig)
+
+
+def out_kernel(me_ref, own_ref, near_ref, far_ref, open_ref, weight_ref, out_ref, grad_ref, full_ref):
+    places = [(own_ref, 0), (near_ref, SIDE), (far_ref, 0), (far_ref, PIECE)]
+    for (ref, at), offset in zip(places, LEFT_OFFSETS):
+        piece = ref[at : at + PIECE, :].astype(F32).reshape(ROWS, 4, ROWS, 128)
+        for n, start in enumerate(columns_of(me_ref[0] ^ offset, RIGHT_OFFSETS)):
+            full_ref[:, pl.ds(start, ROWS), :] = piece[:, n]
+    for row in range(ROWS):
+        out = full_ref[row]
+        out_ref[row] = out.astype(BF16)
+        grad_gate = (open_ref[row] * out).astype(BF16)
+        grad_ref[row] = dot(weight_ref[...], grad_gate, NT)
+
+
+def pair_kernel(*refs):
+    left_refs, right_refs = refs[0:3], refs[3:7]
+    factor_ref, normed_ref, inverse_ref, gain_t_ref, gate_ref, weight_ref = refs[7:13]
+    out_ref, rows_ref = refs[13:]
+    half = SIDE // 2
+    left = [r[:SIDE, :].astype(F32) for r in left_refs]
+    rows_ref[0] = left[0] + left[1] + left[2]
+    for part in range(2):
+        at = slice(part * half, (part + 1) * half)
+        right = right_refs[0][at, :].astype(F32) + right_refs[1][at, :].astype(F32)
+        rows_ref[1, at, :] = right + right_refs[2 + part][...].astype(F32)
+    for row in range(ROWS):
+        parts = []
+        for side in range(2):
+            grad = load_side(rows_ref.at[side], row)
+            for place in (256 * side, 256 * side + 128):
+                parts.append((grad * factor_ref[row, place : place + 128, :]).astype(BF16))
+        grad_scaled = dot(weight_ref[...], jnp.concatenate(parts, axis=0), NN) + gate_ref[row]
+        normed = normed_ref[row]
+        grad_hat = grad_scaled * gain_t_ref[...]
+        first = jnp.mean(grad_hat, axis=0, keepdims=True)
+        second = jnp.mean(grad_hat * normed, axis=0, keepdims=True)
+        grad = inverse_ref[row : row + 1, :] * (grad_hat - first - normed * second)
+        out_ref[row] = grad.T.astype(BF16)
+
+
+def swap(values, offset):
+    return lax.ppermute(values, "row", [(s, s ^ offset) for s in range(16)])
+
+
+def blocks_device(
+    pair_rep,
+    pair_mask,
+    cotangent,
+    in_gain,
+    in_bias,
+    proj_weight,
+    gate_weight,
+    mid_gain,
+    mid_bias,
+    out_weight,
+):
+    me = lax.axis_index("row").astype(jnp.int32).reshape(1)
+    gain, bias = in_gain.reshape(1, 128), in_bias.reshape(1, 128)
+    flat = pair_rep.reshape(SIDE, 128)
+    half = SIDE // 2
+    cube = (ROWS, 128, 128)
+    side, piece = ((SIDE, 128), BF16), ((PIECE, 128), BF16)
+    both, halves = ((SIDE + PIECE, 128), BF16), ((half, 128), BF16)
+    sig = ((PIECE, 128), F32)
+    rows_scratch = pltpu.VMEM((2, SIDE, 128), F32)
+    cube_scratch = pltpu.VMEM(cube, F32)
+
+    z_first = swap(flat[:half], Z_HIGH)
+    x_near = swap(flat, CHIP_X)
+    own_message, near_message, far_message = call(
+        pack_kernel,
+        [((HEAD, 128), BF16), ((HEAD + SIDE, 128), BF16), ((2 * HEAD + SIDE, 128), BF16)],
+        smem=[me],
+        hbm=[flat, cotangent, pair_mask],
+        scratch=[cube_scratch],
+    )
+    far = swap(far_message, Z_LOW)
+    near = swap(near_message, CORE)
+    z_second = swap(flat[half:], Z_HIGH)
+    left_0, right_0, sig_0, weight_t, block_weight, mid = call(
+        own_kernel,
+        [side, side, sig, ((512, 128), BF16), ((512, 512), BF16), ((ROWS, 512), F32)],
+        smem=[me],
+        hbm=[
+            flat,
+            pair_mask,
+            proj_weight,
+            gate_weight,
+            out_weight,
+            gain,
+            bias,
+            mid_gain.reshape(1, 128),
+            mid_bias.reshape(1, 128),
+        ],
+        scratch=[rows_scratch, cube_scratch],
+        micros=2,
+    )
+    x_first = swap(z_first, CHIP_X)
+    both_message = swap(far[HEAD:], CORE)
+    x_second = swap(z_second, CHIP_X)
+
+    def peer(message, side_at, piece_at, *right_in):
+        return call(
+            peer_kernel(side_at, piece_at),
+            [side, side, sig],
+            smem=[me],
+            hbm=[],
+            vmem=[message, *right_in, weight_t, gate_weight, gain, bias],
+            scratch=[rows_scratch, cube_scratch],
+            micros=2,
+        )
+
+    left_1, right_1, sig_1 = peer(near, HEAD, 0, x_near)
+    left_2, right_2, sig_2 = peer(far, HEAD, 0, z_first, z_second)
+    left_3, right_3, sig_3 = peer(both_message, 0, SIDE, x_first, x_second)
+
+    out_0, near_back, out_2, both_back, grad_left_0, grad_left_2, *grad_right = call(
+        block_kernel,
+        [piece, both, piece, both, side, side, side, side] + [halves] * 4,
+        smem=[me],
+        vmem=[left_0, left_1, left_2, left_3]
+        + [right_0, right_1, right_2, right_3]
+        + [sig_0, sig_1, sig_2, sig_3]
+        + [own_message, near, far, both_message]
+        + [block_weight, mid],
+        scratch=[pltpu.VMEM((SIDE, 128), F32)],
+        micros=3,
+    )
+    x_got = [swap(grad_right[4], CHIP_X), swap(grad_right[5], CHIP_X)]
+    both_got = swap(both_back, CORE)
+    z_got = []
+    for mine, got in zip(grad_right[2:4], x_got):
+        (total,) = call(add_kernel, [halves], vmem=[mine, got], micros=0.1)
+        z_got.append(swap(total, Z_HIGH))
+    left_sum, out_far = call(
+        add_left_kernel,
+        [side, ((2 * PIECE, 128), BF16)],
+        vmem=[grad_left_2, out_2, both_got],
+        micros=0.1,
+    )
+    out_far = swap(out_far, Z_LOW)
+    left_got = swap(left_sum, Z_LOW)
+    near_got = swap(near_back, CORE)
+    right_near = swap(grad_right[1], CHIP_X)
+
+    factors, normed, inverse, open_part, gain_t = call(
+        factor_kernel,
+        [((ROWS, 512, 128), F32), (cube, F32), ((ROWS, 128), F32), (cube, F32), ((128, 128), F32)],
+        hbm=[flat, cotangent, pair_mask, gate_weight, gain, bias],
+        vmem=[weight_t],
+        micros=2,
+    )
+    output, gate_part = call(
+        out_kernel,
+        [(cube, BF16), (cube, F32)],
+        smem=[me],
+        vmem=[out_0, near_got, out_far, open_part, gate_weight],
+        scratch=[cube_scratch],
+    )
+    (grad_pair,) = call(
+        pair_kernel,
+        [(cube, BF16)],
+        vmem=[grad_left_0, near_got, left_got, grad_right[0], right_near, *z_got]
+        + [factors, normed, inverse, gain_t, gate_part, proj_weight],
+        scratch=[rows_scratch],
+        micros=2,
+    )
+    return (output, grad_pair)
 
 
 def norm_stats(values, reduce_axis):
@@ -32,7 +542,7 @@
     return jnp.stack([grad_left, grad_right]).astype(jnp.bfloat16)
 
 
-def per_device(
+def channels_device(
     pair_rep,
     pair_mask,
     cotangent,
@@ -105,6 +615,7 @@
 
 
 def solution(mesh):
+    blocks = mesh.shape["row"] == 16 and mesh.shape["col"] == 1
     placed = (
         P(("grp", "row"), "col", None),
         P(("grp", "row"), "col"),
@@ -118,7 +629,7 @@
         P(),
     )
     return jax.shard_map(
-        per_device,
+        blocks_device if blocks else channels_device,
         mesh=mesh,
         in_specs=placed,
         out_specs=(P(("grp", "row"), "col", None), P(("grp", "row"), "col", None)),

time: 83 us -> 75.9 us (0.914)
  blocking collectives: 65.6 us -> 0 us
  waiting for transfers between devices: 0 us -> 31.2 us
  starting transfers between devices: 0 us -> 18.5 us
  Pallas kernels: 0 us -> 16.4 us
  matrix products: 5.61 us -> 0 us
  other arithmetic: 1.49 us -> 0 us
    all_to_all x4 -> x0, blocking collectives: 65.6 us -> none  [the longest x1 21.6 us: per_device(): lax.all_to_all(both_sides, 'row', split_axis=1, concat_axis=2, tiled=True)]
    ppermute x0 -> x17, waiting for transfers between devices: none -> 31.2 us  [swap(): return lax.ppermute(values, 'row', [(s, s ^ offset) for s in range(16)])]
    ppermute x0 -> x17, starting transfers between devices: none -> 18.5 us  [swap(): return lax.ppermute(values, 'row', [(s, s ^ offset) for s in range(16)])]
    pallas_call x0 -> x12, Pallas kernels: none -> 16.4 us  [call(): pl.pallas_call(body, out_shape=[jax.ShapeDtypeStruct(s, d) for s, d in ou...]
    dot_general x11 -> x0, matrix products: 5.61 us -> none  [the longest x1 1.33 us: per_device(): jnp.einsum('shij,csh->ijc', grad_value, weights_four[:, :, 1], preferred_...]
    unnamed x33 -> x36, local copies, waits for them, and re-layouts: 4.73 us -> 8.45 us
    convert_element_type x5 -> x0, local copies, waits for them, and re-layouts: 3.54 us -> none  [the longest x2 2.68 us: per_device(): side_float = grad_sides.astype(jnp.float32) * mask_float]
    convert_element_type x5 -> x0, other arithmetic: 1.19 us -> none  [the longest x1 0.73 us: per_device(): mask_float = pair_mask.astype(jnp.float32)]
  transfers between devices with their start and end apart: 0 -> 17, of which waited for: 0 -> 8; matrix products, arithmetic and copies ran while one was open for 0% -> 0% of each run, Pallas kernels for 0% -> 11%
where the time goes in v3:
time: 75.9 us; the launch traced here: 75.4 us
  waiting for transfers between devices  31.2 us (41%)
  starting transfers between devices  18.5 us (24%)
  Pallas kernels  16.4 us (22%)
  local copies, waits for them, and re-layouts  8.5 us (11%)
  between operations  0.88 us (1%)
    ppermute x17, waiting for transfers between devices, swap(): return lax.ppermute(values, 'row', [(s, s ^ offset) for s in range(16)])  31.2 us
    ppermute x17, starting transfers between devices, swap(): return lax.ppermute(values, 'row', [(s, s ^ offset) for s in range(16)])  18.5 us
    pallas_call x12, Pallas kernels, call(): pl.pallas_call(body, out_shape=[jax.ShapeDtypeStruct(s, d) for s, d in ou...  16.4 us
    unnamed x36, local copies, waits for them, and re-layouts  8.45 us
  transfers between devices with their start and end apart: 17, of which 8 were waited for; matrix products, arithmetic and copies ran while one was open for 0% of the time, Pallas kernels for 11%

profile of v3, /device:TPU:0, one launch (start us, length us, event | category | flops | bytes accessed | tf_op | source)
XLA Modules:
  0.0 75.4 jit_solution(5541743391762339261)
XLA Ops:
  0.6 0.0 copy-start
  0.6 0.9 %copy-done = bf16[8,128,128]{2,1,0:T(8,128)(2,1)S(1)} copy-done((bf16[8,128,128]{2,1,0:T(8,128)(2,1)S(1)}, bf16[8,128,128]{2,1,0:T(8,128)(2,1)}, u32[]{:S(2)}) %copy-start) | copy-done | bytes 262168
  1.6 0.9 %copy-done.4 = bf16[8,128,128]{2,1,0:T(8,128)(2,1)S(1)} copy-done((bf16[8,128,128]{2,1,0:T(8,128)(2,1)S(1)}, bf16[8,128,128]{2,1,0:T(8,128)(2,1)}, u32[]{:S(2)}) %copy-start.4) | copy-done | bytes 262168
  2.5 0.7 copy-done.9
  3.2 0.2 shard_map.114
  3.5 3.1 %collective-permute-start.2 = (bf16[1568,128]{1,0:T(8,128)(2,1)S(1)}, bf16[1568,128]{1,0:T(8,128)(2,1)S(1)}, u32[]{:S(2)}, u32[]{:S(2)}) collective-permute-start(bf16[1568,128]{1,0:T(8,128)(2,1)S(1)} %get-tuple-element.45), channel_id=1, source_target_pairs={{0,4},{1,5},{2,6},{3,7},{4,0},{5,1},{6,2},{7,3},{8,12},{9,13},{10,... | collective-permute-start | bytes 1204232 | tf_op jit(solution)/shard_map/ppermute | solution.py:390
  6.5 1.5 %collective-permute-start.1 = (bf16[1024,128]{1,0:T(8,128)(2,1)S(1)}, bf16[1024,128]{1,0:T(8,128)(2,1)S(1)}, u32[]{:S(2)}, u32[]{:S(2)}) collective-permute-start(bf16[1024,128]{1,0:T(8,128)(2,1)S(1)} %bitcast.9), channel_id=1, source_target_pairs={{0,2},{1,3},{2,0},{3,1},{4,6},{5,7},{6,4},{7,5},{8,10},{9,11},{10,... | collective-permute-start | bytes 786440 | tf_op jit(solution)/shard_map/ppermute | solution.py:390
  8.0 0.0 collective-permute-start
  8.0 7.8 %collective-permute-done.2.refs_1_.refs_15_ = bf16[1568,128]{1,0:T(8,128)(2,1)S(1)} collective-permute-done((bf16[1568,128]{1,0:T(8,128)(2,1)S(1)}, bf16[1568,128]{1,0:T(8,128)(2,1)S(1)}, u32[]{:S(2)}, u32[]{:S(2)}) %collective-permute-start.2) | collective-permute-done | bytes 401440 | tf_op jit(solution)/shard_map/ppermute | solution.py:390
  15.9 0.1 collective-permute-start.5
  16.0 2.8 %collective-permute-start.3 = (bf16[512,128]{1,0:T(8,128)(2,1)S(1)}, bf16[512,128]{1,0:T(8,128)(2,1)S(1)}, u32[]{:S(2)}, u32[]{:S(2)}) collective-permute-start(bf16[512,128]{1,0:T(8,128)(2,1)S(1)} %bitcast.25), channel_id=1, source_target_pairs={{0,8},{1,9},{2,10},{3,11},{4,12},{5,13},{6,14},{7,15},{8,0},{9,1},... | collective-permute-start | bytes 393224 | tf_op jit(solution)/shard_map/ppermute | solution.py:390
  18.8 0.2 collective-permute-start.4
  19.0 9.9 %collective-permute-done.3.refs_2_ = bf16[512,128]{1,0:T(8,128)(2,1)S(1)} collective-permute-done((bf16[512,128]{1,0:T(8,128)(2,1)S(1)}, bf16[512,128]{1,0:T(8,128)(2,1)S(1)}, u32[]{:S(2)}, u32[]{:S(2)}) %collective-permute-start.3) | collective-permute-done | bytes 131104 | tf_op jit(solution)/shard_map/ppermute | solution.py:390
  28.8 1.7 %collective-permute-start.6 = (bf16[512,128]{1,0:T(8,128)(2,1)S(1)}, bf16[512,128]{1,0:T(8,128)(2,1)S(1)}, u32[]{:S(2)}, u32[]{:S(2)}) collective-permute-start(bf16[512,128]{1,0:T(8,128)(2,1)S(1)} %collective-permute-done.3.refs_2_), channel_id=1, source_target_pairs={{0,2},{1,3},{2,0},{3,1},{4,6},{5,7},{6,4},{7,5},{8,10},{9,11},{10,... | collective-permute-start | bytes 393224 | tf_op jit(solution)/shard_map/ppermute | solution.py:390
  30.5 0.9 %collective-permute-done.4.refs_3_ = bf16[512,128]{1,0:T(8,128)(2,1)S(1)} collective-permute-done((bf16[512,128]{1,0:T(8,128)(2,1)S(1)}, bf16[512,128]{1,0:T(8,128)(2,1)S(1)}, u32[]{:S(2)}, u32[]{:S(2)}) %collective-permute-start.4) | collective-permute-done | bytes 131104 | tf_op jit(solution)/shard_map/ppermute | solution.py:390
  31.4 1.5 %collective-permute-start.7 = (bf16[512,128]{1,0:T(8,128)(2,1)S(1)}, bf16[512,128]{1,0:T(8,128)(2,1)S(1)}, u32[]{:S(2)}, u32[]{:S(2)}) collective-permute-start(bf16[512,128]{1,0:T(8,128)(2,1)S(1)} %collective-permute-done.4.refs_3_), channel_id=1, source_target_pairs={{0,2},{1,3},{2,0},{3,1},{4,6},{5,7},{6,4},{7,5},{8,10},{9,11},{10,... | collective-permute-start | bytes 393224 | tf_op jit(solution)/shard_map/ppermute | solution.py:390
  32.9 0.8 %copy-done.2 = bf16[128,128]{1,0:T(8,128)(2,1)S(1)} copy-done((bf16[128,128]{1,0:T(8,128)(2,1)S(1)}, bf16[128,128]{1,0:T(8,128)(2,1)}, u32[]{:S(2)}) %copy-start.2) | copy-done | bytes 32792
  33.7 0.9 %copy-done.6 = bf16[128,512]{1,0:T(8,128)(2,1)S(1)} copy-done((bf16[128,512]{1,0:T(8,128)(2,1)S(1)}, bf16[128,512]{1,0:T(8,128)(2,1)}, u32[]{:S(2)}) %copy-start.6) | copy-done | bytes 131096
  34.6 0.8 %copy-done.11 = bf16[128,128]{1,0:T(8,128)(2,1)S(1)} copy-done((bf16[128,128]{1,0:T(8,128)(2,1)S(1)}, bf16[128,128]{1,0:T(8,128)(2,1)}, u32[]{:S(2)}) %copy-start.11) | copy-done | bytes 32792
  35.3 0.7 copy-done.12
  36.0 0.7 copy-done.14
  36.6 0.7 copy-done.16
  37.3 0.7 copy-done.17
  38.0 2.2 %shard_map.113 = (bf16[1024,128]{1,0:T(8,128)(2,1)S(1)}, bf16[1024,128]{1,0:T(8,128)(2,1)S(1)}, f32[256,128]{1,0:T(8,128)S(1)}, bf16[512,128]{1,0:T(8,128)(2,1)S...) custom-call(s32[1]{0:T(128)} %bitcast.refs_0_, bf16[1024,128]{1,0:T(8,128)(2,1)S(1)} %bitcast.10, ...), custom_call_target="tpu_custom_call" | custom-call | bytes 6000000 | tf_op jit(solution)/shard_map/pallas_call | solution.py:65
  40.2 0.8 %copy-done.8 = bf16[512,512]{1,0:T(8,128)(2,1)} copy-done((bf16[512,512]{1,0:T(8,128)(2,1)}, bf16[512,512]{1,0:T(8,128)(2,1)S(1)}, u32[]{:S(2)}) %copy-start.8) | copy-done | bytes 524312
  41.0 0.0 collective-permute-done.1.refs_2_
  41.0 0.0 collective-permute-done.refs_1_.refs_14_
  41.0 1.7 %shard_map.115 = (bf16[1024,128]{1,0:T(8,128)(2,1)S(1)}, bf16[1024,128]{1,0:T(8,128)(2,1)S(1)}, f32[256,128]{1,0:T(8,128)S(1)}) custom-call(s32[1]{0:T(128)} %bitcast.refs_0_, bf16[1296,128]{1,0:T(8,128)(2,1)S(1)} %collective-permute-done.refs_1_.refs_14_, bf16[1024,128]{1,0:T(8,128)(2,1)S(1)} %collective-permute-done.1.refs_2_, ...), custom_call_target="tpu_custom_call" | custom-call | bytes 6000000 | tf_op jit(solution)/shard_map/pallas_call | solution.py:65
  42.7 1.7 %shard_map.116 = (bf16[1024,128]{1,0:T(8,128)(2,1)S(1)}, bf16[1024,128]{1,0:T(8,128)(2,1)S(1)}, f32[256,128]{1,0:T(8,128)S(1)}) custom-call(s32[1]{0:T(128)} %bitcast.refs_0_, bf16[1568,128]{1,0:T(8,128)(2,1)S(1)} %collective-permute-done.2.refs_1_.refs_15_, bf16[512,128]{1,0:T(8,128)(2,1)S(1)} %collective-permute-done.3.refs_2_, ...), custom_call_target="tpu_custom_call" | custom-call | bytes 6000000 | tf_op jit(solution)/shard_map/pallas_call | solution.py:65
  44.4 0.0 collective-permute-done.6.refs_2_
  44.4 0.0 collective-permute-done.7.refs_3_
  44.4 0.0 collective-permute-done.5.refs_1_.refs_16_
  44.4 1.7 %shard_map.117 = (bf16[1024,128]{1,0:T(8,128)(2,1)S(1)}, bf16[1024,128]{1,0:T(8,128)(2,1)S(1)}, f32[256,128]{1,0:T(8,128)S(1)}) custom-call(s32[1]{0:T(128)} %bitcast.refs_0_, bf16[1296,128]{1,0:T(8,128)(2,1)S(1)} %collective-permute-done.5.refs_1_.refs_16_, bf16[512,128]{1,0:T(8,128)(2,1)S(1)} %collective-permute-done.6.refs_2_, ...), custom_call_target="tpu_custom_call" | custom-call | bytes 6000000 | tf_op jit(solution)/shard_map/pallas_call | solution.py:65
  46.1 0.0 copy-start.1
  46.1 0.0 copy-start.3
  46.1 0.0 copy-start.5
  46.2 0.0 copy-start.10
  46.2 0.0 copy-start.13
  46.2 0.0 copy-start.15
  46.2 4.0 %shard_map.118 = (bf16[256,128]{1,0:T(8,128)(2,1)S(1)}, bf16[1280,128]{1,0:T(8,128)(2,1)S(1)}, bf16[256,128]{1,0:T(8,128)(2,1)S(1)}, bf16[1280,128]{1,0:T(8,128)...) custom-call(s32[1]{0:T(128)} %bitcast.refs_0_, ...), custom_call_target="tpu_custom_call" | custom-call | bytes 9000000 | tf_op jit(solution)/shard_map/pallas_call | solution.py:65
  50.2 0.0 copy-start.7
  50.2 0.1 collective-permute-start.9
  50.3 0.5 collective-permute-start.8
  50.8 0.5 collective-permute-start.13
  51.3 1.5 %collective-permute-start.15 = (bf16[512,128]{1,0:T(8,128)(2,1)S(1)}, bf16[512,128]{1,0:T(8,128)(2,1)S(1)}, u32[]{:S(2)}, u32[]{:S(2)}) collective-permute-start(bf16[512,128]{1,0:T(8,128)(2,1)S(1)} %get-tuple-element.74), channel_id=1, source_target_pairs={{0,2},{1,3},{2,0},{3,1},{4,6},{5,7},{6,4},{7,5},{8,10},{9,11},{10,... | collective-permute-start | bytes 393224 | tf_op jit(solution)/shard_map/ppermute | solution.py:390
  52.8 0.5 collective-permute-start.12
  53.3 0.0 collective-permute-done.9.refs_2_
  53.3 0.1 shard_map.119
  53.4 0.8 %collective-permute-start.11 = (bf16[1024,128]{1,0:T(8,128)(2,1)S(1)}, bf16[1024,128]{1,0:T(8,128)(2,1)S(1)}, u32[]{:S(2)}, u32[]{:S(2)}) collective-permute-start(bf16[1024,128]{1,0:T(8,128)(2,1)S(1)} %get-tuple-element.68), channel_id=1, source_target_pairs={{0,4},{1,5},{2,6},{3,7},{4,0},{5,1},{6,2},{7,3},{8,12},{9,13},{10,... | collective-permute-start | bytes 786440 | tf_op jit(solution)/shard_map/ppermute | solution.py:390
  54.2 3.0 %collective-permute-done.13.refs_1_ = bf16[512,128]{1,0:T(8,128)(2,1)S(1)} collective-permute-done((bf16[512,128]{1,0:T(8,128)(2,1)S(1)}, bf16[512,128]{1,0:T(8,128)(2,1)S(1)}, u32[]{:S(2)}, u32[]{:S(2)}) %collective-permute-start.13) | collective-permute-done | bytes 131104 | tf_op jit(solution)/shard_map/ppermute | solution.py:390
  57.2 0.8 %collective-permute-start.10 = (bf16[512,128]{1,0:T(8,128)(2,1)S(1)}, bf16[512,128]{1,0:T(8,128)(2,1)S(1)}, u32[]{:S(2)}, u32[]{:S(2)}) collective-permute-start(bf16[512,128]{1,0:T(8,128)(2,1)S(1)} %get-tuple-element.64), channel_id=1, source_target_pairs={{0,4},{1,5},{2,6},{3,7},{4,0},{5,1},{6,2},{7,3},{8,12},{9,13},{10,... | collective-permute-start | bytes 393224 | tf_op jit(solution)/shard_map/ppermute | solution.py:390
  57.9 2.0 %collective-permute-done.15.refs_1_ = bf16[512,128]{1,0:T(8,128)(2,1)S(1)} collective-permute-done((bf16[512,128]{1,0:T(8,128)(2,1)S(1)}, bf16[512,128]{1,0:T(8,128)(2,1)S(1)}, u32[]{:S(2)}, u32[]{:S(2)}) %collective-permute-start.15) | collective-permute-done | bytes 131104 | tf_op jit(solution)/shard_map/ppermute | solution.py:390
  59.9 1.4 %collective-permute-start.14 = (bf16[512,128]{1,0:T(8,128)(2,1)S(1)}, bf16[512,128]{1,0:T(8,128)(2,1)S(1)}, u32[]{:S(2)}, u32[]{:S(2)}) collective-permute-start(bf16[512,128]{1,0:T(8,128)(2,1)S(1)} %shard_map.122), channel_id=1, source_target_pairs={{0,8},{1,9},{2,10},{3,11},{4,12},{5,13},{6,14},{7,15},{8,0},{9,1},... | collective-permute-start | bytes 393224 | tf_op jit(solution)/shard_map/ppermute | solution.py:390
  61.3 0.0 collective-permute-done.8.refs_2_.refs_1_
  61.3 1.6 %collective-permute-start.16 = (bf16[512,128]{1,0:T(8,128)(2,1)S(1)}, bf16[512,128]{1,0:T(8,128)(2,1)S(1)}, u32[]{:S(2)}, u32[]{:S(2)}) collective-permute-start(bf16[512,128]{1,0:T(8,128)(2,1)S(1)} %shard_map.123), channel_id=1, source_target_pairs={{0,8},{1,9},{2,10},{3,11},{4,12},{5,13},{6,14},{7,15},{8,0},{9,1},... | collective-permute-start | bytes 393224 | tf_op jit(solution)/shard_map/ppermute | solution.py:390
  63.0 0.0 copy-done.1
  63.0 1.5 %shard_map.120 = (f32[8,512,128]{2,1,0:T(8,128)S(1)}, f32[8,128,128]{2,1,0:T(8,128)S(1)}, f32[8,128]{1,0:T(8,128)S(1)}, f32[8,128,128]{2,1,0:T(8,128)S(1)}, f32[128,128]{1,0:T(8,128)S(1)}) custom-call(bf16[1024,128]{1,0:T(8,128)(2,1)S(1)} %bitcast.11, bf16[8,128,128]{2,1,0:T(8,128)(2,1)S(1)} %copy-done.5, s32[8,128]{1,0:T(8,128)S(1)} %copy-done.10, ...), custom_call_target="tpu_custom_call" | custom-call | bytes 6000000 | tf_op jit(solution)/shard_map/pallas_call | solution.py:65
  64.6 2.9 %collective-permute-done.10.refs_3_ = bf16[512,128]{1,0:T(8,128)(2,1)S(1)} collective-permute-done((bf16[512,128]{1,0:T(8,128)(2,1)S(1)}, bf16[512,128]{1,0:T(8,128)(2,1)S(1)}, u32[]{:S(2)}, u32[]{:S(2)}) %collective-permute-start.10) | collective-permute-done | bytes 131104 | tf_op jit(solution)/shard_map/ppermute | solution.py:390
  67.4 0.9 %shard_map.121 = (bf16[8,128,128]{2,1,0:T(8,128)(2,1)}, f32[8,128,128]{2,1,0:T(8,128)S(1)}) custom-call(s32[1]{0:T(128)} %bitcast.refs_0_, bf16[256,128]{1,0:T(8,128)(2,1)S(1)} %get-tuple-element.59.refs_1_, bf16[1280,128]{1,0:T(8,128)(2,1)S(1)} %collective-permute-done.8.refs_2_.refs_1_, bf16[512,128]{1,0:T(8,128)(2,1)S(1)} %collective-permute-done.10.refs_3_, ...), custom_call_target="tpu_custom_call" | custom-call | bytes 3000000 | tf_op jit(solution)/shard_map/pallas_call | solution.py:65
  68.3 3.4 %collective-permute-done.14.refs_5_ = bf16[512,128]{1,0:T(8,128)(2,1)S(1)} collective-permute-done((bf16[512,128]{1,0:T(8,128)(2,1)S(1)}, bf16[512,128]{1,0:T(8,128)(2,1)S(1)}, u32[]{:S(2)}, u32[]{:S(2)}) %collective-permute-start.14) | collective-permute-done | bytes 131104 | tf_op jit(solution)/shard_map/ppermute | solution.py:390
  71.7 1.4 %collective-permute-done.16.refs_6_ = bf16[512,128]{1,0:T(8,128)(2,1)S(1)} collective-permute-done((bf16[512,128]{1,0:T(8,128)(2,1)S(1)}, bf16[512,128]{1,0:T(8,128)(2,1)S(1)}, u32[]{:S(2)}, u32[]{:S(2)}) %collective-permute-start.16) | collective-permute-done | bytes 131104 | tf_op jit(solution)/shard_map/ppermute | solution.py:390
  73.1 0.0 collective-permute-done.12.refs_4_
  73.1 0.0 collective-permute-done.11.refs_2_
  73.1 2.4 %shard_map.124 = bf16[8,128,128]{2,1,0:T(8,128)(2,1)} custom-call(bf16[1024,128]{1,0:T(8,128)(2,1)S(1)} %get-tuple-element.67.refs_0_, bf16[1280,128]{1,0:T(8,128)(2,1)S(1)} %collective-permute-done.8.refs_2_.refs_1_, bf16[1024,128]{1,0:T(8,128)(2,1)S(1)} %collective-permute-done.11.refs_2_, bf16[1024,128]{1,0:T(8,128)(2,1)S(1)} %get-tuple-element.69.refs_3_, ...), custom_call_target="tpu_custom_call" | custom-call | bytes 6000000 | tf_op jit(solution)/shard_map/pallas_call | solution.py:65
  (20 shorter events, 0.1 us)
Async XLA Ops:
  0.6 1.0 %copy-start = (bf16[8,128,128]{2,1,0:T(8,128)(2,1)S(1)}, bf16[8,128,128]{2,1,0:T(8,128)(2,1)}, u32[]{:S(2)}) copy-start(bf16[8,128,128]{2,1,0:T(8,128)(2,1)} %param.10) | copy-start | bytes 786436
  1.6 0.9 %copy-start.4 = (bf16[8,128,128]{2,1,0:T(8,128)(2,1)S(1)}, bf16[8,128,128]{2,1,0:T(8,128)(2,1)}, u32[]{:S(2)}) copy-start(bf16[8,128,128]{2,1,0:T(8,128)(2,1)} %refs_1_.1) | copy-start | bytes 786436
  2.5 0.7 copy-start.9
  3.5 12.4 %collective-permute-start.2 = (bf16[1568,128]{1,0:T(8,128)(2,1)S(1)}, bf16[1568,128]{1,0:T(8,128)(2,1)S(1)}, u32[]{:S(2)}, u32[]{:S(2)}) collective-permute-start(bf16[1568,128]{1,0:T(8,128)(2,1)S(1)} %get-tuple-element.45), channel_id=1, source_target_pairs={{0,4},{1,5},{2,6},{3,7},{4,0},{5,1},{6,2},{7,3},{8,12},{9,13},{10,... | collective-permute-start | bytes 1204232 | tf_op jit(solution)/shard_map/ppermute | solution.py:390
  6.5 34.4 %collective-permute-start.1 = (bf16[1024,128]{1,0:T(8,128)(2,1)S(1)}, bf16[1024,128]{1,0:T(8,128)(2,1)S(1)}, u32[]{:S(2)}, u32[]{:S(2)}) collective-permute-start(bf16[1024,128]{1,0:T(8,128)(2,1)S(1)} %bitcast.9), channel_id=1, source_target_pairs={{0,2},{1,3},{2,0},{3,1},{4,6},{5,7},{6,4},{7,5},{8,10},{9,11},{10,... | collective-permute-start | bytes 786440 | tf_op jit(solution)/shard_map/ppermute | solution.py:390
  8.0 33.0 %collective-permute-start = (bf16[1296,128]{1,0:T(8,128)(2,1)S(1)}, bf16[1296,128]{1,0:T(8,128)(2,1)S(1)}, u32[]{:S(2)}, u32[]{:S(2)}) collective-permute-start(bf16[1296,128]{1,0:T(8,128)(2,1)S(1)} %get-tuple-element.42), channel_id=1, source_target_pairs={{0,1},{1,0},{2,3},{3,2},{4,5},{5,4},{6,7},{7,6},{8,9},{9,8},{10,11... | collective-permute-start | bytes 995336 | tf_op jit(solution)/shard_map/ppermute | solution.py:390
  15.9 28.6 %collective-permute-start.5 = (bf16[1296,128]{1,0:T(8,128)(2,1)S(1)}, bf16[1296,128]{1,0:T(8,128)(2,1)S(1)}, u32[]{:S(2)}, u32[]{:S(2)}) collective-permute-start(bf16[1296,128]{1,0:T(8,128)(2,1)S(1)} %slice.20), channel_id=1, source_target_pairs={{0,1},{1,0},{2,3},{3,2},{4,5},{5,4},{6,7},{7,6},{8,9},{9,8},{10,11... | collective-permute-start | bytes 995336 | tf_op jit(solution)/shard_map/ppermute | solution.py:390
  16.0 12.9 %collective-permute-start.3 = (bf16[512,128]{1,0:T(8,128)(2,1)S(1)}, bf16[512,128]{1,0:T(8,128)(2,1)S(1)}, u32[]{:S(2)}, u32[]{:S(2)}) collective-permute-start(bf16[512,128]{1,0:T(8,128)(2,1)S(1)} %bitcast.25), channel_id=1, source_target_pairs={{0,8},{1,9},{2,10},{3,11},{4,12},{5,13},{6,14},{7,15},{8,0},{9,1},... | collective-permute-start | bytes 393224 | tf_op jit(solution)/shard_map/ppermute | solution.py:390
  18.8 12.6 %collective-permute-start.4 = (bf16[512,128]{1,0:T(8,128)(2,1)S(1)}, bf16[512,128]{1,0:T(8,128)(2,1)S(1)}, u32[]{:S(2)}, u32[]{:S(2)}) collective-permute-start(bf16[512,128]{1,0:T(8,128)(2,1)S(1)} %bitcast.24), channel_id=1, source_target_pairs={{0,8},{1,9},{2,10},{3,11},{4,12},{5,13},{6,14},{7,15},{8,0},{9,1},... | collective-permute-start | bytes 393224 | tf_op jit(solution)/shard_map/ppermute | solution.py:390
  28.8 15.6 %collective-permute-start.6 = (bf16[512,128]{1,0:T(8,128)(2,1)S(1)}, bf16[512,128]{1,0:T(8,128)(2,1)S(1)}, u32[]{:S(2)}, u32[]{:S(2)}) collective-permute-start(bf16[512,128]{1,0:T(8,128)(2,1)S(1)} %collective-permute-done.3.refs_2_), channel_id=1, source_target_pairs={{0,2},{1,3},{2,0},{3,1},{4,6},{5,7},{6,4},{7,5},{8,10},{9,11},{10,... | collective-permute-start | bytes 393224 | tf_op jit(solution)/shard_map/ppermute | solution.py:390
  31.4 13.0 %collective-permute-start.7 = (bf16[512,128]{1,0:T(8,128)(2,1)S(1)}, bf16[512,128]{1,0:T(8,128)(2,1)S(1)}, u32[]{:S(2)}, u32[]{:S(2)}) collective-permute-start(bf16[512,128]{1,0:T(8,128)(2,1)S(1)} %collective-permute-done.4.refs_3_), channel_id=1, source_target_pairs={{0,2},{1,3},{2,0},{3,1},{4,6},{5,7},{6,4},{7,5},{8,10},{9,11},{10,... | collective-permute-start | bytes 393224 | tf_op jit(solution)/shard_map/ppermute | solution.py:390
  32.9 0.8 %copy-start.2 = (bf16[128,128]{1,0:T(8,128)(2,1)S(1)}, bf16[128,128]{1,0:T(8,128)(2,1)}, u32[]{:S(2)}) copy-start(bf16[128,128]{1,0:T(8,128)(2,1)} %refs_5_.7) | copy-start | bytes 98308
  33.7 0.9 %copy-start.6 = (bf16[128,512]{1,0:T(8,128)(2,1)S(1)}, bf16[128,512]{1,0:T(8,128)(2,1)}, u32[]{:S(2)}) copy-start(bf16[128,512]{1,0:T(8,128)(2,1)} %refs_12_.1) | copy-start | bytes 393220
  34.6 0.8 %copy-start.11 = (bf16[128,128]{1,0:T(8,128)(2,1)S(1)}, bf16[128,128]{1,0:T(8,128)(2,1)}, u32[]{:S(2)}) copy-start(bf16[128,128]{1,0:T(8,128)(2,1)} %refs_5_.4) | copy-start | bytes 98308
  35.3 0.7 copy-start.12
  36.0 0.7 copy-start.14
  36.6 0.7 copy-start.16
  37.3 0.7 copy-start.17
  40.2 0.8 %copy-start.8 = (bf16[512,512]{1,0:T(8,128)(2,1)}, bf16[512,512]{1,0:T(8,128)(2,1)S(1)}, u32[]{:S(2)}) copy-start(bf16[512,512]{1,0:T(8,128)(2,1)S(1)} %get-tuple-element.57.refs_17_) | copy-start | bytes 1572868
  46.1 16.8 %copy-start.1 = (bf16[8,128,128]{2,1,0:T(8,128)(2,1)S(1)}, bf16[8,128,128]{2,1,0:T(8,128)(2,1)}, u32[]{:S(2)}) copy-start(bf16[8,128,128]{2,1,0:T(8,128)(2,1)} %param.10) | copy-start | bytes 786436
  46.1 16.8 %copy-start.3 = (bf16[128,128]{1,0:T(8,128)(2,1)S(1)}, bf16[128,128]{1,0:T(8,128)(2,1)}, u32[]{:S(2)}) copy-start(bf16[128,128]{1,0:T(8,128)(2,1)} %refs_5_.7) | copy-start | bytes 98308
  46.1 16.8 %copy-start.5 = (bf16[8,128,128]{2,1,0:T(8,128)(2,1)S(1)}, bf16[8,128,128]{2,1,0:T(8,128)(2,1)}, u32[]{:S(2)}) copy-start(bf16[8,128,128]{2,1,0:T(8,128)(2,1)} %refs_1_.1) | copy-start | bytes 786436
  46.2 16.8 %copy-start.10 = (s32[8,128]{1,0:T(8,128)S(1)}, s32[8,128]{1,0:T(8,128)}, u32[]{:S(2)}) copy-start(s32[8,128]{1,0:T(8,128)} %refs_2_.5) | copy-start | bytes 12292
  46.2 16.8 %copy-start.13 = (f32[128]{0:T(128)S(1)}, f32[128]{0:T(128)}, u32[]{:S(2)}) copy-start(f32[128]{0:T(128)} %param.13) | copy-start | bytes 1540
  46.2 16.8 %copy-start.15 = (f32[128]{0:T(128)S(1)}, f32[128]{0:T(128)}, u32[]{:S(2)}) copy-start(f32[128]{0:T(128)} %param.14) | copy-start | bytes 1540
  50.2 22.9 %copy-start.7 = (bf16[128,512]{1,0:T(8,128)(2,1)S(1)}, bf16[128,512]{1,0:T(8,128)(2,1)}, u32[]{:S(2)}) copy-start(bf16[128,512]{1,0:T(8,128)(2,1)} %refs_12_.1) | copy-start | bytes 393220
  50.2 3.1 %collective-permute-start.9 = (bf16[1280,128]{1,0:T(8,128)(2,1)S(1)}, bf16[1280,128]{1,0:T(8,128)(2,1)S(1)}, u32[]{:S(2)}, u32[]{:S(2)}) collective-permute-start(bf16[1280,128]{1,0:T(8,128)(2,1)S(1)} %get-tuple-element.63), channel_id=1, source_target_pairs={{0,1},{1,0},{2,3},{3,2},{4,5},{5,4},{6,7},{7,6},{8,9},{9,8},{10,11... | collective-permute-start | bytes 983048 | tf_op jit(solution)/shard_map/ppermute | solution.py:390
  50.3 11.1 %collective-permute-start.8 = (bf16[1280,128]{1,0:T(8,128)(2,1)S(1)}, bf16[1280,128]{1,0:T(8,128)(2,1)S(1)}, u32[]{:S(2)}, u32[]{:S(2)}) collective-permute-start(bf16[1280,128]{1,0:T(8,128)(2,1)S(1)} %get-tuple-element.60), channel_id=1, source_target_pairs={{0,1},{1,0},{2,3},{3,2},{4,5},{5,4},{6,7},{7,6},{8,9},{9,8},{10,11... | collective-permute-start | bytes 983048 | tf_op jit(solution)/shard_map/ppermute | solution.py:390
  50.8 6.4 %collective-permute-start.13 = (bf16[512,128]{1,0:T(8,128)(2,1)S(1)}, bf16[512,128]{1,0:T(8,128)(2,1)S(1)}, u32[]{:S(2)}, u32[]{:S(2)}) collective-permute-start(bf16[512,128]{1,0:T(8,128)(2,1)S(1)} %get-tuple-element.72), channel_id=1, source_target_pairs={{0,2},{1,3},{2,0},{3,1},{4,6},{5,7},{6,4},{7,5},{8,10},{9,11},{10,... | collective-permute-start | bytes 393224 | tf_op jit(solution)/shard_map/ppermute | solution.py:390
  51.3 8.7 %collective-permute-start.15 = (bf16[512,128]{1,0:T(8,128)(2,1)S(1)}, bf16[512,128]{1,0:T(8,128)(2,1)S(1)}, u32[]{:S(2)}, u32[]{:S(2)}) collective-permute-start(bf16[512,128]{1,0:T(8,128)(2,1)S(1)} %get-tuple-element.74), channel_id=1, source_target_pairs={{0,2},{1,3},{2,0},{3,1},{4,6},{5,7},{6,4},{7,5},{8,10},{9,11},{10,... | collective-permute-start | bytes 393224 | tf_op jit(solution)/shard_map/ppermute | solution.py:390
  52.8 20.3 %collective-permute-start.12 = (bf16[1024,128]{1,0:T(8,128)(2,1)S(1)}, bf16[1024,128]{1,0:T(8,128)(2,1)S(1)}, u32[]{:S(2)}, u32[]{:S(2)}) collective-permute-start(bf16[1024,128]{1,0:T(8,128)(2,1)S(1)} %get-tuple-element.70), channel_id=1, source_target_pairs={{0,2},{1,3},{2,0},{3,1},{4,6},{5,7},{6,4},{7,5},{8,10},{9,11},{10,... | collective-permute-start | bytes 786440 | tf_op jit(solution)/shard_map/ppermute | solution.py:390
  53.4 19.7 %collective-permute-start.11 = (bf16[1024,128]{1,0:T(8,128)(2,1)S(1)}, bf16[1024,128]{1,0:T(8,128)(2,1)S(1)}, u32[]{:S(2)}, u32[]{:S(2)}) collective-permute-start(bf16[1024,128]{1,0:T(8,128)(2,1)S(1)} %get-tuple-element.68), channel_id=1, source_target_pairs={{0,4},{1,5},{2,6},{3,7},{4,0},{5,1},{6,2},{7,3},{8,12},{9,13},{10,... | collective-permute-start | bytes 786440 | tf_op jit(solution)/shard_map/ppermute | solution.py:390
  57.2 10.3 %collective-permute-start.10 = (bf16[512,128]{1,0:T(8,128)(2,1)S(1)}, bf16[512,128]{1,0:T(8,128)(2,1)S(1)}, u32[]{:S(2)}, u32[]{:S(2)}) collective-permute-start(bf16[512,128]{1,0:T(8,128)(2,1)S(1)} %get-tuple-element.64), channel_id=1, source_target_pairs={{0,4},{1,5},{2,6},{3,7},{4,0},{5,1},{6,2},{7,3},{8,12},{9,13},{10,... | collective-permute-start | bytes 393224 | tf_op jit(solution)/shard_map/ppermute | solution.py:390
  59.9 11.7 %collective-permute-start.14 = (bf16[512,128]{1,0:T(8,128)(2,1)S(1)}, bf16[512,128]{1,0:T(8,128)(2,1)S(1)}, u32[]{:S(2)}, u32[]{:S(2)}) collective-permute-start(bf16[512,128]{1,0:T(8,128)(2,1)S(1)} %shard_map.122), channel_id=1, source_target_pairs={{0,8},{1,9},{2,10},{3,11},{4,12},{5,13},{6,14},{7,15},{8,0},{9,1},... | collective-permute-start | bytes 393224 | tf_op jit(solution)/shard_map/ppermute | solution.py:390
  61.3 11.7 %collective-permute-start.16 = (bf16[512,128]{1,0:T(8,128)(2,1)S(1)}, bf16[512,128]{1,0:T(8,128)(2,1)S(1)}, u32[]{:S(2)}, u32[]{:S(2)}) collective-permute-start(bf16[512,128]{1,0:T(8,128)(2,1)S(1)} %shard_map.123), channel_id=1, source_target_pairs={{0,8},{1,9},{2,10},{3,11},{4,12},{5,13},{6,14},{7,15},{8,0},{9,1},... | collective-permute-start | bytes 393224 | tf_op jit(solution)/shard_map/ppermute | solution.py:390

commit v4 on v3

--- a/solution.py
+++ b/solution.py
@@ -14,9 +14,11 @@
 PIECE = 256
 HEAD = PIECE + 16
 VMEM_BYTES = 48 * 2**20
+WAIT = 5 * 10**9
 
 NT = (((1,), (1,)), ((), ()))
 NN = (((1,), (0,)), ((), ()))
+TN = (((0,), (0,)), ((), ()))
 F32, BF16 = jnp.float32, jnp.bfloat16
 
 
@@ -31,48 +33,36 @@
 
 
 def sigmoid(x):
-    return 1.0 / (1.0 + jnp.exp(-x))
-
-
-def call(kernel, outs, smem=(), hbm=(), vmem=(), scratch=(), micros=1):
-    here, there = len(smem), len(smem) + len(hbm)
-    total = there + len(vmem)
-    count = len(hbm)
-
-    def body(*refs):
-        ins, rest = refs[:total], refs[total:]
-        results, extra = rest[: len(outs)], rest[len(outs) :]
-        buffers, extra = extra[:count], extra[count:]
-        if count:
-            sems, extra = extra[0], extra[1:]
-            copies = [
-                pltpu.make_async_copy(src, dst, sems.at[n])
-                for n, (src, dst) in enumerate(zip(ins[here:there], buffers))
-            ]
-            for c in copies:
-                c.start()
-            for c in copies:
-                c.wait()
-        kernel(*ins[:here], *buffers, *ins[there:], *results, *extra)
-
+    return 0.5 * jnp.tanh(0.5 * x) + 0.5
+
+
+def call(kernel, outs, smem=(), hbm=(), vmem=(), scratch=(), weight=2**26, limit=VMEM_BYTES):
     vmem_spec = pl.BlockSpec(memory_space=pltpu.VMEM)
-    specs = [pl.BlockSpec(memory_space=pltpu.SMEM)] * here
-    specs += [pl.BlockSpec(memory_space=pl.ANY)] * count
+    specs = [pl.BlockSpec(memory_space=pltpu.SMEM)] * len(smem)
+    specs += [pl.BlockSpec(memory_space=pltpu.HBM)] * len(hbm)
     specs += [vmem_spec] * len(vmem)
-    own = [pltpu.VMEM(a.shape, a.dtype) for a in hbm]
-    if count:
-        own.append(pltpu.SemaphoreType.DMA((count,)))
     return pl.pallas_call(
-        body,
+        kernel,
         out_shape=[jax.ShapeDtypeStruct(s, d) for s, d in outs],
         in_specs=specs,
         out_specs=[vmem_spec] * len(outs),
-        scratch_shapes=own + list(scratch),
-        compiler_params=pltpu.CompilerParams(vmem_limit_bytes=VMEM_BYTES),
-        cost_estimate=pl.CostEstimate(
-            flops=0, bytes_accessed=int(micros * 3.0e6), transcendentals=0
-        ),
+        scratch_shapes=list(scratch),
+        compiler_params=pltpu.CompilerParams(vmem_limit_bytes=limit),
+        cost_estimate=pl.CostEstimate(flops=weight, bytes_accessed=2**18, transcendentals=0),
     )(*smem, *hbm, *vmem)
+
+
+def load_kernel(*refs):
+    count = (len(refs) - 3) // 2
+    ins, outs = refs[:count], refs[count:-1]
+    half = SIDE // 2
+    pairs = list(zip(ins, outs[:count]))
+    pairs += [(ins[0].at[pl.ds(n * half, half)], outs[count + n]) for n in range(2)]
+    copies = [pltpu.make_async_copy(a, b, refs[-1].at[n]) for n, (a, b) in enumerate(pairs)]
+    for c in copies:
+        c.start()
+    for c in copies:
+        c.wait()
 
 
 def side_rows(quarter, row):
@@ -211,10 +201,11 @@
         refs[13:17],
     )
     block_ref, mid_ref = refs[17:19]
-    out_refs, out_at = refs[19:23], (0, SIDE, 0, SIDE)
-    left_outs = (refs[23], refs[20], refs[24], refs[22])
-    right_outs = refs[25:31]
-    (pairs_ref,) = refs[31:]
+    core_ref = refs[21]
+    out_refs, out_at = (refs[19], core_ref, refs[20], core_ref), (0, SIDE, 0, 2 * SIDE + PIECE)
+    left_outs, left_at = (refs[22], core_ref, refs[23], core_ref), (0, 0, 0, SIDE + PIECE)
+    right_outs = refs[24:30]
+    (pairs_ref,) = refs[30:]
     piece_at = (0, 0, 0, SIDE)
     me = me_ref[0]
     groups = SIDE // 32
@@ -291,23 +282,32 @@
         for m in range(4):
             part = pairs_ref[g * 32 + m * ROWS : g * 32 + (m + 1) * ROWS, :] * column_valid
             rows += [jnp.where(of_quarter[q], part, 0.0) for q in range(4)]
-        spread = jnp.concatenate(rows, axis=0)
-        grad_right = dot(spread.T.astype(BF16), slab(left_refs, g), NN).astype(BF16)
-        grad_left = dot(spread.astype(BF16), slab(right_refs, g), NN).astype(BF16)
+        spread = jnp.concatenate(rows, axis=0).astype(BF16)
+        grad_right = dot(spread, slab(left_refs, g), TN).astype(BF16)
+        grad_left = dot(spread, slab(right_refs, g), NN).astype(BF16)
         for m in range(4):
-            left_outs[m][g * 32 : (g + 1) * 32, :] = grad_left[m * 32 : (m + 1) * 32]
+            at = left_at[m] + g * 32
+            left_outs[m][at : at + 32, :] = grad_left[m * 32 : (m + 1) * 32]
             ref, at = right_out(m, g)
             ref[at : at + 32, :] = grad_right[m * 32 : (m + 1) * 32]
 
 
+def pass_kernel(start):
+    def kernel(message_ref, *refs):
+        refs[-1][...] = message_ref[start:, :]
+
+    return kernel
+
+
 def add_kernel(mine_ref, got_ref, sum_ref):
     sum_ref[...] = (mine_ref[...].astype(F32) + got_ref[...].astype(F32)).astype(BF16)
 
 
 def add_left_kernel(mine_ref, piece_ref, got_ref, sum_ref, out_ref):
-    sum_ref[...] = (mine_ref[...].astype(F32) + got_ref[:SIDE, :].astype(F32)).astype(BF16)
+    at = SIDE + PIECE
+    sum_ref[...] = (mine_ref[...].astype(F32) + got_ref[at : at + SIDE, :].astype(F32)).astype(BF16)
     out_ref[:PIECE, :] = piece_ref[...]
-    out_ref[PIECE:, :] = got_ref[SIDE:, :]
+    out_ref[PIECE:, :] = got_ref[at + SIDE :, :]
 
 
 def factor_kernel(
@@ -403,68 +403,71 @@
     out_weight,
 ):
     me = lax.axis_index("row").astype(jnp.int32).reshape(1)
-    gain, bias = in_gain.reshape(1, 128), in_bias.reshape(1, 128)
-    flat = pair_rep.reshape(SIDE, 128)
     half = SIDE // 2
     cube = (ROWS, 128, 128)
     side, piece = ((SIDE, 128), BF16), ((PIECE, 128), BF16)
-    both, halves = ((SIDE + PIECE, 128), BF16), ((half, 128), BF16)
+    halves, core = ((half, 128), BF16), ((2 * (SIDE + PIECE), 128), BF16)
     sig = ((PIECE, 128), F32)
     rows_scratch = pltpu.VMEM((2, SIDE, 128), F32)
     cube_scratch = pltpu.VMEM(cube, F32)
 
-    z_first = swap(flat[:half], Z_HIGH)
-    x_near = swap(flat, CHIP_X)
+    inputs = [pair_rep.reshape(SIDE, 128), cotangent, pair_mask]
+    loaded = call(
+        load_kernel,
+        [(a.shape, a.dtype) for a in inputs] + [halves] * 2,
+        hbm=inputs,
+        scratch=[pltpu.SemaphoreType.DMA((len(inputs) + 2,))],
+        limit=None,
+    )
+    flat, cot, mask, first, second = loaded
+    proj, gate, out_w = proj_weight, gate_weight, out_weight
+    gain, bias = in_gain.reshape(1, 128), in_bias.reshape(1, 128)
+    mid_gain, mid_bias = mid_gain.reshape(1, 128), mid_bias.reshape(1, 128)
+
+    z_first = swap(first, Z_HIGH)
     own_message, near_message, far_message = call(
         pack_kernel,
         [((HEAD, 128), BF16), ((HEAD + SIDE, 128), BF16), ((2 * HEAD + SIDE, 128), BF16)],
         smem=[me],
-        hbm=[flat, cotangent, pair_mask],
+        vmem=[flat, cot, mask],
         scratch=[cube_scratch],
     )
     far = swap(far_message, Z_LOW)
+    x_near = swap(flat, CHIP_X)
     near = swap(near_message, CORE)
-    z_second = swap(flat[half:], Z_HIGH)
+    z_second = swap(second, Z_HIGH)
     left_0, right_0, sig_0, weight_t, block_weight, mid = call(
         own_kernel,
         [side, side, sig, ((512, 128), BF16), ((512, 512), BF16), ((ROWS, 512), F32)],
         smem=[me],
-        hbm=[
-            flat,
-            pair_mask,
-            proj_weight,
-            gate_weight,
-            out_weight,
-            gain,
-            bias,
-            mid_gain.reshape(1, 128),
-            mid_bias.reshape(1, 128),
-        ],
+        vmem=[flat, mask, proj, gate, out_w, gain, bias, mid_gain, mid_bias],
         scratch=[rows_scratch, cube_scratch],
-        micros=2,
-    )
-    x_first = swap(z_first, CHIP_X)
-    both_message = swap(far[HEAD:], CORE)
-    x_second = swap(z_second, CHIP_X)
+        weight=WAIT,
+    )
 
     def peer(message, side_at, piece_at, *right_in):
         return call(
             peer_kernel(side_at, piece_at),
             [side, side, sig],
             smem=[me],
-            hbm=[],
-            vmem=[message, *right_in, weight_t, gate_weight, gain, bias],
+            vmem=[message, *right_in, weight_t, gate, gain, bias],
             scratch=[rows_scratch, cube_scratch],
-            micros=2,
+            weight=WAIT,
         )
 
     left_1, right_1, sig_1 = peer(near, HEAD, 0, x_near)
+    (passed,) = call(pass_kernel(HEAD), [((HEAD + SIDE, 128), BF16)], vmem=[far, sig_1])
+    both_message = swap(passed, CORE)
+    (passed,) = call(pass_kernel(0), [halves], vmem=[z_first, sig_1])
+    x_first = swap(passed, CHIP_X)
+    (passed,) = call(pass_kernel(0), [halves], vmem=[z_second, sig_1])
+    x_second = swap(passed, CHIP_X)
     left_2, right_2, sig_2 = peer(far, HEAD, 0, z_first, z_second)
     left_3, right_3, sig_3 = peer(both_message, 0, SIDE, x_first, x_second)
 
-    out_0, near_back, out_2, both_back, grad_left_0, grad_left_2, *grad_right = call(
+    out_0, out_2, core_back, grad_left_0, grad_left_2, *grad_right = call(
         block_kernel,
-        [piece, both, piece, both, side, side, side, side] + [halves] * 4,
+        [piece, piece, core, side, side, side, side] + [halves] * 4,
         smem=[me],
         vmem=[left_0, left_1, left_2, left_3]
         + [right_0, right_1, right_2, right_3]
@@ -472,46 +475,42 @@
         + [own_message, near, far, both_message]
         + [block_weight, mid],
         scratch=[pltpu.VMEM((SIDE, 128), F32)],
-        micros=3,
-    )
+    )
+    core_got = swap(core_back, CORE)
     x_got = [swap(grad_right[4], CHIP_X), swap(grad_right[5], CHIP_X)]
-    both_got = swap(both_back, CORE)
-    z_got = []
-    for mine, got in zip(grad_right[2:4], x_got):
-        (total,) = call(add_kernel, [halves], vmem=[mine, got], micros=0.1)
-        z_got.append(swap(total, Z_HIGH))
     left_sum, out_far = call(
         add_left_kernel,
         [side, ((2 * PIECE, 128), BF16)],
-        vmem=[grad_left_2, out_2, both_got],
-        micros=0.1,
-    )
+        vmem=[grad_left_2, out_2, core_got],
+    )
+    left_got = swap(left_sum, Z_LOW)
     out_far = swap(out_far, Z_LOW)
-    left_got = swap(left_sum, Z_LOW)
-    near_got = swap(near_back, CORE)
-    right_near = swap(grad_right[1], CHIP_X)
+    totals = []
+    for mine, got in zip(grad_right[2:4], x_got):
+        totals += call(add_kernel, [halves], vmem=[mine, got])
+    z_got = [swap(total, Z_HIGH) for total in totals]
+    (passed,) = call(pass_kernel(0), [side], vmem=[grad_right[1], *totals])
+    right_near = swap(passed, CHIP_X)
 
     factors, normed, inverse, open_part, gain_t = call(
         factor_kernel,
         [((ROWS, 512, 128), F32), (cube, F32), ((ROWS, 128), F32), (cube, F32), ((128, 128), F32)],
-        hbm=[flat, cotangent, pair_mask, gate_weight, gain, bias],
-        vmem=[weight_t],
-        micros=2,
+        vmem=[flat, cot, mask, gate, gain, bias, weight_t],
+        weight=WAIT,
     )
     output, gate_part = call(
         out_kernel,
         [(cube, BF16), (cube, F32)],
         smem=[me],
-        vmem=[out_0, near_got, out_far, open_part, gate_weight],
+        vmem=[out_0, core_got, out_far, open_part, gate],
         scratch=[cube_scratch],
     )
     (grad_pair,) = call(
         pair_kernel,
         [(cube, BF16)],
-        vmem=[grad_left_0, near_got, left_got, grad_right[0], right_near, *z_got]
-        + [factors, normed, inverse, gain_t, gate_part, proj_weight],
+        vmem=[grad_left_0, core_got, left_got, grad_right[0], right_near, *z_got]
+        + [factors, normed, inverse, gain_t, gate_part, proj],
         scratch=[rows_scratch],
-        micros=2,
     )
     return (output, grad_pair)
 

time: 75.9 us -> 65.6 us (0.86)
  waiting for transfers between devices: 31.2 us -> 19.6 us
  starting transfers between devices: 18.5 us -> 19.8 us
  Pallas kernels: 16.4 us -> 17.4 us
  local copies, waits for them, and re-layouts: 8.5 us -> 7.68 us
    ppermute x17 -> x16, waiting for transfers between devices: 31.2 us -> 19.6 us  [swap(): return lax.ppermute(values, 'row', [(s, s ^ offset) for s in range(16)])]
    ppermute x17 -> x16, starting transfers between devices: 18.5 us -> 19.8 us  [swap(): return lax.ppermute(values, 'row', [(s, s ^ offset) for s in range(16)])]
    pallas_call x12 -> x17, Pallas kernels: 16.4 us -> 17.4 us  [call(): pl.pallas_call(kernel, out_shape=[jax.ShapeDtypeStruct(s, d) for s, d in...]
    unnamed x36 -> x34, local copies, waits for them, and re-layouts: 8.45 us -> 7.68 us
  transfers between devices with their start and end apart: 17 -> 16, of which waited for: 8 -> 5; matrix products, arithmetic and copies ran while one was open for 0% -> 0% of each run, Pallas kernels for 11% -> 12%
where the time goes in v4:
time: 65.6 us; the launch traced here: 65.2 us
  starting transfers between devices  19.8 us (30%)
  waiting for transfers between devices  19.6 us (30%)
  Pallas kernels  17.4 us (27%)
  local copies, waits for them, and re-layouts  7.68 us (12%)
  between operations  0.81 us (1%)
    ppermute x16, starting transfers between devices, swap(): return lax.ppermute(values, 'row', [(s, s ^ offset) for s in range(16)])  19.8 us
    ppermute x16, waiting for transfers between devices, swap(): return lax.ppermute(values, 'row', [(s, s ^ offset) for s in range(16)])  19.6 us
    pallas_call x17, Pallas kernels, call(): pl.pallas_call(kernel, out_shape=[jax.ShapeDtypeStruct(s, d) for s, d in...  17.4 us
    unnamed x34, local copies, waits for them, and re-layouts  7.68 us
  transfers between devices with their start and end apart: 16, of which 5 were waited for; matrix products, arithmetic and copies ran while one was open for 0% of the time, Pallas kernels for 12%

profile of v4, /device:TPU:0, one launch (start us, length us, event | category | flops | bytes accessed | tf_op | source)
XLA Modules:
  0.0 65.2 jit_solution(16293602093806154602)
XLA Ops:
  0.6 2.0 %shard_map.113 = (bf16[1024,128]{1,0:T(8,128)(2,1)}, bf16[8,128,128]{2,1,0:T(8,128)(2,1)}, s32[8,128]{1,0:T(8,128)}, bf16[512,128]{1,0:T(8,128)(2,1)}, bf16[512,128]{1,0:T(8,128)(2,1)}) custom-call(bf16[1024,128]{1,0:T(8,128)(2,1)} %bitcast.18, bf16[8,128,128]{2,1,0:T(8,128)(2,1)} %refs_1_.1, s32[8,128]{1,0:T(8,128)} %refs_2_.2), custom_call_target="tpu_custom_call" | custom-call | flops 67108864 | bytes 262144 | tf_op jit(solution)/shard_map/pallas_call | solution.py:44
  2.7 4.1 %collective-permute-start.3 = (bf16[512,128]{1,0:T(8,128)(2,1)}, bf16[512,128]{1,0:T(8,128)(2,1)S(1)}, u32[]{:S(2)}, u32[]{:S(2)}) collective-permute-start(bf16[512,128]{1,0:T(8,128)(2,1)} %get-tuple-element.53), channel_id=1, source_target_pairs={{0,8},{1,9},{2,10},{3,11},{4,12},{5,13},{6,14},{7,15},{8,0},{9,1},... | collective-permute-start | bytes 393224 | tf_op jit(solution)/shard_map/ppermute | solution.py:390
  6.8 0.1 collective-permute-start.4
  6.8 1.7 %collective-permute-start.1 = (bf16[1024,128]{1,0:T(8,128)(2,1)}, bf16[1024,128]{1,0:T(8,128)(2,1)S(1)}, u32[]{:S(2)}, u32[]{:S(2)}) collective-permute-start(bf16[1024,128]{1,0:T(8,128)(2,1)} %get-tuple-element.45.x_ref), channel_id=1, source_target_pairs={{0,2},{1,3},{2,0},{3,1},{4,6},{5,7},{6,4},{7,5},{8,10},{9,11},{10,... | collective-permute-start | bytes 786440 | tf_op jit(solution)/shard_map/ppermute | solution.py:390
  8.6 0.0 copy-start
  8.6 1.0 %copy-done = bf16[1024,128]{1,0:T(8,128)(2,1)S(1)} copy-done((bf16[1024,128]{1,0:T(8,128)(2,1)S(1)}, bf16[1024,128]{1,0:T(8,128)(2,1)}, u32[]{:S(2)}) %copy-start) | copy-done | bytes 262168
  9.6 0.0 copy-start.2
  9.6 0.9 %copy-done.2 = bf16[8,128,128]{2,1,0:T(8,128)(2,1)S(1)} copy-done((bf16[8,128,128]{2,1,0:T(8,128)(2,1)S(1)}, bf16[8,128,128]{2,1,0:T(8,128)(2,1)}, u32[]{:S(2)}) %copy-start.2) | copy-done | bytes 262168
  10.5 0.7 %copy-done.8 = s32[8,128]{1,0:T(8,128)S(1)} copy-done((s32[8,128]{1,0:T(8,128)S(1)}, s32[8,128]{1,0:T(8,128)}, u32[]{:S(2)}) %copy-start.8) | copy-done | bytes 4120
  11.2 0.2 shard_map.115
  11.4 0.1 collective-permute-start
  11.5 1.6 %collective-permute-start.2 = (bf16[1568,128]{1,0:T(8,128)(2,1)S(1)}, bf16[1568,128]{1,0:T(8,128)(2,1)S(1)}, u32[]{:S(2)}, u32[]{:S(2)}) collective-permute-start(bf16[1568,128]{1,0:T(8,128)(2,1)S(1)} %get-tuple-element.52), channel_id=1, source_target_pairs={{0,4},{1,5},{2,6},{3,7},{4,0},{5,1},{6,2},{7,3},{8,12},{9,13},{10,... | collective-permute-start | bytes 1204232 | tf_op jit(solution)/shard_map/ppermute | solution.py:390
  13.1 0.9 %copy-done.4 = bf16[128,512]{1,0:T(8,128)(2,1)S(1)} copy-done((bf16[128,512]{1,0:T(8,128)(2,1)S(1)}, bf16[128,512]{1,0:T(8,128)(2,1)}, u32[]{:S(2)}) %copy-start.4) | copy-done | bytes 131096
  14.0 0.8 %copy-done.6 = bf16[128,128]{1,0:T(8,128)(2,1)S(1)} copy-done((bf16[128,128]{1,0:T(8,128)(2,1)S(1)}, bf16[128,128]{1,0:T(8,128)(2,1)}, u32[]{:S(2)}) %copy-start.6) | copy-done | bytes 32792
  14.8 0.8 %copy-done.10 = bf16[128,128]{1,0:T(8,128)(2,1)S(1)} copy-done((bf16[128,128]{1,0:T(8,128)(2,1)S(1)}, bf16[128,128]{1,0:T(8,128)(2,1)}, u32[]{:S(2)}) %copy-start.10) | copy-done | bytes 32792
  15.5 0.7 %copy-done.11 = f32[128]{0:T(128)S(1)} copy-done((f32[128]{0:T(128)S(1)}, f32[128]{0:T(128)}, u32[]{:S(2)}) %copy-start.11) | copy-done | bytes 536
  16.2 0.7 %copy-done.12 = f32[128]{0:T(128)S(1)} copy-done((f32[128]{0:T(128)S(1)}, f32[128]{0:T(128)}, u32[]{:S(2)}) %copy-start.12) | copy-done | bytes 536
  16.8 0.7 %copy-done.13 = f32[128]{0:T(128)S(1)} copy-done((f32[128]{0:T(128)S(1)}, f32[128]{0:T(128)}, u32[]{:S(2)}) %copy-start.13) | copy-done | bytes 536
  17.5 0.7 %copy-done.15 = f32[128]{0:T(128)S(1)} copy-done((f32[128]{0:T(128)S(1)}, f32[128]{0:T(128)}, u32[]{:S(2)}) %copy-start.15) | copy-done | bytes 536
  18.1 1.9 %shard_map.114 = (bf16[1024,128]{1,0:T(8,128)(2,1)S(1)}, bf16[1024,128]{1,0:T(8,128)(2,1)S(1)}, f32[256,128]{1,0:T(8,128)S(1)}, bf16[512,128]{1,0:T(8,128)(2,1)S...) custom-call(s32[1]{0:T(128)} %bitcast.me_ref.refs_0_, bf16[1024,128]{1,0:T(8,128)(2,1)S(1)} %copy-done, ...), custom_call_target="tpu_custom_call" | custom-call | flops 5000000000 | bytes 262144 | tf_op jit(solution)/shard_map/pallas_call | solution.py:44
  20.0 0.0 collective-permute-done.1.refs_0_
  20.0 0.0 collective-permute-done.message_ref.refs_14_
  20.1 0.0 copy-start.7
  20.1 0.0 copy-start.14
  20.1 1.7 %shard_map.116 = (bf16[1024,128]{1,0:T(8,128)(2,1)S(1)}, bf16[1024,128]{1,0:T(8,128)(2,1)S(1)}, f32[256,128]{1,0:T(8,128)S(1)}) custom-call(s32[1]{0:T(128)} %bitcast.me_ref.refs_0_, bf16[1296,128]{1,0:T(8,128)(2,1)S(1)} %collective-permute-done.message_ref.refs_14_, bf16[1024,128]{1,0:T(8,128)(2,1)S(1)} %collective-permute-done.1.refs_0_, ...), custom_call_target="tpu_custom_call" | custom-call | flops 5000000000 | bytes 262144 | tf_op jit(solution)/shard_map/pallas_call | solution.py:44
  21.8 0.0 collective-permute-done.3.refs_0_.message_ref
  21.8 0.6 collective-permute-start.6
  22.4 0.0 collective-permute-done.4.refs_1_.message_ref
  22.4 1.6 %collective-permute-start.7 = (bf16[512,128]{1,0:T(8,128)(2,1)S(1)}, bf16[512,128]{1,0:T(8,128)(2,1)S(1)}, u32[]{:S(2)}, u32[]{:S(2)}) collective-permute-start(bf16[512,128]{1,0:T(8,128)(2,1)S(1)} %shard_map.120), channel_id=1, source_target_pairs={{0,2},{1,3},{2,0},{3,1},{4,6},{5,7},{6,4},{7,5},{8,10},{9,11},{10,... | collective-permute-start | bytes 393224 | tf_op jit(solution)/shard_map/ppermute | solution.py:390
  24.0 3.5 %collective-permute-done.2.message_ref.refs_15_ = bf16[1568,128]{1,0:T(8,128)(2,1)S(1)} collective-permute-done((bf16[1568,128]{1,0:T(8,128)(2,1)S(1)}, bf16[1568,128]{1,0:T(8,128)(2,1)S(1)}, u32[]{:S(2)}, u32[]{:S(2)}) %collective-permute-start.2) | collective-permute-done | bytes 401440 | tf_op jit(solution)/shard_map/ppermute | solution.py:390
  27.5 0.1 collective-permute-start.5
  27.7 0.0 copy-done.7
  27.7 0.0 copy-done.14
  27.7 1.7 %shard_map.117 = (bf16[1024,128]{1,0:T(8,128)(2,1)S(1)}, bf16[1024,128]{1,0:T(8,128)(2,1)S(1)}, f32[256,128]{1,0:T(8,128)S(1)}) custom-call(s32[1]{0:T(128)} %bitcast.me_ref.refs_0_, bf16[1568,128]{1,0:T(8,128)(2,1)S(1)} %collective-permute-done.2.message_ref.refs_15_, bf16[512,128]{1,0:T(8,128)(2,1)S(1)} %collective-permute-done.3.refs_0_.message_ref, ...), custom_call_target="tpu_custom_call" | custom-call | flops 5000000000 | bytes 262144 | tf_op jit(solution)/shard_map/pallas_call | solution.py:44
  29.3 0.0 collective-permute-done.6.refs_0_
  29.4 0.9 %collective-permute-done.7.refs_1_ = bf16[512,128]{1,0:T(8,128)(2,1)S(1)} collective-permute-done((bf16[512,128]{1,0:T(8,128)(2,1)S(1)}, bf16[512,128]{1,0:T(8,128)(2,1)S(1)}, u32[]{:S(2)}, u32[]{:S(2)}) %collective-permute-start.7) | collective-permute-done | bytes 131104 | tf_op jit(solution)/shard_map/ppermute | solution.py:390
  30.2 0.0 collective-permute-done.5.message_ref.refs_16_
  30.2 1.7 %shard_map.121 = (bf16[1024,128]{1,0:T(8,128)(2,1)S(1)}, bf16[1024,128]{1,0:T(8,128)(2,1)S(1)}, f32[256,128]{1,0:T(8,128)S(1)}) custom-call(s32[1]{0:T(128)} %bitcast.me_ref.refs_0_, bf16[1296,128]{1,0:T(8,128)(2,1)S(1)} %collective-permute-done.5.message_ref.refs_16_, bf16[512,128]{1,0:T(8,128)(2,1)S(1)} %collective-permute-done.6.refs_0_, ...), custom_call_target="tpu_custom_call" | custom-call | flops 5000000000 | bytes 262144 | tf_op jit(solution)/shard_map/pallas_call | solution.py:44
  31.9 3.7 %shard_map.122 = (bf16[256,128]{1,0:T(8,128)(2,1)S(1)}, bf16[256,128]{1,0:T(8,128)(2,1)S(1)}, bf16[2560,128]{1,0:T(8,128)(2,1)}, bf16[1024,128]{1,0:T(8,128)(2,1...) custom-call(s32[1]{0:T(128)} %bitcast.me_ref.refs_0_, ...), custom_call_target="tpu_custom_call" | custom-call | flops 67108864 | bytes 262144 | tf_op jit(solution)/shard_map/pallas_call | solution.py:44
  35.6 0.1 collective-permute-start.8
  35.7 0.6 collective-permute-start.11
  36.3 1.5 %collective-permute-start.12 = (bf16[512,128]{1,0:T(8,128)(2,1)S(1)}, bf16[512,128]{1,0:T(8,128)(2,1)S(1)}, u32[]{:S(2)}, u32[]{:S(2)}) collective-permute-start(bf16[512,128]{1,0:T(8,128)(2,1)S(1)} %get-tuple-element.82), channel_id=1, source_target_pairs={{0,2},{1,3},{2,0},{3,1},{4,6},{5,7},{6,4},{7,5},{8,10},{9,11},{10,... | collective-permute-start | bytes 393224 | tf_op jit(solution)/shard_map/ppermute | solution.py:390
  37.8 4.3 %collective-permute-done.11.got_ref = bf16[512,128]{1,0:T(8,128)(2,1)S(1)} collective-permute-done((bf16[512,128]{1,0:T(8,128)(2,1)S(1)}, bf16[512,128]{1,0:T(8,128)(2,1)S(1)}, u32[]{:S(2)}, u32[]{:S(2)}) %collective-permute-start.11) | collective-permute-done | bytes 131104 | tf_op jit(solution)/shard_map/ppermute | solution.py:390
  42.1 2.7 %collective-permute-start.14 = (bf16[512,128]{1,0:T(8,128)(2,1)S(1)}, bf16[512,128]{1,0:T(8,128)(2,1)S(1)}, u32[]{:S(2)}, u32[]{:S(2)}) collective-permute-start(bf16[512,128]{1,0:T(8,128)(2,1)S(1)} %shard_map.126.refs_0_), channel_id=1, source_target_pairs={{0,8},{1,9},{2,10},{3,11},{4,12},{5,13},{6,14},{7,15},{8,0},{9,1},... | collective-permute-start | bytes 393224 | tf_op jit(solution)/shard_map/ppermute | solution.py:390
  44.7 0.0 collective-permute-done.12.got_ref
  44.8 2.3 %collective-permute-start.15 = (bf16[512,128]{1,0:T(8,128)(2,1)S(1)}, bf16[512,128]{1,0:T(8,128)(2,1)S(1)}, u32[]{:S(2)}, u32[]{:S(2)}) collective-permute-start(bf16[512,128]{1,0:T(8,128)(2,1)S(1)} %shard_map.127.refs_1_), channel_id=1, source_target_pairs={{0,8},{1,9},{2,10},{3,11},{4,12},{5,13},{6,14},{7,15},{8,0},{9,1},... | collective-permute-start | bytes 393224 | tf_op jit(solution)/shard_map/ppermute | solution.py:390
  47.1 0.6 collective-permute-start.13
  47.7 0.0 collective-permute-done.8.got_ref.near_ref.refs_1_
  47.7 0.1 shard_map.123
  47.8 1.7 %collective-permute-start.9 = (bf16[512,128]{1,0:T(8,128)(2,1)S(1)}, bf16[512,128]{1,0:T(8,128)(2,1)S(1)}, u32[]{:S(2)}, u32[]{:S(2)}) collective-permute-start(bf16[512,128]{1,0:T(8,128)(2,1)S(1)} %get-tuple-element.72), channel_id=1, source_target_pairs={{0,4},{1,5},{2,6},{3,7},{4,0},{5,1},{6,2},{7,3},{8,12},{9,13},{10,... | collective-permute-start | bytes 393224 | tf_op jit(solution)/shard_map/ppermute | solution.py:390
  49.4 0.4 collective-permute-start.10
  49.9 0.0 copy-done.1
  49.9 0.0 copy-done.3
  49.9 0.0 copy-done.9
  49.9 0.0 copy-done.16
  49.9 1.2 %shard_map.124 = (f32[8,512,128]{2,1,0:T(8,128)S(1)}, f32[8,128,128]{2,1,0:T(8,128)S(1)}, f32[8,128]{1,0:T(8,128)S(1)}, f32[8,128,128]{2,1,0:T(8,128)S(1)}, f32[128,128]{1,0:T(8,128)S(1)}) custom-call(bf16[1024,128]{1,0:T(8,128)(2,1)S(1)} %copy-done.1, bf16[8,128,128]{2,1,0:T(8,128)(2,1)S(1)} %copy-done.3, s32[8,128]{1,0:T(8,128)S(1)} %copy-done.9, ...), custom_call_target="tpu_custom_call" | custom-call | flops 5000000000 | bytes 262144 | tf_op jit(solution)/shard_map/pallas_call | solution.py:44
  51.0 7.1 %collective-permute-done.9.far_ref = bf16[512,128]{1,0:T(8,128)(2,1)S(1)} collective-permute-done((bf16[512,128]{1,0:T(8,128)(2,1)S(1)}, bf16[512,128]{1,0:T(8,128)(2,1)S(1)}, u32[]{:S(2)}, u32[]{:S(2)}) %collective-permute-start.9) | collective-permute-done | bytes 131104 | tf_op jit(solution)/shard_map/ppermute | solution.py:390
  58.2 0.9 %shard_map.125 = (bf16[8,128,128]{2,1,0:T(8,128)(2,1)}, f32[8,128,128]{2,1,0:T(8,128)S(1)}) custom-call(s32[1]{0:T(128)} %bitcast.me_ref.refs_0_, bf16[256,128]{1,0:T(8,128)(2,1)S(1)} %get-tuple-element.68.own_ref, bf16[2560,128]{1,0:T(8,128)(2,1)S(1)} %collective-permute-done.8.got_ref.near_ref.refs_1_, ...), custom_call_target="tpu_custom_call" | custom-call | flops 67108864 | bytes 262144 | tf_op jit(solution)/shard_map/pallas_call | solution.py:44
  59.0 0.0 collective-permute-done.14.refs_5_
  59.0 0.0 collective-permute-done.15.refs_6_
  59.0 0.0 collective-permute-done.13.refs_4_
  59.1 3.8 %collective-permute-done.10.refs_2_ = bf16[1024,128]{1,0:T(8,128)(2,1)S(1)} collective-permute-done((bf16[1024,128]{1,0:T(8,128)(2,1)S(1)}, bf16[1024,128]{1,0:T(8,128)(2,1)S(1)}, u32[]{:S(2)}, u32[]{:S(2)}) %collective-permute-start.10) | collective-permute-done | bytes 262176 | tf_op jit(solution)/shard_map/ppermute | solution.py:390
  62.8 0.0 copy-done.5
  62.8 2.4 %shard_map.129 = bf16[8,128,128]{2,1,0:T(8,128)(2,1)} custom-call(bf16[1024,128]{1,0:T(8,128)(2,1)S(1)} %get-tuple-element.75.refs_0_, bf16[2560,128]{1,0:T(8,128)(2,1)S(1)} %collective-permute-done.8.got_ref.near_ref.refs_1_, bf16[1024,128]{1,0:T(8,128)(2,1)S(1)} %collective-permute-done.10.refs_2_, bf16[1024,128]{1,0:T(8,128)(2,1)S(1)} %get-tuple-element.77.refs_3_, ...), custom_call_target="tpu_custom_call" | custom-call | flops 67108864 | bytes 262144 | tf_op jit(solution)/shard_map/pallas_call | solution.py:44
  (19 shorter events, 0.1 us)
Async XLA Ops:
  2.7 19.1 %collective-permute-start.3 = (bf16[512,128]{1,0:T(8,128)(2,1)}, bf16[512,128]{1,0:T(8,128)(2,1)S(1)}, u32[]{:S(2)}, u32[]{:S(2)}) collective-permute-start(bf16[512,128]{1,0:T(8,128)(2,1)} %get-tuple-element.53), channel_id=1, source_target_pairs={{0,8},{1,9},{2,10},{3,11},{4,12},{5,13},{6,14},{7,15},{8,0},{9,1},... | collective-permute-start | bytes 393224 | tf_op jit(solution)/shard_map/ppermute | solution.py:390
  6.8 15.6 %collective-permute-start.4 = (bf16[512,128]{1,0:T(8,128)(2,1)}, bf16[512,128]{1,0:T(8,128)(2,1)S(1)}, u32[]{:S(2)}, u32[]{:S(2)}) collective-permute-start(bf16[512,128]{1,0:T(8,128)(2,1)} %get-tuple-element.54), channel_id=1, source_target_pairs={{0,8},{1,9},{2,10},{3,11},{4,12},{5,13},{6,14},{7,15},{8,0},{9,1},... | collective-permute-start | bytes 393224 | tf_op jit(solution)/shard_map/ppermute | solution.py:390
  6.8 13.2 %collective-permute-start.1 = (bf16[1024,128]{1,0:T(8,128)(2,1)}, bf16[1024,128]{1,0:T(8,128)(2,1)S(1)}, u32[]{:S(2)}, u32[]{:S(2)}) collective-permute-start(bf16[1024,128]{1,0:T(8,128)(2,1)} %get-tuple-element.45.x_ref), channel_id=1, source_target_pairs={{0,2},{1,3},{2,0},{3,1},{4,6},{5,7},{6,4},{7,5},{8,10},{9,11},{10,... | collective-permute-start | bytes 786440 | tf_op jit(solution)/shard_map/ppermute | solution.py:390
  8.6 1.0 %copy-start = (bf16[1024,128]{1,0:T(8,128)(2,1)S(1)}, bf16[1024,128]{1,0:T(8,128)(2,1)}, u32[]{:S(2)}) copy-start(bf16[1024,128]{1,0:T(8,128)(2,1)} %get-tuple-element.45.x_ref) | copy-start | bytes 786436
  9.6 0.9 %copy-start.2 = (bf16[8,128,128]{2,1,0:T(8,128)(2,1)S(1)}, bf16[8,128,128]{2,1,0:T(8,128)(2,1)}, u32[]{:S(2)}) copy-start(bf16[8,128,128]{2,1,0:T(8,128)(2,1)} %get-tuple-element.48.cot_ref) | copy-start | bytes 786436
  10.5 0.7 %copy-start.8 = (s32[8,128]{1,0:T(8,128)S(1)}, s32[8,128]{1,0:T(8,128)}, u32[]{:S(2)}) copy-start(s32[8,128]{1,0:T(8,128)} %get-tuple-element.46.mask_ref) | copy-start | bytes 12292
  11.4 8.7 %collective-permute-start = (bf16[1296,128]{1,0:T(8,128)(2,1)S(1)}, bf16[1296,128]{1,0:T(8,128)(2,1)S(1)}, u32[]{:S(2)}, u32[]{:S(2)}) collective-permute-start(bf16[1296,128]{1,0:T(8,128)(2,1)S(1)} %get-tuple-element.49), channel_id=1, source_target_pairs={{0,1},{1,0},{2,3},{3,2},{4,5},{5,4},{6,7},{7,6},{8,9},{9,8},{10,11... | collective-permute-start | bytes 995336 | tf_op jit(solution)/shard_map/ppermute | solution.py:390
  11.5 16.1 %collective-permute-start.2 = (bf16[1568,128]{1,0:T(8,128)(2,1)S(1)}, bf16[1568,128]{1,0:T(8,128)(2,1)S(1)}, u32[]{:S(2)}, u32[]{:S(2)}) collective-permute-start(bf16[1568,128]{1,0:T(8,128)(2,1)S(1)} %get-tuple-element.52), channel_id=1, source_target_pairs={{0,4},{1,5},{2,6},{3,7},{4,0},{5,1},{6,2},{7,3},{8,12},{9,13},{10,... | collective-permute-start | bytes 1204232 | tf_op jit(solution)/shard_map/ppermute | solution.py:390
  13.1 0.9 %copy-start.4 = (bf16[128,512]{1,0:T(8,128)(2,1)S(1)}, bf16[128,512]{1,0:T(8,128)(2,1)}, u32[]{:S(2)}) copy-start(bf16[128,512]{1,0:T(8,128)(2,1)} %refs_12_.1) | copy-start | bytes 393220
  14.0 0.8 %copy-start.6 = (bf16[128,128]{1,0:T(8,128)(2,1)S(1)}, bf16[128,128]{1,0:T(8,128)(2,1)}, u32[]{:S(2)}) copy-start(bf16[128,128]{1,0:T(8,128)(2,1)} %weight_ref.3) | copy-start | bytes 98308
  14.8 0.8 %copy-start.10 = (bf16[128,128]{1,0:T(8,128)(2,1)S(1)}, bf16[128,128]{1,0:T(8,128)(2,1)}, u32[]{:S(2)}) copy-start(bf16[128,128]{1,0:T(8,128)(2,1)} %out_weight_ref.1) | copy-start | bytes 98308
  15.5 0.7 %copy-start.11 = (f32[128]{0:T(128)S(1)}, f32[128]{0:T(128)}, u32[]{:S(2)}) copy-start(f32[128]{0:T(128)} %param.17) | copy-start | bytes 1540
  16.2 0.7 %copy-start.12 = (f32[128]{0:T(128)S(1)}, f32[128]{0:T(128)}, u32[]{:S(2)}) copy-start(f32[128]{0:T(128)} %param.18) | copy-start | bytes 1540
  16.8 0.7 %copy-start.13 = (f32[128]{0:T(128)S(1)}, f32[128]{0:T(128)}, u32[]{:S(2)}) copy-start(f32[128]{0:T(128)} %param.13) | copy-start | bytes 1540
  17.5 0.7 %copy-start.15 = (f32[128]{0:T(128)S(1)}, f32[128]{0:T(128)}, u32[]{:S(2)}) copy-start(f32[128]{0:T(128)} %param.14) | copy-start | bytes 1540
  20.1 7.6 %copy-start.7 = (bf16[128,128]{1,0:T(8,128)(2,1)S(1)}, bf16[128,128]{1,0:T(8,128)(2,1)}, u32[]{:S(2)}) copy-start(bf16[128,128]{1,0:T(8,128)(2,1)} %weight_ref.3) | copy-start | bytes 98308
  20.1 7.6 %copy-start.14 = (f32[128]{0:T(128)S(1)}, f32[128]{0:T(128)}, u32[]{:S(2)}) copy-start(f32[128]{0:T(128)} %param.13) | copy-start | bytes 1540
  21.8 7.6 %collective-permute-start.6 = (bf16[512,128]{1,0:T(8,128)(2,1)S(1)}, bf16[512,128]{1,0:T(8,128)(2,1)S(1)}, u32[]{:S(2)}, u32[]{:S(2)}) collective-permute-start(bf16[512,128]{1,0:T(8,128)(2,1)S(1)} %shard_map.119), channel_id=1, source_target_pairs={{0,2},{1,3},{2,0},{3,1},{4,6},{5,7},{6,4},{7,5},{8,10},{9,11},{10,... | collective-permute-start | bytes 393224 | tf_op jit(solution)/shard_map/ppermute | solution.py:390
  22.4 7.8 %collective-permute-start.7 = (bf16[512,128]{1,0:T(8,128)(2,1)S(1)}, bf16[512,128]{1,0:T(8,128)(2,1)S(1)}, u32[]{:S(2)}, u32[]{:S(2)}) collective-permute-start(bf16[512,128]{1,0:T(8,128)(2,1)S(1)} %shard_map.120), channel_id=1, source_target_pairs={{0,2},{1,3},{2,0},{3,1},{4,6},{5,7},{6,4},{7,5},{8,10},{9,11},{10,... | collective-permute-start | bytes 393224 | tf_op jit(solution)/shard_map/ppermute | solution.py:390
  27.5 2.7 %collective-permute-start.5 = (bf16[1296,128]{1,0:T(8,128)(2,1)S(1)}, bf16[1296,128]{1,0:T(8,128)(2,1)S(1)}, u32[]{:S(2)}, u32[]{:S(2)}) collective-permute-start(bf16[1296,128]{1,0:T(8,128)(2,1)S(1)} %shard_map.118), channel_id=1, source_target_pairs={{0,1},{1,0},{2,3},{3,2},{4,5},{5,4},{6,7},{7,6},{8,9},{9,8},{10,11... | collective-permute-start | bytes 995336 | tf_op jit(solution)/shard_map/ppermute | solution.py:390
  35.6 14.3 %copy-start.1 = (bf16[1024,128]{1,0:T(8,128)(2,1)S(1)}, bf16[1024,128]{1,0:T(8,128)(2,1)}, u32[]{:S(2)}) copy-start(bf16[1024,128]{1,0:T(8,128)(2,1)} %get-tuple-element.45.x_ref) | copy-start | bytes 786436
  35.6 14.3 %copy-start.3 = (bf16[8,128,128]{2,1,0:T(8,128)(2,1)S(1)}, bf16[8,128,128]{2,1,0:T(8,128)(2,1)}, u32[]{:S(2)}) copy-start(bf16[8,128,128]{2,1,0:T(8,128)(2,1)} %get-tuple-element.48.cot_ref) | copy-start | bytes 786436
  35.6 14.3 %copy-start.9 = (s32[8,128]{1,0:T(8,128)S(1)}, s32[8,128]{1,0:T(8,128)}, u32[]{:S(2)}) copy-start(s32[8,128]{1,0:T(8,128)} %get-tuple-element.46.mask_ref) | copy-start | bytes 12292
  35.6 14.3 %copy-start.16 = (f32[128]{0:T(128)S(1)}, f32[128]{0:T(128)}, u32[]{:S(2)}) copy-start(f32[128]{0:T(128)} %param.14) | copy-start | bytes 1540
  35.6 12.1 %collective-permute-start.8 = (bf16[2560,128]{1,0:T(8,128)(2,1)}, bf16[2560,128]{1,0:T(8,128)(2,1)S(1)}, u32[]{:S(2)}, u32[]{:S(2)}) collective-permute-start(bf16[2560,128]{1,0:T(8,128)(2,1)} %get-tuple-element.69), channel_id=1, source_target_pairs={{0,1},{1,0},{2,3},{3,2},{4,5},{5,4},{6,7},{7,6},{8,9},{9,8},{10,11... | collective-permute-start | bytes 1966088 | tf_op jit(solution)/shard_map/ppermute | solution.py:390
  35.7 6.4 %collective-permute-start.11 = (bf16[512,128]{1,0:T(8,128)(2,1)S(1)}, bf16[512,128]{1,0:T(8,128)(2,1)S(1)}, u32[]{:S(2)}, u32[]{:S(2)}) collective-permute-start(bf16[512,128]{1,0:T(8,128)(2,1)S(1)} %get-tuple-element.80), channel_id=1, source_target_pairs={{0,2},{1,3},{2,0},{3,1},{4,6},{5,7},{6,4},{7,5},{8,10},{9,11},{10,... | collective-permute-start | bytes 393224 | tf_op jit(solution)/shard_map/ppermute | solution.py:390
  36.3 8.5 %collective-permute-start.12 = (bf16[512,128]{1,0:T(8,128)(2,1)S(1)}, bf16[512,128]{1,0:T(8,128)(2,1)S(1)}, u32[]{:S(2)}, u32[]{:S(2)}) collective-permute-start(bf16[512,128]{1,0:T(8,128)(2,1)S(1)} %get-tuple-element.82), channel_id=1, source_target_pairs={{0,2},{1,3},{2,0},{3,1},{4,6},{5,7},{6,4},{7,5},{8,10},{9,11},{10,... | collective-permute-start | bytes 393224 | tf_op jit(solution)/shard_map/ppermute | solution.py:390
  42.1 17.0 %collective-permute-start.14 = (bf16[512,128]{1,0:T(8,128)(2,1)S(1)}, bf16[512,128]{1,0:T(8,128)(2,1)S(1)}, u32[]{:S(2)}, u32[]{:S(2)}) collective-permute-start(bf16[512,128]{1,0:T(8,128)(2,1)S(1)} %shard_map.126.refs_0_), channel_id=1, source_target_pairs={{0,8},{1,9},{2,10},{3,11},{4,12},{5,13},{6,14},{7,15},{8,0},{9,1},... | collective-permute-start | bytes 393224 | tf_op jit(solution)/shard_map/ppermute | solution.py:390
  44.8 14.3 %collective-permute-start.15 = (bf16[512,128]{1,0:T(8,128)(2,1)S(1)}, bf16[512,128]{1,0:T(8,128)(2,1)S(1)}, u32[]{:S(2)}, u32[]{:S(2)}) collective-permute-start(bf16[512,128]{1,0:T(8,128)(2,1)S(1)} %shard_map.127.refs_1_), channel_id=1, source_target_pairs={{0,8},{1,9},{2,10},{3,11},{4,12},{5,13},{6,14},{7,15},{8,0},{9,1},... | collective-permute-start | bytes 393224 | tf_op jit(solution)/shard_map/ppermute | solution.py:390
  47.1 11.9 %collective-permute-start.13 = (bf16[1024,128]{1,0:T(8,128)(2,1)S(1)}, bf16[1024,128]{1,0:T(8,128)(2,1)S(1)}, u32[]{:S(2)}, u32[]{:S(2)}) collective-permute-start(bf16[1024,128]{1,0:T(8,128)(2,1)S(1)} %shard_map.128), channel_id=1, source_target_pairs={{0,2},{1,3},{2,0},{3,1},{4,6},{5,7},{6,4},{7,5},{8,10},{9,11},{10,... | collective-permute-start | bytes 786440 | tf_op jit(solution)/shard_map/ppermute | solution.py:390
  47.8 10.4 %collective-permute-start.9 = (bf16[512,128]{1,0:T(8,128)(2,1)S(1)}, bf16[512,128]{1,0:T(8,128)(2,1)S(1)}, u32[]{:S(2)}, u32[]{:S(2)}) collective-permute-start(bf16[512,128]{1,0:T(8,128)(2,1)S(1)} %get-tuple-element.72), channel_id=1, source_target_pairs={{0,4},{1,5},{2,6},{3,7},{4,0},{5,1},{6,2},{7,3},{8,12},{9,13},{10,... | collective-permute-start | bytes 393224 | tf_op jit(solution)/shard_map/ppermute | solution.py:390
  49.4 13.4 %copy-start.5 = (bf16[128,512]{1,0:T(8,128)(2,1)S(1)}, bf16[128,512]{1,0:T(8,128)(2,1)}, u32[]{:S(2)}) copy-start(bf16[128,512]{1,0:T(8,128)(2,1)} %refs_12_.1) | copy-start | bytes 393220
  49.4 13.4 %collective-permute-start.10 = (bf16[1024,128]{1,0:T(8,128)(2,1)S(1)}, bf16[1024,128]{1,0:T(8,128)(2,1)S(1)}, u32[]{:S(2)}, u32[]{:S(2)}) collective-permute-start(bf16[1024,128]{1,0:T(8,128)(2,1)S(1)} %get-tuple-element.76), channel_id=1, source_target_pairs={{0,4},{1,5},{2,6},{3,7},{4,0},{5,1},{6,2},{7,3},{8,12},{9,13},{10,... | collective-permute-start | bytes 786440 | tf_op jit(solution)/shard_map/ppermute | solution.py:390

commit v5 on v4

--- a/solution.py
+++ b/solution.py
@@ -36,10 +36,9 @@
     return 0.5 * jnp.tanh(0.5 * x) + 0.5
 
 
-def call(kernel, outs, smem=(), hbm=(), vmem=(), scratch=(), weight=2**26, limit=VMEM_BYTES):
+def call(kernel, outs, smem=(), vmem=(), scratch=(), weight=2**26):
     vmem_spec = pl.BlockSpec(memory_space=pltpu.VMEM)
     specs = [pl.BlockSpec(memory_space=pltpu.SMEM)] * len(smem)
-    specs += [pl.BlockSpec(memory_space=pltpu.HBM)] * len(hbm)
     specs += [vmem_spec] * len(vmem)
     return pl.pallas_call(
         kernel,
@@ -47,22 +46,9 @@
         in_specs=specs,
         out_specs=[vmem_spec] * len(outs),
         scratch_shapes=list(scratch),
-        compiler_params=pltpu.CompilerParams(vmem_limit_bytes=limit),
+        compiler_params=pltpu.CompilerParams(vmem_limit_bytes=VMEM_BYTES),
         cost_estimate=pl.CostEstimate(flops=weight, bytes_accessed=2**18, transcendentals=0),
-    )(*smem, *hbm, *vmem)
-
-
-def load_kernel(*refs):
-    count = (len(refs) - 3) // 2
-    ins, outs = refs[:count], refs[count:-1]
-    half = SIDE // 2
-    pairs = list(zip(ins, outs[:count]))
-    pairs += [(ins[0].at[pl.ds(n * half, half)], outs[count + n]) for n in range(2)]
-    copies = [pltpu.make_async_copy(a, b, refs[-1].at[n]) for n, (a, b) in enumerate(pairs)]
-    for c in copies:
-        c.start()
-    for c in copies:
-        c.wait()
+    )(*smem, *vmem)
 
 
 def side_rows(quarter, row):
@@ -87,30 +73,40 @@
     return jnp.concatenate(columns, axis=1).reshape(PIECE, 128)
 
 
-def pack_kernel(me_ref, x_ref, cot_ref, mask_ref, own_ref, near_ref, far_ref, full_ref):
+def pack_kernel(me_ref, cot_ref, mask_ref, after_ref, own_ref, core_ref, far_ref, full_ref):
     me = me_ref[0]
     full_ref[...] = cot_ref[...].astype(F32)
     mask = jnp.concatenate([mask_ref[...].astype(F32), jnp.zeros((ROWS, 128), F32)], axis=0)
-    places = [(own_ref, 0), (near_ref, 0), (far_ref, 0), (far_ref, HEAD + SIDE)]
+    places = [(own_ref, 0), (core_ref, 0), (far_ref, 0), (far_ref, HEAD)]
     for (ref, place), offset in zip(places, LEFT_OFFSETS):
         piece = pick_columns(full_ref, columns_of(me ^ offset, RIGHT_OFFSETS))
         ref[place : place + PIECE, :] = piece.astype(BF16)
         ref[place + PIECE : place + HEAD, :] = mask.astype(BF16)
-    near_ref[HEAD:, :] = x_ref[...]
-    far_ref[HEAD : HEAD + SIDE, :] = x_ref[...]
+
+
+def rows_of(refs, row):
+    part, start = divmod(row * 128, SIDE // len(refs))
+    return refs[part][start : start + 128, :].astype(F32)
+
+
+def scale_in(values, params_ref):
+    return norm(values, 1)[0] * params_ref[0:1, :] + params_ref[1:2, :]
+
+
+def make_side(projected):
+    return sigmoid(projected[:128]) * projected[128:]
+
+
+def block_gate(me_ref, scaled_ref, weight_ref):
+    picked = pick_columns(scaled_ref, columns_of(me_ref[0], RIGHT_OFFSETS))
+    return sigmoid(dot(picked.astype(BF16), weight_ref[:, 512:640], NN))
 
 
 def own_kernel(
     me_ref,
     x_ref,
-    mask_ref,
     weight_ref,
-    gate_weight_ref,
-    out_weight_ref,
-    gain_ref,
-    bias_ref,
-    mid_gain_ref,
-    mid_bias_ref,
+    params_ref,
     left_ref,
     right_ref,
     sig_ref,
@@ -120,31 +116,25 @@
     rows_ref,
     scaled_ref,
 ):
-    weight_t_ref[...] = weight_ref[...].astype(F32).T.astype(BF16)
-    for row in range(ROWS):
-        normed, _ = norm(x_ref[row * 128 : (row + 1) * 128, :].astype(F32), 1)
-        scaled = normed * gain_ref[...] + bias_ref[...]
+    weight_t_ref[...] = weight_ref[:, :512].astype(F32).T.astype(BF16)
+    for row in range(ROWS):
+        scaled = scale_in(rows_of([x_ref], row), params_ref)
         scaled_ref[row] = scaled
         projected = dot(weight_t_ref[...], scaled.astype(BF16), NT)
-        keep = mask_ref[row : row + 1].astype(F32)
-        for side in range(2):
-            base = 256 * side
-            gate, value = projected[base : base + 128], projected[base + 128 : base + 256]
-            result = sigmoid(gate) * value
-            store_side(rows_ref.at[side], row, result if side else result * keep)
+        store_side(rows_ref.at[0], row, make_side(projected[:256]))
+        store_side(rows_ref.at[1], row, make_side(projected[256:]))
     left_ref[...] = rows_ref[0].astype(BF16)
     right_ref[...] = rows_ref[1].astype(BF16)
-    picked = pick_columns(scaled_ref, columns_of(me_ref[0], RIGHT_OFFSETS))
-    sig_ref[...] = sigmoid(dot(picked.astype(BF16), gate_weight_ref[...], NN))
+    sig_ref[...] = block_gate(me_ref, scaled_ref, weight_ref)
 
     repeat = lax.broadcasted_iota(jnp.int32, (512, 128), 0)
     lane = lax.broadcasted_iota(jnp.int32, (512, 128), 1)
     spread = jnp.where((repeat >> 2) == lane, 1.0, 0.0).astype(BF16)
-    tall = dot(spread, out_weight_ref[...], NN)
+    tall = dot(spread, weight_ref[:, 640:], NN)
     for m in range(4):
         block_ref[:, m * 128 : (m + 1) * 128] = jnp.where((repeat & 3) == m, tall, 0.0).astype(BF16)
     rows = lax.broadcasted_iota(jnp.int32, (ROWS, 128), 0)
-    both = jnp.where(rows == 0, mid_gain_ref[...], mid_bias_ref[...])
+    both = jnp.where(rows == 0, params_ref[2:3, :], params_ref[3:4, :])
     wide = jnp.zeros((ROWS, 512), F32)
     for _ in range(3):
         term = both.astype(BF16)
@@ -153,37 +143,20 @@
     mid_ref[...] = wide
 
 
-def peer_kernel(side_at, piece_at):
-    def kernel(
-        me_ref,
-        message_ref,
-        *refs,
-    ):
-        right_in, rest = refs[:-9], refs[-9:]
-        weight_t_ref, gate_weight_ref, gain_ref, bias_ref = rest[:4]
-        left_ref, right_ref, sig_ref, rows_ref, scaled_ref = rest[4:]
-        per = SIDE // len(right_in)
-        for row in range(ROWS):
-            start = side_at + row * 128
-            normed, _ = norm(message_ref[start : start + 128, :].astype(F32), 1)
-            scaled = normed * gain_ref[...] + bias_ref[...]
-            scaled_ref[row] = scaled
-            projected = dot(weight_t_ref[:256, :], scaled.astype(BF16), NT)
-            at = piece_at + PIECE
-            keep = message_ref[at : at + 16, :].astype(F32)[row : row + 1]
-            store_side(rows_ref.at[0], row, sigmoid(projected[:128]) * projected[128:] * keep)
-        for row in range(ROWS):
-            ref, start = right_in[row * 128 // per], row * 128 % per
-            normed, _ = norm(ref[start : start + 128, :].astype(F32), 1)
-            scaled = normed * gain_ref[...] + bias_ref[...]
-            projected = dot(weight_t_ref[256:, :], scaled.astype(BF16), NT)
-            store_side(rows_ref.at[1], row, sigmoid(projected[:128]) * projected[128:])
-        left_ref[...] = rows_ref[0].astype(BF16)
-        right_ref[...] = rows_ref[1].astype(BF16)
-        picked = pick_columns(scaled_ref, columns_of(me_ref[0], RIGHT_OFFSETS))
-        sig_ref[...] = sigmoid(dot(picked.astype(BF16), gate_weight_ref[...], NN))
-
-    return kernel
+def peer_kernel(me_ref, left_in, *refs):
+    right_in, rest = refs[:-8], refs[-8:]
+    weight_t_ref, weight_ref, params_ref, left_ref, right_ref, sig_ref, rows_ref, scaled_ref = rest
+    for row in range(ROWS):
+        scaled = scale_in(rows_of([left_in], row), params_ref)
+        scaled_ref[row] = scaled
+        projected = dot(weight_t_ref[:256, :], scaled.astype(BF16), NT)
+        store_side(rows_ref.at[0], row, make_side(projected))
+        scaled = scale_in(rows_of(right_in, row), params_ref)
+        projected = dot(weight_t_ref[256:, :], scaled.astype(BF16), NT)
+        store_side(rows_ref.at[1], row, make_side(projected))
+    left_ref[...] = rows_ref[0].astype(BF16)
+    right_ref[...] = rows_ref[1].astype(BF16)
+    sig_ref[...] = block_gate(me_ref, scaled_ref, weight_ref)
 
 
 def split_sum(values, ones):
@@ -193,27 +166,20 @@
 
 
 def block_kernel(*refs):
-    me_ref, left_refs, right_refs, sig_refs, message_refs = (
-        refs[0],
-        refs[1:5],
-        refs[5:9],
-        refs[9:13],
-        refs[13:17],
-    )
-    block_ref, mid_ref = refs[17:19]
-    core_ref = refs[21]
-    out_refs, out_at = (refs[19], core_ref, refs[20], core_ref), (0, SIDE, 0, 2 * SIDE + PIECE)
-    left_outs, left_at = (refs[22], core_ref, refs[23], core_ref), (0, 0, 0, SIDE + PIECE)
-    right_outs = refs[24:30]
-    (pairs_ref,) = refs[30:]
-    piece_at = (0, 0, 0, SIDE)
+    me_ref, left_refs, right_refs, sig_refs = refs[0], refs[1:5], refs[5:9], refs[9:13]
+    own_ref, core_in, far_in, block_ref, mid_ref = refs[13:18]
+    pieces = [(own_ref, 0), (core_in, 0), (far_in, 0), (core_in, HEAD)]
+    out_0, out_2, core_ref, left_0, left_2 = refs[18:23]
+    outs = [(out_0, 0), (core_ref, SIDE), (out_2, 0), (core_ref, 2 * SIDE + PIECE)]
+    lefts = [(left_0, 0), (core_ref, 0), (left_2, 0), (core_ref, SIDE + PIECE)]
+    right_outs, pairs_ref = refs[23:29], refs[29]
     me = me_ref[0]
     groups = SIDE // 32
     lane = lax.broadcasted_iota(jnp.int32, (ROWS, 128), 1)
     of_quarter = [((lane >> 3) & 3) == q for q in range(4)]
 
-    seen = [r[a + PIECE : a + HEAD, :].astype(F32) for r, a in zip(message_refs, piece_at)]
-    valid = jnp.max(jnp.concatenate(seen, axis=0), axis=0, keepdims=True)
+    masks = [ref[at + PIECE : at + HEAD, :].astype(F32) for ref, at in pieces]
+    valid = jnp.max(jnp.concatenate(masks, axis=0), axis=0, keepdims=True)
     src = lax.broadcasted_iota(jnp.int32, (128, 128), 0)
     dst = lax.broadcasted_iota(jnp.int32, (128, 128), 1)
     pick = jnp.zeros((128, 128), F32)
@@ -222,17 +188,19 @@
         pick = jnp.where((src == wanted) & ((dst >> 5) == n), 1.0, pick)
     spread = jnp.broadcast_to(valid, (ROWS, 128)).astype(BF16)
     column_valid = dot(spread, pick.astype(BF16), NN)
+    pair_valid = [jnp.max(k[:ROWS], axis=1, keepdims=True) * column_valid for k in masks]
+    valid = jnp.broadcast_to(valid, (128, 128)).astype(BF16)
 
     def slab(side_refs, g):
         return jnp.concatenate([r[g * 32 : (g + 1) * 32, :] for r in side_refs], axis=0)
 
     for g in range(groups):
-        full = dot(slab(left_refs, g), slab(right_refs, g), NT).reshape(4, 4, ROWS, 128)
+        full = dot(slab(left_refs, g) * valid, slab(right_refs, g), NT).reshape(4, 4, ROWS, 128)
         for m in range(4):
             kept = full[m, 3]
             for q in range(3):
                 kept = jnp.where(of_quarter[q], full[m, q], kept)
-            pairs_ref[g * 32 + m * ROWS : g * 32 + (m + 1) * ROWS, :] = kept * column_valid
+            pairs_ref[g * 32 + m * ROWS : g * 32 + (m + 1) * ROWS, :] = kept * pair_valid[m]
 
     turned = []
     for row in range(ROWS):
@@ -257,8 +225,10 @@
     for m in range(4):
         sig = sig_refs[m][...]
         out = sig * update[:, m * 128 : (m + 1) * 128]
-        out_refs[m][out_at[m] : out_at[m] + PIECE, :] = out.astype(BF16)
-        cot = message_refs[m][piece_at[m] : piece_at[m] + PIECE, :].astype(F32)
+        ref, at = outs[m]
+        ref[at : at + PIECE, :] = out.astype(BF16)
+        ref, at = pieces[m]
+        cot = ref[at : at + PIECE, :].astype(F32)
         grad_update.append((cot * sig).astype(BF16))
     grad_hat = dot(jnp.concatenate(grad_update, axis=1), block_ref[...], NT) * mid_gain
     first = channel_mean(grad_hat)
@@ -280,26 +250,30 @@
     for g in range(groups):
         rows = []
         for m in range(4):
-            part = pairs_ref[g * 32 + m * ROWS : g * 32 + (m + 1) * ROWS, :] * column_valid
+            part = pairs_ref[g * 32 + m * ROWS : g * 32 + (m + 1) * ROWS, :] * pair_valid[m]
             rows += [jnp.where(of_quarter[q], part, 0.0) for q in range(4)]
         spread = jnp.concatenate(rows, axis=0).astype(BF16)
         grad_right = dot(spread, slab(left_refs, g), TN).astype(BF16)
         grad_left = dot(spread, slab(right_refs, g), NN).astype(BF16)
         for m in range(4):
-            at = left_at[m] + g * 32
-            left_outs[m][at : at + 32, :] = grad_left[m * 32 : (m + 1) * 32]
+            ref, at = lefts[m]
+            at += g * 32
+            ref[at : at + 32, :] = grad_left[m * 32 : (m + 1) * 32]
             ref, at = right_out(m, g)
             ref[at : at + 32, :] = grad_right[m * 32 : (m + 1) * 32]
 
 
-def pass_kernel(start):
-    def kernel(message_ref, *refs):
-        refs[-1][...] = message_ref[start:, :]
-
-    return kernel
-
-
-def add_kernel(mine_ref, got_ref, sum_ref):
+def pass_kernel(message_ref, *refs):
+    refs[-1][...] = message_ref[...]
+
+
+def join_kernel(mine_ref, got_ref, both_ref):
+    both_ref[:HEAD, :] = mine_ref[...]
+    both_ref[HEAD:, :] = got_ref[HEAD:, :]
+
+
+def add_kernel(mine_ref, got_ref, *refs):
+    sum_ref = refs[-1]
     sum_ref[...] = (mine_ref[...].astype(F32) + got_ref[...].astype(F32)).astype(BF16)
 
 
@@ -314,9 +288,8 @@
     x_ref,
     cot_ref,
     mask_ref,
-    gate_weight_ref,
-    gain_ref,
-    bias_ref,
+    weight_ref,
+    params_ref,
     weight_t_ref,
     factor_ref,
     normed_ref,
@@ -324,11 +297,11 @@
     open_ref,
     gain_t_ref,
 ):
-    gain_t = jnp.broadcast_to(gain_ref[...], (128, 128)).T
-    bias_t = jnp.broadcast_to(bias_ref[...], (128, 128)).T
+    gain_t = jnp.broadcast_to(params_ref[0:1, :], (128, 128)).T
+    bias_t = jnp.broadcast_to(params_ref[1:2, :], (128, 128)).T
     gain_t_ref[...] = gain_t
     for row in range(ROWS):
-        x = x_ref[row * 128 : (row + 1) * 128, :].astype(F32)
+        x = rows_of([x_ref], row)
         normed, inverse = norm(x.T, 0)
         normed_ref[row] = normed
         inverse_ref[row : row + 1, :] = inverse
@@ -341,9 +314,8 @@
             value = projected[base + 128 : base + 256]
             factor_ref[row, base : base + 128, :] = keep * value * gate * (1.0 - gate)
             factor_ref[row, base + 128 : base + 256, :] = keep * gate
-        normed, _ = norm(x, 1)
-        scaled = (normed * gain_ref[...] + bias_ref[...]).astype(BF16)
-        gate_sig = sigmoid(dot(scaled, gate_weight_ref[...], NN))
+        scaled = scale_in(x, params_ref).astype(BF16)
+        gate_sig = sigmoid(dot(scaled, weight_ref[:, 512:640], NN))
         open_ref[row] = cot_ref[row].astype(F32) * (1.0 - gate_sig)
 
 
@@ -357,7 +329,7 @@
         out = full_ref[row]
         out_ref[row] = out.astype(BF16)
         grad_gate = (open_ref[row] * out).astype(BF16)
-        grad_ref[row] = dot(weight_ref[...], grad_gate, NT)
+        grad_ref[row] = dot(weight_ref[:, 512:640], grad_gate, NT)
 
 
 def pair_kernel(*refs):
@@ -377,7 +349,7 @@
             grad = load_side(rows_ref.at[side], row)
             for place in (256 * side, 256 * side + 128):
                 parts.append((grad * factor_ref[row, place : place + 128, :]).astype(BF16))
-        grad_scaled = dot(weight_ref[...], jnp.concatenate(parts, axis=0), NN) + gate_ref[row]
+        grad_scaled = dot(weight_ref[:, :512], jnp.concatenate(parts, axis=0), NN) + gate_ref[row]
         normed = normed_ref[row]
         grad_hat = grad_scaled * gain_t_ref[...]
         first = jnp.mean(grad_hat, axis=0, keepdims=True)
@@ -411,59 +383,52 @@
     rows_scratch = pltpu.VMEM((2, SIDE, 128), F32)
     cube_scratch = pltpu.VMEM(cube, F32)
 
-    inputs = [pair_rep.reshape(SIDE, 128), cotangent, pair_mask]
-    loaded = call(
-        load_kernel,
-        [(a.shape, a.dtype) for a in inputs] + [halves] * 2,
-        hbm=inputs,
-        scratch=[pltpu.SemaphoreType.DMA((len(inputs) + 2,))],
-        limit=None,
-    )
-    flat, cot, mask, first, second = loaded
-    proj, gate, out_w = proj_weight, gate_weight, out_weight
-    gain, bias = in_gain.reshape(1, 128), in_bias.reshape(1, 128)
-    mid_gain, mid_bias = mid_gain.reshape(1, 128), mid_bias.reshape(1, 128)
-
-    z_first = swap(first, Z_HIGH)
-    own_message, near_message, far_message = call(
-        pack_kernel,
-        [((HEAD, 128), BF16), ((HEAD + SIDE, 128), BF16), ((2 * HEAD + SIDE, 128), BF16)],
-        smem=[me],
-        vmem=[flat, cot, mask],
-        scratch=[cube_scratch],
-    )
-    far = swap(far_message, Z_LOW)
+    flat = pair_rep.reshape(SIDE, 128)
+    weights = jnp.concatenate([proj_weight, gate_weight, out_weight], axis=1)
+    params = jnp.stack([in_gain, in_bias, mid_gain, mid_bias])
+
+    far = swap(flat, Z_LOW)
     x_near = swap(flat, CHIP_X)
-    near = swap(near_message, CORE)
-    z_second = swap(second, Z_HIGH)
+    near = swap(flat, CORE)
+    z_first, z_second = swap(flat[:half], Z_HIGH), swap(flat[half:], Z_HIGH)
     left_0, right_0, sig_0, weight_t, block_weight, mid = call(
         own_kernel,
         [side, side, sig, ((512, 128), BF16), ((512, 512), BF16), ((ROWS, 512), F32)],
         smem=[me],
-        vmem=[flat, mask, proj, gate, out_w, gain, bias, mid_gain, mid_bias],
+        vmem=[flat, weights, params],
         scratch=[rows_scratch, cube_scratch],
         weight=WAIT,
     )
 
-    def peer(message, side_at, piece_at, *right_in):
+    def peer(*messages):
         return call(
-            peer_kernel(side_at, piece_at),
+            peer_kernel,
             [side, side, sig],
             smem=[me],
-            vmem=[message, *right_in, weight_t, gate, gain, bias],
+            vmem=[*messages, weight_t, weights, params],
             scratch=[rows_scratch, cube_scratch],
             weight=WAIT,
         )
 
-    left_1, right_1, sig_1 = peer(near, HEAD, 0, x_near)
-    (passed,) = call(pass_kernel(HEAD), [((HEAD + SIDE, 128), BF16)], vmem=[far, sig_1])
-    both_message = swap(passed, CORE)
-    (passed,) = call(pass_kernel(0), [halves], vmem=[z_first, sig_1])
-    x_first = swap(passed, CHIP_X)
-    (passed,) = call(pass_kernel(0), [halves], vmem=[z_second, sig_1])
-    x_second = swap(passed, CHIP_X)
-    left_2, right_2, sig_2 = peer(far, HEAD, 0, z_first, z_second)
-    left_3, right_3, sig_3 = peer(both_message, 0, SIDE, x_first, x_second)
+    def after(message, *others):
+        return call(pass_kernel, [(message.shape, BF16)], vmem=[message, *others])[0]
+
+    left_1, right_1, sig_1 = peer(near, x_near)
+    own_piece, core_piece, far_piece = call(
+        pack_kernel,
+        [((HEAD, 128), BF16), ((HEAD, 128), BF16), ((2 * HEAD, 128), BF16)],
+        smem=[me],
+        vmem=[cotangent, pair_mask, sig_1],
+        scratch=[cube_scratch],
+    )
+    far_got = swap(far_piece, Z_LOW)
+    both = swap(far, CORE)
+    x_first = swap(after(z_first, sig_1, core_piece), CHIP_X)
+    x_second = swap(after(z_second, sig_1, core_piece), CHIP_X)
+    (joined,) = call(join_kernel, [((2 * HEAD, 128), BF16)], vmem=[core_piece, far_got])
+    core_pieces = swap(joined, CORE)
+    left_2, right_2, sig_2 = peer(far, z_first, z_second)
+    left_3, right_3, sig_3 = peer(both, x_first, x_second)
 
     out_0, out_2, core_back, grad_left_0, grad_left_2, *grad_right = call(
         block_kernel,
@@ -472,8 +437,7 @@
         vmem=[left_0, left_1, left_2, left_3]
         + [right_0, right_1, right_2, right_3]
         + [sig_0, sig_1, sig_2, sig_3]
-        + [own_message, near, far, both_message]
-        + [block_weight, mid],
+        + [own_piece, core_pieces, far_got, block_weight, mid],
         scratch=[pltpu.VMEM((SIDE, 128), F32)],
     )
     core_got = swap(core_back, CORE)
@@ -487,29 +451,28 @@
     out_far = swap(out_far, Z_LOW)
     totals = []
     for mine, got in zip(grad_right[2:4], x_got):
-        totals += call(add_kernel, [halves], vmem=[mine, got])
+        totals += call(add_kernel, [halves], vmem=[mine, got, left_sum])
     z_got = [swap(total, Z_HIGH) for total in totals]
-    (passed,) = call(pass_kernel(0), [side], vmem=[grad_right[1], *totals])
-    right_near = swap(passed, CHIP_X)
+    right_near = swap(after(grad_right[1], *totals), CHIP_X)
 
     factors, normed, inverse, open_part, gain_t = call(
         factor_kernel,
         [((ROWS, 512, 128), F32), (cube, F32), ((ROWS, 128), F32), (cube, F32), ((128, 128), F32)],
-        vmem=[flat, cot, mask, gate, gain, bias, weight_t],
+        vmem=[flat, cotangent, pair_mask, weights, params, weight_t],
         weight=WAIT,
     )
     output, gate_part = call(
         out_kernel,
         [(cube, BF16), (cube, F32)],
         smem=[me],
-        vmem=[out_0, core_got, out_far, open_part, gate],
+        vmem=[out_0, core_got, out_far, open_part, weights],
         scratch=[cube_scratch],
     )
     (grad_pair,) = call(
         pair_kernel,
         [(cube, BF16)],
         vmem=[grad_left_0, core_got, left_got, grad_right[0], right_near, *z_got]
-        + [factors, normed, inverse, gain_t, gate_part, proj],
+        + [factors, normed, inverse, gain_t, gate_part, weights],
         scratch=[rows_scratch],
     )
     return (output, grad_pair)

time: 65.6 us -> 56 us (0.85)
  local copies, waits for them, and re-layouts: 7.68 us -> 4.41 us
  waiting for transfers between devices: 19.6 us -> 16.5 us
  starting transfers between devices: 19.8 us -> 17.8 us
  Pallas kernels: 17.4 us -> 15.4 us
  other arithmetic: 0 us -> 0.71 us
    unnamed x34 -> x10, local copies, waits for them, and re-layouts: 7.68 us -> 2.65 us
    ppermute x16 -> x18, waiting for transfers between devices: 19.6 us -> 16.5 us  [swap(): return lax.ppermute(values, 'row', [(s, s ^ offset) for s in range(16)])]
    pallas_call x17 -> x16, Pallas kernels: 17.4 us -> 15.4 us  [call(): pl.pallas_call(kernel, out_shape=[jax.ShapeDtypeStruct(s, d) for s, d in...]
    ppermute x16 -> x18, starting transfers between devices: 19.8 us -> 17.8 us  [swap(): return lax.ppermute(values, 'row', [(s, s ^ offset) for s in range(16)])]
    slice x0 -> x1, local copies, waits for them, and re-layouts: none -> 0.99 us  [blocks_device(): z_first, z_second = (swap(flat[:half], Z_HIGH), swap(flat[half:], Z_HIGH))]
    concatenate x0 -> x1, local copies, waits for them, and re-layouts: none -> 0.77 us  [blocks_device(): weights = jnp.concatenate([proj_weight, gate_weight, out_weight], axis=1)]
    another operation x0 -> x1, other arithmetic: none -> 0.71 us  [blocks_device(): params = jnp.stack([in_gain, in_bias, mid_gain, mid_bias])]
  transfers between devices with their start and end apart: 16 -> 18, of which waited for: 5 -> 8; matrix products, arithmetic and copies ran while one was open for 0% -> 7% of each run, Pallas kernels for 12% -> 18%
where the time goes in v5:
time: 56 us; the launch traced here: 55.7 us
  starting transfers between devices  17.8 us (32%)
  waiting for transfers between devices  16.5 us (29%)
  Pallas kernels  15.4 us (28%)
  local copies, waits for them, and re-layouts  4.41 us (8%)
  between operations  0.83 us (1%)
  other arithmetic  0.71 us (1%)
    ppermute x18, starting transfers between devices, swap(): return lax.ppermute(values, 'row', [(s, s ^ offset) for s in range(16)])  17.8 us
    ppermute x18, waiting for transfers between devices, swap(): return lax.ppermute(values, 'row', [(s, s ^ offset) for s in range(16)])  16.5 us
    pallas_call x16, Pallas kernels, call(): pl.pallas_call(kernel, out_shape=[jax.ShapeDtypeStruct(s, d) for s, d in...  15.4 us
    unnamed x10, local copies, waits for them, and re-layouts  2.65 us
  transfers between devices with their start and end apart: 18, of which 8 were waited for; matrix products, arithmetic and copies ran while one was open for 7% of the time, Pallas kernels for 18%

profile of v5, /device:TPU:0, one launch (start us, length us, event | category | flops | bytes accessed | tf_op | source)
XLA Modules:
  0.0 55.7 jit_solution(7940590463569390502)
XLA Ops:
  0.6 3.1 %collective-permute-start.2 = (bf16[1024,128]{1,0:T(8,128)(2,1)}, bf16[1024,128]{1,0:T(8,128)(2,1)S(1)}, u32[]{:S(2)}, u32[]{:S(2)}) collective-permute-start(bf16[1024,128]{1,0:T(8,128)(2,1)} %bitcast.8), channel_id=1, source_target_pairs={{0,4},{1,5},{2,6},{3,7},{4,0},{5,1},{6,2},{7,3},{8,12},{9,13},{10,... | collective-permute-start | bytes 786440 | tf_op jit(solution)/shard_map/ppermute | solution.py:362
  3.7 1.5 %collective-permute-start.1 = (bf16[1024,128]{1,0:T(8,128)(2,1)}, bf16[1024,128]{1,0:T(8,128)(2,1)S(1)}, u32[]{:S(2)}, u32[]{:S(2)}) collective-permute-start(bf16[1024,128]{1,0:T(8,128)(2,1)} %bitcast.9), channel_id=1, source_target_pairs={{0,2},{1,3},{2,0},{3,1},{4,6},{5,7},{6,4},{7,5},{8,10},{9,11},{10,... | collective-permute-start | bytes 786440 | tf_op jit(solution)/shard_map/ppermute | solution.py:362
  5.2 0.0 collective-permute-start
  5.2 1.0 %fusion = (bf16[4,128,128]{2,1,0:T(8,128)(2,1)S(1)}, bf16[4,128,128]{2,1,0:T(8,128)(2,1)S(1)}) fusion(bf16[8,128,128]{2,1,0:T(8,128)(2,1)} %param.10), kind=kLoop, calls=%fused_computation.4 | loop fusion | bytes 524288 | tf_op jit(solution)/shard_map/slice | solution.py:393
  6.2 2.7 %collective-permute-start.3 = (bf16[512,128]{1,0:T(8,128)(2,1)S(1)}, bf16[512,128]{1,0:T(8,128)(2,1)S(1)}, u32[]{:S(2)}, u32[]{:S(2)}) collective-permute-start(bf16[512,128]{1,0:T(8,128)(2,1)S(1)} %bitcast.14), channel_id=1, source_target_pairs={{0,8},{1,9},{2,10},{3,11},{4,12},{5,13},{6,14},{7,15},{8,0},{9,1},... | collective-permute-start | bytes 393224 | tf_op jit(solution)/shard_map/ppermute | solution.py:362
  8.9 0.3 collective-permute-start.4
  9.2 0.9 %constant_dynamic-update-slice_fusion.2 = bf16[128,768]{1,0:T(8,128)(2,1)S(1)} fusion(bf16[128,512]{1,0:T(8,128)(2,1)} %param.15), kind=kLoop, calls=%fused_computation.2 | loop fusion | bytes 262144
  10.1 0.8 %constant_dynamic-update-slice_fusion.1 = bf16[128,768]{1,0:T(8,128)(2,1)S(1)} fusion(bf16[128,768]{1,0:T(8,128)(2,1)S(1)} %constant_dynamic-update-slice_fusion.2, bf16[128,128]{1,0:T(8,128)(2,1)} %param.16), kind=kLoop, calls=%fused_computation.1 | loop fusion | bytes 65536
  10.9 0.8 %constant_dynamic-update-slice_fusion.weight_ref.refs_2_.refs_3_.refs_12_ = bf16[128,768]{1,0:T(8,128)(2,1)S(1)} fusion(bf16[128,768]{1,0:T(8,128)(2,1)S(1)} %constant_dynamic-update-slice_fusion.1, bf16[128,128]{1,0:T(8,128)(2,1)} %param.19), kind=kLoop, calls=%fused_computation | loop fusion | bytes 65536 | tf_op jit(solution)/shard_map/concatenate | solution.py:387
  11.7 0.7 %pad_maximum_fusion.params_ref.refs_3_.refs_4_ = f32[4,128]{1,0:T(4,128)S(1)} fusion(f32[1,128]{1,0:T(1,128)} %bitcast.15, f32[1,128]{1,0:T(1,128)} %bitcast.16, f32[1,128]{1,0:T(1,128)} %bitcast.17, f32[1,128]{1,0:T(1,128)} %bitcast.18), kind=kLoop, calls=%fused_computation.3 | loop fusion | flops 1536 | bytes 4096 | tf_op jit(solution)/shard_map/stack | solution.py:388
  12.4 0.0 copy-start.1
  12.4 0.9 %copy-done.1 = bf16[8,128,128]{2,1,0:T(8,128)(2,1)S(1)} copy-done((bf16[8,128,128]{2,1,0:T(8,128)(2,1)S(1)}, bf16[8,128,128]{2,1,0:T(8,128)(2,1)}, u32[]{:S(2)}) %copy-start.1) | copy-done | bytes 262168
  13.3 1.9 %shard_map.113 = (bf16[1024,128]{1,0:T(8,128)(2,1)S(1)}, bf16[1024,128]{1,0:T(8,128)(2,1)S(1)}, f32[256,128]{1,0:T(8,128)S(1)}, bf16[512,128]{1,0:T(8,128)(2,1)S...) custom-call(s32[1]{0:T(128)} %bitcast.me_ref.refs_0_, bf16[1024,128]{1,0:T(8,128)(2,1)S(1)} %bitcast.11, ...), custom_call_target="tpu_custom_call" | custom-call | flops 5000000000 | bytes 262144 | tf_op jit(solution)/shard_map/pallas_call | solution.py:43
  15.2 0.0 collective-permute-done.1.refs_0_
  15.2 0.0 collective-permute-done.left_in
  15.3 0.0 copy-start
  15.3 0.0 copy-start.3
  15.3 1.9 %shard_map.114 = (bf16[1024,128]{1,0:T(8,128)(2,1)S(1)}, bf16[1024,128]{1,0:T(8,128)(2,1)S(1)}, f32[256,128]{1,0:T(8,128)S(1)}) custom-call(s32[1]{0:T(128)} %bitcast.me_ref.refs_0_, bf16[1024,128]{1,0:T(8,128)(2,1)S(1)} %collective-permute-done.left_in, bf16[1024,128]{1,0:T(8,128)(2,1)S(1)} %collective-permute-done.1.refs_0_, ...), custom_call_target="tpu_custom_call" | custom-call | flops 5000000000 | bytes 262144 | tf_op jit(solution)/shard_map/pallas_call | solution.py:43
  17.2 0.0 copy-done
  17.2 0.0 copy-done.3
  17.2 0.1 shard_map.116
  17.4 1.7 %collective-permute-done.3.refs_0_.message_ref = bf16[512,128]{1,0:T(8,128)(2,1)S(1)} collective-permute-done((bf16[512,128]{1,0:T(8,128)(2,1)S(1)}, bf16[512,128]{1,0:T(8,128)(2,1)S(1)}, u32[]{:S(2)}, u32[]{:S(2)}) %collective-permute-start.3) | collective-permute-done | bytes 131104 | tf_op jit(solution)/shard_map/ppermute | solution.py:362
  19.1 0.6 %collective-permute-start.6 = (bf16[512,128]{1,0:T(8,128)(2,1)S(1)}, bf16[512,128]{1,0:T(8,128)(2,1)S(1)}, u32[]{:S(2)}, u32[]{:S(2)}) collective-permute-start(bf16[512,128]{1,0:T(8,128)(2,1)S(1)} %shard_map.117), channel_id=1, source_target_pairs={{0,2},{1,3},{2,0},{3,1},{4,6},{5,7},{6,4},{7,5},{8,10},{9,11},{10,... | collective-permute-start | bytes 393224 | tf_op jit(solution)/shard_map/ppermute | solution.py:362
  19.7 1.8 %collective-permute-done.4.refs_1_.message_ref = bf16[512,128]{1,0:T(8,128)(2,1)S(1)} collective-permute-done((bf16[512,128]{1,0:T(8,128)(2,1)S(1)}, bf16[512,128]{1,0:T(8,128)(2,1)S(1)}, u32[]{:S(2)}, u32[]{:S(2)}) %collective-permute-start.4) | collective-permute-done | bytes 131104 | tf_op jit(solution)/shard_map/ppermute | solution.py:362
  21.5 0.6 %collective-permute-start.7 = (bf16[512,128]{1,0:T(8,128)(2,1)S(1)}, bf16[512,128]{1,0:T(8,128)(2,1)S(1)}, u32[]{:S(2)}, u32[]{:S(2)}) collective-permute-start(bf16[512,128]{1,0:T(8,128)(2,1)S(1)} %shard_map.118), channel_id=1, source_target_pairs={{0,2},{1,3},{2,0},{3,1},{4,6},{5,7},{6,4},{7,5},{8,10},{9,11},{10,... | collective-permute-start | bytes 393224 | tf_op jit(solution)/shard_map/ppermute | solution.py:362
  22.2 0.0 collective-permute-start.8
  22.2 0.0 collective-permute-done.2.left_in
  22.2 0.0 collective-permute-start.5
  22.2 1.9 %shard_map.115 = (bf16[1024,128]{1,0:T(8,128)(2,1)S(1)}, bf16[1024,128]{1,0:T(8,128)(2,1)S(1)}, f32[256,128]{1,0:T(8,128)S(1)}) custom-call(s32[1]{0:T(128)} %bitcast.me_ref.refs_0_, bf16[1024,128]{1,0:T(8,128)(2,1)S(1)} %collective-permute-done.2.left_in, bf16[512,128]{1,0:T(8,128)(2,1)S(1)} %collective-permute-done.3.refs_0_.message_ref, ...), custom_call_target="tpu_custom_call" | custom-call | flops 5000000000 | bytes 262144 | tf_op jit(solution)/shard_map/pallas_call | solution.py:43
  24.1 3.1 %collective-permute-done.8.got_ref.refs_15_ = bf16[544,128]{1,0:T(8,128)(2,1)S(1)} collective-permute-done((bf16[544,128]{1,0:T(8,128)(2,1)S(1)}, bf16[544,128]{1,0:T(8,128)(2,1)S(1)}, u32[]{:S(2)}, u32[]{:S(2)}) %collective-permute-start.8) | collective-permute-done | bytes 139296 | tf_op jit(solution)/shard_map/ppermute | solution.py:362
  27.2 0.1 collective-permute-start.9
  27.3 0.0 collective-permute-done.6.refs_0_
  27.3 0.0 collective-permute-done.7.refs_1_
  27.3 0.0 collective-permute-done.5.left_in
  27.3 1.9 %shard_map.119 = (bf16[1024,128]{1,0:T(8,128)(2,1)S(1)}, bf16[1024,128]{1,0:T(8,128)(2,1)S(1)}, f32[256,128]{1,0:T(8,128)S(1)}) custom-call(s32[1]{0:T(128)} %bitcast.me_ref.refs_0_, bf16[1024,128]{1,0:T(8,128)(2,1)S(1)} %collective-permute-done.5.left_in, bf16[512,128]{1,0:T(8,128)(2,1)S(1)} %collective-permute-done.6.refs_0_, ...), custom_call_target="tpu_custom_call" | custom-call | flops 5000000000 | bytes 262144 | tf_op jit(solution)/shard_map/pallas_call | solution.py:43
  29.3 0.0 collective-permute-done.9.refs_14_
  29.3 3.0 %shard_map.121 = (bf16[256,128]{1,0:T(8,128)(2,1)S(1)}, bf16[256,128]{1,0:T(8,128)(2,1)S(1)}, bf16[2560,128]{1,0:T(8,128)(2,1)S(1)}, bf16[1024,128]{1,0:T(8,128)...) custom-call(s32[1]{0:T(128)} %bitcast.me_ref.refs_0_, ...), custom_call_target="tpu_custom_call" | custom-call | flops 67108864 | bytes 262144 | tf_op jit(solution)/shard_map/pallas_call | solution.py:43
  32.3 0.0 copy-start.2
  32.3 0.5 collective-permute-start.10
  32.8 1.5 %collective-permute-start.13 = (bf16[512,128]{1,0:T(8,128)(2,1)S(1)}, bf16[512,128]{1,0:T(8,128)(2,1)S(1)}, u32[]{:S(2)}, u32[]{:S(2)}) collective-permute-start(bf16[512,128]{1,0:T(8,128)(2,1)S(1)} %get-tuple-element.70), channel_id=1, source_target_pairs={{0,2},{1,3},{2,0},{3,1},{4,6},{5,7},{6,4},{7,5},{8,10},{9,11},{10,... | collective-permute-start | bytes 393224 | tf_op jit(solution)/shard_map/ppermute | solution.py:362
  34.3 0.6 %collective-permute-start.14 = (bf16[512,128]{1,0:T(8,128)(2,1)S(1)}, bf16[512,128]{1,0:T(8,128)(2,1)S(1)}, u32[]{:S(2)}, u32[]{:S(2)}) collective-permute-start(bf16[512,128]{1,0:T(8,128)(2,1)S(1)} %get-tuple-element.72), channel_id=1, source_target_pairs={{0,2},{1,3},{2,0},{3,1},{4,6},{5,7},{6,4},{7,5},{8,10},{9,11},{10,... | collective-permute-start | bytes 393224 | tf_op jit(solution)/shard_map/ppermute | solution.py:362
  34.8 0.0 collective-permute-done.10.got_ref.near_ref.refs_1_
  34.8 0.1 shard_map.122
  34.9 0.3 collective-permute-start.12
  35.2 3.9 %collective-permute-done.13.got_ref = bf16[512,128]{1,0:T(8,128)(2,1)S(1)} collective-permute-done((bf16[512,128]{1,0:T(8,128)(2,1)S(1)}, bf16[512,128]{1,0:T(8,128)(2,1)S(1)}, u32[]{:S(2)}, u32[]{:S(2)}) %collective-permute-start.13) | collective-permute-done | bytes 131104 | tf_op jit(solution)/shard_map/ppermute | solution.py:362
  39.2 1.4 %collective-permute-start.16 = (bf16[512,128]{1,0:T(8,128)(2,1)S(1)}, bf16[512,128]{1,0:T(8,128)(2,1)S(1)}, u32[]{:S(2)}, u32[]{:S(2)}) collective-permute-start(bf16[512,128]{1,0:T(8,128)(2,1)S(1)} %shard_map.125.refs_0_), channel_id=1, source_target_pairs={{0,8},{1,9},{2,10},{3,11},{4,12},{5,13},{6,14},{7,15},{8,0},{9,1},... | collective-permute-start | bytes 393224 | tf_op jit(solution)/shard_map/ppermute | solution.py:362
  40.6 0.5 collective-permute-done.14.got_ref
  41.1 1.4 %collective-permute-start.17 = (bf16[512,128]{1,0:T(8,128)(2,1)S(1)}, bf16[512,128]{1,0:T(8,128)(2,1)S(1)}, u32[]{:S(2)}, u32[]{:S(2)}) collective-permute-start(bf16[512,128]{1,0:T(8,128)(2,1)S(1)} %shard_map.126.refs_1_), channel_id=1, source_target_pairs={{0,8},{1,9},{2,10},{3,11},{4,12},{5,13},{6,14},{7,15},{8,0},{9,1},... | collective-permute-start | bytes 393224 | tf_op jit(solution)/shard_map/ppermute | solution.py:362
  42.5 1.8 %collective-permute-start.11 = (bf16[512,128]{1,0:T(8,128)(2,1)S(1)}, bf16[512,128]{1,0:T(8,128)(2,1)S(1)}, u32[]{:S(2)}, u32[]{:S(2)}) collective-permute-start(bf16[512,128]{1,0:T(8,128)(2,1)S(1)} %get-tuple-element.62), channel_id=1, source_target_pairs={{0,4},{1,5},{2,6},{3,7},{4,0},{5,1},{6,2},{7,3},{8,12},{9,13},{10,... | collective-permute-start | bytes 393224 | tf_op jit(solution)/shard_map/ppermute | solution.py:362
  44.3 1.5 %collective-permute-start.15 = (bf16[1024,128]{1,0:T(8,128)(2,1)S(1)}, bf16[1024,128]{1,0:T(8,128)(2,1)S(1)}, u32[]{:S(2)}, u32[]{:S(2)}) collective-permute-start(bf16[1024,128]{1,0:T(8,128)(2,1)S(1)} %shard_map.127), channel_id=1, source_target_pairs={{0,2},{1,3},{2,0},{3,1},{4,6},{5,7},{6,4},{7,5},{8,10},{9,11},{10,... | collective-permute-start | bytes 786440 | tf_op jit(solution)/shard_map/ppermute | solution.py:362
  45.8 0.0 copy-done.2
  45.8 1.1 %shard_map.123 = (f32[8,512,128]{2,1,0:T(8,128)S(1)}, f32[8,128,128]{2,1,0:T(8,128)S(1)}, f32[8,128]{1,0:T(8,128)S(1)}, f32[8,128,128]{2,1,0:T(8,128)S(1)}, f32[128,128]{1,0:T(8,128)S(1)}) custom-call(bf16[1024,128]{1,0:T(8,128)(2,1)S(1)} %bitcast.12, bf16[8,128,128]{2,1,0:T(8,128)(2,1)S(1)} %copy-done, s32[8,128]{1,0:T(8,128)S(1)} %copy-done.3, ...), custom_call_target="tpu_custom_call" | custom-call | flops 5000000000 | bytes 262144 | tf_op jit(solution)/shard_map/pallas_call | solution.py:43
  47.0 2.6 %collective-permute-done.11.far_ref = bf16[512,128]{1,0:T(8,128)(2,1)S(1)} collective-permute-done((bf16[512,128]{1,0:T(8,128)(2,1)S(1)}, bf16[512,128]{1,0:T(8,128)(2,1)S(1)}, u32[]{:S(2)}, u32[]{:S(2)}) %collective-permute-start.11) | collective-permute-done | bytes 131104 | tf_op jit(solution)/shard_map/ppermute | solution.py:362
  49.5 0.9 %shard_map.124 = (bf16[8,128,128]{2,1,0:T(8,128)(2,1)}, f32[8,128,128]{2,1,0:T(8,128)S(1)}) custom-call(s32[1]{0:T(128)} %bitcast.me_ref.refs_0_, bf16[256,128]{1,0:T(8,128)(2,1)S(1)} %get-tuple-element.58.own_ref, bf16[2560,128]{1,0:T(8,128)(2,1)S(1)} %collective-permute-done.10.got_ref.near_ref.refs_1_, ...), custom_call_target="tpu_custom_call" | custom-call | flops 67108864 | bytes 262144 | tf_op jit(solution)/shard_map/pallas_call | solution.py:43
  50.4 1.4 %collective-permute-done.16.refs_5_ = bf16[512,128]{1,0:T(8,128)(2,1)S(1)} collective-permute-done((bf16[512,128]{1,0:T(8,128)(2,1)S(1)}, bf16[512,128]{1,0:T(8,128)(2,1)S(1)}, u32[]{:S(2)}, u32[]{:S(2)}) %collective-permute-start.16) | collective-permute-done | bytes 131104 | tf_op jit(solution)/shard_map/ppermute | solution.py:362
  51.8 1.5 %collective-permute-done.17.refs_6_ = bf16[512,128]{1,0:T(8,128)(2,1)S(1)} collective-permute-done((bf16[512,128]{1,0:T(8,128)(2,1)S(1)}, bf16[512,128]{1,0:T(8,128)(2,1)S(1)}, u32[]{:S(2)}, u32[]{:S(2)}) %collective-permute-start.17) | collective-permute-done | bytes 131104 | tf_op jit(solution)/shard_map/ppermute | solution.py:362
  53.3 0.0 collective-permute-done.15.refs_4_
  53.3 0.0 collective-permute-done.12.refs_2_
  53.3 2.4 %shard_map.128 = bf16[8,128,128]{2,1,0:T(8,128)(2,1)} custom-call(bf16[1024,128]{1,0:T(8,128)(2,1)S(1)} %get-tuple-element.65.refs_0_, bf16[2560,128]{1,0:T(8,128)(2,1)S(1)} %collective-permute-done.10.got_ref.near_ref.refs_1_, bf16[1024,128]{1,0:T(8,128)(2,1)S(1)} %collective-permute-done.12.refs_2_, bf16[1024,128]{1,0:T(8,128)(2,1)S(1)} %get-tuple-element.67.refs_3_, ...), custom_call_target="tpu_custom_call" | custom-call | flops 67108864 | bytes 262144 | tf_op jit(solution)/shard_map/pallas_call | solution.py:43
  (6 shorter events, 0.1 us)
Async XLA Ops:
  0.6 21.5 %collective-permute-start.2 = (bf16[1024,128]{1,0:T(8,128)(2,1)}, bf16[1024,128]{1,0:T(8,128)(2,1)S(1)}, u32[]{:S(2)}, u32[]{:S(2)}) collective-permute-start(bf16[1024,128]{1,0:T(8,128)(2,1)} %bitcast.8), channel_id=1, source_target_pairs={{0,4},{1,5},{2,6},{3,7},{4,0},{5,1},{6,2},{7,3},{8,12},{9,13},{10,... | collective-permute-start | bytes 786440 | tf_op jit(solution)/shard_map/ppermute | solution.py:362
  3.7 11.5 %collective-permute-start.1 = (bf16[1024,128]{1,0:T(8,128)(2,1)}, bf16[1024,128]{1,0:T(8,128)(2,1)S(1)}, u32[]{:S(2)}, u32[]{:S(2)}) collective-permute-start(bf16[1024,128]{1,0:T(8,128)(2,1)} %bitcast.9), channel_id=1, source_target_pairs={{0,2},{1,3},{2,0},{3,1},{4,6},{5,7},{6,4},{7,5},{8,10},{9,11},{10,... | collective-permute-start | bytes 786440 | tf_op jit(solution)/shard_map/ppermute | solution.py:362
  5.2 10.0 %collective-permute-start = (bf16[1024,128]{1,0:T(8,128)(2,1)}, bf16[1024,128]{1,0:T(8,128)(2,1)S(1)}, u32[]{:S(2)}, u32[]{:S(2)}) collective-permute-start(bf16[1024,128]{1,0:T(8,128)(2,1)} %bitcast.10), channel_id=1, source_target_pairs={{0,1},{1,0},{2,3},{3,2},{4,5},{5,4},{6,7},{7,6},{8,9},{9,8},{10,11... | collective-permute-start | bytes 786440 | tf_op jit(solution)/shard_map/ppermute | solution.py:362
  6.2 12.9 %collective-permute-start.3 = (bf16[512,128]{1,0:T(8,128)(2,1)S(1)}, bf16[512,128]{1,0:T(8,128)(2,1)S(1)}, u32[]{:S(2)}, u32[]{:S(2)}) collective-permute-start(bf16[512,128]{1,0:T(8,128)(2,1)S(1)} %bitcast.14), channel_id=1, source_target_pairs={{0,8},{1,9},{2,10},{3,11},{4,12},{5,13},{6,14},{7,15},{8,0},{9,1},... | collective-permute-start | bytes 393224 | tf_op jit(solution)/shard_map/ppermute | solution.py:362
  8.9 12.6 %collective-permute-start.4 = (bf16[512,128]{1,0:T(8,128)(2,1)S(1)}, bf16[512,128]{1,0:T(8,128)(2,1)S(1)}, u32[]{:S(2)}, u32[]{:S(2)}) collective-permute-start(bf16[512,128]{1,0:T(8,128)(2,1)S(1)} %bitcast.13), channel_id=1, source_target_pairs={{0,8},{1,9},{2,10},{3,11},{4,12},{5,13},{6,14},{7,15},{8,0},{9,1},... | collective-permute-start | bytes 393224 | tf_op jit(solution)/shard_map/ppermute | solution.py:362
  12.4 0.9 %copy-start.1 = (bf16[8,128,128]{2,1,0:T(8,128)(2,1)S(1)}, bf16[8,128,128]{2,1,0:T(8,128)(2,1)}, u32[]{:S(2)}) copy-start(bf16[8,128,128]{2,1,0:T(8,128)(2,1)} %param.10) | copy-start | bytes 786436
  15.3 2.0 %copy-start = (bf16[8,128,128]{2,1,0:T(8,128)(2,1)S(1)}, bf16[8,128,128]{2,1,0:T(8,128)(2,1)}, u32[]{:S(2)}) copy-start(bf16[8,128,128]{2,1,0:T(8,128)(2,1)} %cot_ref.3) | copy-start | bytes 786436
  15.3 2.0 %copy-start.3 = (s32[8,128]{1,0:T(8,128)S(1)}, s32[8,128]{1,0:T(8,128)}, u32[]{:S(2)}) copy-start(s32[8,128]{1,0:T(8,128)} %mask_ref.3) | copy-start | bytes 12292
  19.1 8.2 %collective-permute-start.6 = (bf16[512,128]{1,0:T(8,128)(2,1)S(1)}, bf16[512,128]{1,0:T(8,128)(2,1)S(1)}, u32[]{:S(2)}, u32[]{:S(2)}) collective-permute-start(bf16[512,128]{1,0:T(8,128)(2,1)S(1)} %shard_map.117), channel_id=1, source_target_pairs={{0,2},{1,3},{2,0},{3,1},{4,6},{5,7},{6,4},{7,5},{8,10},{9,11},{10,... | collective-permute-start | bytes 393224 | tf_op jit(solution)/shard_map/ppermute | solution.py:362
  21.5 5.8 %collective-permute-start.7 = (bf16[512,128]{1,0:T(8,128)(2,1)S(1)}, bf16[512,128]{1,0:T(8,128)(2,1)S(1)}, u32[]{:S(2)}, u32[]{:S(2)}) collective-permute-start(bf16[512,128]{1,0:T(8,128)(2,1)S(1)} %shard_map.118), channel_id=1, source_target_pairs={{0,2},{1,3},{2,0},{3,1},{4,6},{5,7},{6,4},{7,5},{8,10},{9,11},{10,... | collective-permute-start | bytes 393224 | tf_op jit(solution)/shard_map/ppermute | solution.py:362
  22.2 5.1 %collective-permute-start.8 = (bf16[544,128]{1,0:T(8,128)(2,1)S(1)}, bf16[544,128]{1,0:T(8,128)(2,1)S(1)}, u32[]{:S(2)}, u32[]{:S(2)}) collective-permute-start(bf16[544,128]{1,0:T(8,128)(2,1)S(1)} %get-tuple-element.55), channel_id=1, source_target_pairs={{0,4},{1,5},{2,6},{3,7},{4,0},{5,1},{6,2},{7,3},{8,12},{9,13},{10,... | collective-permute-start | bytes 417800 | tf_op jit(solution)/shard_map/ppermute | solution.py:362
  22.2 5.2 %collective-permute-start.5 = (bf16[1024,128]{1,0:T(8,128)(2,1)S(1)}, bf16[1024,128]{1,0:T(8,128)(2,1)S(1)}, u32[]{:S(2)}, u32[]{:S(2)}) collective-permute-start(bf16[1024,128]{1,0:T(8,128)(2,1)S(1)} %collective-permute-done.2.left_in), channel_id=1, source_target_pairs={{0,1},{1,0},{2,3},{3,2},{4,5},{5,4},{6,7},{7,6},{8,9},{9,8},{10,11... | collective-permute-start | bytes 786440 | tf_op jit(solution)/shard_map/ppermute | solution.py:362
  27.2 2.1 %collective-permute-start.9 = (bf16[544,128]{1,0:T(8,128)(2,1)S(1)}, bf16[544,128]{1,0:T(8,128)(2,1)S(1)}, u32[]{:S(2)}, u32[]{:S(2)}) collective-permute-start(bf16[544,128]{1,0:T(8,128)(2,1)S(1)} %shard_map.120), channel_id=1, source_target_pairs={{0,1},{1,0},{2,3},{3,2},{4,5},{5,4},{6,7},{7,6},{8,9},{9,8},{10,11... | collective-permute-start | bytes 417800 | tf_op jit(solution)/shard_map/ppermute | solution.py:362
  32.3 13.6 %copy-start.2 = (bf16[8,128,128]{2,1,0:T(8,128)(2,1)S(1)}, bf16[8,128,128]{2,1,0:T(8,128)(2,1)}, u32[]{:S(2)}) copy-start(bf16[8,128,128]{2,1,0:T(8,128)(2,1)} %param.10) | copy-start | bytes 786436
  32.3 2.6 %collective-permute-start.10 = (bf16[2560,128]{1,0:T(8,128)(2,1)S(1)}, bf16[2560,128]{1,0:T(8,128)(2,1)S(1)}, u32[]{:S(2)}, u32[]{:S(2)}) collective-permute-start(bf16[2560,128]{1,0:T(8,128)(2,1)S(1)} %get-tuple-element.59), channel_id=1, source_target_pairs={{0,1},{1,0},{2,3},{3,2},{4,5},{5,4},{6,7},{7,6},{8,9},{9,8},{10,11... | collective-permute-start | bytes 1966088 | tf_op jit(solution)/shard_map/ppermute | solution.py:362
  32.8 6.4 %collective-permute-start.13 = (bf16[512,128]{1,0:T(8,128)(2,1)S(1)}, bf16[512,128]{1,0:T(8,128)(2,1)S(1)}, u32[]{:S(2)}, u32[]{:S(2)}) collective-permute-start(bf16[512,128]{1,0:T(8,128)(2,1)S(1)} %get-tuple-element.70), channel_id=1, source_target_pairs={{0,2},{1,3},{2,0},{3,1},{4,6},{5,7},{6,4},{7,5},{8,10},{9,11},{10,... | collective-permute-start | bytes 393224 | tf_op jit(solution)/shard_map/ppermute | solution.py:362
  34.3 6.8 %collective-permute-start.14 = (bf16[512,128]{1,0:T(8,128)(2,1)S(1)}, bf16[512,128]{1,0:T(8,128)(2,1)S(1)}, u32[]{:S(2)}, u32[]{:S(2)}) collective-permute-start(bf16[512,128]{1,0:T(8,128)(2,1)S(1)} %get-tuple-element.72), channel_id=1, source_target_pairs={{0,2},{1,3},{2,0},{3,1},{4,6},{5,7},{6,4},{7,5},{8,10},{9,11},{10,... | collective-permute-start | bytes 393224 | tf_op jit(solution)/shard_map/ppermute | solution.py:362
  34.9 18.4 %collective-permute-start.12 = (bf16[1024,128]{1,0:T(8,128)(2,1)S(1)}, bf16[1024,128]{1,0:T(8,128)(2,1)S(1)}, u32[]{:S(2)}, u32[]{:S(2)}) collective-permute-start(bf16[1024,128]{1,0:T(8,128)(2,1)S(1)} %get-tuple-element.66.refs_0_), channel_id=1, source_target_pairs={{0,4},{1,5},{2,6},{3,7},{4,0},{5,1},{6,2},{7,3},{8,12},{9,13},{10,... | collective-permute-start | bytes 786440 | tf_op jit(solution)/shard_map/ppermute | solution.py:362
  39.2 12.5 %collective-permute-start.16 = (bf16[512,128]{1,0:T(8,128)(2,1)S(1)}, bf16[512,128]{1,0:T(8,128)(2,1)S(1)}, u32[]{:S(2)}, u32[]{:S(2)}) collective-permute-start(bf16[512,128]{1,0:T(8,128)(2,1)S(1)} %shard_map.125.refs_0_), channel_id=1, source_target_pairs={{0,8},{1,9},{2,10},{3,11},{4,12},{5,13},{6,14},{7,15},{8,0},{9,1},... | collective-permute-start | bytes 393224 | tf_op jit(solution)/shard_map/ppermute | solution.py:362
  41.1 12.1 %collective-permute-start.17 = (bf16[512,128]{1,0:T(8,128)(2,1)S(1)}, bf16[512,128]{1,0:T(8,128)(2,1)S(1)}, u32[]{:S(2)}, u32[]{:S(2)}) collective-permute-start(bf16[512,128]{1,0:T(8,128)(2,1)S(1)} %shard_map.126.refs_1_), channel_id=1, source_target_pairs={{0,8},{1,9},{2,10},{3,11},{4,12},{5,13},{6,14},{7,15},{8,0},{9,1},... | collective-permute-start | bytes 393224 | tf_op jit(solution)/shard_map/ppermute | solution.py:362
  42.5 7.0 %collective-permute-start.11 = (bf16[512,128]{1,0:T(8,128)(2,1)S(1)}, bf16[512,128]{1,0:T(8,128)(2,1)S(1)}, u32[]{:S(2)}, u32[]{:S(2)}) collective-permute-start(bf16[512,128]{1,0:T(8,128)(2,1)S(1)} %get-tuple-element.62), channel_id=1, source_target_pairs={{0,4},{1,5},{2,6},{3,7},{4,0},{5,1},{6,2},{7,3},{8,12},{9,13},{10,... | collective-permute-start | bytes 393224 | tf_op jit(solution)/shard_map/ppermute | solution.py:362
  44.3 8.9 %collective-permute-start.15 = (bf16[1024,128]{1,0:T(8,128)(2,1)S(1)}, bf16[1024,128]{1,0:T(8,128)(2,1)S(1)}, u32[]{:S(2)}, u32[]{:S(2)}) collective-permute-start(bf16[1024,128]{1,0:T(8,128)(2,1)S(1)} %shard_map.127), channel_id=1, source_target_pairs={{0,2},{1,3},{2,0},{3,1},{4,6},{5,7},{6,4},{7,5},{8,10},{9,11},{10,... | collective-permute-start | bytes 786440 | tf_op jit(solution)/shard_map/ppermute | solution.py:362

commit v6 on v5

--- a/solution.py
+++ b/solution.py
@@ -159,24 +159,57 @@
     sig_ref[...] = block_gate(me_ref, scaled_ref, weight_ref)
 
 
+def left_kernel(
+    me_ref, x_ref, weight_t_ref, weight_ref, params_ref, left_ref, sig_ref, rows_ref, scaled_ref
+):
+    for row in range(ROWS):
+        scaled = scale_in(rows_of([x_ref], row), params_ref)
+        scaled_ref[row] = scaled
+        store_side(rows_ref, row, make_side(dot(weight_t_ref[:256, :], scaled.astype(BF16), NT)))
+    left_ref[...] = rows_ref[...].astype(BF16)
+    sig_ref[...] = block_gate(me_ref, scaled_ref, weight_ref)
+
+
+def right_kernel(first, last):
+    def kernel(x_ref, weight_t_ref, params_ref, rest_ref, right_ref, rows_ref):
+        if last:
+            rows_ref[...] = rest_ref[...]
+        else:
+            rows_ref[...] = jnp.zeros_like(rows_ref)
+        for row in range(ROWS // 2):
+            scaled = scale_in(x_ref[row * 128 : (row + 1) * 128, :].astype(F32), params_ref)
+            projected = dot(weight_t_ref[256:, :], scaled.astype(BF16), NT)
+            store_side(rows_ref, first + row, make_side(projected))
+        right_ref[...] = rows_ref[...].astype(right_ref.dtype)
+
+    return kernel
+
+
 def split_sum(values, ones):
     high = values.astype(BF16)
     low = (values - high.astype(F32)).astype(BF16)
     return dot(high, ones, NN) + dot(low, ones, NN)
 
 
+GROUPS = SIDE // 32
+
+
+def quarters():
+    lane = lax.broadcasted_iota(jnp.int32, (ROWS, 128), 1)
+    return [((lane >> 3) & 3) == q for q in range(4)]
+
+
+def slab(side_refs, g):
+    return jnp.concatenate([r[g * 32 : (g + 1) * 32, :] for r in side_refs], axis=0)
+
+
 def block_kernel(*refs):
     me_ref, left_refs, right_refs, sig_refs = refs[0], refs[1:5], refs[5:9], refs[9:13]
     own_ref, core_in, far_in, block_ref, mid_ref = refs[13:18]
     pieces = [(own_ref, 0), (core_in, 0), (far_in, 0), (core_in, HEAD)]
-    out_0, out_2, core_ref, left_0, left_2 = refs[18:23]
-    outs = [(out_0, 0), (core_ref, SIDE), (out_2, 0), (core_ref, 2 * SIDE + PIECE)]
-    lefts = [(left_0, 0), (core_ref, 0), (left_2, 0), (core_ref, SIDE + PIECE)]
-    right_outs, pairs_ref = refs[23:29], refs[29]
+    out_refs, pairs_ref = refs[18:22], refs[22]
     me = me_ref[0]
-    groups = SIDE // 32
-    lane = lax.broadcasted_iota(jnp.int32, (ROWS, 128), 1)
-    of_quarter = [((lane >> 3) & 3) == q for q in range(4)]
+    of_quarter = quarters()
 
     masks = [ref[at + PIECE : at + HEAD, :].astype(F32) for ref, at in pieces]
     valid = jnp.max(jnp.concatenate(masks, axis=0), axis=0, keepdims=True)
@@ -191,10 +224,7 @@
     pair_valid = [jnp.max(k[:ROWS], axis=1, keepdims=True) * column_valid for k in masks]
     valid = jnp.broadcast_to(valid, (128, 128)).astype(BF16)
 
-    def slab(side_refs, g):
-        return jnp.concatenate([r[g * 32 : (g + 1) * 32, :] for r in side_refs], axis=0)
-
-    for g in range(groups):
+    for g in range(GROUPS):
         full = dot(slab(left_refs, g) * valid, slab(right_refs, g), NT).reshape(4, 4, ROWS, 128)
         for m in range(4):
             kept = full[m, 3]
@@ -225,8 +255,7 @@
     for m in range(4):
         sig = sig_refs[m][...]
         out = sig * update[:, m * 128 : (m + 1) * 128]
-        ref, at = outs[m]
-        ref[at : at + PIECE, :] = out.astype(BF16)
+        out_refs[m][...] = out.astype(BF16)
         ref, at = pieces[m]
         cot = ref[at : at + PIECE, :].astype(F32)
         grad_update.append((cot * sig).astype(BF16))
@@ -235,32 +264,53 @@
     second = channel_mean(grad_hat * normed)
     grad_mixed = inverse * (grad_hat - first - normed * second)
 
+    mask = jnp.concatenate(pair_valid, axis=0)
     for row in range(ROWS):
         part = grad_mixed[row * 32 : (row + 1) * 32]
         parts = [part[:, q * 128 : (q + 1) * 128].reshape(4, 1, ROWS, 128) for q in range(4)]
         turn = jnp.concatenate(parts, axis=1).reshape(128, 128)
         pairs_ref[pl.ds(row, 128, stride=ROWS), :] = turn.T
-
-    def right_out(n, g):
-        if n < 2:
-            return right_outs[n], g * 32
-        half = groups // 2
-        return right_outs[2 * n - 2 + g // half], (g % half) * 32
-
-    for g in range(groups):
-        rows = []
-        for m in range(4):
-            part = pairs_ref[g * 32 + m * ROWS : g * 32 + (m + 1) * ROWS, :] * pair_valid[m]
-            rows += [jnp.where(of_quarter[q], part, 0.0) for q in range(4)]
-        spread = jnp.concatenate(rows, axis=0).astype(BF16)
-        grad_right = dot(spread, slab(left_refs, g), TN).astype(BF16)
-        grad_left = dot(spread, slab(right_refs, g), NN).astype(BF16)
-        for m in range(4):
-            ref, at = lefts[m]
-            at += g * 32
-            ref[at : at + 32, :] = grad_left[m * 32 : (m + 1) * 32]
-            ref, at = right_out(m, g)
-            ref[at : at + 32, :] = grad_right[m * 32 : (m + 1) * 32]
+    for g in range(GROUPS):
+        pairs_ref[g * 32 : (g + 1) * 32, :] = pairs_ref[g * 32 : (g + 1) * 32, :] * mask
+
+
+def spread_group(pairs_ref, g, of_quarter):
+    rows = []
+    for m in range(4):
+        part = pairs_ref[g * 32 + m * ROWS : g * 32 + (m + 1) * ROWS, :]
+        rows += [jnp.where(of_quarter[q], part, 0.0) for q in range(4)]
+    return jnp.concatenate(rows, axis=0).astype(BF16)
+
+
+def grad_right_kernel(half):
+    def kernel(pairs_ref, *refs):
+        left_refs, out_refs = refs[:4], refs[4:]
+        of_quarter = quarters()
+        for g in range(GROUPS // 2):
+            spread = spread_group(pairs_ref, half * GROUPS // 2 + g, of_quarter)
+            grad = dot(spread, slab(left_refs, half * GROUPS // 2 + g), TN).astype(BF16)
+            for n in range(4):
+                out_refs[n][g * 32 : (g + 1) * 32, :] = grad[n * 32 : (n + 1) * 32]
+
+    return kernel
+
+
+def grad_left_kernel(pairs_ref, *refs):
+    right_refs, (out_near, out_both), (left_0, core_ref, left_2) = refs[:4], refs[4:6], refs[7:]
+    lefts = [(left_0, 0), (core_ref, 0), (left_2, 0), (core_ref, SIDE + PIECE)]
+    of_quarter = quarters()
+    for g in range(GROUPS):
+        spread = spread_group(pairs_ref, g, of_quarter)
+        grad = dot(spread, slab(right_refs, g), NN).astype(BF16)
+        for m, (ref, at) in enumerate(lefts):
+            ref[at + g * 32 : at + (g + 1) * 32, :] = grad[m * 32 : (m + 1) * 32]
+    core_ref[SIDE : SIDE + PIECE, :] = out_near[...]
+    core_ref[2 * SIDE + PIECE :, :] = out_both[...]
+
+
+def halves_kernel(x_ref, first_ref, second_ref):
+    first_ref[...] = x_ref[: SIDE // 2, :]
+    second_ref[...] = x_ref[SIDE // 2 :, :]
 
 
 def pass_kernel(message_ref, *refs):
@@ -275,6 +325,11 @@
 def add_kernel(mine_ref, got_ref, *refs):
     sum_ref = refs[-1]
     sum_ref[...] = (mine_ref[...].astype(F32) + got_ref[...].astype(F32)).astype(BF16)
+
+
+def near_kernel(first_ref, second_ref, after_ref, both_ref):
+    both_ref[: SIDE // 2, :] = first_ref[...]
+    both_ref[SIDE // 2 :, :] = second_ref[...]
 
 
 def add_left_kernel(mine_ref, piece_ref, got_ref, sum_ref, out_ref):
@@ -332,24 +387,51 @@
         grad_ref[row] = dot(weight_ref[:, 512:640], grad_gate, NT)
 
 
-def pair_kernel(*refs):
-    left_refs, right_refs = refs[0:3], refs[3:7]
-    factor_ref, normed_ref, inverse_ref, gain_t_ref, gate_ref, weight_ref = refs[7:13]
-    out_ref, rows_ref = refs[13:]
-    half = SIDE // 2
+def right_terms(rows_ref, factor_ref, row, half):
+    parts = []
+    nothing = jnp.zeros((16, 128), BF16)
+    for place in (256, 384):
+        for q in range(4):
+            grad = rows_ref[pl.ds(q * ROWS + row, 16, stride=4 * ROWS), :]
+            at = place + q * 32 + half * 16
+            term = (grad * factor_ref[row, at : at + 16, :]).astype(BF16)
+            parts += [nothing, term] if half else [term, nothing]
+    return jnp.concatenate(parts, axis=0)
+
+
+def partial_kernel(*refs):
+    left_refs, (own_ref, near_ref, got_ref) = refs[0:3], refs[3:6]
+    factor_ref, gate_ref, weight_ref, sum_ref, left_rows, right_rows = refs[6:]
     left = [r[:SIDE, :].astype(F32) for r in left_refs]
-    rows_ref[0] = left[0] + left[1] + left[2]
-    for part in range(2):
-        at = slice(part * half, (part + 1) * half)
-        right = right_refs[0][at, :].astype(F32) + right_refs[1][at, :].astype(F32)
-        rows_ref[1, at, :] = right + right_refs[2 + part][...].astype(F32)
-    for row in range(ROWS):
-        parts = []
-        for side in range(2):
-            grad = load_side(rows_ref.at[side], row)
-            for place in (256 * side, 256 * side + 128):
-                parts.append((grad * factor_ref[row, place : place + 128, :]).astype(BF16))
-        grad_scaled = dot(weight_ref[:, :512], jnp.concatenate(parts, axis=0), NN) + gate_ref[row]
+    left_rows[...] = left[0] + left[1] + left[2]
+    right = own_ref[...].astype(F32) + near_ref[: SIDE // 2, :].astype(F32)
+    right_rows[...] = right + got_ref[...].astype(F32)
+    for row in range(ROWS):
+        grad = load_side(left_rows, row)
+        parts = [(grad * factor_ref[row, a : a + 128, :]).astype(BF16) for a in (0, 128)]
+        parts.append(right_terms(right_rows, factor_ref, row, 0))
+        grad_projected = jnp.concatenate(parts, axis=0)
+        sum_ref[row] = dot(weight_ref[:, :512], grad_projected, NN) + gate_ref[row]
+
+
+def pair_kernel(
+    own_ref,
+    near_ref,
+    got_ref,
+    factor_ref,
+    sum_ref,
+    normed_ref,
+    inverse_ref,
+    gain_t_ref,
+    weight_ref,
+    out_ref,
+    right_rows,
+):
+    right = own_ref[...].astype(F32) + near_ref[SIDE // 2 :, :].astype(F32)
+    right_rows[...] = right + got_ref[...].astype(F32)
+    for row in range(ROWS):
+        terms = right_terms(right_rows, factor_ref, row, 1)
+        grad_scaled = dot(weight_ref[:, 256:512], terms, NN) + sum_ref[row]
         normed = normed_ref[row]
         grad_hat = grad_scaled * gain_t_ref[...]
         first = jnp.mean(grad_hat, axis=0, keepdims=True)
@@ -383,14 +465,19 @@
     rows_scratch = pltpu.VMEM((2, SIDE, 128), F32)
     cube_scratch = pltpu.VMEM(cube, F32)
 
+    def after(message, *others):
+        return call(pass_kernel, [(message.shape, BF16)], vmem=[message, *others])[0]
+
     flat = pair_rep.reshape(SIDE, 128)
     weights = jnp.concatenate([proj_weight, gate_weight, out_weight], axis=1)
     params = jnp.stack([in_gain, in_bias, mid_gain, mid_bias])
 
-    far = swap(flat, Z_LOW)
-    x_near = swap(flat, CHIP_X)
-    near = swap(flat, CORE)
-    z_first, z_second = swap(flat[:half], Z_HIGH), swap(flat[half:], Z_HIGH)
+    first, second = call(halves_kernel, [halves] * 2, vmem=[flat])
+    z_first, z_second = swap(first, Z_HIGH), swap(second, Z_HIGH)
+    whole = after(flat, second)
+    far = swap(whole, Z_LOW)
+    x_near = swap(whole, CHIP_X)
+    near = swap(whole, CORE)
     left_0, right_0, sig_0, weight_t, block_weight, mid = call(
         own_kernel,
         [side, side, sig, ((512, 128), BF16), ((512, 512), BF16), ((ROWS, 512), F32)],
@@ -410,38 +497,62 @@
             weight=WAIT,
         )
 
-    def after(message, *others):
-        return call(pass_kernel, [(message.shape, BF16)], vmem=[message, *others])[0]
-
     left_1, right_1, sig_1 = peer(near, x_near)
     own_piece, core_piece, far_piece = call(
         pack_kernel,
         [((HEAD, 128), BF16), ((HEAD, 128), BF16), ((2 * HEAD, 128), BF16)],
         smem=[me],
-        vmem=[cotangent, pair_mask, sig_1],
+        vmem=[cotangent, pair_mask, x_near],
         scratch=[cube_scratch],
     )
     far_got = swap(far_piece, Z_LOW)
     both = swap(far, CORE)
-    x_first = swap(after(z_first, sig_1, core_piece), CHIP_X)
-    x_second = swap(after(z_second, sig_1, core_piece), CHIP_X)
+    x_second = swap(z_second, CHIP_X)
+    x_first = swap(after(z_first, x_second, left_0), CHIP_X)
     (joined,) = call(join_kernel, [((2 * HEAD, 128), BF16)], vmem=[core_piece, far_got])
     core_pieces = swap(joined, CORE)
     left_2, right_2, sig_2 = peer(far, z_first, z_second)
-    left_3, right_3, sig_3 = peer(both, x_first, x_second)
-
-    out_0, out_2, core_back, grad_left_0, grad_left_2, *grad_right = call(
+    left_3, sig_3 = call(
+        left_kernel,
+        [side, sig],
+        smem=[me],
+        vmem=[both, weight_t, weights, params],
+        scratch=[pltpu.VMEM((SIDE, 128), F32), cube_scratch],
+        weight=WAIT,
+    )
+
+    def right_half(first, last, *operands):
+        return call(
+            right_kernel(first, last),
+            [((SIDE, 128), BF16 if last else F32)],
+            vmem=operands,
+            scratch=[pltpu.VMEM((SIDE, 128), F32)],
+            weight=WAIT // 4,
+        )[0]
+
+    right_part = right_half(ROWS // 2, False, x_second, weight_t, params, left_3)
+    right_3 = right_half(0, True, x_first, weight_t, params, right_part)
+
+    lefts, rights = [left_0, left_1, left_2, left_3], [right_0, right_1, right_2, right_3]
+    out_0, out_1, out_2, out_3, pairs = call(
         block_kernel,
-        [piece, piece, core, side, side, side, side] + [halves] * 4,
+        [piece] * 4 + [((SIDE, 128), F32)],
         smem=[me],
-        vmem=[left_0, left_1, left_2, left_3]
-        + [right_0, right_1, right_2, right_3]
+        vmem=lefts
+        + rights
         + [sig_0, sig_1, sig_2, sig_3]
         + [own_piece, core_pieces, far_got, block_weight, mid],
-        scratch=[pltpu.VMEM((SIDE, 128), F32)],
+    )
+    right_a = call(grad_right_kernel(0), [halves] * 4, vmem=[pairs, *lefts])
+    x_got = [swap(right_a[3], CHIP_X)]
+    grad_left_0, core_back, grad_left_2 = call(
+        grad_left_kernel,
+        [side, core, side],
+        vmem=[pairs, *rights, out_1, out_3, right_a[3]],
     )
     core_got = swap(core_back, CORE)
-    x_got = [swap(grad_right[4], CHIP_X), swap(grad_right[5], CHIP_X)]
+    right_b = call(grad_right_kernel(1), [halves] * 4, vmem=[pairs, *lefts])
+    x_got.append(swap(after(right_b[3], x_got[0]), CHIP_X))
     left_sum, out_far = call(
         add_left_kernel,
         [side, ((2 * PIECE, 128), BF16)],
@@ -449,11 +560,12 @@
     )
     left_got = swap(left_sum, Z_LOW)
     out_far = swap(out_far, Z_LOW)
-    totals = []
-    for mine, got in zip(grad_right[2:4], x_got):
-        totals += call(add_kernel, [halves], vmem=[mine, got, left_sum])
-    z_got = [swap(total, Z_HIGH) for total in totals]
-    right_near = swap(after(grad_right[1], *totals), CHIP_X)
+    (total,) = call(add_kernel, [halves], vmem=[right_a[2], x_got[0]])
+    z_got = [swap(total, Z_HIGH)]
+    (total,) = call(add_kernel, [halves], vmem=[right_b[2], x_got[1], left_sum])
+    z_got.append(swap(total, Z_HIGH))
+    (near_back,) = call(near_kernel, [side], vmem=[right_a[1], right_b[1], total])
+    right_near = swap(near_back, CHIP_X)
 
     factors, normed, inverse, open_part, gain_t = call(
         factor_kernel,
@@ -468,12 +580,21 @@
         vmem=[out_0, core_got, out_far, open_part, weights],
         scratch=[cube_scratch],
     )
+    half_scratch = pltpu.VMEM((half, 128), F32)
+    (partial,) = call(
+        partial_kernel,
+        [(cube, F32)],
+        vmem=[grad_left_0, core_got, left_got, right_a[0], right_near, z_got[0]]
+        + [factors, gate_part, weights],
+        scratch=[pltpu.VMEM((SIDE, 128), F32), half_scratch],
+        weight=WAIT // 4,
+    )
     (grad_pair,) = call(
         pair_kernel,
         [(cube, BF16)],
-        vmem=[grad_left_0, core_got, left_got, grad_right[0], right_near, *z_got]
-        + [factors, normed, inverse, gain_t, gate_part, weights],
-        scratch=[rows_scratch],
+        vmem=[right_b[0], right_near, z_got[1]]
+        + [factors, partial, normed, inverse, gain_t, weights],
+        scratch=[half_scratch],
     )
     return (output, grad_pair)
 

time: 56 us -> 57 us (1.018)
  starting transfers between devices: 17.8 us -> 21.3 us
  waiting for transfers between devices: 16.5 us -> 13.3 us
  Pallas kernels: 15.4 us -> 16.1 us
    ppermute x18, starting transfers between devices: 17.8 us -> 21.3 us  [swap(): return lax.ppermute(values, 'row', [(s, s ^ offset) for s in range(16)])]
    ppermute x18, waiting for transfers between devices: 16.5 us -> 13.3 us  [swap(): return lax.ppermute(values, 'row', [(s, s ^ offset) for s in range(16)])]
    slice x1 -> x0, local copies, waits for them, and re-layouts: 0.99 us -> none  [blocks_device(): z_first, z_second = (swap(flat[:half], Z_HIGH), swap(flat[half:], Z_HIGH))]
    unnamed x10 -> x12, local copies, waits for them, and re-layouts: 2.65 us -> 3.59 us
    pallas_call x16 -> x24, Pallas kernels: 15.4 us -> 16.1 us  [call(): pl.pallas_call(kernel, out_shape=[jax.ShapeDtypeStruct(s, d) for s, d in...]
  transfers between devices with their start and end apart: 18 -> 18, of which waited for: 8 -> 4; matrix products, arithmetic and copies ran while one was open for 7% -> 6% of each run, Pallas kernels for 18% -> 21%
where the time goes in v6:
time: 57 us; the launch traced here: 56.7 us
  starting transfers between devices  21.3 us (37%)
  Pallas kernels  16.1 us (28%)
  waiting for transfers between devices  13.3 us (23%)
  local copies, waits for them, and re-layouts  4.36 us (8%)
  between operations  0.86 us (2%)
  other arithmetic  0.71 us (1%)
    ppermute x18, starting transfers between devices, swap(): return lax.ppermute(values, 'row', [(s, s ^ offset) for s in range(16)])  21.3 us
    pallas_call x24, Pallas kernels, call(): pl.pallas_call(kernel, out_shape=[jax.ShapeDtypeStruct(s, d) for s, d in...  16.1 us
    ppermute x18, waiting for transfers between devices, swap(): return lax.ppermute(values, 'row', [(s, s ^ offset) for s in range(16)])  13.3 us
    unnamed x12, local copies, waits for them, and re-layouts  3.59 us
  transfers between devices with their start and end apart: 18, of which 4 were waited for; matrix products, arithmetic and copies ran while one was open for 6% of the time, Pallas kernels for 21%

profile of v6, /device:TPU:0, one launch (start us, length us, event | category | flops | bytes accessed | tf_op | source)
XLA Modules:
  0.0 56.7 jit_solution(10015562455798320101)
XLA Ops:
  0.6 0.0 copy-start
  0.6 0.9 %copy-done = bf16[8,128,128]{2,1,0:T(8,128)(2,1)S(1)} copy-done((bf16[8,128,128]{2,1,0:T(8,128)(2,1)S(1)}, bf16[8,128,128]{2,1,0:T(8,128)(2,1)}, u32[]{:S(2)}) %copy-start) | copy-done | bytes 262168
  1.6 4.1 %collective-permute-start.4 = (bf16[512,128]{1,0:T(8,128)(2,1)S(1)}, bf16[512,128]{1,0:T(8,128)(2,1)S(1)}, u32[]{:S(2)}, u32[]{:S(2)}) collective-permute-start(bf16[512,128]{1,0:T(8,128)(2,1)S(1)} %get-tuple-element.47.refs_0_), channel_id=1, source_target_pairs={{0,8},{1,9},{2,10},{3,11},{4,12},{5,13},{6,14},{7,15},{8,0},{9,1},... | collective-permute-start | bytes 393224 | tf_op jit(solution)/shard_map/ppermute | solution.py:444
  5.7 1.6 %collective-permute-start.2 = (bf16[1024,128]{1,0:T(8,128)(2,1)S(1)}, bf16[1024,128]{1,0:T(8,128)(2,1)S(1)}, u32[]{:S(2)}, u32[]{:S(2)}) collective-permute-start(bf16[1024,128]{1,0:T(8,128)(2,1)S(1)} %shard_map.115), channel_id=1, source_target_pairs={{0,4},{1,5},{2,6},{3,7},{4,0},{5,1},{6,2},{7,3},{8,12},{9,13},{10,... | collective-permute-start | bytes 786440 | tf_op jit(solution)/shard_map/ppermute | solution.py:444
  7.4 1.5 %collective-permute-start.1 = (bf16[1024,128]{1,0:T(8,128)(2,1)S(1)}, bf16[1024,128]{1,0:T(8,128)(2,1)S(1)}, u32[]{:S(2)}, u32[]{:S(2)}) collective-permute-start(bf16[1024,128]{1,0:T(8,128)(2,1)S(1)} %shard_map.115), channel_id=1, source_target_pairs={{0,2},{1,3},{2,0},{3,1},{4,6},{5,7},{6,4},{7,5},{8,10},{9,11},{10,... | collective-permute-start | bytes 786440 | tf_op jit(solution)/shard_map/ppermute | solution.py:444
  8.9 0.0 collective-permute-start
  8.9 0.3 collective-permute-start.3
  9.2 0.9 %constant_dynamic-update-slice_fusion.2 = bf16[128,768]{1,0:T(8,128)(2,1)S(1)} fusion(bf16[128,512]{1,0:T(8,128)(2,1)} %param.15), kind=kLoop, calls=%fused_computation.2 | loop fusion | bytes 262144
  10.1 0.8 %constant_dynamic-update-slice_fusion.1 = bf16[128,768]{1,0:T(8,128)(2,1)S(1)} fusion(bf16[128,768]{1,0:T(8,128)(2,1)S(1)} %constant_dynamic-update-slice_fusion.2, bf16[128,128]{1,0:T(8,128)(2,1)} %param.16), kind=kLoop, calls=%fused_computation.1 | loop fusion | bytes 65536
  10.9 0.7 %pad_maximum_fusion.params_ref.refs_3_.refs_4_ = f32[4,128]{1,0:T(4,128)S(1)} fusion(f32[1,128]{1,0:T(1,128)} %bitcast.10, f32[1,128]{1,0:T(1,128)} %bitcast.11, f32[1,128]{1,0:T(1,128)} %bitcast.12, f32[1,128]{1,0:T(1,128)} %bitcast.13), kind=kLoop, calls=%fused_computation.3 | loop fusion | flops 1536 | bytes 4096 | tf_op jit(solution)/shard_map/stack | solution.py:473
  11.6 0.8 %constant_dynamic-update-slice_fusion.weight_ref.refs_2_.refs_3_.refs_8_ = bf16[128,768]{1,0:T(8,128)(2,1)S(1)} fusion(bf16[128,768]{1,0:T(8,128)(2,1)S(1)} %constant_dynamic-update-slice_fusion.1, bf16[128,128]{1,0:T(8,128)(2,1)} %param.19), kind=kLoop, calls=%fused_computation | loop fusion | bytes 65536 | tf_op jit(solution)/shard_map/concatenate | solution.py:472
  12.4 0.0 collective-permute-done.4.refs_1_
  12.4 1.4 %collective-permute-start.6 = (bf16[512,128]{1,0:T(8,128)(2,1)S(1)}, bf16[512,128]{1,0:T(8,128)(2,1)S(1)}, u32[]{:S(2)}, u32[]{:S(2)}) collective-permute-start(bf16[512,128]{1,0:T(8,128)(2,1)S(1)} %collective-permute-done.4.refs_1_), channel_id=1, source_target_pairs={{0,2},{1,3},{2,0},{3,1},{4,6},{5,7},{6,4},{7,5},{8,10},{9,11},{10,... | collective-permute-start | bytes 393224 | tf_op jit(solution)/shard_map/ppermute | solution.py:444
  13.7 0.0 copy-start.1
  13.7 0.9 %copy-done.1 = bf16[8,128,128]{2,1,0:T(8,128)(2,1)S(1)} copy-done((bf16[8,128,128]{2,1,0:T(8,128)(2,1)S(1)}, bf16[8,128,128]{2,1,0:T(8,128)(2,1)}, u32[]{:S(2)}) %copy-start.1) | copy-done | bytes 262168
  14.7 1.9 %shard_map.113 = (bf16[1024,128]{1,0:T(8,128)(2,1)S(1)}, bf16[1024,128]{1,0:T(8,128)(2,1)S(1)}, f32[256,128]{1,0:T(8,128)S(1)}, bf16[512,128]{1,0:T(8,128)(2,1)S...) custom-call(s32[1]{0:T(128)} %bitcast.me_ref.refs_0_, bf16[1024,128]{1,0:T(8,128)(2,1)S(1)} %bitcast.8, ...), custom_call_target="tpu_custom_call" | custom-call | flops 5000000000 | bytes 262144 | tf_op jit(solution)/shard_map/pallas_call | solution.py:43
  16.6 0.0 collective-permute-done.1.refs_0_.after_ref
  16.6 0.0 copy-done.3
  16.6 0.0 copy-done.4
  16.6 0.1 shard_map.122
  16.8 0.7 %collective-permute-start.8 = (bf16[544,128]{1,0:T(8,128)(2,1)S(1)}, bf16[544,128]{1,0:T(8,128)(2,1)S(1)}, u32[]{:S(2)}, u32[]{:S(2)}) collective-permute-start(bf16[544,128]{1,0:T(8,128)(2,1)S(1)} %get-tuple-element.62), channel_id=1, source_target_pairs={{0,4},{1,5},{2,6},{3,7},{4,0},{5,1},{6,2},{7,3},{8,12},{9,13},{10,... | collective-permute-start | bytes 417800 | tf_op jit(solution)/shard_map/ppermute | solution.py:444
  17.4 0.0 collective-permute-done.3.refs_0_.message_ref
  17.4 0.6 %collective-permute-done.6.refs_0_.x_ref = bf16[512,128]{1,0:T(8,128)(2,1)S(1)} collective-permute-done((bf16[512,128]{1,0:T(8,128)(2,1)S(1)}, bf16[512,128]{1,0:T(8,128)(2,1)S(1)}, u32[]{:S(2)}, u32[]{:S(2)}) %collective-permute-start.6) | collective-permute-done | bytes 131104 | tf_op jit(solution)/shard_map/ppermute | solution.py:444
  18.1 1.1 %collective-permute-start.7 = (bf16[512,128]{1,0:T(8,128)(2,1)S(1)}, bf16[512,128]{1,0:T(8,128)(2,1)S(1)}, u32[]{:S(2)}, u32[]{:S(2)}) collective-permute-start(bf16[512,128]{1,0:T(8,128)(2,1)S(1)} %shard_map.119), channel_id=1, source_target_pairs={{0,2},{1,3},{2,0},{3,1},{4,6},{5,7},{6,4},{7,5},{8,10},{9,11},{10,... | collective-permute-start | bytes 393224 | tf_op jit(solution)/shard_map/ppermute | solution.py:444
  19.2 0.0 collective-permute-done.2.left_in
  19.2 0.0 collective-permute-start.5
  19.2 1.9 %shard_map.117 = (bf16[1024,128]{1,0:T(8,128)(2,1)S(1)}, bf16[1024,128]{1,0:T(8,128)(2,1)S(1)}, f32[256,128]{1,0:T(8,128)S(1)}) custom-call(s32[1]{0:T(128)} %bitcast.me_ref.refs_0_, bf16[1024,128]{1,0:T(8,128)(2,1)S(1)} %collective-permute-done.2.left_in, bf16[512,128]{1,0:T(8,128)(2,1)S(1)} %collective-permute-done.3.refs_0_.message_ref, ...), custom_call_target="tpu_custom_call" | custom-call | flops 5000000000 | bytes 262144 | tf_op jit(solution)/shard_map/pallas_call | solution.py:43
  21.2 0.0 collective-permute-done.left_in
  21.2 1.9 %shard_map.116 = (bf16[1024,128]{1,0:T(8,128)(2,1)S(1)}, bf16[1024,128]{1,0:T(8,128)(2,1)S(1)}, f32[256,128]{1,0:T(8,128)S(1)}) custom-call(s32[1]{0:T(128)} %bitcast.me_ref.refs_0_, bf16[1024,128]{1,0:T(8,128)(2,1)S(1)} %collective-permute-done.left_in, bf16[1024,128]{1,0:T(8,128)(2,1)S(1)} %collective-permute-done.1.refs_0_.after_ref, ...), custom_call_target="tpu_custom_call" | custom-call | flops 5000000000 | bytes 262144 | tf_op jit(solution)/shard_map/pallas_call | solution.py:43
  23.1 0.0 collective-permute-done.8.got_ref.refs_15_
  23.2 0.6 %collective-permute-start.9 = (bf16[544,128]{1,0:T(8,128)(2,1)S(1)}, bf16[544,128]{1,0:T(8,128)(2,1)S(1)}, u32[]{:S(2)}, u32[]{:S(2)}) collective-permute-start(bf16[544,128]{1,0:T(8,128)(2,1)S(1)} %shard_map.123), channel_id=1, source_target_pairs={{0,1},{1,0},{2,3},{3,2},{4,5},{5,4},{6,7},{7,6},{8,9},{9,8},{10,11... | collective-permute-start | bytes 417800 | tf_op jit(solution)/shard_map/ppermute | solution.py:444
  23.7 0.0 collective-permute-done.5.x_ref
  23.7 1.0 %shard_map.118 = (bf16[1024,128]{1,0:T(8,128)(2,1)S(1)}, f32[256,128]{1,0:T(8,128)S(1)}) custom-call(s32[1]{0:T(128)} %bitcast.me_ref.refs_0_, bf16[1024,128]{1,0:T(8,128)(2,1)S(1)} %collective-permute-done.5.x_ref, bf16[512,128]{1,0:T(8,128)(2,1)S(1)} %get-tuple-element.48.refs_1_.refs_2_.weight_t_ref, ...), custom_call_target="tpu_custom_call" | custom-call | flops 5000000000 | bytes 262144 | tf_op jit(solution)/shard_map/pallas_call | solution.py:43
  24.8 0.7 %shard_map.120.rest_ref = f32[1024,128]{1,0:T(8,128)S(1)} custom-call(bf16[512,128]{1,0:T(8,128)(2,1)S(1)} %collective-permute-done.6.refs_0_.x_ref, bf16[512,128]{1,0:T(8,128)(2,1)S(1)} %get-tuple-element.48.refs_1_.refs_2_.weight_t_ref, f32[4,128]{1,0:T(4,128)S(1)} %pad_maximum_fusion.params_ref.refs_3_.refs_4_, ...), custom_call_target="tpu_custom_call" | custom-call | flops 1250000000 | bytes 262144 | tf_op jit(solution)/shard_map/pallas_call | solution.py:43
  25.4 0.0 collective-permute-done.7.x_ref
  25.4 0.7 %shard_map.121.refs_8_.refs_3_ = bf16[1024,128]{1,0:T(8,128)(2,1)S(1)} custom-call(bf16[512,128]{1,0:T(8,128)(2,1)S(1)} %collective-permute-done.7.x_ref, bf16[512,128]{1,0:T(8,128)(2,1)S(1)} %get-tuple-element.48.refs_1_.refs_2_.weight_t_ref, f32[4,128]{1,0:T(4,128)S(1)} %pad_maximum_fusion.params_ref.refs_3_.refs_4_, f32[1024,128]{1,0:T(8,128)S(1)} %shard_map.120.rest_ref), custom_call_target="tpu_custom_call" | custom-call | flops 1250000000 | bytes 262144 | tf_op jit(solution)/shard_map/pallas_call | solution.py:43
  26.1 0.0 collective-permute-done.9.refs_14_
  26.1 2.2 %shard_map.124 = (bf16[256,128]{1,0:T(8,128)(2,1)S(1)}, bf16[256,128]{1,0:T(8,128)(2,1)S(1)}, bf16[256,128]{1,0:T(8,128)(2,1)S(1)}, bf16[256,128]{1,0:T(8,128)(2,1)S(1)}, f32[1024,128]{1,0:T(8,128)S(1)}) custom-call(s32[1]{0:T(128)} %bitcast.me_ref.refs_0_, bf16[1024,128]{1,0:T(8,128)(2,1)S(1)} %get-tuple-element.46.refs_1_.refs_0_, ...), custom_call_target="tpu_custom_call" | custom-call | flops 67108864 | bytes 262144 | tf_op jit(solution)/shard_map/pallas_call | solution.py:43
  28.3 0.4 shard_map.125
  28.7 0.4 shard_map.126
  29.1 0.0 copy-start.2
  29.2 0.1 collective-permute-start.10
  29.2 1.0 %collective-permute-start.12 = (bf16[512,128]{1,0:T(8,128)(2,1)S(1)}, bf16[512,128]{1,0:T(8,128)(2,1)S(1)}, u32[]{:S(2)}, u32[]{:S(2)}) collective-permute-start(bf16[512,128]{1,0:T(8,128)(2,1)S(1)} %get-tuple-element.69.refs_6_), channel_id=1, source_target_pairs={{0,2},{1,3},{2,0},{3,1},{4,6},{5,7},{6,4},{7,5},{8,10},{9,11},{10,... | collective-permute-start | bytes 393224 | tf_op jit(solution)/shard_map/ppermute | solution.py:444
  30.3 0.3 shard_map.130
  30.6 4.5 %collective-permute-done.12.refs_0_.got_ref = bf16[512,128]{1,0:T(8,128)(2,1)S(1)} collective-permute-done((bf16[512,128]{1,0:T(8,128)(2,1)S(1)}, bf16[512,128]{1,0:T(8,128)(2,1)S(1)}, u32[]{:S(2)}, u32[]{:S(2)}) %collective-permute-start.12) | collective-permute-done | bytes 131104 | tf_op jit(solution)/shard_map/ppermute | solution.py:444
  35.2 1.0 %collective-permute-start.13 = (bf16[512,128]{1,0:T(8,128)(2,1)S(1)}, bf16[512,128]{1,0:T(8,128)(2,1)S(1)}, u32[]{:S(2)}, u32[]{:S(2)}) collective-permute-start(bf16[512,128]{1,0:T(8,128)(2,1)S(1)} %shard_map.131), channel_id=1, source_target_pairs={{0,2},{1,3},{2,0},{3,1},{4,6},{5,7},{6,4},{7,5},{8,10},{9,11},{10,... | collective-permute-start | bytes 393224 | tf_op jit(solution)/shard_map/ppermute | solution.py:444
  36.2 2.9 %collective-permute-start.17 = (bf16[512,128]{1,0:T(8,128)(2,1)S(1)}, bf16[512,128]{1,0:T(8,128)(2,1)S(1)}, u32[]{:S(2)}, u32[]{:S(2)}) collective-permute-start(bf16[512,128]{1,0:T(8,128)(2,1)S(1)} %shard_map.134), channel_id=1, source_target_pairs={{0,8},{1,9},{2,10},{3,11},{4,12},{5,13},{6,14},{7,15},{8,0},{9,1},... | collective-permute-start | bytes 393224 | tf_op jit(solution)/shard_map/ppermute | solution.py:444
  39.1 0.0 collective-permute-done.10.got_ref.near_ref.refs_1_
  39.1 0.1 shard_map.127
  39.2 0.8 %collective-permute-start.11 = (bf16[512,128]{1,0:T(8,128)(2,1)S(1)}, bf16[512,128]{1,0:T(8,128)(2,1)S(1)}, u32[]{:S(2)}, u32[]{:S(2)}) collective-permute-start(bf16[512,128]{1,0:T(8,128)(2,1)S(1)} %get-tuple-element.73), channel_id=1, source_target_pairs={{0,4},{1,5},{2,6},{3,7},{4,0},{5,1},{6,2},{7,3},{8,12},{9,13},{10,... | collective-permute-start | bytes 393224 | tf_op jit(solution)/shard_map/ppermute | solution.py:444
  39.9 1.3 %collective-permute-start.16 = (bf16[1024,128]{1,0:T(8,128)(2,1)S(1)}, bf16[1024,128]{1,0:T(8,128)(2,1)S(1)}, u32[]{:S(2)}, u32[]{:S(2)}) collective-permute-start(bf16[1024,128]{1,0:T(8,128)(2,1)S(1)} %get-tuple-element.81.refs_0_), channel_id=1, source_target_pairs={{0,4},{1,5},{2,6},{3,7},{4,0},{5,1},{6,2},{7,3},{8,12},{9,13},{10,... | collective-permute-start | bytes 786440 | tf_op jit(solution)/shard_map/ppermute | solution.py:444
  41.3 0.0 collective-permute-done.13.got_ref
  41.3 2.0 %collective-permute-start.15 = (bf16[512,128]{1,0:T(8,128)(2,1)S(1)}, bf16[512,128]{1,0:T(8,128)(2,1)S(1)}, u32[]{:S(2)}, u32[]{:S(2)}) collective-permute-start(bf16[512,128]{1,0:T(8,128)(2,1)S(1)} %shard_map.132.after_ref), channel_id=1, source_target_pairs={{0,8},{1,9},{2,10},{3,11},{4,12},{5,13},{6,14},{7,15},{8,0},{9,1},... | collective-permute-start | bytes 393224 | tf_op jit(solution)/shard_map/ppermute | solution.py:444
  43.3 0.9 %collective-permute-start.14 = (bf16[1024,128]{1,0:T(8,128)(2,1)S(1)}, bf16[1024,128]{1,0:T(8,128)(2,1)S(1)}, u32[]{:S(2)}, u32[]{:S(2)}) collective-permute-start(bf16[1024,128]{1,0:T(8,128)(2,1)S(1)} %shard_map.133), channel_id=1, source_target_pairs={{0,2},{1,3},{2,0},{3,1},{4,6},{5,7},{6,4},{7,5},{8,10},{9,11},{10,... | collective-permute-start | bytes 786440 | tf_op jit(solution)/shard_map/ppermute | solution.py:444
  44.2 0.0 copy-done.2
  44.2 1.1 %shard_map.128 = (f32[8,512,128]{2,1,0:T(8,128)S(1)}, f32[8,128,128]{2,1,0:T(8,128)S(1)}, f32[8,128]{1,0:T(8,128)S(1)}, f32[8,128,128]{2,1,0:T(8,128)S(1)}, f32[128,128]{1,0:T(8,128)S(1)}) custom-call(bf16[1024,128]{1,0:T(8,128)(2,1)S(1)} %bitcast.9, bf16[8,128,128]{2,1,0:T(8,128)(2,1)S(1)} %copy-done.3, s32[8,128]{1,0:T(8,128)S(1)} %copy-done.4, ...), custom_call_target="tpu_custom_call" | custom-call | flops 5000000000 | bytes 262144 | tf_op jit(solution)/shard_map/pallas_call | solution.py:43
  45.4 4.5 %collective-permute-done.11.far_ref = bf16[512,128]{1,0:T(8,128)(2,1)S(1)} collective-permute-done((bf16[512,128]{1,0:T(8,128)(2,1)S(1)}, bf16[512,128]{1,0:T(8,128)(2,1)S(1)}, u32[]{:S(2)}, u32[]{:S(2)}) %collective-permute-start.11) | collective-permute-done | bytes 131104 | tf_op jit(solution)/shard_map/ppermute | solution.py:444
  49.9 0.9 %shard_map.129 = (bf16[8,128,128]{2,1,0:T(8,128)(2,1)}, f32[8,128,128]{2,1,0:T(8,128)S(1)}) custom-call(s32[1]{0:T(128)} %bitcast.me_ref.refs_0_, bf16[256,128]{1,0:T(8,128)(2,1)S(1)} %get-tuple-element.65.own_ref, bf16[2560,128]{1,0:T(8,128)(2,1)S(1)} %collective-permute-done.10.got_ref.near_ref.refs_1_, ...), custom_call_target="tpu_custom_call" | custom-call | flops 67108864 | bytes 262144 | tf_op jit(solution)/shard_map/pallas_call | solution.py:43
  50.8 0.0 collective-permute-done.17.refs_5_
  50.8 0.0 collective-permute-done.14.refs_4_.near_ref
  50.8 3.6 %collective-permute-done.16.refs_2_ = bf16[1024,128]{1,0:T(8,128)(2,1)S(1)} collective-permute-done((bf16[1024,128]{1,0:T(8,128)(2,1)S(1)}, bf16[1024,128]{1,0:T(8,128)(2,1)S(1)}, u32[]{:S(2)}, u32[]{:S(2)}) %collective-permute-start.16) | collective-permute-done | bytes 262176 | tf_op jit(solution)/shard_map/ppermute | solution.py:444
  54.4 1.0 %shard_map.135.sum_ref = f32[8,128,128]{2,1,0:T(8,128)S(1)} custom-call(bf16[1024,128]{1,0:T(8,128)(2,1)S(1)} %get-tuple-element.83.refs_0_, bf16[2560,128]{1,0:T(8,128)(2,1)S(1)} %collective-permute-done.10.got_ref.near_ref.refs_1_, bf16[1024,128]{1,0:T(8,128)(2,1)S(1)} %collective-permute-done.16.refs_2_, bf16[512,128]{1,0:T(8,128)(2,1)S(1)} %get-tuple-element.84.refs_3_, ...), custom_call_target="tpu_custom_call" | custom-call | flops 1250000000 | bytes 262144 | tf_op jit(solution)/shard_map/pallas_call | solution.py:43
  55.4 0.0 collective-permute-done.15.got_ref
  55.4 1.3 %shard_map.136 = bf16[8,128,128]{2,1,0:T(8,128)(2,1)} custom-call(bf16[512,128]{1,0:T(8,128)(2,1)S(1)} %get-tuple-element.76.own_ref, bf16[1024,128]{1,0:T(8,128)(2,1)S(1)} %collective-permute-done.14.refs_4_.near_ref, bf16[512,128]{1,0:T(8,128)(2,1)S(1)} %collective-permute-done.15.got_ref, f32[8,512,128]{2,1,0:T(8,128)S(1)} %get-tuple-element.82.refs_6_.factor_ref, ...), custom_call_target="tpu_custom_call" | custom-call | flops 67108864 | bytes 262144 | tf_op jit(solution)/shard_map/pallas_call | solution.py:43
  (10 shorter events, 0.2 us)
Async XLA Ops:
  0.6 1.0 %copy-start = (bf16[8,128,128]{2,1,0:T(8,128)(2,1)S(1)}, bf16[8,128,128]{2,1,0:T(8,128)(2,1)}, u32[]{:S(2)}) copy-start(bf16[8,128,128]{2,1,0:T(8,128)(2,1)} %param.10) | copy-start | bytes 786436
  1.6 10.8 %collective-permute-start.4 = (bf16[512,128]{1,0:T(8,128)(2,1)S(1)}, bf16[512,128]{1,0:T(8,128)(2,1)S(1)}, u32[]{:S(2)}, u32[]{:S(2)}) collective-permute-start(bf16[512,128]{1,0:T(8,128)(2,1)S(1)} %get-tuple-element.47.refs_0_), channel_id=1, source_target_pairs={{0,8},{1,9},{2,10},{3,11},{4,12},{5,13},{6,14},{7,15},{8,0},{9,1},... | collective-permute-start | bytes 393224 | tf_op jit(solution)/shard_map/ppermute | solution.py:444
  5.7 13.5 %collective-permute-start.2 = (bf16[1024,128]{1,0:T(8,128)(2,1)S(1)}, bf16[1024,128]{1,0:T(8,128)(2,1)S(1)}, u32[]{:S(2)}, u32[]{:S(2)}) collective-permute-start(bf16[1024,128]{1,0:T(8,128)(2,1)S(1)} %shard_map.115), channel_id=1, source_target_pairs={{0,4},{1,5},{2,6},{3,7},{4,0},{5,1},{6,2},{7,3},{8,12},{9,13},{10,... | collective-permute-start | bytes 786440 | tf_op jit(solution)/shard_map/ppermute | solution.py:444
  7.4 9.2 %collective-permute-start.1 = (bf16[1024,128]{1,0:T(8,128)(2,1)S(1)}, bf16[1024,128]{1,0:T(8,128)(2,1)S(1)}, u32[]{:S(2)}, u32[]{:S(2)}) collective-permute-start(bf16[1024,128]{1,0:T(8,128)(2,1)S(1)} %shard_map.115), channel_id=1, source_target_pairs={{0,2},{1,3},{2,0},{3,1},{4,6},{5,7},{6,4},{7,5},{8,10},{9,11},{10,... | collective-permute-start | bytes 786440 | tf_op jit(solution)/shard_map/ppermute | solution.py:444
  8.9 12.3 %collective-permute-start = (bf16[1024,128]{1,0:T(8,128)(2,1)S(1)}, bf16[1024,128]{1,0:T(8,128)(2,1)S(1)}, u32[]{:S(2)}, u32[]{:S(2)}) collective-permute-start(bf16[1024,128]{1,0:T(8,128)(2,1)S(1)} %shard_map.115), channel_id=1, source_target_pairs={{0,1},{1,0},{2,3},{3,2},{4,5},{5,4},{6,7},{7,6},{8,9},{9,8},{10,11... | collective-permute-start | bytes 786440 | tf_op jit(solution)/shard_map/ppermute | solution.py:444
  8.9 8.6 %collective-permute-start.3 = (bf16[512,128]{1,0:T(8,128)(2,1)S(1)}, bf16[512,128]{1,0:T(8,128)(2,1)S(1)}, u32[]{:S(2)}, u32[]{:S(2)}) collective-permute-start(bf16[512,128]{1,0:T(8,128)(2,1)S(1)} %get-tuple-element.50), channel_id=1, source_target_pairs={{0,8},{1,9},{2,10},{3,11},{4,12},{5,13},{6,14},{7,15},{8,0},{9,1},... | collective-permute-start | bytes 393224 | tf_op jit(solution)/shard_map/ppermute | solution.py:444
  12.4 5.7 %collective-permute-start.6 = (bf16[512,128]{1,0:T(8,128)(2,1)S(1)}, bf16[512,128]{1,0:T(8,128)(2,1)S(1)}, u32[]{:S(2)}, u32[]{:S(2)}) collective-permute-start(bf16[512,128]{1,0:T(8,128)(2,1)S(1)} %collective-permute-done.4.refs_1_), channel_id=1, source_target_pairs={{0,2},{1,3},{2,0},{3,1},{4,6},{5,7},{6,4},{7,5},{8,10},{9,11},{10,... | collective-permute-start | bytes 393224 | tf_op jit(solution)/shard_map/ppermute | solution.py:444
  13.7 0.9 %copy-start.1 = (bf16[8,128,128]{2,1,0:T(8,128)(2,1)S(1)}, bf16[8,128,128]{2,1,0:T(8,128)(2,1)}, u32[]{:S(2)}) copy-start(bf16[8,128,128]{2,1,0:T(8,128)(2,1)} %param.10) | copy-start | bytes 786436
  14.7 1.9 %copy-start.3 = (bf16[8,128,128]{2,1,0:T(8,128)(2,1)S(1)}, bf16[8,128,128]{2,1,0:T(8,128)(2,1)}, u32[]{:S(2)}) copy-start(bf16[8,128,128]{2,1,0:T(8,128)(2,1)} %cot_ref.3) | copy-start | bytes 786436
  14.7 1.9 %copy-start.4 = (s32[8,128]{1,0:T(8,128)S(1)}, s32[8,128]{1,0:T(8,128)}, u32[]{:S(2)}) copy-start(s32[8,128]{1,0:T(8,128)} %mask_ref.3) | copy-start | bytes 12292
  16.8 6.4 %collective-permute-start.8 = (bf16[544,128]{1,0:T(8,128)(2,1)S(1)}, bf16[544,128]{1,0:T(8,128)(2,1)S(1)}, u32[]{:S(2)}, u32[]{:S(2)}) collective-permute-start(bf16[544,128]{1,0:T(8,128)(2,1)S(1)} %get-tuple-element.62), channel_id=1, source_target_pairs={{0,4},{1,5},{2,6},{3,7},{4,0},{5,1},{6,2},{7,3},{8,12},{9,13},{10,... | collective-permute-start | bytes 417800 | tf_op jit(solution)/shard_map/ppermute | solution.py:444
  18.1 7.4 %collective-permute-start.7 = (bf16[512,128]{1,0:T(8,128)(2,1)S(1)}, bf16[512,128]{1,0:T(8,128)(2,1)S(1)}, u32[]{:S(2)}, u32[]{:S(2)}) collective-permute-start(bf16[512,128]{1,0:T(8,128)(2,1)S(1)} %shard_map.119), channel_id=1, source_target_pairs={{0,2},{1,3},{2,0},{3,1},{4,6},{5,7},{6,4},{7,5},{8,10},{9,11},{10,... | collective-permute-start | bytes 393224 | tf_op jit(solution)/shard_map/ppermute | solution.py:444
  19.2 4.5 %collective-permute-start.5 = (bf16[1024,128]{1,0:T(8,128)(2,1)S(1)}, bf16[1024,128]{1,0:T(8,128)(2,1)S(1)}, u32[]{:S(2)}, u32[]{:S(2)}) collective-permute-start(bf16[1024,128]{1,0:T(8,128)(2,1)S(1)} %collective-permute-done.2.left_in), channel_id=1, source_target_pairs={{0,1},{1,0},{2,3},{3,2},{4,5},{5,4},{6,7},{7,6},{8,9},{9,8},{10,11... | collective-permute-start | bytes 786440 | tf_op jit(solution)/shard_map/ppermute | solution.py:444
  23.2 2.9 %collective-permute-start.9 = (bf16[544,128]{1,0:T(8,128)(2,1)S(1)}, bf16[544,128]{1,0:T(8,128)(2,1)S(1)}, u32[]{:S(2)}, u32[]{:S(2)}) collective-permute-start(bf16[544,128]{1,0:T(8,128)(2,1)S(1)} %shard_map.123), channel_id=1, source_target_pairs={{0,1},{1,0},{2,3},{3,2},{4,5},{5,4},{6,7},{7,6},{8,9},{9,8},{10,11... | collective-permute-start | bytes 417800 | tf_op jit(solution)/shard_map/ppermute | solution.py:444
  29.1 15.1 %copy-start.2 = (bf16[8,128,128]{2,1,0:T(8,128)(2,1)S(1)}, bf16[8,128,128]{2,1,0:T(8,128)(2,1)}, u32[]{:S(2)}) copy-start(bf16[8,128,128]{2,1,0:T(8,128)(2,1)} %param.10) | copy-start | bytes 786436
  29.2 9.9 %collective-permute-start.10 = (bf16[2560,128]{1,0:T(8,128)(2,1)S(1)}, bf16[2560,128]{1,0:T(8,128)(2,1)S(1)}, u32[]{:S(2)}, u32[]{:S(2)}) collective-permute-start(bf16[2560,128]{1,0:T(8,128)(2,1)S(1)} %get-tuple-element.70), channel_id=1, source_target_pairs={{0,1},{1,0},{2,3},{3,2},{4,5},{5,4},{6,7},{7,6},{8,9},{9,8},{10,11... | collective-permute-start | bytes 1966088 | tf_op jit(solution)/shard_map/ppermute | solution.py:444
  29.2 5.9 %collective-permute-start.12 = (bf16[512,128]{1,0:T(8,128)(2,1)S(1)}, bf16[512,128]{1,0:T(8,128)(2,1)S(1)}, u32[]{:S(2)}, u32[]{:S(2)}) collective-permute-start(bf16[512,128]{1,0:T(8,128)(2,1)S(1)} %get-tuple-element.69.refs_6_), channel_id=1, source_target_pairs={{0,2},{1,3},{2,0},{3,1},{4,6},{5,7},{6,4},{7,5},{8,10},{9,11},{10,... | collective-permute-start | bytes 393224 | tf_op jit(solution)/shard_map/ppermute | solution.py:444
  35.2 6.1 %collective-permute-start.13 = (bf16[512,128]{1,0:T(8,128)(2,1)S(1)}, bf16[512,128]{1,0:T(8,128)(2,1)S(1)}, u32[]{:S(2)}, u32[]{:S(2)}) collective-permute-start(bf16[512,128]{1,0:T(8,128)(2,1)S(1)} %shard_map.131), channel_id=1, source_target_pairs={{0,2},{1,3},{2,0},{3,1},{4,6},{5,7},{6,4},{7,5},{8,10},{9,11},{10,... | collective-permute-start | bytes 393224 | tf_op jit(solution)/shard_map/ppermute | solution.py:444
  36.2 14.5 %collective-permute-start.17 = (bf16[512,128]{1,0:T(8,128)(2,1)S(1)}, bf16[512,128]{1,0:T(8,128)(2,1)S(1)}, u32[]{:S(2)}, u32[]{:S(2)}) collective-permute-start(bf16[512,128]{1,0:T(8,128)(2,1)S(1)} %shard_map.134), channel_id=1, source_target_pairs={{0,8},{1,9},{2,10},{3,11},{4,12},{5,13},{6,14},{7,15},{8,0},{9,1},... | collective-permute-start | bytes 393224 | tf_op jit(solution)/shard_map/ppermute | solution.py:444
  39.2 10.7 %collective-permute-start.11 = (bf16[512,128]{1,0:T(8,128)(2,1)S(1)}, bf16[512,128]{1,0:T(8,128)(2,1)S(1)}, u32[]{:S(2)}, u32[]{:S(2)}) collective-permute-start(bf16[512,128]{1,0:T(8,128)(2,1)S(1)} %get-tuple-element.73), channel_id=1, source_target_pairs={{0,4},{1,5},{2,6},{3,7},{4,0},{5,1},{6,2},{7,3},{8,12},{9,13},{10,... | collective-permute-start | bytes 393224 | tf_op jit(solution)/shard_map/ppermute | solution.py:444
  39.9 14.4 %collective-permute-start.16 = (bf16[1024,128]{1,0:T(8,128)(2,1)S(1)}, bf16[1024,128]{1,0:T(8,128)(2,1)S(1)}, u32[]{:S(2)}, u32[]{:S(2)}) collective-permute-start(bf16[1024,128]{1,0:T(8,128)(2,1)S(1)} %get-tuple-element.81.refs_0_), channel_id=1, source_target_pairs={{0,4},{1,5},{2,6},{3,7},{4,0},{5,1},{6,2},{7,3},{8,12},{9,13},{10,... | collective-permute-start | bytes 786440 | tf_op jit(solution)/shard_map/ppermute | solution.py:444
  41.3 14.1 %collective-permute-start.15 = (bf16[512,128]{1,0:T(8,128)(2,1)S(1)}, bf16[512,128]{1,0:T(8,128)(2,1)S(1)}, u32[]{:S(2)}, u32[]{:S(2)}) collective-permute-start(bf16[512,128]{1,0:T(8,128)(2,1)S(1)} %shard_map.132.after_ref), channel_id=1, source_target_pairs={{0,8},{1,9},{2,10},{3,11},{4,12},{5,13},{6,14},{7,15},{8,0},{9,1},... | collective-permute-start | bytes 393224 | tf_op jit(solution)/shard_map/ppermute | solution.py:444
  43.3 7.5 %collective-permute-start.14 = (bf16[1024,128]{1,0:T(8,128)(2,1)S(1)}, bf16[1024,128]{1,0:T(8,128)(2,1)S(1)}, u32[]{:S(2)}, u32[]{:S(2)}) collective-permute-start(bf16[1024,128]{1,0:T(8,128)(2,1)S(1)} %shard_map.133), channel_id=1, source_target_pairs={{0,2},{1,3},{2,0},{3,1},{4,6},{5,7},{6,4},{7,5},{8,10},{9,11},{10,... | collective-permute-start | bytes 786440 | tf_op jit(solution)/shard_map/ppermute | solution.py:444

commit v7 on v6

--- a/solution.py
+++ b/solution.py
@@ -84,13 +84,21 @@
         ref[place + PIECE : place + HEAD, :] = mask.astype(BF16)
 
 
-def rows_of(refs, row):
-    part, start = divmod(row * 128, SIDE // len(refs))
-    return refs[part][start : start + 128, :].astype(F32)
-
-
-def scale_in(values, params_ref):
-    return norm(values, 1)[0] * params_ref[0:1, :] + params_ref[1:2, :]
+def split_sum(values, ones):
+    high = values.astype(BF16)
+    low = (values - high.astype(F32)).astype(BF16)
+    return dot(high, ones, NN) + dot(low, ones, NN)
+
+
+def scale_in(x, params_ref):
+    ones = jnp.ones((128, 128), BF16)
+    center = x.astype(F32) - dot(x, ones, NN) * (1.0 / 128.0)
+    inverse = lax.rsqrt(split_sum(center * center, ones) * (1.0 / 128.0) + EPSILON)
+    return center * inverse * params_ref[0:1, :] + params_ref[1:2, :]
+
+
+def block_of(values, row):
+    return values[row * 128 : (row + 1) * 128]
 
 
 def make_side(projected):
@@ -117,10 +125,11 @@
     scaled_ref,
 ):
     weight_t_ref[...] = weight_ref[:, :512].astype(F32).T.astype(BF16)
-    for row in range(ROWS):
-        scaled = scale_in(rows_of([x_ref], row), params_ref)
-        scaled_ref[row] = scaled
-        projected = dot(weight_t_ref[...], scaled.astype(BF16), NT)
+    scaled = scale_in(x_ref[...], params_ref)
+    scaled_ref[...] = scaled.reshape(scaled_ref.shape)
+    scaled = scaled.astype(BF16)
+    for row in range(ROWS):
+        projected = dot(weight_t_ref[...], block_of(scaled, row), NT)
         store_side(rows_ref.at[0], row, make_side(projected[:256]))
         store_side(rows_ref.at[1], row, make_side(projected[256:]))
     left_ref[...] = rows_ref[0].astype(BF16)
@@ -146,13 +155,16 @@
 def peer_kernel(me_ref, left_in, *refs):
     right_in, rest = refs[:-8], refs[-8:]
     weight_t_ref, weight_ref, params_ref, left_ref, right_ref, sig_ref, rows_ref, scaled_ref = rest
-    for row in range(ROWS):
-        scaled = scale_in(rows_of([left_in], row), params_ref)
-        scaled_ref[row] = scaled
-        projected = dot(weight_t_ref[:256, :], scaled.astype(BF16), NT)
+    scaled = scale_in(left_in[...], params_ref)
+    scaled_ref[...] = scaled.reshape(scaled_ref.shape)
+    scaled = scaled.astype(BF16)
+    for row in range(ROWS):
+        projected = dot(weight_t_ref[:256, :], block_of(scaled, row), NT)
         store_side(rows_ref.at[0], row, make_side(projected))
-        scaled = scale_in(rows_of(right_in, row), params_ref)
-        projected = dot(weight_t_ref[256:, :], scaled.astype(BF16), NT)
+    scaled = [scale_in(r[...], params_ref).astype(BF16) for r in right_in]
+    for row in range(ROWS):
+        part, place = divmod(row, ROWS // len(right_in))
+        projected = dot(weight_t_ref[256:, :], block_of(scaled[part], place), NT)
         store_side(rows_ref.at[1], row, make_side(projected))
     left_ref[...] = rows_ref[0].astype(BF16)
     right_ref[...] = rows_ref[1].astype(BF16)
@@ -162,10 +174,12 @@
 def left_kernel(
     me_ref, x_ref, weight_t_ref, weight_ref, params_ref, left_ref, sig_ref, rows_ref, scaled_ref
 ):
-    for row in range(ROWS):
-        scaled = scale_in(rows_of([x_ref], row), params_ref)
-        scaled_ref[row] = scaled
-        store_side(rows_ref, row, make_side(dot(weight_t_ref[:256, :], scaled.astype(BF16), NT)))
+    scaled = scale_in(x_ref[...], params_ref)
+    scaled_ref[...] = scaled.reshape(scaled_ref.shape)
+    scaled = scaled.astype(BF16)
+    for row in range(ROWS):
+        projected = dot(weight_t_ref[:256, :], block_of(scaled, row), NT)
+        store_side(rows_ref, row, make_side(projected))
     left_ref[...] = rows_ref[...].astype(BF16)
     sig_ref[...] = block_gate(me_ref, scaled_ref, weight_ref)
 
@@ -176,19 +190,13 @@
             rows_ref[...] = rest_ref[...]
         else:
             rows_ref[...] = jnp.zeros_like(rows_ref)
+        scaled = scale_in(x_ref[...], params_ref).astype(BF16)
         for row in range(ROWS // 2):
-            scaled = scale_in(x_ref[row * 128 : (row + 1) * 128, :].astype(F32), params_ref)
-            projected = dot(weight_t_ref[256:, :], scaled.astype(BF16), NT)
+            projected = dot(weight_t_ref[256:, :], block_of(scaled, row), NT)
             store_side(rows_ref, first + row, make_side(projected))
         right_ref[...] = rows_ref[...].astype(right_ref.dtype)
 
     return kernel
-
-
-def split_sum(values, ones):
-    high = values.astype(BF16)
-    low = (values - high.astype(F32)).astype(BF16)
-    return dot(high, ones, NN) + dot(low, ones, NN)
 
 
 GROUPS = SIDE // 32
@@ -296,16 +304,15 @@
 
 
 def grad_left_kernel(pairs_ref, *refs):
-    right_refs, (out_near, out_both), (left_0, core_ref, left_2) = refs[:4], refs[4:6], refs[7:]
-    lefts = [(left_0, 0), (core_ref, 0), (left_2, 0), (core_ref, SIDE + PIECE)]
+    right_refs, (out_near, out_both), lefts = refs[:4], refs[4:6], refs[7:]
     of_quarter = quarters()
     for g in range(GROUPS):
         spread = spread_group(pairs_ref, g, of_quarter)
         grad = dot(spread, slab(right_refs, g), NN).astype(BF16)
-        for m, (ref, at) in enumerate(lefts):
-            ref[at + g * 32 : at + (g + 1) * 32, :] = grad[m * 32 : (m + 1) * 32]
-    core_ref[SIDE : SIDE + PIECE, :] = out_near[...]
-    core_ref[2 * SIDE + PIECE :, :] = out_both[...]
+        for m, ref in enumerate(lefts):
+            ref[g * 32 : (g + 1) * 32, :] = grad[m * 32 : (m + 1) * 32]
+    lefts[1][SIDE:, :] = out_near[...]
+    lefts[3][SIDE:, :] = out_both[...]
 
 
 def halves_kernel(x_ref, first_ref, second_ref):
@@ -333,10 +340,9 @@
 
 
 def add_left_kernel(mine_ref, piece_ref, got_ref, sum_ref, out_ref):
-    at = SIDE + PIECE
-    sum_ref[...] = (mine_ref[...].astype(F32) + got_ref[at : at + SIDE, :].astype(F32)).astype(BF16)
+    sum_ref[...] = (mine_ref[...].astype(F32) + got_ref[:SIDE, :].astype(F32)).astype(BF16)
     out_ref[:PIECE, :] = piece_ref[...]
-    out_ref[PIECE:, :] = got_ref[at + SIDE :, :]
+    out_ref[PIECE:, :] = got_ref[SIDE:, :]
 
 
 def factor_kernel(
@@ -356,8 +362,8 @@
     bias_t = jnp.broadcast_to(params_ref[1:2, :], (128, 128)).T
     gain_t_ref[...] = gain_t
     for row in range(ROWS):
-        x = rows_of([x_ref], row)
-        normed, inverse = norm(x.T, 0)
+        x = x_ref[row * 128 : (row + 1) * 128, :]
+        normed, inverse = norm(x.astype(F32).T, 0)
         normed_ref[row] = normed
         inverse_ref[row : row + 1, :] = inverse
         scaled = (normed * gain_t + bias_t).astype(BF16)
@@ -460,7 +466,7 @@
     half = SIDE // 2
     cube = (ROWS, 128, 128)
     side, piece = ((SIDE, 128), BF16), ((PIECE, 128), BF16)
-    halves, core = ((half, 128), BF16), ((2 * (SIDE + PIECE), 128), BF16)
+    halves, core = ((half, 128), BF16), ((SIDE + PIECE, 128), BF16)
     sig = ((PIECE, 128), F32)
     rows_scratch = pltpu.VMEM((2, SIDE, 128), F32)
     cube_scratch = pltpu.VMEM(cube, F32)
@@ -545,27 +551,28 @@
     )
     right_a = call(grad_right_kernel(0), [halves] * 4, vmem=[pairs, *lefts])
     x_got = [swap(right_a[3], CHIP_X)]
-    grad_left_0, core_back, grad_left_2 = call(
+    grad_left_0, near_back, grad_left_2, both_back = call(
         grad_left_kernel,
-        [side, core, side],
+        [side, core, side, core],
         vmem=[pairs, *rights, out_1, out_3, right_a[3]],
     )
-    core_got = swap(core_back, CORE)
+    both_got = swap(both_back, CORE)
     right_b = call(grad_right_kernel(1), [halves] * 4, vmem=[pairs, *lefts])
-    x_got.append(swap(after(right_b[3], x_got[0]), CHIP_X))
     left_sum, out_far = call(
         add_left_kernel,
         [side, ((2 * PIECE, 128), BF16)],
-        vmem=[grad_left_2, out_2, core_got],
-    )
+        vmem=[grad_left_2, out_2, both_got],
+    )
+    x_got.append(swap(after(right_b[3], left_sum), CHIP_X))
     left_got = swap(left_sum, Z_LOW)
     out_far = swap(out_far, Z_LOW)
-    (total,) = call(add_kernel, [halves], vmem=[right_a[2], x_got[0]])
+    (total,) = call(add_kernel, [halves], vmem=[right_a[2], x_got[0], left_sum])
     z_got = [swap(total, Z_HIGH)]
     (total,) = call(add_kernel, [halves], vmem=[right_b[2], x_got[1], left_sum])
     z_got.append(swap(total, Z_HIGH))
-    (near_back,) = call(near_kernel, [side], vmem=[right_a[1], right_b[1], total])
-    right_near = swap(near_back, CHIP_X)
+    (right_back,) = call(near_kernel, [side], vmem=[right_a[1], right_b[1], total])
+    right_near = swap(right_back, CHIP_X)
+    near_got = swap(after(near_back, total), CORE)
 
     factors, normed, inverse, open_part, gain_t = call(
         factor_kernel,
@@ -577,14 +584,14 @@
         out_kernel,
         [(cube, BF16), (cube, F32)],
         smem=[me],
-        vmem=[out_0, core_got, out_far, open_part, weights],
+        vmem=[out_0, near_got, out_far, open_part, weights],
         scratch=[cube_scratch],
     )
     half_scratch = pltpu.VMEM((half, 128), F32)
     (partial,) = call(
         partial_kernel,
         [(cube, F32)],
-        vmem=[grad_left_0, core_got, left_got, right_a[0], right_near, z_got[0]]
+        vmem=[grad_left_0, near_got, left_got, right_a[0], right_near, z_got[0]]
         + [factors, gate_part, weights],
         scratch=[pltpu.VMEM((SIDE, 128), F32), half_scratch],
         weight=WAIT // 4,

time: 57 us -> 52.2 us (0.916)
  waiting for transfers between devices: 13.3 us -> 5.52 us
  Pallas kernels: 16.1 us -> 18.5 us
    ppermute x18 -> x19, waiting for transfers between devices: 13.3 us -> 5.52 us  [swap(): return lax.ppermute(values, 'row', [(s, s ^ offset) for s in range(16)])]
    pallas_call x24 -> x25, Pallas kernels: 16.1 us -> 18.5 us  [call(): pl.pallas_call(kernel, out_shape=[jax.ShapeDtypeStruct(s, d) for s, d in...]
    ppermute x18 -> x19, starting transfers between devices: 21.3 us -> 21.8 us  [swap(): return lax.ppermute(values, 'row', [(s, s ^ offset) for s in range(16)])]
  transfers between devices with their start and end apart: 18 -> 19, of which waited for: 4 -> 6; matrix products, arithmetic and copies ran while one was open for 6% -> 6% of each run, Pallas kernels for 21% -> 27%
where the time goes in v7:
time: 52.2 us; the launch traced here: 51.8 us
  starting transfers between devices  21.8 us (42%)
  Pallas kernels  18.5 us (35%)
  waiting for transfers between devices  5.52 us (11%)
  local copies, waits for them, and re-layouts  4.36 us (8%)
  between operations  0.9 us (2%)
  other arithmetic  0.71 us (1%)
    ppermute x19, starting transfers between devices, swap(): return lax.ppermute(values, 'row', [(s, s ^ offset) for s in range(16)])  21.8 us
    pallas_call x25, Pallas kernels, call(): pl.pallas_call(kernel, out_shape=[jax.ShapeDtypeStruct(s, d) for s, d in...  18.5 us
    ppermute x19, waiting for transfers between devices, swap(): return lax.ppermute(values, 'row', [(s, s ^ offset) for s in range(16)])  5.52 us
    unnamed x12, local copies, waits for them, and re-layouts  3.59 us
  transfers between devices with their start and end apart: 19, of which 6 were waited for; matrix products, arithmetic and copies ran while one was open for 6% of the time, Pallas kernels for 27%

profile of v7, /device:TPU:0, one launch (start us, length us, event | category | flops | bytes accessed | tf_op | source)
XLA Modules:
  0.0 51.8 jit_solution(9398421632981407344)
XLA Ops:
  0.6 0.0 copy-start
  0.6 0.9 %copy-done = bf16[8,128,128]{2,1,0:T(8,128)(2,1)S(1)} copy-done((bf16[8,128,128]{2,1,0:T(8,128)(2,1)S(1)}, bf16[8,128,128]{2,1,0:T(8,128)(2,1)}, u32[]{:S(2)}) %copy-start) | copy-done | bytes 262168
  1.6 4.1 %collective-permute-start.4 = (bf16[512,128]{1,0:T(8,128)(2,1)S(1)}, bf16[512,128]{1,0:T(8,128)(2,1)S(1)}, u32[]{:S(2)}, u32[]{:S(2)}) collective-permute-start(bf16[512,128]{1,0:T(8,128)(2,1)S(1)} %get-tuple-element.48.refs_0_), channel_id=1, source_target_pairs={{0,8},{1,9},{2,10},{3,11},{4,12},{5,13},{6,14},{7,15},{8,0},{9,1},... | collective-permute-start | bytes 393224 | tf_op jit(solution)/shard_map/ppermute | solution.py:450
  5.7 1.6 %collective-permute-start.2 = (bf16[1024,128]{1,0:T(8,128)(2,1)S(1)}, bf16[1024,128]{1,0:T(8,128)(2,1)S(1)}, u32[]{:S(2)}, u32[]{:S(2)}) collective-permute-start(bf16[1024,128]{1,0:T(8,128)(2,1)S(1)} %shard_map.115), channel_id=1, source_target_pairs={{0,4},{1,5},{2,6},{3,7},{4,0},{5,1},{6,2},{7,3},{8,12},{9,13},{10,... | collective-permute-start | bytes 786440 | tf_op jit(solution)/shard_map/ppermute | solution.py:450
  7.4 1.5 %collective-permute-start.1 = (bf16[1024,128]{1,0:T(8,128)(2,1)S(1)}, bf16[1024,128]{1,0:T(8,128)(2,1)S(1)}, u32[]{:S(2)}, u32[]{:S(2)}) collective-permute-start(bf16[1024,128]{1,0:T(8,128)(2,1)S(1)} %shard_map.115), channel_id=1, source_target_pairs={{0,2},{1,3},{2,0},{3,1},{4,6},{5,7},{6,4},{7,5},{8,10},{9,11},{10,... | collective-permute-start | bytes 786440 | tf_op jit(solution)/shard_map/ppermute | solution.py:450
  8.9 0.0 collective-permute-start
  8.9 0.3 collective-permute-start.3
  9.2 0.9 %constant_dynamic-update-slice_fusion.2 = bf16[128,768]{1,0:T(8,128)(2,1)S(1)} fusion(bf16[128,512]{1,0:T(8,128)(2,1)} %param.15), kind=kLoop, calls=%fused_computation.2 | loop fusion | bytes 262144
  10.1 0.8 %constant_dynamic-update-slice_fusion.1 = bf16[128,768]{1,0:T(8,128)(2,1)S(1)} fusion(bf16[128,768]{1,0:T(8,128)(2,1)S(1)} %constant_dynamic-update-slice_fusion.2, bf16[128,128]{1,0:T(8,128)(2,1)} %param.16), kind=kLoop, calls=%fused_computation.1 | loop fusion | bytes 65536
  10.9 0.7 %pad_maximum_fusion.params_ref.refs_3_.refs_4_ = f32[4,128]{1,0:T(4,128)S(1)} fusion(f32[1,128]{1,0:T(1,128)} %bitcast.10, f32[1,128]{1,0:T(1,128)} %bitcast.11, f32[1,128]{1,0:T(1,128)} %bitcast.12, f32[1,128]{1,0:T(1,128)} %bitcast.13), kind=kLoop, calls=%fused_computation.3 | loop fusion | flops 1536 | bytes 4096 | tf_op jit(solution)/shard_map/stack | solution.py:479
  11.6 0.8 %constant_dynamic-update-slice_fusion.weight_ref.refs_2_.refs_3_.refs_8_ = bf16[128,768]{1,0:T(8,128)(2,1)S(1)} fusion(bf16[128,768]{1,0:T(8,128)(2,1)S(1)} %constant_dynamic-update-slice_fusion.1, bf16[128,128]{1,0:T(8,128)(2,1)} %param.19), kind=kLoop, calls=%fused_computation | loop fusion | bytes 65536 | tf_op jit(solution)/shard_map/concatenate | solution.py:478
  12.4 0.0 collective-permute-done.4.refs_1_
  12.4 1.4 %collective-permute-start.6 = (bf16[512,128]{1,0:T(8,128)(2,1)S(1)}, bf16[512,128]{1,0:T(8,128)(2,1)S(1)}, u32[]{:S(2)}, u32[]{:S(2)}) collective-permute-start(bf16[512,128]{1,0:T(8,128)(2,1)S(1)} %collective-permute-done.4.refs_1_), channel_id=1, source_target_pairs={{0,2},{1,3},{2,0},{3,1},{4,6},{5,7},{6,4},{7,5},{8,10},{9,11},{10,... | collective-permute-start | bytes 393224 | tf_op jit(solution)/shard_map/ppermute | solution.py:450
  13.7 0.9 %copy-done.1 = bf16[8,128,128]{2,1,0:T(8,128)(2,1)S(1)} copy-done((bf16[8,128,128]{2,1,0:T(8,128)(2,1)S(1)}, bf16[8,128,128]{2,1,0:T(8,128)(2,1)}, u32[]{:S(2)}) %copy-start.1) | copy-done | bytes 262168
  14.7 2.0 %shard_map.113 = (bf16[1024,128]{1,0:T(8,128)(2,1)S(1)}, bf16[1024,128]{1,0:T(8,128)(2,1)S(1)}, f32[256,128]{1,0:T(8,128)S(1)}, bf16[512,128]{1,0:T(8,128)(2,1)S...) custom-call(s32[1]{0:T(128)} %bitcast.me_ref.refs_0_, bf16[1024,128]{1,0:T(8,128)(2,1)S(1)} %bitcast.8, ...), custom_call_target="tpu_custom_call" | custom-call | flops 5000000000 | bytes 262144 | tf_op jit(solution)/shard_map/pallas_call | solution.py:43
  16.7 0.0 collective-permute-done.1.refs_0_.after_ref
  16.7 0.0 copy-done.3
  16.7 0.0 copy-done.4
  16.7 0.1 shard_map.122
  16.8 0.7 %collective-permute-start.8 = (bf16[544,128]{1,0:T(8,128)(2,1)S(1)}, bf16[544,128]{1,0:T(8,128)(2,1)S(1)}, u32[]{:S(2)}, u32[]{:S(2)}) collective-permute-start(bf16[544,128]{1,0:T(8,128)(2,1)S(1)} %get-tuple-element.63), channel_id=1, source_target_pairs={{0,4},{1,5},{2,6},{3,7},{4,0},{5,1},{6,2},{7,3},{8,12},{9,13},{10,... | collective-permute-start | bytes 417800 | tf_op jit(solution)/shard_map/ppermute | solution.py:450
  17.5 0.0 collective-permute-done.3.refs_0_.message_ref
  17.5 0.5 %collective-permute-done.6.refs_0_.x_ref = bf16[512,128]{1,0:T(8,128)(2,1)S(1)} collective-permute-done((bf16[512,128]{1,0:T(8,128)(2,1)S(1)}, bf16[512,128]{1,0:T(8,128)(2,1)S(1)}, u32[]{:S(2)}, u32[]{:S(2)}) %collective-permute-start.6) | collective-permute-done | bytes 131104 | tf_op jit(solution)/shard_map/ppermute | solution.py:450
  18.1 1.1 %collective-permute-start.7 = (bf16[512,128]{1,0:T(8,128)(2,1)S(1)}, bf16[512,128]{1,0:T(8,128)(2,1)S(1)}, u32[]{:S(2)}, u32[]{:S(2)}) collective-permute-start(bf16[512,128]{1,0:T(8,128)(2,1)S(1)} %shard_map.119), channel_id=1, source_target_pairs={{0,2},{1,3},{2,0},{3,1},{4,6},{5,7},{6,4},{7,5},{8,10},{9,11},{10,... | collective-permute-start | bytes 393224 | tf_op jit(solution)/shard_map/ppermute | solution.py:450
  19.2 0.0 collective-permute-done.2.left_in
  19.2 0.0 collective-permute-start.5
  19.2 2.1 %shard_map.117 = (bf16[1024,128]{1,0:T(8,128)(2,1)S(1)}, bf16[1024,128]{1,0:T(8,128)(2,1)S(1)}, f32[256,128]{1,0:T(8,128)S(1)}) custom-call(s32[1]{0:T(128)} %bitcast.me_ref.refs_0_, bf16[1024,128]{1,0:T(8,128)(2,1)S(1)} %collective-permute-done.2.left_in, bf16[512,128]{1,0:T(8,128)(2,1)S(1)} %collective-permute-done.3.refs_0_.message_ref, ...), custom_call_target="tpu_custom_call" | custom-call | flops 5000000000 | bytes 262144 | tf_op jit(solution)/shard_map/pallas_call | solution.py:43
  21.4 0.0 collective-permute-done.left_in
  21.4 2.2 %shard_map.116 = (bf16[1024,128]{1,0:T(8,128)(2,1)S(1)}, bf16[1024,128]{1,0:T(8,128)(2,1)S(1)}, f32[256,128]{1,0:T(8,128)S(1)}) custom-call(s32[1]{0:T(128)} %bitcast.me_ref.refs_0_, bf16[1024,128]{1,0:T(8,128)(2,1)S(1)} %collective-permute-done.left_in, bf16[1024,128]{1,0:T(8,128)(2,1)S(1)} %collective-permute-done.1.refs_0_.after_ref, ...), custom_call_target="tpu_custom_call" | custom-call | flops 5000000000 | bytes 262144 | tf_op jit(solution)/shard_map/pallas_call | solution.py:43
  23.6 0.0 collective-permute-done.8.got_ref.refs_15_
  23.7 0.6 %collective-permute-start.9 = (bf16[544,128]{1,0:T(8,128)(2,1)S(1)}, bf16[544,128]{1,0:T(8,128)(2,1)S(1)}, u32[]{:S(2)}, u32[]{:S(2)}) collective-permute-start(bf16[544,128]{1,0:T(8,128)(2,1)S(1)} %shard_map.123), channel_id=1, source_target_pairs={{0,1},{1,0},{2,3},{3,2},{4,5},{5,4},{6,7},{7,6},{8,9},{9,8},{10,11... | collective-permute-start | bytes 417800 | tf_op jit(solution)/shard_map/ppermute | solution.py:450
  24.2 0.0 collective-permute-done.5.x_ref
  24.2 1.2 %shard_map.118 = (bf16[1024,128]{1,0:T(8,128)(2,1)S(1)}, f32[256,128]{1,0:T(8,128)S(1)}) custom-call(s32[1]{0:T(128)} %bitcast.me_ref.refs_0_, bf16[1024,128]{1,0:T(8,128)(2,1)S(1)} %collective-permute-done.5.x_ref, bf16[512,128]{1,0:T(8,128)(2,1)S(1)} %get-tuple-element.49.refs_1_.refs_2_.weight_t_ref, ...), custom_call_target="tpu_custom_call" | custom-call | flops 5000000000 | bytes 262144 | tf_op jit(solution)/shard_map/pallas_call | solution.py:43
  25.4 0.8 %shard_map.120.rest_ref = f32[1024,128]{1,0:T(8,128)S(1)} custom-call(bf16[512,128]{1,0:T(8,128)(2,1)S(1)} %collective-permute-done.6.refs_0_.x_ref, bf16[512,128]{1,0:T(8,128)(2,1)S(1)} %get-tuple-element.49.refs_1_.refs_2_.weight_t_ref, f32[4,128]{1,0:T(4,128)S(1)} %pad_maximum_fusion.params_ref.refs_3_.refs_4_, ...), custom_call_target="tpu_custom_call" | custom-call | flops 1250000000 | bytes 262144 | tf_op jit(solution)/shard_map/pallas_call | solution.py:43
  26.3 0.0 collective-permute-done.7.x_ref
  26.3 0.8 %shard_map.121.refs_8_.refs_3_ = bf16[1024,128]{1,0:T(8,128)(2,1)S(1)} custom-call(bf16[512,128]{1,0:T(8,128)(2,1)S(1)} %collective-permute-done.7.x_ref, bf16[512,128]{1,0:T(8,128)(2,1)S(1)} %get-tuple-element.49.refs_1_.refs_2_.weight_t_ref, f32[4,128]{1,0:T(4,128)S(1)} %pad_maximum_fusion.params_ref.refs_3_.refs_4_, f32[1024,128]{1,0:T(8,128)S(1)} %shard_map.120.rest_ref), custom_call_target="tpu_custom_call" | custom-call | flops 1250000000 | bytes 262144 | tf_op jit(solution)/shard_map/pallas_call | solution.py:43
  27.1 0.0 collective-permute-done.9.refs_14_
  27.1 2.2 %shard_map.124 = (bf16[256,128]{1,0:T(8,128)(2,1)S(1)}, bf16[256,128]{1,0:T(8,128)(2,1)S(1)}, bf16[256,128]{1,0:T(8,128)(2,1)S(1)}, bf16[256,128]{1,0:T(8,128)(2,1)S(1)}, f32[1024,128]{1,0:T(8,128)S(1)}) custom-call(s32[1]{0:T(128)} %bitcast.me_ref.refs_0_, bf16[1024,128]{1,0:T(8,128)(2,1)S(1)} %get-tuple-element.47.refs_1_.refs_0_, ...), custom_call_target="tpu_custom_call" | custom-call | flops 67108864 | bytes 262144 | tf_op jit(solution)/shard_map/pallas_call | solution.py:43
  29.3 0.4 shard_map.125
  29.7 0.4 shard_map.126
  30.1 0.1 collective-permute-start.10
  30.2 1.0 %collective-permute-start.17 = (bf16[512,128]{1,0:T(8,128)(2,1)S(1)}, bf16[512,128]{1,0:T(8,128)(2,1)S(1)}, u32[]{:S(2)}, u32[]{:S(2)}) collective-permute-start(bf16[512,128]{1,0:T(8,128)(2,1)S(1)} %get-tuple-element.70.refs_6_), channel_id=1, source_target_pairs={{0,2},{1,3},{2,0},{3,1},{4,6},{5,7},{6,4},{7,5},{8,10},{9,11},{10,... | collective-permute-start | bytes 393224 | tf_op jit(solution)/shard_map/ppermute | solution.py:450
  31.2 0.3 shard_map.127
  31.5 0.0 copy-start.2
  31.6 0.3 collective-permute-done.10.got_ref
  31.8 0.1 shard_map.128
  31.9 1.0 %collective-permute-start.11 = (bf16[512,128]{1,0:T(8,128)(2,1)S(1)}, bf16[512,128]{1,0:T(8,128)(2,1)S(1)}, u32[]{:S(2)}, u32[]{:S(2)}) collective-permute-start(bf16[512,128]{1,0:T(8,128)(2,1)S(1)} %shard_map.129), channel_id=1, source_target_pairs={{0,2},{1,3},{2,0},{3,1},{4,6},{5,7},{6,4},{7,5},{8,10},{9,11},{10,... | collective-permute-start | bytes 393224 | tf_op jit(solution)/shard_map/ppermute | solution.py:450
  32.9 1.6 %collective-permute-start.13 = (bf16[512,128]{1,0:T(8,128)(2,1)S(1)}, bf16[512,128]{1,0:T(8,128)(2,1)S(1)}, u32[]{:S(2)}, u32[]{:S(2)}) collective-permute-start(bf16[512,128]{1,0:T(8,128)(2,1)S(1)} %get-tuple-element.78), channel_id=1, source_target_pairs={{0,4},{1,5},{2,6},{3,7},{4,0},{5,1},{6,2},{7,3},{8,12},{9,13},{10,... | collective-permute-start | bytes 393224 | tf_op jit(solution)/shard_map/ppermute | solution.py:450
  34.5 0.5 collective-permute-start.16
  34.9 1.6 %collective-permute-done.17.got_ref = bf16[512,128]{1,0:T(8,128)(2,1)S(1)} collective-permute-done((bf16[512,128]{1,0:T(8,128)(2,1)S(1)}, bf16[512,128]{1,0:T(8,128)(2,1)S(1)}, u32[]{:S(2)}, u32[]{:S(2)}) %collective-permute-start.17) | collective-permute-done | bytes 131104 | tf_op jit(solution)/shard_map/ppermute | solution.py:450
  36.6 2.9 %collective-permute-start.18 = (bf16[512,128]{1,0:T(8,128)(2,1)S(1)}, bf16[512,128]{1,0:T(8,128)(2,1)S(1)}, u32[]{:S(2)}, u32[]{:S(2)}) collective-permute-start(bf16[512,128]{1,0:T(8,128)(2,1)S(1)} %shard_map.135), channel_id=1, source_target_pairs={{0,8},{1,9},{2,10},{3,11},{4,12},{5,13},{6,14},{7,15},{8,0},{9,1},... | collective-permute-start | bytes 393224 | tf_op jit(solution)/shard_map/ppermute | solution.py:450
  39.5 0.0 collective-permute-done.11.got_ref
  39.5 2.3 %collective-permute-start.15 = (bf16[512,128]{1,0:T(8,128)(2,1)S(1)}, bf16[512,128]{1,0:T(8,128)(2,1)S(1)}, u32[]{:S(2)}, u32[]{:S(2)}) collective-permute-start(bf16[512,128]{1,0:T(8,128)(2,1)S(1)} %shard_map.130.refs_0_.after_ref), channel_id=1, source_target_pairs={{0,8},{1,9},{2,10},{3,11},{4,12},{5,13},{6,14},{7,15},{8,0},{9,1},... | collective-permute-start | bytes 393224 | tf_op jit(solution)/shard_map/ppermute | solution.py:450
  41.8 1.1 %collective-permute-start.14 = (bf16[1024,128]{1,0:T(8,128)(2,1)S(1)}, bf16[1024,128]{1,0:T(8,128)(2,1)S(1)}, u32[]{:S(2)}, u32[]{:S(2)}) collective-permute-start(bf16[1024,128]{1,0:T(8,128)(2,1)S(1)} %shard_map.134), channel_id=1, source_target_pairs={{0,2},{1,3},{2,0},{3,1},{4,6},{5,7},{6,4},{7,5},{8,10},{9,11},{10,... | collective-permute-start | bytes 786440 | tf_op jit(solution)/shard_map/ppermute | solution.py:450
  43.0 0.0 collective-permute-done.13.far_ref
  43.0 0.1 collective-permute-start.12
  43.1 2.5 %shard_map.132 = (f32[8,512,128]{2,1,0:T(8,128)S(1)}, f32[8,128,128]{2,1,0:T(8,128)S(1)}, f32[8,128]{1,0:T(8,128)S(1)}, f32[8,128,128]{2,1,0:T(8,128)S(1)}, f32[128,128]{1,0:T(8,128)S(1)}) custom-call(bf16[1024,128]{1,0:T(8,128)(2,1)S(1)} %bitcast.9, bf16[8,128,128]{2,1,0:T(8,128)(2,1)S(1)} %copy-done.3, s32[8,128]{1,0:T(8,128)S(1)} %copy-done.4, ...), custom_call_target="tpu_custom_call" | custom-call | flops 5000000000 | bytes 262144 | tf_op jit(solution)/shard_map/pallas_call | solution.py:43
  45.6 0.0 collective-permute-done.12.near_ref.refs_1_
  45.6 0.9 %shard_map.133 = (bf16[8,128,128]{2,1,0:T(8,128)(2,1)}, f32[8,128,128]{2,1,0:T(8,128)S(1)}) custom-call(s32[1]{0:T(128)} %bitcast.me_ref.refs_0_, bf16[256,128]{1,0:T(8,128)(2,1)S(1)} %get-tuple-element.66.own_ref, bf16[1280,128]{1,0:T(8,128)(2,1)S(1)} %collective-permute-done.12.near_ref.refs_1_, bf16[512,128]{1,0:T(8,128)(2,1)S(1)} %collective-permute-done.13.far_ref, ...), custom_call_target="tpu_custom_call" | custom-call | flops 67108864 | bytes 262144 | tf_op jit(solution)/shard_map/pallas_call | solution.py:43
  46.4 0.4 collective-permute-done.18.refs_5_
  46.8 2.5 %collective-permute-done.16.refs_2_ = bf16[1024,128]{1,0:T(8,128)(2,1)S(1)} collective-permute-done((bf16[1024,128]{1,0:T(8,128)(2,1)S(1)}, bf16[1024,128]{1,0:T(8,128)(2,1)S(1)}, u32[]{:S(2)}, u32[]{:S(2)}) %collective-permute-start.16) | collective-permute-done | bytes 262176 | tf_op jit(solution)/shard_map/ppermute | solution.py:450
  49.4 0.1 collective-permute-done.14.refs_4_.near_ref
  49.5 1.0 %shard_map.136.sum_ref = f32[8,128,128]{2,1,0:T(8,128)S(1)} custom-call(bf16[1024,128]{1,0:T(8,128)(2,1)S(1)} %get-tuple-element.85.refs_0_, bf16[1280,128]{1,0:T(8,128)(2,1)S(1)} %collective-permute-done.12.near_ref.refs_1_, bf16[1024,128]{1,0:T(8,128)(2,1)S(1)} %collective-permute-done.16.refs_2_, bf16[512,128]{1,0:T(8,128)(2,1)S(1)} %get-tuple-element.86.refs_3_, ...), custom_call_target="tpu_custom_call" | custom-call | flops 1250000000 | bytes 262144 | tf_op jit(solution)/shard_map/pallas_call | solution.py:43
  50.5 0.0 collective-permute-done.15.got_ref
  50.5 1.3 %shard_map.137 = bf16[8,128,128]{2,1,0:T(8,128)(2,1)} custom-call(bf16[512,128]{1,0:T(8,128)(2,1)S(1)} %get-tuple-element.81.own_ref, bf16[1024,128]{1,0:T(8,128)(2,1)S(1)} %collective-permute-done.14.refs_4_.near_ref, bf16[512,128]{1,0:T(8,128)(2,1)S(1)} %collective-permute-done.15.got_ref, f32[8,512,128]{2,1,0:T(8,128)S(1)} %get-tuple-element.84.refs_6_.factor_ref, ...), custom_call_target="tpu_custom_call" | custom-call | flops 67108864 | bytes 262144 | tf_op jit(solution)/shard_map/pallas_call | solution.py:43
  (13 shorter events, 0.2 us)
Async XLA Ops:
  0.6 1.0 %copy-start = (bf16[8,128,128]{2,1,0:T(8,128)(2,1)S(1)}, bf16[8,128,128]{2,1,0:T(8,128)(2,1)}, u32[]{:S(2)}) copy-start(bf16[8,128,128]{2,1,0:T(8,128)(2,1)} %param.10) | copy-start | bytes 786436
  1.6 10.8 %collective-permute-start.4 = (bf16[512,128]{1,0:T(8,128)(2,1)S(1)}, bf16[512,128]{1,0:T(8,128)(2,1)S(1)}, u32[]{:S(2)}, u32[]{:S(2)}) collective-permute-start(bf16[512,128]{1,0:T(8,128)(2,1)S(1)} %get-tuple-element.48.refs_0_), channel_id=1, source_target_pairs={{0,8},{1,9},{2,10},{3,11},{4,12},{5,13},{6,14},{7,15},{8,0},{9,1},... | collective-permute-start | bytes 393224 | tf_op jit(solution)/shard_map/ppermute | solution.py:450
  5.7 13.5 %collective-permute-start.2 = (bf16[1024,128]{1,0:T(8,128)(2,1)S(1)}, bf16[1024,128]{1,0:T(8,128)(2,1)S(1)}, u32[]{:S(2)}, u32[]{:S(2)}) collective-permute-start(bf16[1024,128]{1,0:T(8,128)(2,1)S(1)} %shard_map.115), channel_id=1, source_target_pairs={{0,4},{1,5},{2,6},{3,7},{4,0},{5,1},{6,2},{7,3},{8,12},{9,13},{10,... | collective-permute-start | bytes 786440 | tf_op jit(solution)/shard_map/ppermute | solution.py:450
  7.4 9.3 %collective-permute-start.1 = (bf16[1024,128]{1,0:T(8,128)(2,1)S(1)}, bf16[1024,128]{1,0:T(8,128)(2,1)S(1)}, u32[]{:S(2)}, u32[]{:S(2)}) collective-permute-start(bf16[1024,128]{1,0:T(8,128)(2,1)S(1)} %shard_map.115), channel_id=1, source_target_pairs={{0,2},{1,3},{2,0},{3,1},{4,6},{5,7},{6,4},{7,5},{8,10},{9,11},{10,... | collective-permute-start | bytes 786440 | tf_op jit(solution)/shard_map/ppermute | solution.py:450
  8.9 12.5 %collective-permute-start = (bf16[1024,128]{1,0:T(8,128)(2,1)S(1)}, bf16[1024,128]{1,0:T(8,128)(2,1)S(1)}, u32[]{:S(2)}, u32[]{:S(2)}) collective-permute-start(bf16[1024,128]{1,0:T(8,128)(2,1)S(1)} %shard_map.115), channel_id=1, source_target_pairs={{0,1},{1,0},{2,3},{3,2},{4,5},{5,4},{6,7},{7,6},{8,9},{9,8},{10,11... | collective-permute-start | bytes 786440 | tf_op jit(solution)/shard_map/ppermute | solution.py:450
  8.9 8.7 %collective-permute-start.3 = (bf16[512,128]{1,0:T(8,128)(2,1)S(1)}, bf16[512,128]{1,0:T(8,128)(2,1)S(1)}, u32[]{:S(2)}, u32[]{:S(2)}) collective-permute-start(bf16[512,128]{1,0:T(8,128)(2,1)S(1)} %get-tuple-element.51), channel_id=1, source_target_pairs={{0,8},{1,9},{2,10},{3,11},{4,12},{5,13},{6,14},{7,15},{8,0},{9,1},... | collective-permute-start | bytes 393224 | tf_op jit(solution)/shard_map/ppermute | solution.py:450
  12.4 5.7 %collective-permute-start.6 = (bf16[512,128]{1,0:T(8,128)(2,1)S(1)}, bf16[512,128]{1,0:T(8,128)(2,1)S(1)}, u32[]{:S(2)}, u32[]{:S(2)}) collective-permute-start(bf16[512,128]{1,0:T(8,128)(2,1)S(1)} %collective-permute-done.4.refs_1_), channel_id=1, source_target_pairs={{0,2},{1,3},{2,0},{3,1},{4,6},{5,7},{6,4},{7,5},{8,10},{9,11},{10,... | collective-permute-start | bytes 393224 | tf_op jit(solution)/shard_map/ppermute | solution.py:450
  13.7 0.9 %copy-start.1 = (bf16[8,128,128]{2,1,0:T(8,128)(2,1)S(1)}, bf16[8,128,128]{2,1,0:T(8,128)(2,1)}, u32[]{:S(2)}) copy-start(bf16[8,128,128]{2,1,0:T(8,128)(2,1)} %param.10) | copy-start | bytes 786436
  14.7 2.0 %copy-start.3 = (bf16[8,128,128]{2,1,0:T(8,128)(2,1)S(1)}, bf16[8,128,128]{2,1,0:T(8,128)(2,1)}, u32[]{:S(2)}) copy-start(bf16[8,128,128]{2,1,0:T(8,128)(2,1)} %cot_ref.3) | copy-start | bytes 786436
  14.7 2.0 %copy-start.4 = (s32[8,128]{1,0:T(8,128)S(1)}, s32[8,128]{1,0:T(8,128)}, u32[]{:S(2)}) copy-start(s32[8,128]{1,0:T(8,128)} %mask_ref.3) | copy-start | bytes 12292
  16.8 6.8 %collective-permute-start.8 = (bf16[544,128]{1,0:T(8,128)(2,1)S(1)}, bf16[544,128]{1,0:T(8,128)(2,1)S(1)}, u32[]{:S(2)}, u32[]{:S(2)}) collective-permute-start(bf16[544,128]{1,0:T(8,128)(2,1)S(1)} %get-tuple-element.63), channel_id=1, source_target_pairs={{0,4},{1,5},{2,6},{3,7},{4,0},{5,1},{6,2},{7,3},{8,12},{9,13},{10,... | collective-permute-start | bytes 417800 | tf_op jit(solution)/shard_map/ppermute | solution.py:450
  18.1 8.2 %collective-permute-start.7 = (bf16[512,128]{1,0:T(8,128)(2,1)S(1)}, bf16[512,128]{1,0:T(8,128)(2,1)S(1)}, u32[]{:S(2)}, u32[]{:S(2)}) collective-permute-start(bf16[512,128]{1,0:T(8,128)(2,1)S(1)} %shard_map.119), channel_id=1, source_target_pairs={{0,2},{1,3},{2,0},{3,1},{4,6},{5,7},{6,4},{7,5},{8,10},{9,11},{10,... | collective-permute-start | bytes 393224 | tf_op jit(solution)/shard_map/ppermute | solution.py:450
  19.2 5.0 %collective-permute-start.5 = (bf16[1024,128]{1,0:T(8,128)(2,1)S(1)}, bf16[1024,128]{1,0:T(8,128)(2,1)S(1)}, u32[]{:S(2)}, u32[]{:S(2)}) collective-permute-start(bf16[1024,128]{1,0:T(8,128)(2,1)S(1)} %collective-permute-done.2.left_in), channel_id=1, source_target_pairs={{0,1},{1,0},{2,3},{3,2},{4,5},{5,4},{6,7},{7,6},{8,9},{9,8},{10,11... | collective-permute-start | bytes 786440 | tf_op jit(solution)/shard_map/ppermute | solution.py:450
  23.7 3.4 %collective-permute-start.9 = (bf16[544,128]{1,0:T(8,128)(2,1)S(1)}, bf16[544,128]{1,0:T(8,128)(2,1)S(1)}, u32[]{:S(2)}, u32[]{:S(2)}) collective-permute-start(bf16[544,128]{1,0:T(8,128)(2,1)S(1)} %shard_map.123), channel_id=1, source_target_pairs={{0,1},{1,0},{2,3},{3,2},{4,5},{5,4},{6,7},{7,6},{8,9},{9,8},{10,11... | collective-permute-start | bytes 417800 | tf_op jit(solution)/shard_map/ppermute | solution.py:450
  30.1 1.7 %collective-permute-start.10 = (bf16[1280,128]{1,0:T(8,128)(2,1)S(1)}, bf16[1280,128]{1,0:T(8,128)(2,1)S(1)}, u32[]{:S(2)}, u32[]{:S(2)}) collective-permute-start(bf16[1280,128]{1,0:T(8,128)(2,1)S(1)} %get-tuple-element.76), channel_id=1, source_target_pairs={{0,1},{1,0},{2,3},{3,2},{4,5},{5,4},{6,7},{7,6},{8,9},{9,8},{10,11... | collective-permute-start | bytes 983048 | tf_op jit(solution)/shard_map/ppermute | solution.py:450
  30.2 6.4 %collective-permute-start.17 = (bf16[512,128]{1,0:T(8,128)(2,1)S(1)}, bf16[512,128]{1,0:T(8,128)(2,1)S(1)}, u32[]{:S(2)}, u32[]{:S(2)}) collective-permute-start(bf16[512,128]{1,0:T(8,128)(2,1)S(1)} %get-tuple-element.70.refs_6_), channel_id=1, source_target_pairs={{0,2},{1,3},{2,0},{3,1},{4,6},{5,7},{6,4},{7,5},{8,10},{9,11},{10,... | collective-permute-start | bytes 393224 | tf_op jit(solution)/shard_map/ppermute | solution.py:450
  31.5 11.5 %copy-start.2 = (bf16[8,128,128]{2,1,0:T(8,128)(2,1)S(1)}, bf16[8,128,128]{2,1,0:T(8,128)(2,1)}, u32[]{:S(2)}) copy-start(bf16[8,128,128]{2,1,0:T(8,128)(2,1)} %param.10) | copy-start | bytes 786436
  31.9 7.6 %collective-permute-start.11 = (bf16[512,128]{1,0:T(8,128)(2,1)S(1)}, bf16[512,128]{1,0:T(8,128)(2,1)S(1)}, u32[]{:S(2)}, u32[]{:S(2)}) collective-permute-start(bf16[512,128]{1,0:T(8,128)(2,1)S(1)} %shard_map.129), channel_id=1, source_target_pairs={{0,2},{1,3},{2,0},{3,1},{4,6},{5,7},{6,4},{7,5},{8,10},{9,11},{10,... | collective-permute-start | bytes 393224 | tf_op jit(solution)/shard_map/ppermute | solution.py:450
  32.9 10.1 %collective-permute-start.13 = (bf16[512,128]{1,0:T(8,128)(2,1)S(1)}, bf16[512,128]{1,0:T(8,128)(2,1)S(1)}, u32[]{:S(2)}, u32[]{:S(2)}) collective-permute-start(bf16[512,128]{1,0:T(8,128)(2,1)S(1)} %get-tuple-element.78), channel_id=1, source_target_pairs={{0,4},{1,5},{2,6},{3,7},{4,0},{5,1},{6,2},{7,3},{8,12},{9,13},{10,... | collective-permute-start | bytes 393224 | tf_op jit(solution)/shard_map/ppermute | solution.py:450
  34.5 14.9 %collective-permute-start.16 = (bf16[1024,128]{1,0:T(8,128)(2,1)S(1)}, bf16[1024,128]{1,0:T(8,128)(2,1)S(1)}, u32[]{:S(2)}, u32[]{:S(2)}) collective-permute-start(bf16[1024,128]{1,0:T(8,128)(2,1)S(1)} %get-tuple-element.77.refs_0_), channel_id=1, source_target_pairs={{0,4},{1,5},{2,6},{3,7},{4,0},{5,1},{6,2},{7,3},{8,12},{9,13},{10,... | collective-permute-start | bytes 786440 | tf_op jit(solution)/shard_map/ppermute | solution.py:450
  36.6 10.2 %collective-permute-start.18 = (bf16[512,128]{1,0:T(8,128)(2,1)S(1)}, bf16[512,128]{1,0:T(8,128)(2,1)S(1)}, u32[]{:S(2)}, u32[]{:S(2)}) collective-permute-start(bf16[512,128]{1,0:T(8,128)(2,1)S(1)} %shard_map.135), channel_id=1, source_target_pairs={{0,8},{1,9},{2,10},{3,11},{4,12},{5,13},{6,14},{7,15},{8,0},{9,1},... | collective-permute-start | bytes 393224 | tf_op jit(solution)/shard_map/ppermute | solution.py:450
  39.5 11.0 %collective-permute-start.15 = (bf16[512,128]{1,0:T(8,128)(2,1)S(1)}, bf16[512,128]{1,0:T(8,128)(2,1)S(1)}, u32[]{:S(2)}, u32[]{:S(2)}) collective-permute-start(bf16[512,128]{1,0:T(8,128)(2,1)S(1)} %shard_map.130.refs_0_.after_ref), channel_id=1, source_target_pairs={{0,8},{1,9},{2,10},{3,11},{4,12},{5,13},{6,14},{7,15},{8,0},{9,1},... | collective-permute-start | bytes 393224 | tf_op jit(solution)/shard_map/ppermute | solution.py:450
  41.8 7.7 %collective-permute-start.14 = (bf16[1024,128]{1,0:T(8,128)(2,1)S(1)}, bf16[1024,128]{1,0:T(8,128)(2,1)S(1)}, u32[]{:S(2)}, u32[]{:S(2)}) collective-permute-start(bf16[1024,128]{1,0:T(8,128)(2,1)S(1)} %shard_map.134), channel_id=1, source_target_pairs={{0,2},{1,3},{2,0},{3,1},{4,6},{5,7},{6,4},{7,5},{8,10},{9,11},{10,... | collective-permute-start | bytes 786440 | tf_op jit(solution)/shard_map/ppermute | solution.py:450
  43.0 2.6 %collective-permute-start.12 = (bf16[1280,128]{1,0:T(8,128)(2,1)S(1)}, bf16[1280,128]{1,0:T(8,128)(2,1)S(1)}, u32[]{:S(2)}, u32[]{:S(2)}) collective-permute-start(bf16[1280,128]{1,0:T(8,128)(2,1)S(1)} %shard_map.131), channel_id=1, source_target_pairs={{0,1},{1,0},{2,3},{3,2},{4,5},{5,4},{6,7},{7,6},{8,9},{9,8},{10,11... | collective-permute-start | bytes 983048 | tf_op jit(solution)/shard_map/ppermute | solution.py:450

commit v8 on v7

--- a/solution.py
+++ b/solution.py
@@ -91,14 +91,11 @@
 
 
 def scale_in(x, params_ref):
-    ones = jnp.ones((128, 128), BF16)
-    center = x.astype(F32) - dot(x, ones, NN) * (1.0 / 128.0)
-    inverse = lax.rsqrt(split_sum(center * center, ones) * (1.0 / 128.0) + EPSILON)
-    return center * inverse * params_ref[0:1, :] + params_ref[1:2, :]
-
-
-def block_of(values, row):
-    return values[row * 128 : (row + 1) * 128]
+    return norm(x.astype(F32), 1)[0] * params_ref[0:1, :] + params_ref[1:2, :]
+
+
+def project(weight_t, scaled, row):
+    return dot(weight_t, scaled[row * 128 : (row + 1) * 128], NT)
 
 
 def make_side(projected):
@@ -129,7 +126,7 @@
     scaled_ref[...] = scaled.reshape(scaled_ref.shape)
     scaled = scaled.astype(BF16)
     for row in range(ROWS):
-        projected = dot(weight_t_ref[...], block_of(scaled, row), NT)
+        projected = project(weight_t_ref[...], scaled, row)
         store_side(rows_ref.at[0], row, make_side(projected[:256]))
         store_side(rows_ref.at[1], row, make_side(projected[256:]))
     left_ref[...] = rows_ref[0].astype(BF16)
@@ -159,12 +156,12 @@
     scaled_ref[...] = scaled.reshape(scaled_ref.shape)
     scaled = scaled.astype(BF16)
     for row in range(ROWS):
-        projected = dot(weight_t_ref[:256, :], block_of(scaled, row), NT)
+        projected = project(weight_t_ref[:256, :], scaled, row)
         store_side(rows_ref.at[0], row, make_side(projected))
     scaled = [scale_in(r[...], params_ref).astype(BF16) for r in right_in]
     for row in range(ROWS):
         part, place = divmod(row, ROWS // len(right_in))
-        projected = dot(weight_t_ref[256:, :], block_of(scaled[part], place), NT)
+        projected = project(weight_t_ref[256:, :], scaled[part], place)
         store_side(rows_ref.at[1], row, make_side(projected))
     left_ref[...] = rows_ref[0].astype(BF16)
     right_ref[...] = rows_ref[1].astype(BF16)
@@ -178,7 +175,7 @@
     scaled_ref[...] = scaled.reshape(scaled_ref.shape)
     scaled = scaled.astype(BF16)
     for row in range(ROWS):
-        projected = dot(weight_t_ref[:256, :], block_of(scaled, row), NT)
+        projected = project(weight_t_ref[:256, :], scaled, row)
         store_side(rows_ref, row, make_side(projected))
     left_ref[...] = rows_ref[...].astype(BF16)
     sig_ref[...] = block_gate(me_ref, scaled_ref, weight_ref)
@@ -192,7 +189,7 @@
             rows_ref[...] = jnp.zeros_like(rows_ref)
         scaled = scale_in(x_ref[...], params_ref).astype(BF16)
         for row in range(ROWS // 2):
-            projected = dot(weight_t_ref[256:, :], block_of(scaled, row), NT)
+            projected = project(weight_t_ref[256:, :], scaled, row)
             store_side(rows_ref, first + row, make_side(projected))
         right_ref[...] = rows_ref[...].astype(right_ref.dtype)
 
@@ -334,7 +331,12 @@
     sum_ref[...] = (mine_ref[...].astype(F32) + got_ref[...].astype(F32)).astype(BF16)
 
 
-def near_kernel(first_ref, second_ref, after_ref, both_ref):
+def early_kernel(mine_ref, got_ref, sum_ref):
+    sum_ref[...] = mine_ref[...].astype(F32) + got_ref[:SIDE, :].astype(F32)
+
+
+def near_kernel(first_ref, second_ref, *refs):
+    both_ref = refs[-1]
     both_ref[: SIDE // 2, :] = first_ref[...]
     both_ref[SIDE // 2 :, :] = second_ref[...]
 
@@ -361,6 +363,9 @@
     gain_t = jnp.broadcast_to(params_ref[0:1, :], (128, 128)).T
     bias_t = jnp.broadcast_to(params_ref[1:2, :], (128, 128)).T
     gain_t_ref[...] = gain_t
+    scaled = scale_in(x_ref[...], params_ref).astype(BF16)
+    gate_sig = sigmoid(dot(scaled, weight_ref[:, 512:640], NN)).reshape(cot_ref.shape)
+    open_ref[...] = cot_ref[...].astype(F32) * (1.0 - gate_sig)
     for row in range(ROWS):
         x = x_ref[row * 128 : (row + 1) * 128, :]
         normed, inverse = norm(x.astype(F32).T, 0)
@@ -375,9 +380,6 @@
             value = projected[base + 128 : base + 256]
             factor_ref[row, base : base + 128, :] = keep * value * gate * (1.0 - gate)
             factor_ref[row, base + 128 : base + 256, :] = keep * gate
-        scaled = scale_in(x, params_ref).astype(BF16)
-        gate_sig = sigmoid(dot(scaled, weight_ref[:, 512:640], NN))
-        open_ref[row] = cot_ref[row].astype(F32) * (1.0 - gate_sig)
 
 
 def out_kernel(me_ref, own_ref, near_ref, far_ref, open_ref, weight_ref, out_ref, grad_ref, full_ref):
@@ -406,10 +408,9 @@
 
 
 def partial_kernel(*refs):
-    left_refs, (own_ref, near_ref, got_ref) = refs[0:3], refs[3:6]
-    factor_ref, gate_ref, weight_ref, sum_ref, left_rows, right_rows = refs[6:]
-    left = [r[:SIDE, :].astype(F32) for r in left_refs]
-    left_rows[...] = left[0] + left[1] + left[2]
+    left_ref, left_got_ref, own_ref, near_ref, got_ref = refs[:5]
+    factor_ref, gate_ref, weight_ref, sum_ref, left_rows, right_rows = refs[5:]
+    left_rows[...] = left_ref[...] + left_got_ref[...].astype(F32)
     right = own_ref[...].astype(F32) + near_ref[: SIDE // 2, :].astype(F32)
     right_rows[...] = right + got_ref[...].astype(F32)
     for row in range(ROWS):
@@ -475,7 +476,9 @@
         return call(pass_kernel, [(message.shape, BF16)], vmem=[message, *others])[0]
 
     flat = pair_rep.reshape(SIDE, 128)
-    weights = jnp.concatenate([proj_weight, gate_weight, out_weight], axis=1)
+    weights = jnp.zeros((), BF16)
+    for at, weight in ((0, proj_weight), (512, gate_weight), (640, out_weight)):
+        weights = weights + jnp.pad(weight, ((0, 0), (at, 768 - at - weight.shape[1])))
     params = jnp.stack([in_gain, in_bias, mid_gain, mid_bias])
 
     first, second = call(halves_kernel, [halves] * 2, vmem=[flat])
@@ -488,7 +491,7 @@
         own_kernel,
         [side, side, sig, ((512, 128), BF16), ((512, 512), BF16), ((ROWS, 512), F32)],
         smem=[me],
-        vmem=[flat, weights, params],
+        vmem=[whole, weights, params],
         scratch=[rows_scratch, cube_scratch],
         weight=WAIT,
     )
@@ -557,27 +560,28 @@
         vmem=[pairs, *rights, out_1, out_3, right_a[3]],
     )
     both_got = swap(both_back, CORE)
-    right_b = call(grad_right_kernel(1), [halves] * 4, vmem=[pairs, *lefts])
+    right_b = call(grad_right_kernel(1), [halves] * 4, vmem=[pairs, *lefts], weight=WAIT)
     left_sum, out_far = call(
         add_left_kernel,
         [side, ((2 * PIECE, 128), BF16)],
         vmem=[grad_left_2, out_2, both_got],
     )
     x_got.append(swap(after(right_b[3], left_sum), CHIP_X))
+    near_got = swap(after(near_back, left_sum), CORE)
+    (left_part,) = call(early_kernel, [((SIDE, 128), F32)], vmem=[grad_left_0, near_got])
     left_got = swap(left_sum, Z_LOW)
     out_far = swap(out_far, Z_LOW)
     (total,) = call(add_kernel, [halves], vmem=[right_a[2], x_got[0], left_sum])
     z_got = [swap(total, Z_HIGH)]
     (total,) = call(add_kernel, [halves], vmem=[right_b[2], x_got[1], left_sum])
     z_got.append(swap(total, Z_HIGH))
-    (right_back,) = call(near_kernel, [side], vmem=[right_a[1], right_b[1], total])
+    (right_back,) = call(near_kernel, [side], vmem=[right_a[1], right_b[1], total, left_part])
     right_near = swap(right_back, CHIP_X)
-    near_got = swap(after(near_back, total), CORE)
 
     factors, normed, inverse, open_part, gain_t = call(
         factor_kernel,
         [((ROWS, 512, 128), F32), (cube, F32), ((ROWS, 128), F32), (cube, F32), ((128, 128), F32)],
-        vmem=[flat, cotangent, pair_mask, weights, params, weight_t],
+        vmem=[whole, cotangent, pair_mask, weights, params, weight_t],
         weight=WAIT,
     )
     output, gate_part = call(
@@ -591,7 +595,7 @@
     (partial,) = call(
         partial_kernel,
         [(cube, F32)],
-        vmem=[grad_left_0, near_got, left_got, right_a[0], right_near, z_got[0]]
+        vmem=[left_part, left_got, right_a[0], right_near, z_got[0]]
         + [factors, gate_part, weights],
         scratch=[pltpu.VMEM((SIDE, 128), F32), half_scratch],
         weight=WAIT // 4,

time: 52.2 us -> 53 us (1.015)
  waiting for transfers between devices: 5.52 us -> 10.1 us
  local copies, waits for them, and re-layouts: 4.36 us -> 0.95 us
  Pallas kernels: 18.5 us -> 15.7 us
  starting transfers between devices: 21.8 us -> 23.5 us
  other arithmetic: 0.71 us -> 1.67 us
    ppermute x19, waiting for transfers between devices: 5.52 us -> 10.1 us  [swap(): return lax.ppermute(values, 'row', [(s, s ^ offset) for s in range(16)])]
    pallas_call x25 -> x26, Pallas kernels: 18.5 us -> 15.7 us  [call(): pl.pallas_call(kernel, out_shape=[jax.ShapeDtypeStruct(s, d) for s, d in...]
    unnamed x12 -> x6, local copies, waits for them, and re-layouts: 3.59 us -> 0.95 us
    ppermute x19, starting transfers between devices: 21.8 us -> 23.5 us  [swap(): return lax.ppermute(values, 'row', [(s, s ^ offset) for s in range(16)])]
    add x0 -> x1, other arithmetic: none -> 0.96 us  [blocks_device(): weights + jnp.pad(weight, ((0, 0), (at, 768 - at - weight.shape[1])))]
    concatenate x1 -> x0, local copies, waits for them, and re-layouts: 0.77 us -> none  [blocks_device(): weights = jnp.concatenate([proj_weight, gate_weight, out_weight], axis=1)]
  transfers between devices with their start and end apart: 19 -> 19, of which waited for: 6 -> 7; matrix products, arithmetic and copies ran while one was open for 6% -> 3% of each run, Pallas kernels for 27% -> 21%
where the time goes in v8:
time: 53 us; the launch traced here: 52.8 us
  starting transfers between devices  23.5 us (44%)
  Pallas kernels  15.7 us (30%)
  waiting for transfers between devices  10.1 us (19%)
  other arithmetic  1.67 us (3%)
  local copies, waits for them, and re-layouts  0.95 us (2%)
  between operations  0.85 us (2%)
    ppermute x19, starting transfers between devices, swap(): return lax.ppermute(values, 'row', [(s, s ^ offset) for s in range(16)])  23.5 us
    pallas_call x26, Pallas kernels, call(): pl.pallas_call(kernel, out_shape=[jax.ShapeDtypeStruct(s, d) for s, d in...  15.7 us
    ppermute x19, waiting for transfers between devices, swap(): return lax.ppermute(values, 'row', [(s, s ^ offset) for s in range(16)])  10.1 us
  transfers between devices with their start and end apart: 19, of which 7 were waited for; matrix products, arithmetic and copies ran while one was open for 3% of the time, Pallas kernels for 21%

profile of v8, /device:TPU:0, one launch (start us, length us, event | category | flops | bytes accessed | tf_op | source)
XLA Modules:
  0.0 52.8 jit_solution(12789205857175302695)
XLA Ops:
  0.6 0.0 copy-start
  0.6 0.9 %copy-done = bf16[8,128,128]{2,1,0:T(8,128)(2,1)S(1)} copy-done((bf16[8,128,128]{2,1,0:T(8,128)(2,1)S(1)}, bf16[8,128,128]{2,1,0:T(8,128)(2,1)}, u32[]{:S(2)}) %copy-start) | copy-done | bytes 262168
  1.6 4.1 %collective-permute-start.4 = (bf16[512,128]{1,0:T(8,128)(2,1)S(1)}, bf16[512,128]{1,0:T(8,128)(2,1)S(1)}, u32[]{:S(2)}, u32[]{:S(2)}) collective-permute-start(bf16[512,128]{1,0:T(8,128)(2,1)S(1)} %get-tuple-element.47.refs_0_), channel_id=1, source_target_pairs={{0,8},{1,9},{2,10},{3,11},{4,12},{5,13},{6,14},{7,15},{8,0},{9,1},... | collective-permute-start | bytes 393224 | tf_op jit(solution)/shard_map/ppermute | solution.py:451
  5.7 1.6 %collective-permute-start.2 = (bf16[1024,128]{1,0:T(8,128)(2,1)S(1)}, bf16[1024,128]{1,0:T(8,128)(2,1)S(1)}, u32[]{:S(2)}, u32[]{:S(2)}) collective-permute-start(bf16[1024,128]{1,0:T(8,128)(2,1)S(1)} %shard_map.114.x_ref), channel_id=1, source_target_pairs={{0,4},{1,5},{2,6},{3,7},{4,0},{5,1},{6,2},{7,3},{8,12},{9,13},{10,... | collective-permute-start | bytes 786440 | tf_op jit(solution)/shard_map/ppermute | solution.py:451
  7.4 1.5 %collective-permute-start.1 = (bf16[1024,128]{1,0:T(8,128)(2,1)S(1)}, bf16[1024,128]{1,0:T(8,128)(2,1)S(1)}, u32[]{:S(2)}, u32[]{:S(2)}) collective-permute-start(bf16[1024,128]{1,0:T(8,128)(2,1)S(1)} %shard_map.114.x_ref), channel_id=1, source_target_pairs={{0,2},{1,3},{2,0},{3,1},{4,6},{5,7},{6,4},{7,5},{8,10},{9,11},{10,... | collective-permute-start | bytes 786440 | tf_op jit(solution)/shard_map/ppermute | solution.py:451
  8.9 0.0 collective-permute-start
  8.9 0.3 collective-permute-start.3
  9.2 0.7 %pad_maximum_fusion.params_ref.refs_3_.refs_4_ = f32[4,128]{1,0:T(4,128)S(1)} fusion(f32[1,128]{1,0:T(1,128)} %bitcast.8, f32[1,128]{1,0:T(1,128)} %bitcast.9, f32[1,128]{1,0:T(1,128)} %bitcast.10, f32[1,128]{1,0:T(1,128)} %bitcast.11), kind=kLoop, calls=%fused_computation.1 | loop fusion | flops 1536 | bytes 4096 | tf_op jit(solution)/shard_map/stack | solution.py:482
  9.9 1.0 %pad_add_fusion.weight_ref.refs_2_.refs_3_.refs_7_ = bf16[128,768]{1,0:T(8,128)(2,1)S(1)} fusion(bf16[128,128]{1,0:T(8,128)(2,1)} %param.19, bf16[128,128]{1,0:T(8,128)(2,1)} %param.16, bf16[128,512]{1,0:T(8,128)(2,1)} %param.15), kind=kLoop, calls=%fused_computation | loop fusion | flops 589824 | bytes 393216 | tf_op jit(solution)/shard_map/add | solution.py:481
  10.9 1.2 %collective-permute-done.4.refs_1_ = bf16[512,128]{1,0:T(8,128)(2,1)S(1)} collective-permute-done((bf16[512,128]{1,0:T(8,128)(2,1)S(1)}, bf16[512,128]{1,0:T(8,128)(2,1)S(1)}, u32[]{:S(2)}, u32[]{:S(2)}) %collective-permute-start.4) | collective-permute-done | bytes 131104 | tf_op jit(solution)/shard_map/ppermute | solution.py:451
  12.1 1.6 %collective-permute-start.6 = (bf16[512,128]{1,0:T(8,128)(2,1)S(1)}, bf16[512,128]{1,0:T(8,128)(2,1)S(1)}, u32[]{:S(2)}, u32[]{:S(2)}) collective-permute-start(bf16[512,128]{1,0:T(8,128)(2,1)S(1)} %collective-permute-done.4.refs_1_), channel_id=1, source_target_pairs={{0,2},{1,3},{2,0},{3,1},{4,6},{5,7},{6,4},{7,5},{8,10},{9,11},{10,... | collective-permute-start | bytes 393224 | tf_op jit(solution)/shard_map/ppermute | solution.py:451
  13.7 0.0 copy-start.1
  13.7 0.0 copy-start.2
  13.7 1.9 %shard_map.115 = (bf16[1024,128]{1,0:T(8,128)(2,1)S(1)}, bf16[1024,128]{1,0:T(8,128)(2,1)S(1)}, f32[256,128]{1,0:T(8,128)S(1)}, bf16[512,128]{1,0:T(8,128)(2,1)S...) custom-call(s32[1]{0:T(128)} %bitcast.me_ref.refs_0_, bf16[1024,128]{1,0:T(8,128)(2,1)S(1)} %shard_map.114.x_ref, ...), custom_call_target="tpu_custom_call" | custom-call | flops 5000000000 | bytes 262144 | tf_op jit(solution)/shard_map/pallas_call | solution.py:43
  15.7 0.2 collective-permute-done.1.refs_0_.after_ref
  15.9 0.0 copy-done.1
  15.9 0.0 copy-done.2
  15.9 0.1 shard_map.122
  16.0 0.5 collective-permute-start.8
  16.5 1.0 %collective-permute-done.3.refs_0_.message_ref = bf16[512,128]{1,0:T(8,128)(2,1)S(1)} collective-permute-done((bf16[512,128]{1,0:T(8,128)(2,1)S(1)}, bf16[512,128]{1,0:T(8,128)(2,1)S(1)}, u32[]{:S(2)}, u32[]{:S(2)}) %collective-permute-start.3) | collective-permute-done | bytes 131104 | tf_op jit(solution)/shard_map/ppermute | solution.py:451
  17.5 0.2 collective-permute-done.6.refs_0_.x_ref
  17.7 1.9 %collective-permute-start.7 = (bf16[512,128]{1,0:T(8,128)(2,1)S(1)}, bf16[512,128]{1,0:T(8,128)(2,1)S(1)}, u32[]{:S(2)}, u32[]{:S(2)}) collective-permute-start(bf16[512,128]{1,0:T(8,128)(2,1)S(1)} %shard_map.119), channel_id=1, source_target_pairs={{0,2},{1,3},{2,0},{3,1},{4,6},{5,7},{6,4},{7,5},{8,10},{9,11},{10,... | collective-permute-start | bytes 393224 | tf_op jit(solution)/shard_map/ppermute | solution.py:451
  19.6 0.0 collective-permute-done.2.left_in
  19.6 0.0 collective-permute-start.5
  19.6 1.7 %shard_map.117 = (bf16[1024,128]{1,0:T(8,128)(2,1)S(1)}, bf16[1024,128]{1,0:T(8,128)(2,1)S(1)}, f32[256,128]{1,0:T(8,128)S(1)}) custom-call(s32[1]{0:T(128)} %bitcast.me_ref.refs_0_, bf16[1024,128]{1,0:T(8,128)(2,1)S(1)} %collective-permute-done.2.left_in, bf16[512,128]{1,0:T(8,128)(2,1)S(1)} %collective-permute-done.3.refs_0_.message_ref, ...), custom_call_target="tpu_custom_call" | custom-call | flops 5000000000 | bytes 262144 | tf_op jit(solution)/shard_map/pallas_call | solution.py:43
  21.3 0.0 collective-permute-done.left_in
  21.3 1.7 %shard_map.116 = (bf16[1024,128]{1,0:T(8,128)(2,1)S(1)}, bf16[1024,128]{1,0:T(8,128)(2,1)S(1)}, f32[256,128]{1,0:T(8,128)S(1)}) custom-call(s32[1]{0:T(128)} %bitcast.me_ref.refs_0_, bf16[1024,128]{1,0:T(8,128)(2,1)S(1)} %collective-permute-done.left_in, bf16[1024,128]{1,0:T(8,128)(2,1)S(1)} %collective-permute-done.1.refs_0_.after_ref, ...), custom_call_target="tpu_custom_call" | custom-call | flops 5000000000 | bytes 262144 | tf_op jit(solution)/shard_map/pallas_call | solution.py:43
  23.0 0.0 collective-permute-done.8.got_ref.refs_15_
  23.0 0.6 %collective-permute-start.9 = (bf16[544,128]{1,0:T(8,128)(2,1)S(1)}, bf16[544,128]{1,0:T(8,128)(2,1)S(1)}, u32[]{:S(2)}, u32[]{:S(2)}) collective-permute-start(bf16[544,128]{1,0:T(8,128)(2,1)S(1)} %shard_map.123), channel_id=1, source_target_pairs={{0,1},{1,0},{2,3},{3,2},{4,5},{5,4},{6,7},{7,6},{8,9},{9,8},{10,11... | collective-permute-start | bytes 417800 | tf_op jit(solution)/shard_map/ppermute | solution.py:451
  23.6 0.0 collective-permute-done.5.x_ref
  23.6 1.0 %shard_map.118 = (bf16[1024,128]{1,0:T(8,128)(2,1)S(1)}, f32[256,128]{1,0:T(8,128)S(1)}) custom-call(s32[1]{0:T(128)} %bitcast.me_ref.refs_0_, bf16[1024,128]{1,0:T(8,128)(2,1)S(1)} %collective-permute-done.5.x_ref, bf16[512,128]{1,0:T(8,128)(2,1)S(1)} %get-tuple-element.49.refs_1_.refs_2_.weight_t_ref, ...), custom_call_target="tpu_custom_call" | custom-call | flops 5000000000 | bytes 262144 | tf_op jit(solution)/shard_map/pallas_call | solution.py:43
  24.6 0.7 %shard_map.120.rest_ref = f32[1024,128]{1,0:T(8,128)S(1)} custom-call(bf16[512,128]{1,0:T(8,128)(2,1)S(1)} %collective-permute-done.6.refs_0_.x_ref, bf16[512,128]{1,0:T(8,128)(2,1)S(1)} %get-tuple-element.49.refs_1_.refs_2_.weight_t_ref, f32[4,128]{1,0:T(4,128)S(1)} %pad_maximum_fusion.params_ref.refs_3_.refs_4_, ...), custom_call_target="tpu_custom_call" | custom-call | flops 1250000000 | bytes 262144 | tf_op jit(solution)/shard_map/pallas_call | solution.py:43
  25.3 0.0 collective-permute-done.7.x_ref
  25.3 0.7 %shard_map.121.refs_8_.refs_3_ = bf16[1024,128]{1,0:T(8,128)(2,1)S(1)} custom-call(bf16[512,128]{1,0:T(8,128)(2,1)S(1)} %collective-permute-done.7.x_ref, bf16[512,128]{1,0:T(8,128)(2,1)S(1)} %get-tuple-element.49.refs_1_.refs_2_.weight_t_ref, f32[4,128]{1,0:T(4,128)S(1)} %pad_maximum_fusion.params_ref.refs_3_.refs_4_, f32[1024,128]{1,0:T(8,128)S(1)} %shard_map.120.rest_ref), custom_call_target="tpu_custom_call" | custom-call | flops 1250000000 | bytes 262144 | tf_op jit(solution)/shard_map/pallas_call | solution.py:43
  26.0 0.0 collective-permute-done.9.refs_14_
  26.0 2.2 %shard_map.124 = (bf16[256,128]{1,0:T(8,128)(2,1)S(1)}, bf16[256,128]{1,0:T(8,128)(2,1)S(1)}, bf16[256,128]{1,0:T(8,128)(2,1)S(1)}, bf16[256,128]{1,0:T(8,128)(2,1)S(1)}, f32[1024,128]{1,0:T(8,128)S(1)}) custom-call(s32[1]{0:T(128)} %bitcast.me_ref.refs_0_, bf16[1024,128]{1,0:T(8,128)(2,1)S(1)} %get-tuple-element.48.refs_1_.refs_0_, ...), custom_call_target="tpu_custom_call" | custom-call | flops 67108864 | bytes 262144 | tf_op jit(solution)/shard_map/pallas_call | solution.py:43
  28.3 0.3 shard_map.125
  28.6 0.4 shard_map.126
  29.1 0.1 collective-permute-start.10
  29.1 1.4 %collective-permute-start.17 = (bf16[512,128]{1,0:T(8,128)(2,1)S(1)}, bf16[512,128]{1,0:T(8,128)(2,1)S(1)}, u32[]{:S(2)}, u32[]{:S(2)}) collective-permute-start(bf16[512,128]{1,0:T(8,128)(2,1)S(1)} %get-tuple-element.70.refs_6_), channel_id=1, source_target_pairs={{0,2},{1,3},{2,0},{3,1},{4,6},{5,7},{6,4},{7,5},{8,10},{9,11},{10,... | collective-permute-start | bytes 393224 | tf_op jit(solution)/shard_map/ppermute | solution.py:451
  30.6 0.2 collective-permute-done.10.got_ref
  30.7 0.1 shard_map.127
  30.8 0.2 collective-permute-start.11
  31.0 0.3 shard_map.131
  31.4 1.5 %collective-permute-start.13 = (bf16[512,128]{1,0:T(8,128)(2,1)S(1)}, bf16[512,128]{1,0:T(8,128)(2,1)S(1)}, u32[]{:S(2)}, u32[]{:S(2)}) collective-permute-start(bf16[512,128]{1,0:T(8,128)(2,1)S(1)} %shard_map.132), channel_id=1, source_target_pairs={{0,2},{1,3},{2,0},{3,1},{4,6},{5,7},{6,4},{7,5},{8,10},{9,11},{10,... | collective-permute-start | bytes 393224 | tf_op jit(solution)/shard_map/ppermute | solution.py:451
  32.9 0.4 collective-permute-start.16
  33.3 1.6 %collective-permute-start.12 = (bf16[512,128]{1,0:T(8,128)(2,1)S(1)}, bf16[512,128]{1,0:T(8,128)(2,1)S(1)}, u32[]{:S(2)}, u32[]{:S(2)}) collective-permute-start(bf16[512,128]{1,0:T(8,128)(2,1)S(1)} %get-tuple-element.76), channel_id=1, source_target_pairs={{0,4},{1,5},{2,6},{3,7},{4,0},{5,1},{6,2},{7,3},{8,12},{9,13},{10,... | collective-permute-start | bytes 393224 | tf_op jit(solution)/shard_map/ppermute | solution.py:451
  34.9 0.6 %collective-permute-done.17.got_ref = bf16[512,128]{1,0:T(8,128)(2,1)S(1)} collective-permute-done((bf16[512,128]{1,0:T(8,128)(2,1)S(1)}, bf16[512,128]{1,0:T(8,128)(2,1)S(1)}, u32[]{:S(2)}, u32[]{:S(2)}) %collective-permute-start.17) | collective-permute-done | bytes 131104 | tf_op jit(solution)/shard_map/ppermute | solution.py:451
  35.5 3.4 %collective-permute-start.18 = (bf16[512,128]{1,0:T(8,128)(2,1)S(1)}, bf16[512,128]{1,0:T(8,128)(2,1)S(1)}, u32[]{:S(2)}, u32[]{:S(2)}) collective-permute-start(bf16[512,128]{1,0:T(8,128)(2,1)S(1)} %shard_map.136), channel_id=1, source_target_pairs={{0,8},{1,9},{2,10},{3,11},{4,12},{5,13},{6,14},{7,15},{8,0},{9,1},... | collective-permute-start | bytes 393224 | tf_op jit(solution)/shard_map/ppermute | solution.py:451
  39.0 0.0 collective-permute-done.13.got_ref
  39.0 2.3 %collective-permute-start.15 = (bf16[512,128]{1,0:T(8,128)(2,1)S(1)}, bf16[512,128]{1,0:T(8,128)(2,1)S(1)}, u32[]{:S(2)}, u32[]{:S(2)}) collective-permute-start(bf16[512,128]{1,0:T(8,128)(2,1)S(1)} %shard_map.133.refs_0_), channel_id=1, source_target_pairs={{0,8},{1,9},{2,10},{3,11},{4,12},{5,13},{6,14},{7,15},{8,0},{9,1},... | collective-permute-start | bytes 393224 | tf_op jit(solution)/shard_map/ppermute | solution.py:451
  41.3 0.0 collective-permute-done.11.near_ref.got_ref
  41.3 0.1 shard_map.134.refs_1_.refs_0_
  41.4 0.3 collective-permute-start.14
  41.8 1.1 %shard_map.129 = (f32[8,512,128]{2,1,0:T(8,128)S(1)}, f32[8,128,128]{2,1,0:T(8,128)S(1)}, f32[8,128]{1,0:T(8,128)S(1)}, f32[8,128,128]{2,1,0:T(8,128)S(1)}, f32[128,128]{1,0:T(8,128)S(1)}) custom-call(bf16[1024,128]{1,0:T(8,128)(2,1)S(1)} %shard_map.114.x_ref, bf16[8,128,128]{2,1,0:T(8,128)(2,1)S(1)} %copy-done.1, s32[8,128]{1,0:T(8,128)S(1)} %copy-done.2, ...), custom_call_target="tpu_custom_call" | custom-call | flops 5000000000 | bytes 262144 | tf_op jit(solution)/shard_map/pallas_call | solution.py:43
  42.9 6.7 %collective-permute-done.12.far_ref = bf16[512,128]{1,0:T(8,128)(2,1)S(1)} collective-permute-done((bf16[512,128]{1,0:T(8,128)(2,1)S(1)}, bf16[512,128]{1,0:T(8,128)(2,1)S(1)}, u32[]{:S(2)}, u32[]{:S(2)}) %collective-permute-start.12) | collective-permute-done | bytes 131104 | tf_op jit(solution)/shard_map/ppermute | solution.py:451
  49.6 0.9 %shard_map.130 = (bf16[8,128,128]{2,1,0:T(8,128)(2,1)}, f32[8,128,128]{2,1,0:T(8,128)S(1)}) custom-call(s32[1]{0:T(128)} %bitcast.me_ref.refs_0_, bf16[256,128]{1,0:T(8,128)(2,1)S(1)} %get-tuple-element.66.own_ref, bf16[1280,128]{1,0:T(8,128)(2,1)S(1)} %collective-permute-done.11.near_ref.got_ref, bf16[512,128]{1,0:T(8,128)(2,1)S(1)} %collective-permute-done.12.far_ref, ...), custom_call_target="tpu_custom_call" | custom-call | flops 67108864 | bytes 262144 | tf_op jit(solution)/shard_map/pallas_call | solution.py:43
  50.5 0.0 collective-permute-done.18.refs_4_
  50.5 0.0 collective-permute-done.16.refs_1_
  50.5 0.0 collective-permute-done.14.refs_3_.near_ref
  50.5 1.0 %shard_map.137.sum_ref = f32[8,128,128]{2,1,0:T(8,128)S(1)} custom-call(f32[1024,128]{1,0:T(8,128)S(1)} %shard_map.134.refs_1_.refs_0_, bf16[1024,128]{1,0:T(8,128)(2,1)S(1)} %collective-permute-done.16.refs_1_, bf16[512,128]{1,0:T(8,128)(2,1)S(1)} %get-tuple-element.86.refs_2_, bf16[1024,128]{1,0:T(8,128)(2,1)S(1)} %collective-permute-done.14.refs_3_.near_ref, ...), custom_call_target="tpu_custom_call" | custom-call | flops 1250000000 | bytes 262144 | tf_op jit(solution)/shard_map/pallas_call | solution.py:43
  51.5 0.0 collective-permute-done.15.got_ref
  51.5 1.3 %shard_map.138 = bf16[8,128,128]{2,1,0:T(8,128)(2,1)} custom-call(bf16[512,128]{1,0:T(8,128)(2,1)S(1)} %get-tuple-element.79.own_ref, bf16[1024,128]{1,0:T(8,128)(2,1)S(1)} %collective-permute-done.14.refs_3_.near_ref, bf16[512,128]{1,0:T(8,128)(2,1)S(1)} %collective-permute-done.15.got_ref, f32[8,512,128]{2,1,0:T(8,128)S(1)} %get-tuple-element.85.refs_5_.factor_ref, ...), custom_call_target="tpu_custom_call" | custom-call | flops 67108864 | bytes 262144 | tf_op jit(solution)/shard_map/pallas_call | solution.py:43
  (9 shorter events, 0.2 us)
Async XLA Ops:
  0.6 1.0 %copy-start = (bf16[8,128,128]{2,1,0:T(8,128)(2,1)S(1)}, bf16[8,128,128]{2,1,0:T(8,128)(2,1)}, u32[]{:S(2)}) copy-start(bf16[8,128,128]{2,1,0:T(8,128)(2,1)} %param.10) | copy-start | bytes 786436
  1.6 10.5 %collective-permute-start.4 = (bf16[512,128]{1,0:T(8,128)(2,1)S(1)}, bf16[512,128]{1,0:T(8,128)(2,1)S(1)}, u32[]{:S(2)}, u32[]{:S(2)}) collective-permute-start(bf16[512,128]{1,0:T(8,128)(2,1)S(1)} %get-tuple-element.47.refs_0_), channel_id=1, source_target_pairs={{0,8},{1,9},{2,10},{3,11},{4,12},{5,13},{6,14},{7,15},{8,0},{9,1},... | collective-permute-start | bytes 393224 | tf_op jit(solution)/shard_map/ppermute | solution.py:451
  5.7 13.9 %collective-permute-start.2 = (bf16[1024,128]{1,0:T(8,128)(2,1)S(1)}, bf16[1024,128]{1,0:T(8,128)(2,1)S(1)}, u32[]{:S(2)}, u32[]{:S(2)}) collective-permute-start(bf16[1024,128]{1,0:T(8,128)(2,1)S(1)} %shard_map.114.x_ref), channel_id=1, source_target_pairs={{0,4},{1,5},{2,6},{3,7},{4,0},{5,1},{6,2},{7,3},{8,12},{9,13},{10,... | collective-permute-start | bytes 786440 | tf_op jit(solution)/shard_map/ppermute | solution.py:451
  7.4 8.5 %collective-permute-start.1 = (bf16[1024,128]{1,0:T(8,128)(2,1)S(1)}, bf16[1024,128]{1,0:T(8,128)(2,1)S(1)}, u32[]{:S(2)}, u32[]{:S(2)}) collective-permute-start(bf16[1024,128]{1,0:T(8,128)(2,1)S(1)} %shard_map.114.x_ref), channel_id=1, source_target_pairs={{0,2},{1,3},{2,0},{3,1},{4,6},{5,7},{6,4},{7,5},{8,10},{9,11},{10,... | collective-permute-start | bytes 786440 | tf_op jit(solution)/shard_map/ppermute | solution.py:451
  8.9 12.4 %collective-permute-start = (bf16[1024,128]{1,0:T(8,128)(2,1)S(1)}, bf16[1024,128]{1,0:T(8,128)(2,1)S(1)}, u32[]{:S(2)}, u32[]{:S(2)}) collective-permute-start(bf16[1024,128]{1,0:T(8,128)(2,1)S(1)} %shard_map.114.x_ref), channel_id=1, source_target_pairs={{0,1},{1,0},{2,3},{3,2},{4,5},{5,4},{6,7},{7,6},{8,9},{9,8},{10,11... | collective-permute-start | bytes 786440 | tf_op jit(solution)/shard_map/ppermute | solution.py:451
  8.9 8.6 %collective-permute-start.3 = (bf16[512,128]{1,0:T(8,128)(2,1)S(1)}, bf16[512,128]{1,0:T(8,128)(2,1)S(1)}, u32[]{:S(2)}, u32[]{:S(2)}) collective-permute-start(bf16[512,128]{1,0:T(8,128)(2,1)S(1)} %get-tuple-element.51), channel_id=1, source_target_pairs={{0,8},{1,9},{2,10},{3,11},{4,12},{5,13},{6,14},{7,15},{8,0},{9,1},... | collective-permute-start | bytes 393224 | tf_op jit(solution)/shard_map/ppermute | solution.py:451
  12.1 5.5 %collective-permute-start.6 = (bf16[512,128]{1,0:T(8,128)(2,1)S(1)}, bf16[512,128]{1,0:T(8,128)(2,1)S(1)}, u32[]{:S(2)}, u32[]{:S(2)}) collective-permute-start(bf16[512,128]{1,0:T(8,128)(2,1)S(1)} %collective-permute-done.4.refs_1_), channel_id=1, source_target_pairs={{0,2},{1,3},{2,0},{3,1},{4,6},{5,7},{6,4},{7,5},{8,10},{9,11},{10,... | collective-permute-start | bytes 393224 | tf_op jit(solution)/shard_map/ppermute | solution.py:451
  13.7 2.1 %copy-start.1 = (bf16[8,128,128]{2,1,0:T(8,128)(2,1)S(1)}, bf16[8,128,128]{2,1,0:T(8,128)(2,1)}, u32[]{:S(2)}) copy-start(bf16[8,128,128]{2,1,0:T(8,128)(2,1)} %cot_ref.3) | copy-start | bytes 786436
  13.7 2.1 %copy-start.2 = (s32[8,128]{1,0:T(8,128)S(1)}, s32[8,128]{1,0:T(8,128)}, u32[]{:S(2)}) copy-start(s32[8,128]{1,0:T(8,128)} %mask_ref.3) | copy-start | bytes 12292
  16.0 7.0 %collective-permute-start.8 = (bf16[544,128]{1,0:T(8,128)(2,1)S(1)}, bf16[544,128]{1,0:T(8,128)(2,1)S(1)}, u32[]{:S(2)}, u32[]{:S(2)}) collective-permute-start(bf16[544,128]{1,0:T(8,128)(2,1)S(1)} %get-tuple-element.63), channel_id=1, source_target_pairs={{0,4},{1,5},{2,6},{3,7},{4,0},{5,1},{6,2},{7,3},{8,12},{9,13},{10,... | collective-permute-start | bytes 417800 | tf_op jit(solution)/shard_map/ppermute | solution.py:451
  17.7 7.6 %collective-permute-start.7 = (bf16[512,128]{1,0:T(8,128)(2,1)S(1)}, bf16[512,128]{1,0:T(8,128)(2,1)S(1)}, u32[]{:S(2)}, u32[]{:S(2)}) collective-permute-start(bf16[512,128]{1,0:T(8,128)(2,1)S(1)} %shard_map.119), channel_id=1, source_target_pairs={{0,2},{1,3},{2,0},{3,1},{4,6},{5,7},{6,4},{7,5},{8,10},{9,11},{10,... | collective-permute-start | bytes 393224 | tf_op jit(solution)/shard_map/ppermute | solution.py:451
  19.6 4.0 %collective-permute-start.5 = (bf16[1024,128]{1,0:T(8,128)(2,1)S(1)}, bf16[1024,128]{1,0:T(8,128)(2,1)S(1)}, u32[]{:S(2)}, u32[]{:S(2)}) collective-permute-start(bf16[1024,128]{1,0:T(8,128)(2,1)S(1)} %collective-permute-done.2.left_in), channel_id=1, source_target_pairs={{0,1},{1,0},{2,3},{3,2},{4,5},{5,4},{6,7},{7,6},{8,9},{9,8},{10,11... | collective-permute-start | bytes 786440 | tf_op jit(solution)/shard_map/ppermute | solution.py:451
  23.0 3.0 %collective-permute-start.9 = (bf16[544,128]{1,0:T(8,128)(2,1)S(1)}, bf16[544,128]{1,0:T(8,128)(2,1)S(1)}, u32[]{:S(2)}, u32[]{:S(2)}) collective-permute-start(bf16[544,128]{1,0:T(8,128)(2,1)S(1)} %shard_map.123), channel_id=1, source_target_pairs={{0,1},{1,0},{2,3},{3,2},{4,5},{5,4},{6,7},{7,6},{8,9},{9,8},{10,11... | collective-permute-start | bytes 417800 | tf_op jit(solution)/shard_map/ppermute | solution.py:451
  29.1 1.7 %collective-permute-start.10 = (bf16[1280,128]{1,0:T(8,128)(2,1)S(1)}, bf16[1280,128]{1,0:T(8,128)(2,1)S(1)}, u32[]{:S(2)}, u32[]{:S(2)}) collective-permute-start(bf16[1280,128]{1,0:T(8,128)(2,1)S(1)} %get-tuple-element.74), channel_id=1, source_target_pairs={{0,1},{1,0},{2,3},{3,2},{4,5},{5,4},{6,7},{7,6},{8,9},{9,8},{10,11... | collective-permute-start | bytes 983048 | tf_op jit(solution)/shard_map/ppermute | solution.py:451
  29.1 6.3 %collective-permute-start.17 = (bf16[512,128]{1,0:T(8,128)(2,1)S(1)}, bf16[512,128]{1,0:T(8,128)(2,1)S(1)}, u32[]{:S(2)}, u32[]{:S(2)}) collective-permute-start(bf16[512,128]{1,0:T(8,128)(2,1)S(1)} %get-tuple-element.70.refs_6_), channel_id=1, source_target_pairs={{0,2},{1,3},{2,0},{3,1},{4,6},{5,7},{6,4},{7,5},{8,10},{9,11},{10,... | collective-permute-start | bytes 393224 | tf_op jit(solution)/shard_map/ppermute | solution.py:451
  30.8 10.5 %collective-permute-start.11 = (bf16[1280,128]{1,0:T(8,128)(2,1)S(1)}, bf16[1280,128]{1,0:T(8,128)(2,1)S(1)}, u32[]{:S(2)}, u32[]{:S(2)}) collective-permute-start(bf16[1280,128]{1,0:T(8,128)(2,1)S(1)} %shard_map.128), channel_id=1, source_target_pairs={{0,1},{1,0},{2,3},{3,2},{4,5},{5,4},{6,7},{7,6},{8,9},{9,8},{10,11... | collective-permute-start | bytes 983048 | tf_op jit(solution)/shard_map/ppermute | solution.py:451
  31.4 7.6 %collective-permute-start.13 = (bf16[512,128]{1,0:T(8,128)(2,1)S(1)}, bf16[512,128]{1,0:T(8,128)(2,1)S(1)}, u32[]{:S(2)}, u32[]{:S(2)}) collective-permute-start(bf16[512,128]{1,0:T(8,128)(2,1)S(1)} %shard_map.132), channel_id=1, source_target_pairs={{0,2},{1,3},{2,0},{3,1},{4,6},{5,7},{6,4},{7,5},{8,10},{9,11},{10,... | collective-permute-start | bytes 393224 | tf_op jit(solution)/shard_map/ppermute | solution.py:451
  32.9 17.6 %collective-permute-start.16 = (bf16[1024,128]{1,0:T(8,128)(2,1)S(1)}, bf16[1024,128]{1,0:T(8,128)(2,1)S(1)}, u32[]{:S(2)}, u32[]{:S(2)}) collective-permute-start(bf16[1024,128]{1,0:T(8,128)(2,1)S(1)} %get-tuple-element.75.refs_0_), channel_id=1, source_target_pairs={{0,4},{1,5},{2,6},{3,7},{4,0},{5,1},{6,2},{7,3},{8,12},{9,13},{10,... | collective-permute-start | bytes 786440 | tf_op jit(solution)/shard_map/ppermute | solution.py:451
  33.3 16.3 %collective-permute-start.12 = (bf16[512,128]{1,0:T(8,128)(2,1)S(1)}, bf16[512,128]{1,0:T(8,128)(2,1)S(1)}, u32[]{:S(2)}, u32[]{:S(2)}) collective-permute-start(bf16[512,128]{1,0:T(8,128)(2,1)S(1)} %get-tuple-element.76), channel_id=1, source_target_pairs={{0,4},{1,5},{2,6},{3,7},{4,0},{5,1},{6,2},{7,3},{8,12},{9,13},{10,... | collective-permute-start | bytes 393224 | tf_op jit(solution)/shard_map/ppermute | solution.py:451
  35.5 14.9 %collective-permute-start.18 = (bf16[512,128]{1,0:T(8,128)(2,1)S(1)}, bf16[512,128]{1,0:T(8,128)(2,1)S(1)}, u32[]{:S(2)}, u32[]{:S(2)}) collective-permute-start(bf16[512,128]{1,0:T(8,128)(2,1)S(1)} %shard_map.136), channel_id=1, source_target_pairs={{0,8},{1,9},{2,10},{3,11},{4,12},{5,13},{6,14},{7,15},{8,0},{9,1},... | collective-permute-start | bytes 393224 | tf_op jit(solution)/shard_map/ppermute | solution.py:451
  39.0 12.5 %collective-permute-start.15 = (bf16[512,128]{1,0:T(8,128)(2,1)S(1)}, bf16[512,128]{1,0:T(8,128)(2,1)S(1)}, u32[]{:S(2)}, u32[]{:S(2)}) collective-permute-start(bf16[512,128]{1,0:T(8,128)(2,1)S(1)} %shard_map.133.refs_0_), channel_id=1, source_target_pairs={{0,8},{1,9},{2,10},{3,11},{4,12},{5,13},{6,14},{7,15},{8,0},{9,1},... | collective-permute-start | bytes 393224 | tf_op jit(solution)/shard_map/ppermute | solution.py:451
  41.4 9.0 %collective-permute-start.14 = (bf16[1024,128]{1,0:T(8,128)(2,1)S(1)}, bf16[1024,128]{1,0:T(8,128)(2,1)S(1)}, u32[]{:S(2)}, u32[]{:S(2)}) collective-permute-start(bf16[1024,128]{1,0:T(8,128)(2,1)S(1)} %shard_map.135), channel_id=1, source_target_pairs={{0,2},{1,3},{2,0},{3,1},{4,6},{5,7},{6,4},{7,5},{8,10},{9,11},{10,... | collective-permute-start | bytes 786440 | tf_op jit(solution)/shard_map/ppermute | solution.py:451

commit v9 on v8

--- a/solution.py
+++ b/solution.py
@@ -212,7 +212,8 @@
     me_ref, left_refs, right_refs, sig_refs = refs[0], refs[1:5], refs[5:9], refs[9:13]
     own_ref, core_in, far_in, block_ref, mid_ref = refs[13:18]
     pieces = [(own_ref, 0), (core_in, 0), (far_in, 0), (core_in, HEAD)]
-    out_refs, pairs_ref = refs[18:22], refs[22]
+    own_out, near_out, far_out, pairs_ref = refs[18:22]
+    outs = [(own_out, 0), (near_out, 0), (far_out, 0), (far_out, PIECE)]
     me = me_ref[0]
     of_quarter = quarters()
 
@@ -260,7 +261,8 @@
     for m in range(4):
         sig = sig_refs[m][...]
         out = sig * update[:, m * 128 : (m + 1) * 128]
-        out_refs[m][...] = out.astype(BF16)
+        ref, at = outs[m]
+        ref[at : at + PIECE, :] = out.astype(BF16)
         ref, at = pieces[m]
         cot = ref[at : at + PIECE, :].astype(F32)
         grad_update.append((cot * sig).astype(BF16))
@@ -289,7 +291,7 @@
 
 def grad_right_kernel(half):
     def kernel(pairs_ref, *refs):
-        left_refs, out_refs = refs[:4], refs[4:]
+        left_refs, out_refs = refs[:4], refs[-4:]
         of_quarter = quarters()
         for g in range(GROUPS // 2):
             spread = spread_group(pairs_ref, half * GROUPS // 2 + g, of_quarter)
@@ -301,15 +303,13 @@
 
 
 def grad_left_kernel(pairs_ref, *refs):
-    right_refs, (out_near, out_both), lefts = refs[:4], refs[4:6], refs[7:]
+    right_refs, lefts = refs[:4], refs[5:]
     of_quarter = quarters()
     for g in range(GROUPS):
         spread = spread_group(pairs_ref, g, of_quarter)
         grad = dot(spread, slab(right_refs, g), NN).astype(BF16)
         for m, ref in enumerate(lefts):
             ref[g * 32 : (g + 1) * 32, :] = grad[m * 32 : (m + 1) * 32]
-    lefts[1][SIDE:, :] = out_near[...]
-    lefts[3][SIDE:, :] = out_both[...]
 
 
 def halves_kernel(x_ref, first_ref, second_ref):
@@ -341,10 +341,10 @@
     both_ref[SIDE // 2 :, :] = second_ref[...]
 
 
-def add_left_kernel(mine_ref, piece_ref, got_ref, sum_ref, out_ref):
-    sum_ref[...] = (mine_ref[...].astype(F32) + got_ref[:SIDE, :].astype(F32)).astype(BF16)
-    out_ref[:PIECE, :] = piece_ref[...]
-    out_ref[PIECE:, :] = got_ref[SIDE:, :]
+def back_kernel(left_ref, own_ref, far_ref, after_ref, both_ref):
+    both_ref[:SIDE, :] = left_ref[...]
+    both_ref[SIDE : SIDE + PIECE, :] = own_ref[...]
+    both_ref[SIDE + PIECE :, :] = far_ref[PIECE:, :]
 
 
 def factor_kernel(
@@ -383,7 +383,7 @@
 
 
 def out_kernel(me_ref, own_ref, near_ref, far_ref, open_ref, weight_ref, out_ref, grad_ref, full_ref):
-    places = [(own_ref, 0), (near_ref, SIDE), (far_ref, 0), (far_ref, PIECE)]
+    places = [(own_ref, 0), (near_ref, SIDE), (far_ref, 0), (near_ref, SIDE + PIECE)]
     for (ref, at), offset in zip(places, LEFT_OFFSETS):
         piece = ref[at : at + PIECE, :].astype(F32).reshape(ROWS, 4, ROWS, 128)
         for n, start in enumerate(columns_of(me_ref[0] ^ offset, RIGHT_OFFSETS)):
@@ -467,7 +467,7 @@
     half = SIDE // 2
     cube = (ROWS, 128, 128)
     side, piece = ((SIDE, 128), BF16), ((PIECE, 128), BF16)
-    halves, core = ((half, 128), BF16), ((SIDE + PIECE, 128), BF16)
+    halves, core = ((half, 128), BF16), ((SIDE + 2 * PIECE, 128), BF16)
     sig = ((PIECE, 128), F32)
     rows_scratch = pltpu.VMEM((2, SIDE, 128), F32)
     cube_scratch = pltpu.VMEM(cube, F32)
@@ -516,7 +516,7 @@
     )
     far_got = swap(far_piece, Z_LOW)
     both = swap(far, CORE)
-    x_second = swap(z_second, CHIP_X)
+    x_second = swap(after(z_second, left_0), CHIP_X)
     x_first = swap(after(z_first, x_second, left_0), CHIP_X)
     (joined,) = call(join_kernel, [((2 * HEAD, 128), BF16)], vmem=[core_piece, far_got])
     core_pieces = swap(joined, CORE)
@@ -543,39 +543,34 @@
     right_3 = right_half(0, True, x_first, weight_t, params, right_part)
 
     lefts, rights = [left_0, left_1, left_2, left_3], [right_0, right_1, right_2, right_3]
-    out_0, out_1, out_2, out_3, pairs = call(
+    out_0, out_1, out_far, pairs = call(
         block_kernel,
-        [piece] * 4 + [((SIDE, 128), F32)],
+        [piece, piece, ((2 * PIECE, 128), BF16), ((SIDE, 128), F32)],
         smem=[me],
         vmem=lefts
         + rights
         + [sig_0, sig_1, sig_2, sig_3]
         + [own_piece, core_pieces, far_got, block_weight, mid],
     )
+    out_far = swap(out_far, Z_LOW)
     right_a = call(grad_right_kernel(0), [halves] * 4, vmem=[pairs, *lefts])
     x_got = [swap(right_a[3], CHIP_X)]
-    grad_left_0, near_back, grad_left_2, both_back = call(
-        grad_left_kernel,
-        [side, core, side, core],
-        vmem=[pairs, *rights, out_1, out_3, right_a[3]],
-    )
-    both_got = swap(both_back, CORE)
-    right_b = call(grad_right_kernel(1), [halves] * 4, vmem=[pairs, *lefts], weight=WAIT)
-    left_sum, out_far = call(
-        add_left_kernel,
-        [side, ((2 * PIECE, 128), BF16)],
-        vmem=[grad_left_2, out_2, both_got],
-    )
-    x_got.append(swap(after(right_b[3], left_sum), CHIP_X))
-    near_got = swap(after(near_back, left_sum), CORE)
-    (left_part,) = call(early_kernel, [((SIDE, 128), F32)], vmem=[grad_left_0, near_got])
+    left_parts = call(
+        grad_left_kernel, [side] * 4, vmem=[pairs, *rights, right_a[3]]
+    )
+    both_got = swap(left_parts[3], CORE)
+    (left_sum,) = call(add_kernel, [side], vmem=[left_parts[2], both_got])
     left_got = swap(left_sum, Z_LOW)
-    out_far = swap(out_far, Z_LOW)
     (total,) = call(add_kernel, [halves], vmem=[right_a[2], x_got[0], left_sum])
     z_got = [swap(total, Z_HIGH)]
+    right_b = call(grad_right_kernel(1), [halves] * 4, vmem=[pairs, *lefts], weight=WAIT)
+    x_got.append(swap(after(right_b[3], left_sum), CHIP_X))
     (total,) = call(add_kernel, [halves], vmem=[right_b[2], x_got[1], left_sum])
     z_got.append(swap(total, Z_HIGH))
-    (right_back,) = call(near_kernel, [side], vmem=[right_a[1], right_b[1], total, left_part])
+    (near_back,) = call(back_kernel, [core], vmem=[left_parts[1], out_1, out_far, total])
+    near_got = swap(near_back, CORE)
+    (left_part,) = call(early_kernel, [((SIDE, 128), F32)], vmem=[left_parts[0], near_got])
+    (right_back,) = call(near_kernel, [side], vmem=[right_a[1], right_b[1], total])
     right_near = swap(right_back, CHIP_X)
 
     factors, normed, inverse, open_part, gain_t = call(

time: 53 us -> 62.7 us (1.18)
  waiting for transfers between devices: 10.1 us -> 21.8 us
  starting transfers between devices: 23.5 us -> 21.5 us
    ppermute x19, waiting for transfers between devices: 10.1 us -> 21.8 us  [swap(): return lax.ppermute(values, 'row', [(s, s ^ offset) for s in range(16)])]
    ppermute x19, starting transfers between devices: 23.5 us -> 21.5 us  [swap(): return lax.ppermute(values, 'row', [(s, s ^ offset) for s in range(16)])]
    pallas_call x26 -> x27, Pallas kernels: 15.7 us -> 15.6 us  [call(): pl.pallas_call(kernel, out_shape=[jax.ShapeDtypeStruct(s, d) for s, d in...]
  transfers between devices with their start and end apart: 19 -> 19, of which waited for: 7 -> 8; matrix products, arithmetic and copies ran while one was open for 3% -> 3% of each run, Pallas kernels for 21% -> 18%
where the time goes in v9:
time: 62.7 us; the launch traced here: 62.5 us
  waiting for transfers between devices  21.8 us (35%)
  starting transfers between devices  21.5 us (34%)
  Pallas kernels  15.6 us (25%)
  other arithmetic  1.68 us (3%)
  local copies, waits for them, and re-layouts  0.95 us (2%)
  between operations  0.9 us (1%)
    ppermute x19, waiting for transfers between devices, swap(): return lax.ppermute(values, 'row', [(s, s ^ offset) for s in range(16)])  21.8 us
    ppermute x19, starting transfers between devices, swap(): return lax.ppermute(values, 'row', [(s, s ^ offset) for s in range(16)])  21.5 us
    pallas_call x27, Pallas kernels, call(): pl.pallas_call(kernel, out_shape=[jax.ShapeDtypeStruct(s, d) for s, d in...  15.6 us
  transfers between devices with their start and end apart: 19, of which 8 were waited for; matrix products, arithmetic and copies ran while one was open for 3% of the time, Pallas kernels for 18%

profile of v9, /device:TPU:0, one launch (start us, length us, event | category | flops | bytes accessed | tf_op | source)
XLA Modules:
  0.0 62.5 jit_solution(11720980182373741906)
XLA Ops:
  0.6 0.0 copy-start
  0.6 0.9 %copy-done = bf16[8,128,128]{2,1,0:T(8,128)(2,1)S(1)} copy-done((bf16[8,128,128]{2,1,0:T(8,128)(2,1)S(1)}, bf16[8,128,128]{2,1,0:T(8,128)(2,1)}, u32[]{:S(2)}) %copy-start) | copy-done | bytes 262168
  1.6 3.0 %collective-permute-start.1 = (bf16[1024,128]{1,0:T(8,128)(2,1)S(1)}, bf16[1024,128]{1,0:T(8,128)(2,1)S(1)}, u32[]{:S(2)}, u32[]{:S(2)}) collective-permute-start(bf16[1024,128]{1,0:T(8,128)(2,1)S(1)} %shard_map.114.x_ref), channel_id=1, source_target_pairs={{0,2},{1,3},{2,0},{3,1},{4,6},{5,7},{6,4},{7,5},{8,10},{9,11},{10,... | collective-permute-start | bytes 786440 | tf_op jit(solution)/shard_map/ppermute | solution.py:451
  4.6 1.6 %collective-permute-start.2 = (bf16[1024,128]{1,0:T(8,128)(2,1)S(1)}, bf16[1024,128]{1,0:T(8,128)(2,1)S(1)}, u32[]{:S(2)}, u32[]{:S(2)}) collective-permute-start(bf16[1024,128]{1,0:T(8,128)(2,1)S(1)} %shard_map.114.x_ref), channel_id=1, source_target_pairs={{0,4},{1,5},{2,6},{3,7},{4,0},{5,1},{6,2},{7,3},{8,12},{9,13},{10,... | collective-permute-start | bytes 786440 | tf_op jit(solution)/shard_map/ppermute | solution.py:451
  6.2 2.6 %collective-permute-start.4 = (bf16[512,128]{1,0:T(8,128)(2,1)S(1)}, bf16[512,128]{1,0:T(8,128)(2,1)S(1)}, u32[]{:S(2)}, u32[]{:S(2)}) collective-permute-start(bf16[512,128]{1,0:T(8,128)(2,1)S(1)} %get-tuple-element.44.refs_0_), channel_id=1, source_target_pairs={{0,8},{1,9},{2,10},{3,11},{4,12},{5,13},{6,14},{7,15},{8,0},{9,1},... | collective-permute-start | bytes 393224 | tf_op jit(solution)/shard_map/ppermute | solution.py:451
  8.8 0.3 collective-permute-start.3
  9.1 1.0 %pad_add_fusion.weight_ref.refs_2_.refs_3_.refs_7_ = bf16[128,768]{1,0:T(8,128)(2,1)S(1)} fusion(bf16[128,128]{1,0:T(8,128)(2,1)} %param.19, bf16[128,128]{1,0:T(8,128)(2,1)} %param.16, bf16[128,512]{1,0:T(8,128)(2,1)} %param.15), kind=kLoop, calls=%fused_computation | loop fusion | flops 589824 | bytes 393216 | tf_op jit(solution)/shard_map/add | solution.py:481
  10.1 0.7 %pad_maximum_fusion.params_ref.refs_3_.refs_4_ = f32[4,128]{1,0:T(4,128)S(1)} fusion(f32[1,128]{1,0:T(1,128)} %bitcast.8, f32[1,128]{1,0:T(1,128)} %bitcast.9, f32[1,128]{1,0:T(1,128)} %bitcast.10, f32[1,128]{1,0:T(1,128)} %bitcast.11), kind=kLoop, calls=%fused_computation.1 | loop fusion | flops 1536 | bytes 4096 | tf_op jit(solution)/shard_map/stack | solution.py:482
  10.8 0.0 copy-start.1
  10.8 0.0 copy-start.2
  10.8 1.9 %shard_map.115 = (bf16[1024,128]{1,0:T(8,128)(2,1)S(1)}, bf16[1024,128]{1,0:T(8,128)(2,1)S(1)}, f32[256,128]{1,0:T(8,128)S(1)}, bf16[512,128]{1,0:T(8,128)(2,1)S...) custom-call(s32[1]{0:T(128)} %bitcast.me_ref.refs_0_, bf16[1024,128]{1,0:T(8,128)(2,1)S(1)} %shard_map.114.x_ref, ...), custom_call_target="tpu_custom_call" | custom-call | flops 5000000000 | bytes 262144 | tf_op jit(solution)/shard_map/pallas_call | solution.py:43
  12.7 3.0 %collective-permute-done.4.refs_1_.message_ref = bf16[512,128]{1,0:T(8,128)(2,1)S(1)} collective-permute-done((bf16[512,128]{1,0:T(8,128)(2,1)S(1)}, bf16[512,128]{1,0:T(8,128)(2,1)S(1)}, u32[]{:S(2)}, u32[]{:S(2)}) %collective-permute-start.4) | collective-permute-done | bytes 131104 | tf_op jit(solution)/shard_map/ppermute | solution.py:451
  15.8 0.6 collective-permute-start.6
  16.4 0.0 collective-permute-start
  16.4 4.1 %collective-permute-done.3.refs_0_.message_ref = bf16[512,128]{1,0:T(8,128)(2,1)S(1)} collective-permute-done((bf16[512,128]{1,0:T(8,128)(2,1)S(1)}, bf16[512,128]{1,0:T(8,128)(2,1)S(1)}, u32[]{:S(2)}, u32[]{:S(2)}) %collective-permute-start.3) | collective-permute-done | bytes 131104 | tf_op jit(solution)/shard_map/ppermute | solution.py:451
  20.5 1.4 %collective-permute-done.6.refs_0_.x_ref = bf16[512,128]{1,0:T(8,128)(2,1)S(1)} collective-permute-done((bf16[512,128]{1,0:T(8,128)(2,1)S(1)}, bf16[512,128]{1,0:T(8,128)(2,1)S(1)}, u32[]{:S(2)}, u32[]{:S(2)}) %collective-permute-start.6) | collective-permute-done | bytes 131104 | tf_op jit(solution)/shard_map/ppermute | solution.py:451
  21.9 0.1 collective-permute-start.7
  22.0 0.0 collective-permute-done.1.refs_0_.after_ref
  22.0 0.0 copy-done.1
  22.0 0.0 copy-done.2
  22.0 0.1 shard_map.123
  22.1 3.8 %collective-permute-start.8 = (bf16[544,128]{1,0:T(8,128)(2,1)S(1)}, bf16[544,128]{1,0:T(8,128)(2,1)S(1)}, u32[]{:S(2)}, u32[]{:S(2)}) collective-permute-start(bf16[544,128]{1,0:T(8,128)(2,1)S(1)} %get-tuple-element.60), channel_id=1, source_target_pairs={{0,4},{1,5},{2,6},{3,7},{4,0},{5,1},{6,2},{7,3},{8,12},{9,13},{10,... | collective-permute-start | bytes 417800 | tf_op jit(solution)/shard_map/ppermute | solution.py:451
  25.9 0.0 collective-permute-done.2.left_in
  25.9 0.0 collective-permute-start.5
  25.9 1.7 %shard_map.117 = (bf16[1024,128]{1,0:T(8,128)(2,1)S(1)}, bf16[1024,128]{1,0:T(8,128)(2,1)S(1)}, f32[256,128]{1,0:T(8,128)S(1)}) custom-call(s32[1]{0:T(128)} %bitcast.me_ref.refs_0_, bf16[1024,128]{1,0:T(8,128)(2,1)S(1)} %collective-permute-done.2.left_in, bf16[512,128]{1,0:T(8,128)(2,1)S(1)} %collective-permute-done.3.refs_0_.message_ref, ...), custom_call_target="tpu_custom_call" | custom-call | flops 5000000000 | bytes 262144 | tf_op jit(solution)/shard_map/pallas_call | solution.py:43
  27.6 0.0 collective-permute-done.left_in
  27.6 1.7 %shard_map.116 = (bf16[1024,128]{1,0:T(8,128)(2,1)S(1)}, bf16[1024,128]{1,0:T(8,128)(2,1)S(1)}, f32[256,128]{1,0:T(8,128)S(1)}) custom-call(s32[1]{0:T(128)} %bitcast.me_ref.refs_0_, bf16[1024,128]{1,0:T(8,128)(2,1)S(1)} %collective-permute-done.left_in, bf16[1024,128]{1,0:T(8,128)(2,1)S(1)} %collective-permute-done.1.refs_0_.after_ref, ...), custom_call_target="tpu_custom_call" | custom-call | flops 5000000000 | bytes 262144 | tf_op jit(solution)/shard_map/pallas_call | solution.py:43
  29.3 0.0 collective-permute-done.8.got_ref.refs_15_
  29.3 0.6 collective-permute-start.9
  29.9 0.0 collective-permute-done.5.x_ref
  29.9 1.0 %shard_map.118 = (bf16[1024,128]{1,0:T(8,128)(2,1)S(1)}, f32[256,128]{1,0:T(8,128)S(1)}) custom-call(s32[1]{0:T(128)} %bitcast.me_ref.refs_0_, bf16[1024,128]{1,0:T(8,128)(2,1)S(1)} %collective-permute-done.5.x_ref, bf16[512,128]{1,0:T(8,128)(2,1)S(1)} %get-tuple-element.46.refs_1_.refs_2_.weight_t_ref, ...), custom_call_target="tpu_custom_call" | custom-call | flops 5000000000 | bytes 262144 | tf_op jit(solution)/shard_map/pallas_call | solution.py:43
  30.9 0.7 %shard_map.121.rest_ref = f32[1024,128]{1,0:T(8,128)S(1)} custom-call(bf16[512,128]{1,0:T(8,128)(2,1)S(1)} %collective-permute-done.6.refs_0_.x_ref, bf16[512,128]{1,0:T(8,128)(2,1)S(1)} %get-tuple-element.46.refs_1_.refs_2_.weight_t_ref, f32[4,128]{1,0:T(4,128)S(1)} %pad_maximum_fusion.params_ref.refs_3_.refs_4_, ...), custom_call_target="tpu_custom_call" | custom-call | flops 1250000000 | bytes 262144 | tf_op jit(solution)/shard_map/pallas_call | solution.py:43
  31.6 0.0 collective-permute-done.7.x_ref
  31.6 0.7 %shard_map.122.refs_8_.refs_3_ = bf16[1024,128]{1,0:T(8,128)(2,1)S(1)} custom-call(bf16[512,128]{1,0:T(8,128)(2,1)S(1)} %collective-permute-done.7.x_ref, bf16[512,128]{1,0:T(8,128)(2,1)S(1)} %get-tuple-element.46.refs_1_.refs_2_.weight_t_ref, f32[4,128]{1,0:T(4,128)S(1)} %pad_maximum_fusion.params_ref.refs_3_.refs_4_, f32[1024,128]{1,0:T(8,128)S(1)} %shard_map.121.rest_ref), custom_call_target="tpu_custom_call" | custom-call | flops 1250000000 | bytes 262144 | tf_op jit(solution)/shard_map/pallas_call | solution.py:43
  32.3 0.0 collective-permute-done.9.refs_14_
  32.3 2.2 %shard_map.125 = (bf16[256,128]{1,0:T(8,128)(2,1)S(1)}, bf16[256,128]{1,0:T(8,128)(2,1)S(1)}, bf16[512,128]{1,0:T(8,128)(2,1)S(1)}, f32[1024,128]{1,0:T(8,128)S(1)}) custom-call(s32[1]{0:T(128)} %bitcast.me_ref.refs_0_, bf16[1024,128]{1,0:T(8,128)(2,1)S(1)} %get-tuple-element.45.refs_0_.refs_1_, bf16[1024,128]{1,0:T(8,128)(2,1)S(1)} %get-tuple-element.47.refs_2_.refs_1_, ...), custom_call_target="tpu_custom_call" | custom-call | flops 67108864 | bytes 262144 | tf_op jit(solution)/shard_map/pallas_call | solution.py:43
  34.5 0.4 shard_map.126
  34.9 0.4 shard_map.127
  35.3 2.1 %collective-permute-start.17 = (bf16[512,128]{1,0:T(8,128)(2,1)S(1)}, bf16[512,128]{1,0:T(8,128)(2,1)S(1)}, u32[]{:S(2)}, u32[]{:S(2)}) collective-permute-start(bf16[512,128]{1,0:T(8,128)(2,1)S(1)} %get-tuple-element.65.refs_4_), channel_id=1, source_target_pairs={{0,2},{1,3},{2,0},{3,1},{4,6},{5,7},{6,4},{7,5},{8,10},{9,11},{10,... | collective-permute-start | bytes 393224 | tf_op jit(solution)/shard_map/ppermute | solution.py:451
  37.4 0.0 collective-permute-start.11
  37.4 0.3 shard_map.128
  37.7 1.2 %collective-permute-done.11.got_ref = bf16[1024,128]{1,0:T(8,128)(2,1)S(1)} collective-permute-done((bf16[1024,128]{1,0:T(8,128)(2,1)S(1)}, bf16[1024,128]{1,0:T(8,128)(2,1)S(1)}, u32[]{:S(2)}, u32[]{:S(2)}) %collective-permute-start.11) | collective-permute-done | bytes 262176 | tf_op jit(solution)/shard_map/ppermute | solution.py:451
  38.9 0.1 shard_map.129.refs_0_
  39.0 0.1 collective-permute-start.12
  39.1 1.3 %collective-permute-start.10 = (bf16[512,128]{1,0:T(8,128)(2,1)S(1)}, bf16[512,128]{1,0:T(8,128)(2,1)S(1)}, u32[]{:S(2)}, u32[]{:S(2)}) collective-permute-start(bf16[512,128]{1,0:T(8,128)(2,1)S(1)} %get-tuple-element.68), channel_id=1, source_target_pairs={{0,4},{1,5},{2,6},{3,7},{4,0},{5,1},{6,2},{7,3},{8,12},{9,13},{10,... | collective-permute-start | bytes 393224 | tf_op jit(solution)/shard_map/ppermute | solution.py:451
  40.4 0.7 %collective-permute-start.16 = (bf16[1024,128]{1,0:T(8,128)(2,1)S(1)}, bf16[1024,128]{1,0:T(8,128)(2,1)S(1)}, u32[]{:S(2)}, u32[]{:S(2)}) collective-permute-start(bf16[1024,128]{1,0:T(8,128)(2,1)S(1)} %shard_map.129.refs_0_), channel_id=1, source_target_pairs={{0,4},{1,5},{2,6},{3,7},{4,0},{5,1},{6,2},{7,3},{8,12},{9,13},{10,... | collective-permute-start | bytes 786440 | tf_op jit(solution)/shard_map/ppermute | solution.py:451
  41.2 0.0 collective-permute-done.17.got_ref
  41.2 1.5 %collective-permute-start.18 = (bf16[512,128]{1,0:T(8,128)(2,1)S(1)}, bf16[512,128]{1,0:T(8,128)(2,1)S(1)}, u32[]{:S(2)}, u32[]{:S(2)}) collective-permute-start(bf16[512,128]{1,0:T(8,128)(2,1)S(1)} %shard_map.137), channel_id=1, source_target_pairs={{0,8},{1,9},{2,10},{3,11},{4,12},{5,13},{6,14},{7,15},{8,0},{9,1},... | collective-permute-start | bytes 393224 | tf_op jit(solution)/shard_map/ppermute | solution.py:451
  42.7 1.9 %collective-permute-done.12.got_ref = bf16[512,128]{1,0:T(8,128)(2,1)S(1)} collective-permute-done((bf16[512,128]{1,0:T(8,128)(2,1)S(1)}, bf16[512,128]{1,0:T(8,128)(2,1)S(1)}, u32[]{:S(2)}, u32[]{:S(2)}) %collective-permute-start.12) | collective-permute-done | bytes 131104 | tf_op jit(solution)/shard_map/ppermute | solution.py:451
  44.6 1.2 %collective-permute-start.15 = (bf16[512,128]{1,0:T(8,128)(2,1)S(1)}, bf16[512,128]{1,0:T(8,128)(2,1)S(1)}, u32[]{:S(2)}, u32[]{:S(2)}) collective-permute-start(bf16[512,128]{1,0:T(8,128)(2,1)S(1)} %shard_map.131.after_ref.refs_0_), channel_id=1, source_target_pairs={{0,8},{1,9},{2,10},{3,11},{4,12},{5,13},{6,14},{7,15},{8,0},{9,1},... | collective-permute-start | bytes 393224 | tf_op jit(solution)/shard_map/ppermute | solution.py:451
  45.8 5.2 %collective-permute-done.10.far_ref = bf16[512,128]{1,0:T(8,128)(2,1)S(1)} collective-permute-done((bf16[512,128]{1,0:T(8,128)(2,1)S(1)}, bf16[512,128]{1,0:T(8,128)(2,1)S(1)}, u32[]{:S(2)}, u32[]{:S(2)}) %collective-permute-start.10) | collective-permute-done | bytes 131104 | tf_op jit(solution)/shard_map/ppermute | solution.py:451
  51.1 0.1 collective-permute-start.13
  51.2 2.0 %collective-permute-start.14 = (bf16[1024,128]{1,0:T(8,128)(2,1)S(1)}, bf16[1024,128]{1,0:T(8,128)(2,1)S(1)}, u32[]{:S(2)}, u32[]{:S(2)}) collective-permute-start(bf16[1024,128]{1,0:T(8,128)(2,1)S(1)} %shard_map.135), channel_id=1, source_target_pairs={{0,2},{1,3},{2,0},{3,1},{4,6},{5,7},{6,4},{7,5},{8,10},{9,11},{10,... | collective-permute-start | bytes 786440 | tf_op jit(solution)/shard_map/ppermute | solution.py:451
  53.2 1.1 %shard_map.133 = (f32[8,512,128]{2,1,0:T(8,128)S(1)}, f32[8,128,128]{2,1,0:T(8,128)S(1)}, f32[8,128]{1,0:T(8,128)S(1)}, f32[8,128,128]{2,1,0:T(8,128)S(1)}, f32[128,128]{1,0:T(8,128)S(1)}) custom-call(bf16[1024,128]{1,0:T(8,128)(2,1)S(1)} %shard_map.114.x_ref, bf16[8,128,128]{2,1,0:T(8,128)(2,1)S(1)} %copy-done.1, s32[8,128]{1,0:T(8,128)S(1)} %copy-done.2, ...), custom_call_target="tpu_custom_call" | custom-call | flops 5000000000 | bytes 262144 | tf_op jit(solution)/shard_map/pallas_call | solution.py:43
  54.3 0.0 collective-permute-done.13.near_ref.got_ref
  54.3 0.1 shard_map.136.refs_0_
  54.4 0.9 %shard_map.134 = (bf16[8,128,128]{2,1,0:T(8,128)(2,1)}, f32[8,128,128]{2,1,0:T(8,128)S(1)}) custom-call(s32[1]{0:T(128)} %bitcast.me_ref.refs_0_, bf16[256,128]{1,0:T(8,128)(2,1)S(1)} %get-tuple-element.63.own_ref, bf16[1536,128]{1,0:T(8,128)(2,1)S(1)} %collective-permute-done.13.near_ref.got_ref, bf16[512,128]{1,0:T(8,128)(2,1)S(1)} %collective-permute-done.10.far_ref, ...), custom_call_target="tpu_custom_call" | custom-call | flops 67108864 | bytes 262144 | tf_op jit(solution)/shard_map/pallas_call | solution.py:43
  55.3 0.0 collective-permute-done.18.refs_4_
  55.3 0.6 %collective-permute-done.16.refs_1_ = bf16[1024,128]{1,0:T(8,128)(2,1)S(1)} collective-permute-done((bf16[1024,128]{1,0:T(8,128)(2,1)S(1)}, bf16[1024,128]{1,0:T(8,128)(2,1)S(1)}, u32[]{:S(2)}, u32[]{:S(2)}) %collective-permute-start.16) | collective-permute-done | bytes 262176 | tf_op jit(solution)/shard_map/ppermute | solution.py:451
  55.9 4.3 %collective-permute-done.14.refs_3_.near_ref = bf16[1024,128]{1,0:T(8,128)(2,1)S(1)} collective-permute-done((bf16[1024,128]{1,0:T(8,128)(2,1)S(1)}, bf16[1024,128]{1,0:T(8,128)(2,1)S(1)}, u32[]{:S(2)}, u32[]{:S(2)}) %collective-permute-start.14) | collective-permute-done | bytes 262176 | tf_op jit(solution)/shard_map/ppermute | solution.py:451
  60.2 1.0 %shard_map.138.sum_ref = f32[8,128,128]{2,1,0:T(8,128)S(1)} custom-call(f32[1024,128]{1,0:T(8,128)S(1)} %shard_map.136.refs_0_, bf16[1024,128]{1,0:T(8,128)(2,1)S(1)} %collective-permute-done.16.refs_1_, bf16[512,128]{1,0:T(8,128)(2,1)S(1)} %get-tuple-element.80.refs_2_, bf16[1024,128]{1,0:T(8,128)(2,1)S(1)} %collective-permute-done.14.refs_3_.near_ref, ...), custom_call_target="tpu_custom_call" | custom-call | flops 1250000000 | bytes 262144 | tf_op jit(solution)/shard_map/pallas_call | solution.py:43
  61.2 0.0 collective-permute-done.15.got_ref
  61.2 1.3 %shard_map.139 = bf16[8,128,128]{2,1,0:T(8,128)(2,1)} custom-call(bf16[512,128]{1,0:T(8,128)(2,1)S(1)} %get-tuple-element.75.own_ref, bf16[1024,128]{1,0:T(8,128)(2,1)S(1)} %collective-permute-done.14.refs_3_.near_ref, bf16[512,128]{1,0:T(8,128)(2,1)S(1)} %collective-permute-done.15.got_ref, f32[8,512,128]{2,1,0:T(8,128)S(1)} %get-tuple-element.78.refs_5_.factor_ref, ...), custom_call_target="tpu_custom_call" | custom-call | flops 67108864 | bytes 262144 | tf_op jit(solution)/shard_map/pallas_call | solution.py:43
  (10 shorter events, 0.2 us)
Async XLA Ops:
  0.6 1.0 %copy-start = (bf16[8,128,128]{2,1,0:T(8,128)(2,1)S(1)}, bf16[8,128,128]{2,1,0:T(8,128)(2,1)}, u32[]{:S(2)}) copy-start(bf16[8,128,128]{2,1,0:T(8,128)(2,1)} %param.10) | copy-start | bytes 786436
  1.6 20.4 %collective-permute-start.1 = (bf16[1024,128]{1,0:T(8,128)(2,1)S(1)}, bf16[1024,128]{1,0:T(8,128)(2,1)S(1)}, u32[]{:S(2)}, u32[]{:S(2)}) collective-permute-start(bf16[1024,128]{1,0:T(8,128)(2,1)S(1)} %shard_map.114.x_ref), channel_id=1, source_target_pairs={{0,2},{1,3},{2,0},{3,1},{4,6},{5,7},{6,4},{7,5},{8,10},{9,11},{10,... | collective-permute-start | bytes 786440 | tf_op jit(solution)/shard_map/ppermute | solution.py:451
  4.6 21.3 %collective-permute-start.2 = (bf16[1024,128]{1,0:T(8,128)(2,1)S(1)}, bf16[1024,128]{1,0:T(8,128)(2,1)S(1)}, u32[]{:S(2)}, u32[]{:S(2)}) collective-permute-start(bf16[1024,128]{1,0:T(8,128)(2,1)S(1)} %shard_map.114.x_ref), channel_id=1, source_target_pairs={{0,4},{1,5},{2,6},{3,7},{4,0},{5,1},{6,2},{7,3},{8,12},{9,13},{10,... | collective-permute-start | bytes 786440 | tf_op jit(solution)/shard_map/ppermute | solution.py:451
  6.2 9.6 %collective-permute-start.4 = (bf16[512,128]{1,0:T(8,128)(2,1)S(1)}, bf16[512,128]{1,0:T(8,128)(2,1)S(1)}, u32[]{:S(2)}, u32[]{:S(2)}) collective-permute-start(bf16[512,128]{1,0:T(8,128)(2,1)S(1)} %get-tuple-element.44.refs_0_), channel_id=1, source_target_pairs={{0,8},{1,9},{2,10},{3,11},{4,12},{5,13},{6,14},{7,15},{8,0},{9,1},... | collective-permute-start | bytes 393224 | tf_op jit(solution)/shard_map/ppermute | solution.py:451
  8.8 11.7 %collective-permute-start.3 = (bf16[512,128]{1,0:T(8,128)(2,1)S(1)}, bf16[512,128]{1,0:T(8,128)(2,1)S(1)}, u32[]{:S(2)}, u32[]{:S(2)}) collective-permute-start(bf16[512,128]{1,0:T(8,128)(2,1)S(1)} %get-tuple-element.48), channel_id=1, source_target_pairs={{0,8},{1,9},{2,10},{3,11},{4,12},{5,13},{6,14},{7,15},{8,0},{9,1},... | collective-permute-start | bytes 393224 | tf_op jit(solution)/shard_map/ppermute | solution.py:451
  10.8 11.2 %copy-start.1 = (bf16[8,128,128]{2,1,0:T(8,128)(2,1)S(1)}, bf16[8,128,128]{2,1,0:T(8,128)(2,1)}, u32[]{:S(2)}) copy-start(bf16[8,128,128]{2,1,0:T(8,128)(2,1)} %cot_ref.3) | copy-start | bytes 786436
  10.8 11.2 %copy-start.2 = (s32[8,128]{1,0:T(8,128)S(1)}, s32[8,128]{1,0:T(8,128)}, u32[]{:S(2)}) copy-start(s32[8,128]{1,0:T(8,128)} %mask_ref.3) | copy-start | bytes 12292
  15.8 6.1 %collective-permute-start.6 = (bf16[512,128]{1,0:T(8,128)(2,1)S(1)}, bf16[512,128]{1,0:T(8,128)(2,1)S(1)}, u32[]{:S(2)}, u32[]{:S(2)}) collective-permute-start(bf16[512,128]{1,0:T(8,128)(2,1)S(1)} %shard_map.119), channel_id=1, source_target_pairs={{0,2},{1,3},{2,0},{3,1},{4,6},{5,7},{6,4},{7,5},{8,10},{9,11},{10,... | collective-permute-start | bytes 393224 | tf_op jit(solution)/shard_map/ppermute | solution.py:451
  16.4 11.2 %collective-permute-start = (bf16[1024,128]{1,0:T(8,128)(2,1)S(1)}, bf16[1024,128]{1,0:T(8,128)(2,1)S(1)}, u32[]{:S(2)}, u32[]{:S(2)}) collective-permute-start(bf16[1024,128]{1,0:T(8,128)(2,1)S(1)} %shard_map.114.x_ref), channel_id=1, source_target_pairs={{0,1},{1,0},{2,3},{3,2},{4,5},{5,4},{6,7},{7,6},{8,9},{9,8},{10,11... | collective-permute-start | bytes 786440 | tf_op jit(solution)/shard_map/ppermute | solution.py:451
  21.9 9.7 %collective-permute-start.7 = (bf16[512,128]{1,0:T(8,128)(2,1)S(1)}, bf16[512,128]{1,0:T(8,128)(2,1)S(1)}, u32[]{:S(2)}, u32[]{:S(2)}) collective-permute-start(bf16[512,128]{1,0:T(8,128)(2,1)S(1)} %shard_map.120), channel_id=1, source_target_pairs={{0,2},{1,3},{2,0},{3,1},{4,6},{5,7},{6,4},{7,5},{8,10},{9,11},{10,... | collective-permute-start | bytes 393224 | tf_op jit(solution)/shard_map/ppermute | solution.py:451
  22.1 7.2 %collective-permute-start.8 = (bf16[544,128]{1,0:T(8,128)(2,1)S(1)}, bf16[544,128]{1,0:T(8,128)(2,1)S(1)}, u32[]{:S(2)}, u32[]{:S(2)}) collective-permute-start(bf16[544,128]{1,0:T(8,128)(2,1)S(1)} %get-tuple-element.60), channel_id=1, source_target_pairs={{0,4},{1,5},{2,6},{3,7},{4,0},{5,1},{6,2},{7,3},{8,12},{9,13},{10,... | collective-permute-start | bytes 417800 | tf_op jit(solution)/shard_map/ppermute | solution.py:451
  25.9 4.0 %collective-permute-start.5 = (bf16[1024,128]{1,0:T(8,128)(2,1)S(1)}, bf16[1024,128]{1,0:T(8,128)(2,1)S(1)}, u32[]{:S(2)}, u32[]{:S(2)}) collective-permute-start(bf16[1024,128]{1,0:T(8,128)(2,1)S(1)} %collective-permute-done.2.left_in), channel_id=1, source_target_pairs={{0,1},{1,0},{2,3},{3,2},{4,5},{5,4},{6,7},{7,6},{8,9},{9,8},{10,11... | collective-permute-start | bytes 786440 | tf_op jit(solution)/shard_map/ppermute | solution.py:451
  29.3 2.9 %collective-permute-start.9 = (bf16[544,128]{1,0:T(8,128)(2,1)S(1)}, bf16[544,128]{1,0:T(8,128)(2,1)S(1)}, u32[]{:S(2)}, u32[]{:S(2)}) collective-permute-start(bf16[544,128]{1,0:T(8,128)(2,1)S(1)} %shard_map.124), channel_id=1, source_target_pairs={{0,1},{1,0},{2,3},{3,2},{4,5},{5,4},{6,7},{7,6},{8,9},{9,8},{10,11... | collective-permute-start | bytes 417800 | tf_op jit(solution)/shard_map/ppermute | solution.py:451
  35.3 5.9 %collective-permute-start.17 = (bf16[512,128]{1,0:T(8,128)(2,1)S(1)}, bf16[512,128]{1,0:T(8,128)(2,1)S(1)}, u32[]{:S(2)}, u32[]{:S(2)}) collective-permute-start(bf16[512,128]{1,0:T(8,128)(2,1)S(1)} %get-tuple-element.65.refs_4_), channel_id=1, source_target_pairs={{0,2},{1,3},{2,0},{3,1},{4,6},{5,7},{6,4},{7,5},{8,10},{9,11},{10,... | collective-permute-start | bytes 393224 | tf_op jit(solution)/shard_map/ppermute | solution.py:451
  37.4 1.5 %collective-permute-start.11 = (bf16[1024,128]{1,0:T(8,128)(2,1)S(1)}, bf16[1024,128]{1,0:T(8,128)(2,1)S(1)}, u32[]{:S(2)}, u32[]{:S(2)}) collective-permute-start(bf16[1024,128]{1,0:T(8,128)(2,1)S(1)} %get-tuple-element.72), channel_id=1, source_target_pairs={{0,1},{1,0},{2,3},{3,2},{4,5},{5,4},{6,7},{7,6},{8,9},{9,8},{10,11... | collective-permute-start | bytes 786440 | tf_op jit(solution)/shard_map/ppermute | solution.py:451
  39.0 5.6 %collective-permute-start.12 = (bf16[512,128]{1,0:T(8,128)(2,1)S(1)}, bf16[512,128]{1,0:T(8,128)(2,1)S(1)}, u32[]{:S(2)}, u32[]{:S(2)}) collective-permute-start(bf16[512,128]{1,0:T(8,128)(2,1)S(1)} %shard_map.130), channel_id=1, source_target_pairs={{0,2},{1,3},{2,0},{3,1},{4,6},{5,7},{6,4},{7,5},{8,10},{9,11},{10,... | collective-permute-start | bytes 393224 | tf_op jit(solution)/shard_map/ppermute | solution.py:451
  39.1 11.9 %collective-permute-start.10 = (bf16[512,128]{1,0:T(8,128)(2,1)S(1)}, bf16[512,128]{1,0:T(8,128)(2,1)S(1)}, u32[]{:S(2)}, u32[]{:S(2)}) collective-permute-start(bf16[512,128]{1,0:T(8,128)(2,1)S(1)} %get-tuple-element.68), channel_id=1, source_target_pairs={{0,4},{1,5},{2,6},{3,7},{4,0},{5,1},{6,2},{7,3},{8,12},{9,13},{10,... | collective-permute-start | bytes 393224 | tf_op jit(solution)/shard_map/ppermute | solution.py:451
  40.4 15.5 %collective-permute-start.16 = (bf16[1024,128]{1,0:T(8,128)(2,1)S(1)}, bf16[1024,128]{1,0:T(8,128)(2,1)S(1)}, u32[]{:S(2)}, u32[]{:S(2)}) collective-permute-start(bf16[1024,128]{1,0:T(8,128)(2,1)S(1)} %shard_map.129.refs_0_), channel_id=1, source_target_pairs={{0,4},{1,5},{2,6},{3,7},{4,0},{5,1},{6,2},{7,3},{8,12},{9,13},{10,... | collective-permute-start | bytes 786440 | tf_op jit(solution)/shard_map/ppermute | solution.py:451
  41.2 14.1 %collective-permute-start.18 = (bf16[512,128]{1,0:T(8,128)(2,1)S(1)}, bf16[512,128]{1,0:T(8,128)(2,1)S(1)}, u32[]{:S(2)}, u32[]{:S(2)}) collective-permute-start(bf16[512,128]{1,0:T(8,128)(2,1)S(1)} %shard_map.137), channel_id=1, source_target_pairs={{0,8},{1,9},{2,10},{3,11},{4,12},{5,13},{6,14},{7,15},{8,0},{9,1},... | collective-permute-start | bytes 393224 | tf_op jit(solution)/shard_map/ppermute | solution.py:451
  44.6 16.6 %collective-permute-start.15 = (bf16[512,128]{1,0:T(8,128)(2,1)S(1)}, bf16[512,128]{1,0:T(8,128)(2,1)S(1)}, u32[]{:S(2)}, u32[]{:S(2)}) collective-permute-start(bf16[512,128]{1,0:T(8,128)(2,1)S(1)} %shard_map.131.after_ref.refs_0_), channel_id=1, source_target_pairs={{0,8},{1,9},{2,10},{3,11},{4,12},{5,13},{6,14},{7,15},{8,0},{9,1},... | collective-permute-start | bytes 393224 | tf_op jit(solution)/shard_map/ppermute | solution.py:451
  51.1 3.2 %collective-permute-start.13 = (bf16[1536,128]{1,0:T(8,128)(2,1)S(1)}, bf16[1536,128]{1,0:T(8,128)(2,1)S(1)}, u32[]{:S(2)}, u32[]{:S(2)}) collective-permute-start(bf16[1536,128]{1,0:T(8,128)(2,1)S(1)} %shard_map.132), channel_id=1, source_target_pairs={{0,1},{1,0},{2,3},{3,2},{4,5},{5,4},{6,7},{7,6},{8,9},{9,8},{10,11... | collective-permute-start | bytes 1179656 | tf_op jit(solution)/shard_map/ppermute | solution.py:451
  51.2 9.0 %collective-permute-start.14 = (bf16[1024,128]{1,0:T(8,128)(2,1)S(1)}, bf16[1024,128]{1,0:T(8,128)(2,1)S(1)}, u32[]{:S(2)}, u32[]{:S(2)}) collective-permute-start(bf16[1024,128]{1,0:T(8,128)(2,1)S(1)} %shard_map.135), channel_id=1, source_target_pairs={{0,2},{1,3},{2,0},{3,1},{4,6},{5,7},{6,4},{7,5},{8,10},{9,11},{10,... | collective-permute-start | bytes 786440 | tf_op jit(solution)/shard_map/ppermute | solution.py:451

commit v10 on v8

--- a/solution.py
+++ b/solution.py
@@ -331,12 +331,7 @@
     sum_ref[...] = (mine_ref[...].astype(F32) + got_ref[...].astype(F32)).astype(BF16)
 
 
-def early_kernel(mine_ref, got_ref, sum_ref):
-    sum_ref[...] = mine_ref[...].astype(F32) + got_ref[:SIDE, :].astype(F32)
-
-
-def near_kernel(first_ref, second_ref, *refs):
-    both_ref = refs[-1]
+def near_kernel(first_ref, second_ref, after_ref, both_ref):
     both_ref[: SIDE // 2, :] = first_ref[...]
     both_ref[SIDE // 2 :, :] = second_ref[...]
 
@@ -408,9 +403,10 @@
 
 
 def partial_kernel(*refs):
-    left_ref, left_got_ref, own_ref, near_ref, got_ref = refs[:5]
-    factor_ref, gate_ref, weight_ref, sum_ref, left_rows, right_rows = refs[5:]
-    left_rows[...] = left_ref[...] + left_got_ref[...].astype(F32)
+    left_refs, (own_ref, near_ref, got_ref) = refs[0:3], refs[3:6]
+    factor_ref, gate_ref, weight_ref, sum_ref, left_rows, right_rows = refs[6:]
+    left = [r[:SIDE, :].astype(F32) for r in left_refs]
+    left_rows[...] = left[0] + left[1] + left[2]
     right = own_ref[...].astype(F32) + near_ref[: SIDE // 2, :].astype(F32)
     right_rows[...] = right + got_ref[...].astype(F32)
     for row in range(ROWS):
@@ -567,16 +563,15 @@
         vmem=[grad_left_2, out_2, both_got],
     )
     x_got.append(swap(after(right_b[3], left_sum), CHIP_X))
-    near_got = swap(after(near_back, left_sum), CORE)
-    (left_part,) = call(early_kernel, [((SIDE, 128), F32)], vmem=[grad_left_0, near_got])
     left_got = swap(left_sum, Z_LOW)
     out_far = swap(out_far, Z_LOW)
     (total,) = call(add_kernel, [halves], vmem=[right_a[2], x_got[0], left_sum])
     z_got = [swap(total, Z_HIGH)]
     (total,) = call(add_kernel, [halves], vmem=[right_b[2], x_got[1], left_sum])
     z_got.append(swap(total, Z_HIGH))
-    (right_back,) = call(near_kernel, [side], vmem=[right_a[1], right_b[1], total, left_part])
+    (right_back,) = call(near_kernel, [side], vmem=[right_a[1], right_b[1], total])
     right_near = swap(right_back, CHIP_X)
+    near_got = swap(after(near_back, total), CORE)
 
     factors, normed, inverse, open_part, gain_t = call(
         factor_kernel,
@@ -595,7 +590,7 @@
     (partial,) = call(
         partial_kernel,
         [(cube, F32)],
-        vmem=[left_part, left_got, right_a[0], right_near, z_got[0]]
+        vmem=[grad_left_0, near_got, left_got, right_a[0], right_near, z_got[0]]
         + [factors, gate_part, weights],
         scratch=[pltpu.VMEM((SIDE, 128), F32), half_scratch],
         weight=WAIT // 4,

time: 53 us -> 52 us (0.981)
  waiting for transfers between devices: 10.1 us -> 9.3 us
    ppermute x19, waiting for transfers between devices: 10.1 us -> 9.3 us  [swap(): return lax.ppermute(values, 'row', [(s, s ^ offset) for s in range(16)])]
    pallas_call x26 -> x25, Pallas kernels: 15.7 us -> 15.6 us  [call(): pl.pallas_call(kernel, out_shape=[jax.ShapeDtypeStruct(s, d) for s, d in...]
  transfers between devices with their start and end apart: 19 -> 19, of which waited for: 7 -> 8; matrix products, arithmetic and copies ran while one was open for 3% -> 3% of each run, Pallas kernels for 21% -> 23%
where the time goes in v10:
time: 52 us; the launch traced here: 51.8 us
  starting transfers between devices  23.4 us (45%)
  Pallas kernels  15.6 us (30%)
  waiting for transfers between devices  9.3 us (18%)
  other arithmetic  1.67 us (3%)
  local copies, waits for them, and re-layouts  0.95 us (2%)
  between operations  0.84 us (2%)
    ppermute x19, starting transfers between devices, swap(): return lax.ppermute(values, 'row', [(s, s ^ offset) for s in range(16)])  23.4 us
    pallas_call x25, Pallas kernels, call(): pl.pallas_call(kernel, out_shape=[jax.ShapeDtypeStruct(s, d) for s, d in...  15.6 us
    ppermute x19, waiting for transfers between devices, swap(): return lax.ppermute(values, 'row', [(s, s ^ offset) for s in range(16)])  9.3 us
  transfers between devices with their start and end apart: 19, of which 8 were waited for; matrix products, arithmetic and copies ran while one was open for 3% of the time, Pallas kernels for 23%

profile of v10, /device:TPU:0, one launch (start us, length us, event | category | flops | bytes accessed | tf_op | source)
XLA Modules:
  0.0 51.8 jit_solution(4227892490485370929)
XLA Ops:
  0.6 0.0 copy-start
  0.6 0.9 %copy-done = bf16[8,128,128]{2,1,0:T(8,128)(2,1)S(1)} copy-done((bf16[8,128,128]{2,1,0:T(8,128)(2,1)S(1)}, bf16[8,128,128]{2,1,0:T(8,128)(2,1)}, u32[]{:S(2)}) %copy-start) | copy-done | bytes 262168
  1.6 4.1 %collective-permute-start.4 = (bf16[512,128]{1,0:T(8,128)(2,1)S(1)}, bf16[512,128]{1,0:T(8,128)(2,1)S(1)}, u32[]{:S(2)}, u32[]{:S(2)}) collective-permute-start(bf16[512,128]{1,0:T(8,128)(2,1)S(1)} %get-tuple-element.47.refs_0_), channel_id=1, source_target_pairs={{0,8},{1,9},{2,10},{3,11},{4,12},{5,13},{6,14},{7,15},{8,0},{9,1},... | collective-permute-start | bytes 393224 | tf_op jit(solution)/shard_map/ppermute | solution.py:447
  5.7 1.6 %collective-permute-start.2 = (bf16[1024,128]{1,0:T(8,128)(2,1)S(1)}, bf16[1024,128]{1,0:T(8,128)(2,1)S(1)}, u32[]{:S(2)}, u32[]{:S(2)}) collective-permute-start(bf16[1024,128]{1,0:T(8,128)(2,1)S(1)} %shard_map.114.x_ref), channel_id=1, source_target_pairs={{0,4},{1,5},{2,6},{3,7},{4,0},{5,1},{6,2},{7,3},{8,12},{9,13},{10,... | collective-permute-start | bytes 786440 | tf_op jit(solution)/shard_map/ppermute | solution.py:447
  7.4 1.5 %collective-permute-start.1 = (bf16[1024,128]{1,0:T(8,128)(2,1)S(1)}, bf16[1024,128]{1,0:T(8,128)(2,1)S(1)}, u32[]{:S(2)}, u32[]{:S(2)}) collective-permute-start(bf16[1024,128]{1,0:T(8,128)(2,1)S(1)} %shard_map.114.x_ref), channel_id=1, source_target_pairs={{0,2},{1,3},{2,0},{3,1},{4,6},{5,7},{6,4},{7,5},{8,10},{9,11},{10,... | collective-permute-start | bytes 786440 | tf_op jit(solution)/shard_map/ppermute | solution.py:447
  8.9 0.0 collective-permute-start
  8.9 0.3 collective-permute-start.3
  9.2 0.7 %pad_maximum_fusion.params_ref.refs_3_.refs_4_ = f32[4,128]{1,0:T(4,128)S(1)} fusion(f32[1,128]{1,0:T(1,128)} %bitcast.8, f32[1,128]{1,0:T(1,128)} %bitcast.9, f32[1,128]{1,0:T(1,128)} %bitcast.10, f32[1,128]{1,0:T(1,128)} %bitcast.11), kind=kLoop, calls=%fused_computation.1 | loop fusion | flops 1536 | bytes 4096 | tf_op jit(solution)/shard_map/stack | solution.py:478
  9.9 1.0 %pad_add_fusion.weight_ref.refs_2_.refs_3_.refs_8_ = bf16[128,768]{1,0:T(8,128)(2,1)S(1)} fusion(bf16[128,128]{1,0:T(8,128)(2,1)} %param.19, bf16[128,128]{1,0:T(8,128)(2,1)} %param.16, bf16[128,512]{1,0:T(8,128)(2,1)} %param.15), kind=kLoop, calls=%fused_computation | loop fusion | flops 589824 | bytes 393216 | tf_op jit(solution)/shard_map/add | solution.py:477
  10.9 1.2 %collective-permute-done.4.refs_1_ = bf16[512,128]{1,0:T(8,128)(2,1)S(1)} collective-permute-done((bf16[512,128]{1,0:T(8,128)(2,1)S(1)}, bf16[512,128]{1,0:T(8,128)(2,1)S(1)}, u32[]{:S(2)}, u32[]{:S(2)}) %collective-permute-start.4) | collective-permute-done | bytes 131104 | tf_op jit(solution)/shard_map/ppermute | solution.py:447
  12.1 1.6 %collective-permute-start.6 = (bf16[512,128]{1,0:T(8,128)(2,1)S(1)}, bf16[512,128]{1,0:T(8,128)(2,1)S(1)}, u32[]{:S(2)}, u32[]{:S(2)}) collective-permute-start(bf16[512,128]{1,0:T(8,128)(2,1)S(1)} %collective-permute-done.4.refs_1_), channel_id=1, source_target_pairs={{0,2},{1,3},{2,0},{3,1},{4,6},{5,7},{6,4},{7,5},{8,10},{9,11},{10,... | collective-permute-start | bytes 393224 | tf_op jit(solution)/shard_map/ppermute | solution.py:447
  13.7 0.0 copy-start.1
  13.7 0.0 copy-start.2
  13.7 1.9 %shard_map.115 = (bf16[1024,128]{1,0:T(8,128)(2,1)S(1)}, bf16[1024,128]{1,0:T(8,128)(2,1)S(1)}, f32[256,128]{1,0:T(8,128)S(1)}, bf16[512,128]{1,0:T(8,128)(2,1)S...) custom-call(s32[1]{0:T(128)} %bitcast.me_ref.refs_0_, bf16[1024,128]{1,0:T(8,128)(2,1)S(1)} %shard_map.114.x_ref, ...), custom_call_target="tpu_custom_call" | custom-call | flops 5000000000 | bytes 262144 | tf_op jit(solution)/shard_map/pallas_call | solution.py:43
  15.7 0.2 collective-permute-done.1.refs_0_.after_ref
  15.9 0.0 copy-done.1
  15.9 0.0 copy-done.2
  15.9 0.1 shard_map.122
  16.0 0.5 collective-permute-start.8
  16.5 1.0 %collective-permute-done.3.refs_0_.message_ref = bf16[512,128]{1,0:T(8,128)(2,1)S(1)} collective-permute-done((bf16[512,128]{1,0:T(8,128)(2,1)S(1)}, bf16[512,128]{1,0:T(8,128)(2,1)S(1)}, u32[]{:S(2)}, u32[]{:S(2)}) %collective-permute-start.3) | collective-permute-done | bytes 131104 | tf_op jit(solution)/shard_map/ppermute | solution.py:447
  17.5 0.2 collective-permute-done.6.refs_0_.x_ref
  17.7 1.9 %collective-permute-start.7 = (bf16[512,128]{1,0:T(8,128)(2,1)S(1)}, bf16[512,128]{1,0:T(8,128)(2,1)S(1)}, u32[]{:S(2)}, u32[]{:S(2)}) collective-permute-start(bf16[512,128]{1,0:T(8,128)(2,1)S(1)} %shard_map.119), channel_id=1, source_target_pairs={{0,2},{1,3},{2,0},{3,1},{4,6},{5,7},{6,4},{7,5},{8,10},{9,11},{10,... | collective-permute-start | bytes 393224 | tf_op jit(solution)/shard_map/ppermute | solution.py:447
  19.6 0.0 collective-permute-done.2.left_in
  19.6 0.0 collective-permute-start.5
  19.6 1.7 %shard_map.117 = (bf16[1024,128]{1,0:T(8,128)(2,1)S(1)}, bf16[1024,128]{1,0:T(8,128)(2,1)S(1)}, f32[256,128]{1,0:T(8,128)S(1)}) custom-call(s32[1]{0:T(128)} %bitcast.me_ref.refs_0_, bf16[1024,128]{1,0:T(8,128)(2,1)S(1)} %collective-permute-done.2.left_in, bf16[512,128]{1,0:T(8,128)(2,1)S(1)} %collective-permute-done.3.refs_0_.message_ref, ...), custom_call_target="tpu_custom_call" | custom-call | flops 5000000000 | bytes 262144 | tf_op jit(solution)/shard_map/pallas_call | solution.py:43
  21.3 0.0 collective-permute-done.left_in
  21.3 1.7 %shard_map.116 = (bf16[1024,128]{1,0:T(8,128)(2,1)S(1)}, bf16[1024,128]{1,0:T(8,128)(2,1)S(1)}, f32[256,128]{1,0:T(8,128)S(1)}) custom-call(s32[1]{0:T(128)} %bitcast.me_ref.refs_0_, bf16[1024,128]{1,0:T(8,128)(2,1)S(1)} %collective-permute-done.left_in, bf16[1024,128]{1,0:T(8,128)(2,1)S(1)} %collective-permute-done.1.refs_0_.after_ref, ...), custom_call_target="tpu_custom_call" | custom-call | flops 5000000000 | bytes 262144 | tf_op jit(solution)/shard_map/pallas_call | solution.py:43
  23.0 0.0 collective-permute-done.8.got_ref.refs_15_
  23.0 0.6 %collective-permute-start.9 = (bf16[544,128]{1,0:T(8,128)(2,1)S(1)}, bf16[544,128]{1,0:T(8,128)(2,1)S(1)}, u32[]{:S(2)}, u32[]{:S(2)}) collective-permute-start(bf16[544,128]{1,0:T(8,128)(2,1)S(1)} %shard_map.123), channel_id=1, source_target_pairs={{0,1},{1,0},{2,3},{3,2},{4,5},{5,4},{6,7},{7,6},{8,9},{9,8},{10,11... | collective-permute-start | bytes 417800 | tf_op jit(solution)/shard_map/ppermute | solution.py:447
  23.6 0.0 collective-permute-done.5.x_ref
  23.6 1.0 %shard_map.118 = (bf16[1024,128]{1,0:T(8,128)(2,1)S(1)}, f32[256,128]{1,0:T(8,128)S(1)}) custom-call(s32[1]{0:T(128)} %bitcast.me_ref.refs_0_, bf16[1024,128]{1,0:T(8,128)(2,1)S(1)} %collective-permute-done.5.x_ref, bf16[512,128]{1,0:T(8,128)(2,1)S(1)} %get-tuple-element.49.refs_1_.refs_2_.weight_t_ref, ...), custom_call_target="tpu_custom_call" | custom-call | flops 5000000000 | bytes 262144 | tf_op jit(solution)/shard_map/pallas_call | solution.py:43
  24.6 0.7 %shard_map.120.rest_ref = f32[1024,128]{1,0:T(8,128)S(1)} custom-call(bf16[512,128]{1,0:T(8,128)(2,1)S(1)} %collective-permute-done.6.refs_0_.x_ref, bf16[512,128]{1,0:T(8,128)(2,1)S(1)} %get-tuple-element.49.refs_1_.refs_2_.weight_t_ref, f32[4,128]{1,0:T(4,128)S(1)} %pad_maximum_fusion.params_ref.refs_3_.refs_4_, ...), custom_call_target="tpu_custom_call" | custom-call | flops 1250000000 | bytes 262144 | tf_op jit(solution)/shard_map/pallas_call | solution.py:43
  25.3 0.0 collective-permute-done.7.x_ref
  25.3 0.6 %shard_map.121.refs_8_.refs_3_ = bf16[1024,128]{1,0:T(8,128)(2,1)S(1)} custom-call(bf16[512,128]{1,0:T(8,128)(2,1)S(1)} %collective-permute-done.7.x_ref, bf16[512,128]{1,0:T(8,128)(2,1)S(1)} %get-tuple-element.49.refs_1_.refs_2_.weight_t_ref, f32[4,128]{1,0:T(4,128)S(1)} %pad_maximum_fusion.params_ref.refs_3_.refs_4_, f32[1024,128]{1,0:T(8,128)S(1)} %shard_map.120.rest_ref), custom_call_target="tpu_custom_call" | custom-call | flops 1250000000 | bytes 262144 | tf_op jit(solution)/shard_map/pallas_call | solution.py:43
  26.0 0.0 collective-permute-done.9.refs_14_
  26.0 2.2 %shard_map.124 = (bf16[256,128]{1,0:T(8,128)(2,1)S(1)}, bf16[256,128]{1,0:T(8,128)(2,1)S(1)}, bf16[256,128]{1,0:T(8,128)(2,1)S(1)}, bf16[256,128]{1,0:T(8,128)(2,1)S(1)}, f32[1024,128]{1,0:T(8,128)S(1)}) custom-call(s32[1]{0:T(128)} %bitcast.me_ref.refs_0_, bf16[1024,128]{1,0:T(8,128)(2,1)S(1)} %get-tuple-element.48.refs_1_.refs_0_, ...), custom_call_target="tpu_custom_call" | custom-call | flops 67108864 | bytes 262144 | tf_op jit(solution)/shard_map/pallas_call | solution.py:43
  28.2 0.3 shard_map.125
  28.6 1.5 %collective-permute-start.17 = (bf16[512,128]{1,0:T(8,128)(2,1)S(1)}, bf16[512,128]{1,0:T(8,128)(2,1)S(1)}, u32[]{:S(2)}, u32[]{:S(2)}) collective-permute-start(bf16[512,128]{1,0:T(8,128)(2,1)S(1)} %get-tuple-element.70.refs_6_), channel_id=1, source_target_pairs={{0,2},{1,3},{2,0},{3,1},{4,6},{5,7},{6,4},{7,5},{8,10},{9,11},{10,... | collective-permute-start | bytes 393224 | tf_op jit(solution)/shard_map/ppermute | solution.py:447
  30.1 0.4 shard_map.126
  30.5 0.1 collective-permute-start.10
  30.6 0.3 shard_map.127
  30.9 1.3 %collective-permute-done.10.got_ref = bf16[1280,128]{1,0:T(8,128)(2,1)S(1)} collective-permute-done((bf16[1280,128]{1,0:T(8,128)(2,1)S(1)}, bf16[1280,128]{1,0:T(8,128)(2,1)S(1)}, u32[]{:S(2)}, u32[]{:S(2)}) %collective-permute-start.10) | collective-permute-done | bytes 327712 | tf_op jit(solution)/shard_map/ppermute | solution.py:447
  32.2 0.1 shard_map.128
  32.3 0.7 %collective-permute-start.11 = (bf16[512,128]{1,0:T(8,128)(2,1)S(1)}, bf16[512,128]{1,0:T(8,128)(2,1)S(1)}, u32[]{:S(2)}, u32[]{:S(2)}) collective-permute-start(bf16[512,128]{1,0:T(8,128)(2,1)S(1)} %shard_map.129), channel_id=1, source_target_pairs={{0,2},{1,3},{2,0},{3,1},{4,6},{5,7},{6,4},{7,5},{8,10},{9,11},{10,... | collective-permute-start | bytes 393224 | tf_op jit(solution)/shard_map/ppermute | solution.py:447
  33.0 1.3 %collective-permute-start.13 = (bf16[512,128]{1,0:T(8,128)(2,1)S(1)}, bf16[512,128]{1,0:T(8,128)(2,1)S(1)}, u32[]{:S(2)}, u32[]{:S(2)}) collective-permute-start(bf16[512,128]{1,0:T(8,128)(2,1)S(1)} %get-tuple-element.78), channel_id=1, source_target_pairs={{0,4},{1,5},{2,6},{3,7},{4,0},{5,1},{6,2},{7,3},{8,12},{9,13},{10,... | collective-permute-start | bytes 393224 | tf_op jit(solution)/shard_map/ppermute | solution.py:447
  34.2 0.8 %collective-permute-start.16 = (bf16[1024,128]{1,0:T(8,128)(2,1)S(1)}, bf16[1024,128]{1,0:T(8,128)(2,1)S(1)}, u32[]{:S(2)}, u32[]{:S(2)}) collective-permute-start(bf16[1024,128]{1,0:T(8,128)(2,1)S(1)} %get-tuple-element.77.refs_0_), channel_id=1, source_target_pairs={{0,4},{1,5},{2,6},{3,7},{4,0},{5,1},{6,2},{7,3},{8,12},{9,13},{10,... | collective-permute-start | bytes 786440 | tf_op jit(solution)/shard_map/ppermute | solution.py:447
  35.0 0.0 collective-permute-done.17.got_ref
  35.0 3.4 %collective-permute-start.18 = (bf16[512,128]{1,0:T(8,128)(2,1)S(1)}, bf16[512,128]{1,0:T(8,128)(2,1)S(1)}, u32[]{:S(2)}, u32[]{:S(2)}) collective-permute-start(bf16[512,128]{1,0:T(8,128)(2,1)S(1)} %shard_map.135), channel_id=1, source_target_pairs={{0,8},{1,9},{2,10},{3,11},{4,12},{5,13},{6,14},{7,15},{8,0},{9,1},... | collective-permute-start | bytes 393224 | tf_op jit(solution)/shard_map/ppermute | solution.py:447
  38.5 0.0 collective-permute-done.11.got_ref
  38.5 1.9 %collective-permute-start.15 = (bf16[512,128]{1,0:T(8,128)(2,1)S(1)}, bf16[512,128]{1,0:T(8,128)(2,1)S(1)}, u32[]{:S(2)}, u32[]{:S(2)}) collective-permute-start(bf16[512,128]{1,0:T(8,128)(2,1)S(1)} %shard_map.130.refs_0_.after_ref), channel_id=1, source_target_pairs={{0,8},{1,9},{2,10},{3,11},{4,12},{5,13},{6,14},{7,15},{8,0},{9,1},... | collective-permute-start | bytes 393224 | tf_op jit(solution)/shard_map/ppermute | solution.py:447
  40.4 1.7 %collective-permute-start.14 = (bf16[1024,128]{1,0:T(8,128)(2,1)S(1)}, bf16[1024,128]{1,0:T(8,128)(2,1)S(1)}, u32[]{:S(2)}, u32[]{:S(2)}) collective-permute-start(bf16[1024,128]{1,0:T(8,128)(2,1)S(1)} %shard_map.134), channel_id=1, source_target_pairs={{0,2},{1,3},{2,0},{3,1},{4,6},{5,7},{6,4},{7,5},{8,10},{9,11},{10,... | collective-permute-start | bytes 786440 | tf_op jit(solution)/shard_map/ppermute | solution.py:447
  42.1 2.9 %collective-permute-done.13.far_ref = bf16[512,128]{1,0:T(8,128)(2,1)S(1)} collective-permute-done((bf16[512,128]{1,0:T(8,128)(2,1)S(1)}, bf16[512,128]{1,0:T(8,128)(2,1)S(1)}, u32[]{:S(2)}, u32[]{:S(2)}) %collective-permute-start.13) | collective-permute-done | bytes 131104 | tf_op jit(solution)/shard_map/ppermute | solution.py:447
  45.0 0.0 collective-permute-start.12
  45.0 1.1 %shard_map.132 = (f32[8,512,128]{2,1,0:T(8,128)S(1)}, f32[8,128,128]{2,1,0:T(8,128)S(1)}, f32[8,128]{1,0:T(8,128)S(1)}, f32[8,128,128]{2,1,0:T(8,128)S(1)}, f32[128,128]{1,0:T(8,128)S(1)}) custom-call(bf16[1024,128]{1,0:T(8,128)(2,1)S(1)} %shard_map.114.x_ref, bf16[8,128,128]{2,1,0:T(8,128)(2,1)S(1)} %copy-done.1, s32[8,128]{1,0:T(8,128)S(1)} %copy-done.2, ...), custom_call_target="tpu_custom_call" | custom-call | flops 5000000000 | bytes 262144 | tf_op jit(solution)/shard_map/pallas_call | solution.py:43
  46.1 0.5 %collective-permute-done.12.near_ref.refs_1_ = bf16[1280,128]{1,0:T(8,128)(2,1)S(1)} collective-permute-done((bf16[1280,128]{1,0:T(8,128)(2,1)S(1)}, bf16[1280,128]{1,0:T(8,128)(2,1)S(1)}, u32[]{:S(2)}, u32[]{:S(2)}) %collective-permute-start.12) | collective-permute-done | bytes 327712 | tf_op jit(solution)/shard_map/ppermute | solution.py:447
  46.6 0.9 %shard_map.133 = (bf16[8,128,128]{2,1,0:T(8,128)(2,1)}, f32[8,128,128]{2,1,0:T(8,128)S(1)}) custom-call(s32[1]{0:T(128)} %bitcast.me_ref.refs_0_, bf16[256,128]{1,0:T(8,128)(2,1)S(1)} %get-tuple-element.66.own_ref, bf16[1280,128]{1,0:T(8,128)(2,1)S(1)} %collective-permute-done.12.near_ref.refs_1_, bf16[512,128]{1,0:T(8,128)(2,1)S(1)} %collective-permute-done.13.far_ref, ...), custom_call_target="tpu_custom_call" | custom-call | flops 67108864 | bytes 262144 | tf_op jit(solution)/shard_map/pallas_call | solution.py:43
  47.5 0.0 collective-permute-done.18.refs_5_
  47.5 2.0 %collective-permute-done.16.refs_2_ = bf16[1024,128]{1,0:T(8,128)(2,1)S(1)} collective-permute-done((bf16[1024,128]{1,0:T(8,128)(2,1)S(1)}, bf16[1024,128]{1,0:T(8,128)(2,1)S(1)}, u32[]{:S(2)}, u32[]{:S(2)}) %collective-permute-start.16) | collective-permute-done | bytes 262176 | tf_op jit(solution)/shard_map/ppermute | solution.py:447
  49.5 0.0 collective-permute-done.14.refs_4_.near_ref
  49.5 1.0 %shard_map.136.sum_ref = f32[8,128,128]{2,1,0:T(8,128)S(1)} custom-call(bf16[1024,128]{1,0:T(8,128)(2,1)S(1)} %get-tuple-element.85.refs_0_, bf16[1280,128]{1,0:T(8,128)(2,1)S(1)} %collective-permute-done.12.near_ref.refs_1_, bf16[1024,128]{1,0:T(8,128)(2,1)S(1)} %collective-permute-done.16.refs_2_, bf16[512,128]{1,0:T(8,128)(2,1)S(1)} %get-tuple-element.86.refs_3_, ...), custom_call_target="tpu_custom_call" | custom-call | flops 1250000000 | bytes 262144 | tf_op jit(solution)/shard_map/pallas_call | solution.py:43
  50.5 0.0 collective-permute-done.15.got_ref
  50.5 1.3 %shard_map.137 = bf16[8,128,128]{2,1,0:T(8,128)(2,1)} custom-call(bf16[512,128]{1,0:T(8,128)(2,1)S(1)} %get-tuple-element.81.own_ref, bf16[1024,128]{1,0:T(8,128)(2,1)S(1)} %collective-permute-done.14.refs_4_.near_ref, bf16[512,128]{1,0:T(8,128)(2,1)S(1)} %collective-permute-done.15.got_ref, f32[8,512,128]{2,1,0:T(8,128)S(1)} %get-tuple-element.84.refs_6_.factor_ref, ...), custom_call_target="tpu_custom_call" | custom-call | flops 67108864 | bytes 262144 | tf_op jit(solution)/shard_map/pallas_call | solution.py:43
  (9 shorter events, 0.2 us)
Async XLA Ops:
  0.6 1.0 %copy-start = (bf16[8,128,128]{2,1,0:T(8,128)(2,1)S(1)}, bf16[8,128,128]{2,1,0:T(8,128)(2,1)}, u32[]{:S(2)}) copy-start(bf16[8,128,128]{2,1,0:T(8,128)(2,1)} %param.10) | copy-start | bytes 786436
  1.6 10.5 %collective-permute-start.4 = (bf16[512,128]{1,0:T(8,128)(2,1)S(1)}, bf16[512,128]{1,0:T(8,128)(2,1)S(1)}, u32[]{:S(2)}, u32[]{:S(2)}) collective-permute-start(bf16[512,128]{1,0:T(8,128)(2,1)S(1)} %get-tuple-element.47.refs_0_), channel_id=1, source_target_pairs={{0,8},{1,9},{2,10},{3,11},{4,12},{5,13},{6,14},{7,15},{8,0},{9,1},... | collective-permute-start | bytes 393224 | tf_op jit(solution)/shard_map/ppermute | solution.py:447
  5.7 13.9 %collective-permute-start.2 = (bf16[1024,128]{1,0:T(8,128)(2,1)S(1)}, bf16[1024,128]{1,0:T(8,128)(2,1)S(1)}, u32[]{:S(2)}, u32[]{:S(2)}) collective-permute-start(bf16[1024,128]{1,0:T(8,128)(2,1)S(1)} %shard_map.114.x_ref), channel_id=1, source_target_pairs={{0,4},{1,5},{2,6},{3,7},{4,0},{5,1},{6,2},{7,3},{8,12},{9,13},{10,... | collective-permute-start | bytes 786440 | tf_op jit(solution)/shard_map/ppermute | solution.py:447
  7.4 8.5 %collective-permute-start.1 = (bf16[1024,128]{1,0:T(8,128)(2,1)S(1)}, bf16[1024,128]{1,0:T(8,128)(2,1)S(1)}, u32[]{:S(2)}, u32[]{:S(2)}) collective-permute-start(bf16[1024,128]{1,0:T(8,128)(2,1)S(1)} %shard_map.114.x_ref), channel_id=1, source_target_pairs={{0,2},{1,3},{2,0},{3,1},{4,6},{5,7},{6,4},{7,5},{8,10},{9,11},{10,... | collective-permute-start | bytes 786440 | tf_op jit(solution)/shard_map/ppermute | solution.py:447
  8.9 12.5 %collective-permute-start = (bf16[1024,128]{1,0:T(8,128)(2,1)S(1)}, bf16[1024,128]{1,0:T(8,128)(2,1)S(1)}, u32[]{:S(2)}, u32[]{:S(2)}) collective-permute-start(bf16[1024,128]{1,0:T(8,128)(2,1)S(1)} %shard_map.114.x_ref), channel_id=1, source_target_pairs={{0,1},{1,0},{2,3},{3,2},{4,5},{5,4},{6,7},{7,6},{8,9},{9,8},{10,11... | collective-permute-start | bytes 786440 | tf_op jit(solution)/shard_map/ppermute | solution.py:447
  8.9 8.6 %collective-permute-start.3 = (bf16[512,128]{1,0:T(8,128)(2,1)S(1)}, bf16[512,128]{1,0:T(8,128)(2,1)S(1)}, u32[]{:S(2)}, u32[]{:S(2)}) collective-permute-start(bf16[512,128]{1,0:T(8,128)(2,1)S(1)} %get-tuple-element.51), channel_id=1, source_target_pairs={{0,8},{1,9},{2,10},{3,11},{4,12},{5,13},{6,14},{7,15},{8,0},{9,1},... | collective-permute-start | bytes 393224 | tf_op jit(solution)/shard_map/ppermute | solution.py:447
  12.1 5.5 %collective-permute-start.6 = (bf16[512,128]{1,0:T(8,128)(2,1)S(1)}, bf16[512,128]{1,0:T(8,128)(2,1)S(1)}, u32[]{:S(2)}, u32[]{:S(2)}) collective-permute-start(bf16[512,128]{1,0:T(8,128)(2,1)S(1)} %collective-permute-done.4.refs_1_), channel_id=1, source_target_pairs={{0,2},{1,3},{2,0},{3,1},{4,6},{5,7},{6,4},{7,5},{8,10},{9,11},{10,... | collective-permute-start | bytes 393224 | tf_op jit(solution)/shard_map/ppermute | solution.py:447
  13.7 2.1 %copy-start.1 = (bf16[8,128,128]{2,1,0:T(8,128)(2,1)S(1)}, bf16[8,128,128]{2,1,0:T(8,128)(2,1)}, u32[]{:S(2)}) copy-start(bf16[8,128,128]{2,1,0:T(8,128)(2,1)} %cot_ref.3) | copy-start | bytes 786436
  13.7 2.1 %copy-start.2 = (s32[8,128]{1,0:T(8,128)S(1)}, s32[8,128]{1,0:T(8,128)}, u32[]{:S(2)}) copy-start(s32[8,128]{1,0:T(8,128)} %mask_ref.3) | copy-start | bytes 12292
  16.0 7.0 %collective-permute-start.8 = (bf16[544,128]{1,0:T(8,128)(2,1)S(1)}, bf16[544,128]{1,0:T(8,128)(2,1)S(1)}, u32[]{:S(2)}, u32[]{:S(2)}) collective-permute-start(bf16[544,128]{1,0:T(8,128)(2,1)S(1)} %get-tuple-element.63), channel_id=1, source_target_pairs={{0,4},{1,5},{2,6},{3,7},{4,0},{5,1},{6,2},{7,3},{8,12},{9,13},{10,... | collective-permute-start | bytes 417800 | tf_op jit(solution)/shard_map/ppermute | solution.py:447
  17.7 7.7 %collective-permute-start.7 = (bf16[512,128]{1,0:T(8,128)(2,1)S(1)}, bf16[512,128]{1,0:T(8,128)(2,1)S(1)}, u32[]{:S(2)}, u32[]{:S(2)}) collective-permute-start(bf16[512,128]{1,0:T(8,128)(2,1)S(1)} %shard_map.119), channel_id=1, source_target_pairs={{0,2},{1,3},{2,0},{3,1},{4,6},{5,7},{6,4},{7,5},{8,10},{9,11},{10,... | collective-permute-start | bytes 393224 | tf_op jit(solution)/shard_map/ppermute | solution.py:447
  19.6 4.0 %collective-permute-start.5 = (bf16[1024,128]{1,0:T(8,128)(2,1)S(1)}, bf16[1024,128]{1,0:T(8,128)(2,1)S(1)}, u32[]{:S(2)}, u32[]{:S(2)}) collective-permute-start(bf16[1024,128]{1,0:T(8,128)(2,1)S(1)} %collective-permute-done.2.left_in), channel_id=1, source_target_pairs={{0,1},{1,0},{2,3},{3,2},{4,5},{5,4},{6,7},{7,6},{8,9},{9,8},{10,11... | collective-permute-start | bytes 786440 | tf_op jit(solution)/shard_map/ppermute | solution.py:447
  23.0 3.0 %collective-permute-start.9 = (bf16[544,128]{1,0:T(8,128)(2,1)S(1)}, bf16[544,128]{1,0:T(8,128)(2,1)S(1)}, u32[]{:S(2)}, u32[]{:S(2)}) collective-permute-start(bf16[544,128]{1,0:T(8,128)(2,1)S(1)} %shard_map.123), channel_id=1, source_target_pairs={{0,1},{1,0},{2,3},{3,2},{4,5},{5,4},{6,7},{7,6},{8,9},{9,8},{10,11... | collective-permute-start | bytes 417800 | tf_op jit(solution)/shard_map/ppermute | solution.py:447
  28.6 6.4 %collective-permute-start.17 = (bf16[512,128]{1,0:T(8,128)(2,1)S(1)}, bf16[512,128]{1,0:T(8,128)(2,1)S(1)}, u32[]{:S(2)}, u32[]{:S(2)}) collective-permute-start(bf16[512,128]{1,0:T(8,128)(2,1)S(1)} %get-tuple-element.70.refs_6_), channel_id=1, source_target_pairs={{0,2},{1,3},{2,0},{3,1},{4,6},{5,7},{6,4},{7,5},{8,10},{9,11},{10,... | collective-permute-start | bytes 393224 | tf_op jit(solution)/shard_map/ppermute | solution.py:447
  30.5 1.7 %collective-permute-start.10 = (bf16[1280,128]{1,0:T(8,128)(2,1)S(1)}, bf16[1280,128]{1,0:T(8,128)(2,1)S(1)}, u32[]{:S(2)}, u32[]{:S(2)}) collective-permute-start(bf16[1280,128]{1,0:T(8,128)(2,1)S(1)} %get-tuple-element.76), channel_id=1, source_target_pairs={{0,1},{1,0},{2,3},{3,2},{4,5},{5,4},{6,7},{7,6},{8,9},{9,8},{10,11... | collective-permute-start | bytes 983048 | tf_op jit(solution)/shard_map/ppermute | solution.py:447
  32.3 6.2 %collective-permute-start.11 = (bf16[512,128]{1,0:T(8,128)(2,1)S(1)}, bf16[512,128]{1,0:T(8,128)(2,1)S(1)}, u32[]{:S(2)}, u32[]{:S(2)}) collective-permute-start(bf16[512,128]{1,0:T(8,128)(2,1)S(1)} %shard_map.129), channel_id=1, source_target_pairs={{0,2},{1,3},{2,0},{3,1},{4,6},{5,7},{6,4},{7,5},{8,10},{9,11},{10,... | collective-permute-start | bytes 393224 | tf_op jit(solution)/shard_map/ppermute | solution.py:447
  33.0 12.0 %collective-permute-start.13 = (bf16[512,128]{1,0:T(8,128)(2,1)S(1)}, bf16[512,128]{1,0:T(8,128)(2,1)S(1)}, u32[]{:S(2)}, u32[]{:S(2)}) collective-permute-start(bf16[512,128]{1,0:T(8,128)(2,1)S(1)} %get-tuple-element.78), channel_id=1, source_target_pairs={{0,4},{1,5},{2,6},{3,7},{4,0},{5,1},{6,2},{7,3},{8,12},{9,13},{10,... | collective-permute-start | bytes 393224 | tf_op jit(solution)/shard_map/ppermute | solution.py:447
  34.2 15.2 %collective-permute-start.16 = (bf16[1024,128]{1,0:T(8,128)(2,1)S(1)}, bf16[1024,128]{1,0:T(8,128)(2,1)S(1)}, u32[]{:S(2)}, u32[]{:S(2)}) collective-permute-start(bf16[1024,128]{1,0:T(8,128)(2,1)S(1)} %get-tuple-element.77.refs_0_), channel_id=1, source_target_pairs={{0,4},{1,5},{2,6},{3,7},{4,0},{5,1},{6,2},{7,3},{8,12},{9,13},{10,... | collective-permute-start | bytes 786440 | tf_op jit(solution)/shard_map/ppermute | solution.py:447
  35.0 12.4 %collective-permute-start.18 = (bf16[512,128]{1,0:T(8,128)(2,1)S(1)}, bf16[512,128]{1,0:T(8,128)(2,1)S(1)}, u32[]{:S(2)}, u32[]{:S(2)}) collective-permute-start(bf16[512,128]{1,0:T(8,128)(2,1)S(1)} %shard_map.135), channel_id=1, source_target_pairs={{0,8},{1,9},{2,10},{3,11},{4,12},{5,13},{6,14},{7,15},{8,0},{9,1},... | collective-permute-start | bytes 393224 | tf_op jit(solution)/shard_map/ppermute | solution.py:447
  38.5 12.0 %collective-permute-start.15 = (bf16[512,128]{1,0:T(8,128)(2,1)S(1)}, bf16[512,128]{1,0:T(8,128)(2,1)S(1)}, u32[]{:S(2)}, u32[]{:S(2)}) collective-permute-start(bf16[512,128]{1,0:T(8,128)(2,1)S(1)} %shard_map.130.refs_0_.after_ref), channel_id=1, source_target_pairs={{0,8},{1,9},{2,10},{3,11},{4,12},{5,13},{6,14},{7,15},{8,0},{9,1},... | collective-permute-start | bytes 393224 | tf_op jit(solution)/shard_map/ppermute | solution.py:447
  40.4 9.1 %collective-permute-start.14 = (bf16[1024,128]{1,0:T(8,128)(2,1)S(1)}, bf16[1024,128]{1,0:T(8,128)(2,1)S(1)}, u32[]{:S(2)}, u32[]{:S(2)}) collective-permute-start(bf16[1024,128]{1,0:T(8,128)(2,1)S(1)} %shard_map.134), channel_id=1, source_target_pairs={{0,2},{1,3},{2,0},{3,1},{4,6},{5,7},{6,4},{7,5},{8,10},{9,11},{10,... | collective-permute-start | bytes 786440 | tf_op jit(solution)/shard_map/ppermute | solution.py:447
  45.0 1.6 %collective-permute-start.12 = (bf16[1280,128]{1,0:T(8,128)(2,1)S(1)}, bf16[1280,128]{1,0:T(8,128)(2,1)S(1)}, u32[]{:S(2)}, u32[]{:S(2)}) collective-permute-start(bf16[1280,128]{1,0:T(8,128)(2,1)S(1)} %shard_map.131), channel_id=1, source_target_pairs={{0,1},{1,0},{2,3},{3,2},{4,5},{5,4},{6,7},{7,6},{8,9},{9,8},{10,11... | collective-permute-start | bytes 983048 | tf_op jit(solution)/shard_map/ppermute | solution.py:447

commit v11 on v9

--- a/solution.py
+++ b/solution.py
@@ -166,34 +166,6 @@
     left_ref[...] = rows_ref[0].astype(BF16)
     right_ref[...] = rows_ref[1].astype(BF16)
     sig_ref[...] = block_gate(me_ref, scaled_ref, weight_ref)
-
-
-def left_kernel(
-    me_ref, x_ref, weight_t_ref, weight_ref, params_ref, left_ref, sig_ref, rows_ref, scaled_ref
-):
-    scaled = scale_in(x_ref[...], params_ref)
-    scaled_ref[...] = scaled.reshape(scaled_ref.shape)
-    scaled = scaled.astype(BF16)
-    for row in range(ROWS):
-        projected = project(weight_t_ref[:256, :], scaled, row)
-        store_side(rows_ref, row, make_side(projected))
-    left_ref[...] = rows_ref[...].astype(BF16)
-    sig_ref[...] = block_gate(me_ref, scaled_ref, weight_ref)
-
-
-def right_kernel(first, last):
-    def kernel(x_ref, weight_t_ref, params_ref, rest_ref, right_ref, rows_ref):
-        if last:
-            rows_ref[...] = rest_ref[...]
-        else:
-            rows_ref[...] = jnp.zeros_like(rows_ref)
-        scaled = scale_in(x_ref[...], params_ref).astype(BF16)
-        for row in range(ROWS // 2):
-            projected = project(weight_t_ref[256:, :], scaled, row)
-            store_side(rows_ref, first + row, make_side(projected))
-        right_ref[...] = rows_ref[...].astype(right_ref.dtype)
-
-    return kernel
 
 
 GROUPS = SIDE // 32
@@ -291,7 +263,7 @@
 
 def grad_right_kernel(half):
     def kernel(pairs_ref, *refs):
-        left_refs, out_refs = refs[:4], refs[-4:]
+        left_refs, out_refs = refs[:4], refs[4:]
         of_quarter = quarters()
         for g in range(GROUPS // 2):
             spread = spread_group(pairs_ref, half * GROUPS // 2 + g, of_quarter)
@@ -331,12 +303,7 @@
     sum_ref[...] = (mine_ref[...].astype(F32) + got_ref[...].astype(F32)).astype(BF16)
 
 
-def early_kernel(mine_ref, got_ref, sum_ref):
-    sum_ref[...] = mine_ref[...].astype(F32) + got_ref[:SIDE, :].astype(F32)
-
-
-def near_kernel(first_ref, second_ref, *refs):
-    both_ref = refs[-1]
+def near_kernel(first_ref, second_ref, after_ref, both_ref):
     both_ref[: SIDE // 2, :] = first_ref[...]
     both_ref[SIDE // 2 :, :] = second_ref[...]
 
@@ -408,9 +375,10 @@
 
 
 def partial_kernel(*refs):
-    left_ref, left_got_ref, own_ref, near_ref, got_ref = refs[:5]
-    factor_ref, gate_ref, weight_ref, sum_ref, left_rows, right_rows = refs[5:]
-    left_rows[...] = left_ref[...] + left_got_ref[...].astype(F32)
+    left_refs, (own_ref, near_ref, got_ref) = refs[0:3], refs[3:6]
+    factor_ref, gate_ref, weight_ref, sum_ref, left_rows, right_rows = refs[6:]
+    left = [r[:SIDE, :].astype(F32) for r in left_refs]
+    left_rows[...] = left[0] + left[1] + left[2]
     right = own_ref[...].astype(F32) + near_ref[: SIDE // 2, :].astype(F32)
     right_rows[...] = right + got_ref[...].astype(F32)
     for row in range(ROWS):
@@ -516,31 +484,12 @@
     )
     far_got = swap(far_piece, Z_LOW)
     both = swap(far, CORE)
-    x_second = swap(after(z_second, left_0), CHIP_X)
+    x_second = swap(z_second, CHIP_X)
     x_first = swap(after(z_first, x_second, left_0), CHIP_X)
     (joined,) = call(join_kernel, [((2 * HEAD, 128), BF16)], vmem=[core_piece, far_got])
     core_pieces = swap(joined, CORE)
     left_2, right_2, sig_2 = peer(far, z_first, z_second)
-    left_3, sig_3 = call(
-        left_kernel,
-        [side, sig],
-        smem=[me],
-        vmem=[both, weight_t, weights, params],
-        scratch=[pltpu.VMEM((SIDE, 128), F32), cube_scratch],
-        weight=WAIT,
-    )
-
-    def right_half(first, last, *operands):
-        return call(
-            right_kernel(first, last),
-            [((SIDE, 128), BF16 if last else F32)],
-            vmem=operands,
-            scratch=[pltpu.VMEM((SIDE, 128), F32)],
-            weight=WAIT // 4,
-        )[0]
-
-    right_part = right_half(ROWS // 2, False, x_second, weight_t, params, left_3)
-    right_3 = right_half(0, True, x_first, weight_t, params, right_part)
+    left_3, right_3, sig_3 = peer(both, x_first, x_second)
 
     lefts, rights = [left_0, left_1, left_2, left_3], [right_0, right_1, right_2, right_3]
     out_0, out_1, out_far, pairs = call(
@@ -555,21 +504,18 @@
     out_far = swap(out_far, Z_LOW)
     right_a = call(grad_right_kernel(0), [halves] * 4, vmem=[pairs, *lefts])
     x_got = [swap(right_a[3], CHIP_X)]
-    left_parts = call(
-        grad_left_kernel, [side] * 4, vmem=[pairs, *rights, right_a[3]]
-    )
+    left_parts = call(grad_left_kernel, [side] * 4, vmem=[pairs, *rights, right_a[3]])
     both_got = swap(left_parts[3], CORE)
+    right_b = call(grad_right_kernel(1), [halves] * 4, vmem=[pairs, *lefts], weight=WAIT)
     (left_sum,) = call(add_kernel, [side], vmem=[left_parts[2], both_got])
+    x_got.append(swap(after(right_b[3], left_sum), CHIP_X))
     left_got = swap(left_sum, Z_LOW)
-    (total,) = call(add_kernel, [halves], vmem=[right_a[2], x_got[0], left_sum])
-    z_got = [swap(total, Z_HIGH)]
-    right_b = call(grad_right_kernel(1), [halves] * 4, vmem=[pairs, *lefts], weight=WAIT)
-    x_got.append(swap(after(right_b[3], left_sum), CHIP_X))
-    (total,) = call(add_kernel, [halves], vmem=[right_b[2], x_got[1], left_sum])
-    z_got.append(swap(total, Z_HIGH))
-    (near_back,) = call(back_kernel, [core], vmem=[left_parts[1], out_1, out_far, total])
+    z_got = []
+    for mine, got in zip((right_a[2], right_b[2]), x_got):
+        (total,) = call(add_kernel, [halves], vmem=[mine, got, left_sum])
+        z_got.append(swap(total, Z_HIGH))
+    (near_back,) = call(back_kernel, [core], vmem=[left_parts[1], out_1, out_far, left_sum])
     near_got = swap(near_back, CORE)
-    (left_part,) = call(early_kernel, [((SIDE, 128), F32)], vmem=[left_parts[0], near_got])
     (right_back,) = call(near_kernel, [side], vmem=[right_a[1], right_b[1], total])
     right_near = swap(right_back, CHIP_X)
 
@@ -590,7 +536,7 @@
     (partial,) = call(
         partial_kernel,
         [(cube, F32)],
-        vmem=[left_part, left_got, right_a[0], right_near, z_got[0]]
+        vmem=[left_parts[0], near_got, left_got, right_a[0], right_near, z_got[0]]
         + [factors, gate_part, weights],
         scratch=[pltpu.VMEM((SIDE, 128), F32), half_scratch],
         weight=WAIT // 4,

time: 62.7 us -> 51.5 us (0.82)
  waiting for transfers between devices: 21.8 us -> 9.13 us
  starting transfers between devices: 21.5 us -> 23.8 us
  Pallas kernels: 15.6 us -> 14.9 us
    ppermute x19, waiting for transfers between devices: 21.8 us -> 9.13 us  [swap(): return lax.ppermute(values, 'row', [(s, s ^ offset) for s in range(16)])]
    ppermute x19, starting transfers between devices: 21.5 us -> 23.8 us  [swap(): return lax.ppermute(values, 'row', [(s, s ^ offset) for s in range(16)])]
    pallas_call x27 -> x23, Pallas kernels: 15.6 us -> 14.9 us  [call(): pl.pallas_call(kernel, out_shape=[jax.ShapeDtypeStruct(s, d) for s, d in...]
  transfers between devices with their start and end apart: 19 -> 19, of which waited for: 8 -> 10; matrix products, arithmetic and copies ran while one was open for 3% -> 3% of each run, Pallas kernels for 18% -> 21%
where the time goes in v11:
time: 51.5 us; the launch traced here: 51.3 us
  starting transfers between devices  23.8 us (46%)
  Pallas kernels  14.9 us (29%)
  waiting for transfers between devices  9.13 us (18%)
  other arithmetic  1.67 us (3%)
  local copies, waits for them, and re-layouts  0.95 us (2%)
  between operations  0.83 us (2%)
    ppermute x19, starting transfers between devices, swap(): return lax.ppermute(values, 'row', [(s, s ^ offset) for s in range(16)])  23.8 us
    pallas_call x23, Pallas kernels, call(): pl.pallas_call(kernel, out_shape=[jax.ShapeDtypeStruct(s, d) for s, d in...  14.9 us
    ppermute x19, waiting for transfers between devices, swap(): return lax.ppermute(values, 'row', [(s, s ^ offset) for s in range(16)])  9.13 us
  transfers between devices with their start and end apart: 19, of which 10 were waited for; matrix products, arithmetic and copies ran while one was open for 3% of the time, Pallas kernels for 21%

profile of v11, /device:TPU:0, one launch (start us, length us, event | category | flops | bytes accessed | tf_op | source)
XLA Modules:
  0.0 51.3 jit_solution(366064870321216352)
XLA Ops:
  0.6 0.0 copy-start
  0.6 0.9 %copy-done = bf16[8,128,128]{2,1,0:T(8,128)(2,1)S(1)} copy-done((bf16[8,128,128]{2,1,0:T(8,128)(2,1)S(1)}, bf16[8,128,128]{2,1,0:T(8,128)(2,1)}, u32[]{:S(2)}) %copy-start) | copy-done | bytes 262168
  1.6 4.1 %collective-permute-start.4 = (bf16[512,128]{1,0:T(8,128)(2,1)S(1)}, bf16[512,128]{1,0:T(8,128)(2,1)S(1)}, u32[]{:S(2)}, u32[]{:S(2)}) collective-permute-start(bf16[512,128]{1,0:T(8,128)(2,1)S(1)} %get-tuple-element.45.refs_0_), channel_id=1, source_target_pairs={{0,8},{1,9},{2,10},{3,11},{4,12},{5,13},{6,14},{7,15},{8,0},{9,1},... | collective-permute-start | bytes 393224 | tf_op jit(solution)/shard_map/ppermute | solution.py:419
  5.7 1.6 %collective-permute-start.2 = (bf16[1024,128]{1,0:T(8,128)(2,1)S(1)}, bf16[1024,128]{1,0:T(8,128)(2,1)S(1)}, u32[]{:S(2)}, u32[]{:S(2)}) collective-permute-start(bf16[1024,128]{1,0:T(8,128)(2,1)S(1)} %shard_map.114.x_ref), channel_id=1, source_target_pairs={{0,4},{1,5},{2,6},{3,7},{4,0},{5,1},{6,2},{7,3},{8,12},{9,13},{10,... | collective-permute-start | bytes 786440 | tf_op jit(solution)/shard_map/ppermute | solution.py:419
  7.4 1.5 %collective-permute-start.1 = (bf16[1024,128]{1,0:T(8,128)(2,1)S(1)}, bf16[1024,128]{1,0:T(8,128)(2,1)S(1)}, u32[]{:S(2)}, u32[]{:S(2)}) collective-permute-start(bf16[1024,128]{1,0:T(8,128)(2,1)S(1)} %shard_map.114.x_ref), channel_id=1, source_target_pairs={{0,2},{1,3},{2,0},{3,1},{4,6},{5,7},{6,4},{7,5},{8,10},{9,11},{10,... | collective-permute-start | bytes 786440 | tf_op jit(solution)/shard_map/ppermute | solution.py:419
  8.9 0.0 collective-permute-start
  8.9 0.3 collective-permute-start.3
  9.2 0.7 %pad_maximum_fusion.params_ref.refs_3_.refs_4_ = f32[4,128]{1,0:T(4,128)S(1)} fusion(f32[1,128]{1,0:T(1,128)} %bitcast.8, f32[1,128]{1,0:T(1,128)} %bitcast.9, f32[1,128]{1,0:T(1,128)} %bitcast.10, f32[1,128]{1,0:T(1,128)} %bitcast.11), kind=kLoop, calls=%fused_computation.1 | loop fusion | flops 1536 | bytes 4096 | tf_op jit(solution)/shard_map/stack | solution.py:450
  9.9 1.0 %pad_add_fusion.weight_ref.refs_2_.refs_3_.refs_8_ = bf16[128,768]{1,0:T(8,128)(2,1)S(1)} fusion(bf16[128,128]{1,0:T(8,128)(2,1)} %param.19, bf16[128,128]{1,0:T(8,128)(2,1)} %param.16, bf16[128,512]{1,0:T(8,128)(2,1)} %param.15), kind=kLoop, calls=%fused_computation | loop fusion | flops 589824 | bytes 393216 | tf_op jit(solution)/shard_map/add | solution.py:449
  10.9 1.2 %collective-permute-done.4.refs_1_ = bf16[512,128]{1,0:T(8,128)(2,1)S(1)} collective-permute-done((bf16[512,128]{1,0:T(8,128)(2,1)S(1)}, bf16[512,128]{1,0:T(8,128)(2,1)S(1)}, u32[]{:S(2)}, u32[]{:S(2)}) %collective-permute-start.4) | collective-permute-done | bytes 131104 | tf_op jit(solution)/shard_map/ppermute | solution.py:419
  12.1 1.6 %collective-permute-start.6 = (bf16[512,128]{1,0:T(8,128)(2,1)S(1)}, bf16[512,128]{1,0:T(8,128)(2,1)S(1)}, u32[]{:S(2)}, u32[]{:S(2)}) collective-permute-start(bf16[512,128]{1,0:T(8,128)(2,1)S(1)} %collective-permute-done.4.refs_1_), channel_id=1, source_target_pairs={{0,2},{1,3},{2,0},{3,1},{4,6},{5,7},{6,4},{7,5},{8,10},{9,11},{10,... | collective-permute-start | bytes 393224 | tf_op jit(solution)/shard_map/ppermute | solution.py:419
  13.7 0.0 copy-start.1
  13.7 0.0 copy-start.2
  13.7 1.9 %shard_map.115 = (bf16[1024,128]{1,0:T(8,128)(2,1)S(1)}, bf16[1024,128]{1,0:T(8,128)(2,1)S(1)}, f32[256,128]{1,0:T(8,128)S(1)}, bf16[512,128]{1,0:T(8,128)(2,1)S...) custom-call(s32[1]{0:T(128)} %bitcast.me_ref.refs_0_, bf16[1024,128]{1,0:T(8,128)(2,1)S(1)} %shard_map.114.x_ref, ...), custom_call_target="tpu_custom_call" | custom-call | flops 5000000000 | bytes 262144 | tf_op jit(solution)/shard_map/pallas_call | solution.py:43
  15.7 0.2 collective-permute-done.1.refs_0_.after_ref
  15.9 0.0 copy-done.1
  15.9 0.0 copy-done.2
  15.9 0.1 shard_map.120
  16.0 0.5 collective-permute-start.8
  16.5 1.0 %collective-permute-done.3.refs_0_.message_ref = bf16[512,128]{1,0:T(8,128)(2,1)S(1)} collective-permute-done((bf16[512,128]{1,0:T(8,128)(2,1)S(1)}, bf16[512,128]{1,0:T(8,128)(2,1)S(1)}, u32[]{:S(2)}, u32[]{:S(2)}) %collective-permute-start.3) | collective-permute-done | bytes 131104 | tf_op jit(solution)/shard_map/ppermute | solution.py:419
  17.5 0.2 collective-permute-done.6.refs_0_.refs_1_
  17.7 1.9 %collective-permute-start.7 = (bf16[512,128]{1,0:T(8,128)(2,1)S(1)}, bf16[512,128]{1,0:T(8,128)(2,1)S(1)}, u32[]{:S(2)}, u32[]{:S(2)}) collective-permute-start(bf16[512,128]{1,0:T(8,128)(2,1)S(1)} %shard_map.118), channel_id=1, source_target_pairs={{0,2},{1,3},{2,0},{3,1},{4,6},{5,7},{6,4},{7,5},{8,10},{9,11},{10,... | collective-permute-start | bytes 393224 | tf_op jit(solution)/shard_map/ppermute | solution.py:419
  19.6 0.0 collective-permute-done.2.left_in
  19.6 0.0 collective-permute-start.5
  19.6 1.7 %shard_map.117 = (bf16[1024,128]{1,0:T(8,128)(2,1)S(1)}, bf16[1024,128]{1,0:T(8,128)(2,1)S(1)}, f32[256,128]{1,0:T(8,128)S(1)}) custom-call(s32[1]{0:T(128)} %bitcast.me_ref.refs_0_, bf16[1024,128]{1,0:T(8,128)(2,1)S(1)} %collective-permute-done.2.left_in, bf16[512,128]{1,0:T(8,128)(2,1)S(1)} %collective-permute-done.3.refs_0_.message_ref, ...), custom_call_target="tpu_custom_call" | custom-call | flops 5000000000 | bytes 262144 | tf_op jit(solution)/shard_map/pallas_call | solution.py:43
  21.3 0.0 collective-permute-done.left_in
  21.3 1.7 %shard_map.116 = (bf16[1024,128]{1,0:T(8,128)(2,1)S(1)}, bf16[1024,128]{1,0:T(8,128)(2,1)S(1)}, f32[256,128]{1,0:T(8,128)S(1)}) custom-call(s32[1]{0:T(128)} %bitcast.me_ref.refs_0_, bf16[1024,128]{1,0:T(8,128)(2,1)S(1)} %collective-permute-done.left_in, bf16[1024,128]{1,0:T(8,128)(2,1)S(1)} %collective-permute-done.1.refs_0_.after_ref, ...), custom_call_target="tpu_custom_call" | custom-call | flops 5000000000 | bytes 262144 | tf_op jit(solution)/shard_map/pallas_call | solution.py:43
  23.0 0.0 collective-permute-done.8.got_ref.refs_15_
  23.0 0.6 %collective-permute-start.9 = (bf16[544,128]{1,0:T(8,128)(2,1)S(1)}, bf16[544,128]{1,0:T(8,128)(2,1)S(1)}, u32[]{:S(2)}, u32[]{:S(2)}) collective-permute-start(bf16[544,128]{1,0:T(8,128)(2,1)S(1)} %shard_map.121), channel_id=1, source_target_pairs={{0,1},{1,0},{2,3},{3,2},{4,5},{5,4},{6,7},{7,6},{8,9},{9,8},{10,11... | collective-permute-start | bytes 417800 | tf_op jit(solution)/shard_map/ppermute | solution.py:419
  23.6 0.0 collective-permute-done.7.refs_0_
  23.6 0.0 collective-permute-done.5.left_in
  23.6 1.7 %shard_map.119 = (bf16[1024,128]{1,0:T(8,128)(2,1)S(1)}, bf16[1024,128]{1,0:T(8,128)(2,1)S(1)}, f32[256,128]{1,0:T(8,128)S(1)}) custom-call(s32[1]{0:T(128)} %bitcast.me_ref.refs_0_, bf16[1024,128]{1,0:T(8,128)(2,1)S(1)} %collective-permute-done.5.left_in, bf16[512,128]{1,0:T(8,128)(2,1)S(1)} %collective-permute-done.7.refs_0_, ...), custom_call_target="tpu_custom_call" | custom-call | flops 5000000000 | bytes 262144 | tf_op jit(solution)/shard_map/pallas_call | solution.py:43
  25.3 0.0 collective-permute-done.9.refs_14_
  25.3 2.2 %shard_map.122 = (bf16[256,128]{1,0:T(8,128)(2,1)S(1)}, bf16[256,128]{1,0:T(8,128)(2,1)S(1)}, bf16[512,128]{1,0:T(8,128)(2,1)S(1)}, f32[1024,128]{1,0:T(8,128)S(1)}) custom-call(s32[1]{0:T(128)} %bitcast.me_ref.refs_0_, bf16[1024,128]{1,0:T(8,128)(2,1)S(1)} %get-tuple-element.46.refs_1_.refs_0_, bf16[1024,128]{1,0:T(8,128)(2,1)S(1)} %get-tuple-element.48.refs_2_.refs_1_, ...), custom_call_target="tpu_custom_call" | custom-call | flops 67108864 | bytes 262144 | tf_op jit(solution)/shard_map/pallas_call | solution.py:43
  27.5 0.3 shard_map.123
  27.9 0.4 shard_map.124
  28.3 1.4 %collective-permute-start.17 = (bf16[512,128]{1,0:T(8,128)(2,1)S(1)}, bf16[512,128]{1,0:T(8,128)(2,1)S(1)}, u32[]{:S(2)}, u32[]{:S(2)}) collective-permute-start(bf16[512,128]{1,0:T(8,128)(2,1)S(1)} %get-tuple-element.67.refs_4_), channel_id=1, source_target_pairs={{0,2},{1,3},{2,0},{3,1},{4,6},{5,7},{6,4},{7,5},{8,10},{9,11},{10,... | collective-permute-start | bytes 393224 | tf_op jit(solution)/shard_map/ppermute | solution.py:419
  29.8 0.0 collective-permute-start.11
  29.8 0.3 shard_map.129
  30.1 0.9 %collective-permute-start.10 = (bf16[512,128]{1,0:T(8,128)(2,1)S(1)}, bf16[512,128]{1,0:T(8,128)(2,1)S(1)}, u32[]{:S(2)}, u32[]{:S(2)}) collective-permute-start(bf16[512,128]{1,0:T(8,128)(2,1)S(1)} %get-tuple-element.70), channel_id=1, source_target_pairs={{0,4},{1,5},{2,6},{3,7},{4,0},{5,1},{6,2},{7,3},{8,12},{9,13},{10,... | collective-permute-start | bytes 393224 | tf_op jit(solution)/shard_map/ppermute | solution.py:419
  31.0 0.3 collective-permute-done.11.got_ref
  31.3 0.1 shard_map.125.after_ref.refs_0_
  31.4 0.9 %collective-permute-start.13 = (bf16[512,128]{1,0:T(8,128)(2,1)S(1)}, bf16[512,128]{1,0:T(8,128)(2,1)S(1)}, u32[]{:S(2)}, u32[]{:S(2)}) collective-permute-start(bf16[512,128]{1,0:T(8,128)(2,1)S(1)} %shard_map.130), channel_id=1, source_target_pairs={{0,2},{1,3},{2,0},{3,1},{4,6},{5,7},{6,4},{7,5},{8,10},{9,11},{10,... | collective-permute-start | bytes 393224 | tf_op jit(solution)/shard_map/ppermute | solution.py:419
  32.3 1.1 %collective-permute-start.16 = (bf16[1024,128]{1,0:T(8,128)(2,1)S(1)}, bf16[1024,128]{1,0:T(8,128)(2,1)S(1)}, u32[]{:S(2)}, u32[]{:S(2)}) collective-permute-start(bf16[1024,128]{1,0:T(8,128)(2,1)S(1)} %shard_map.125.after_ref.refs_0_), channel_id=1, source_target_pairs={{0,4},{1,5},{2,6},{3,7},{4,0},{5,1},{6,2},{7,3},{8,12},{9,13},{10,... | collective-permute-start | bytes 786440 | tf_op jit(solution)/shard_map/ppermute | solution.py:419
  33.4 0.4 collective-permute-done.17.got_ref
  33.9 3.4 %collective-permute-start.18 = (bf16[512,128]{1,0:T(8,128)(2,1)S(1)}, bf16[512,128]{1,0:T(8,128)(2,1)S(1)}, u32[]{:S(2)}, u32[]{:S(2)}) collective-permute-start(bf16[512,128]{1,0:T(8,128)(2,1)S(1)} %shard_map.133), channel_id=1, source_target_pairs={{0,8},{1,9},{2,10},{3,11},{4,12},{5,13},{6,14},{7,15},{8,0},{9,1},... | collective-permute-start | bytes 393224 | tf_op jit(solution)/shard_map/ppermute | solution.py:419
  37.3 0.0 collective-permute-done.10.far_ref
  37.3 0.1 collective-permute-start.12
  37.4 0.0 collective-permute-done.13.got_ref
  37.5 2.6 %collective-permute-start.15 = (bf16[512,128]{1,0:T(8,128)(2,1)S(1)}, bf16[512,128]{1,0:T(8,128)(2,1)S(1)}, u32[]{:S(2)}, u32[]{:S(2)}) collective-permute-start(bf16[512,128]{1,0:T(8,128)(2,1)S(1)} %shard_map.131.after_ref), channel_id=1, source_target_pairs={{0,8},{1,9},{2,10},{3,11},{4,12},{5,13},{6,14},{7,15},{8,0},{9,1},... | collective-permute-start | bytes 393224 | tf_op jit(solution)/shard_map/ppermute | solution.py:419
  40.1 1.1 %collective-permute-start.14 = (bf16[1024,128]{1,0:T(8,128)(2,1)S(1)}, bf16[1024,128]{1,0:T(8,128)(2,1)S(1)}, u32[]{:S(2)}, u32[]{:S(2)}) collective-permute-start(bf16[1024,128]{1,0:T(8,128)(2,1)S(1)} %shard_map.132), channel_id=1, source_target_pairs={{0,2},{1,3},{2,0},{3,1},{4,6},{5,7},{6,4},{7,5},{8,10},{9,11},{10,... | collective-permute-start | bytes 786440 | tf_op jit(solution)/shard_map/ppermute | solution.py:419
  41.2 1.1 %shard_map.127 = (f32[8,512,128]{2,1,0:T(8,128)S(1)}, f32[8,128,128]{2,1,0:T(8,128)S(1)}, f32[8,128]{1,0:T(8,128)S(1)}, f32[8,128,128]{2,1,0:T(8,128)S(1)}, f32[128,128]{1,0:T(8,128)S(1)}) custom-call(bf16[1024,128]{1,0:T(8,128)(2,1)S(1)} %shard_map.114.x_ref, bf16[8,128,128]{2,1,0:T(8,128)(2,1)S(1)} %copy-done.1, s32[8,128]{1,0:T(8,128)S(1)} %copy-done.2, ...), custom_call_target="tpu_custom_call" | custom-call | flops 5000000000 | bytes 262144 | tf_op jit(solution)/shard_map/pallas_call | solution.py:43
  42.3 0.0 collective-permute-done.12.near_ref.refs_1_
  42.3 0.9 %shard_map.128 = (bf16[8,128,128]{2,1,0:T(8,128)(2,1)}, f32[8,128,128]{2,1,0:T(8,128)S(1)}) custom-call(s32[1]{0:T(128)} %bitcast.me_ref.refs_0_, bf16[256,128]{1,0:T(8,128)(2,1)S(1)} %get-tuple-element.65.own_ref, bf16[1536,128]{1,0:T(8,128)(2,1)S(1)} %collective-permute-done.12.near_ref.refs_1_, bf16[512,128]{1,0:T(8,128)(2,1)S(1)} %collective-permute-done.10.far_ref, ...), custom_call_target="tpu_custom_call" | custom-call | flops 67108864 | bytes 262144 | tf_op jit(solution)/shard_map/pallas_call | solution.py:43
  43.2 0.1 collective-permute-done.18.refs_5_
  43.3 3.9 %collective-permute-done.16.refs_2_ = bf16[1024,128]{1,0:T(8,128)(2,1)S(1)} collective-permute-done((bf16[1024,128]{1,0:T(8,128)(2,1)S(1)}, bf16[1024,128]{1,0:T(8,128)(2,1)S(1)}, u32[]{:S(2)}, u32[]{:S(2)}) %collective-permute-start.16) | collective-permute-done | bytes 262176 | tf_op jit(solution)/shard_map/ppermute | solution.py:419
  47.2 1.0 %collective-permute-done.14.refs_4_.near_ref = bf16[1024,128]{1,0:T(8,128)(2,1)S(1)} collective-permute-done((bf16[1024,128]{1,0:T(8,128)(2,1)S(1)}, bf16[1024,128]{1,0:T(8,128)(2,1)S(1)}, u32[]{:S(2)}, u32[]{:S(2)}) %collective-permute-start.14) | collective-permute-done | bytes 262176 | tf_op jit(solution)/shard_map/ppermute | solution.py:419
  48.2 1.0 %shard_map.134.sum_ref = f32[8,128,128]{2,1,0:T(8,128)S(1)} custom-call(bf16[1024,128]{1,0:T(8,128)(2,1)S(1)} %get-tuple-element.81.refs_0_, bf16[1536,128]{1,0:T(8,128)(2,1)S(1)} %collective-permute-done.12.near_ref.refs_1_, bf16[1024,128]{1,0:T(8,128)(2,1)S(1)} %collective-permute-done.16.refs_2_, bf16[512,128]{1,0:T(8,128)(2,1)S(1)} %get-tuple-element.82.refs_3_, ...), custom_call_target="tpu_custom_call" | custom-call | flops 1250000000 | bytes 262144 | tf_op jit(solution)/shard_map/pallas_call | solution.py:43
  49.2 0.8 %collective-permute-done.15.got_ref = bf16[512,128]{1,0:T(8,128)(2,1)S(1)} collective-permute-done((bf16[512,128]{1,0:T(8,128)(2,1)S(1)}, bf16[512,128]{1,0:T(8,128)(2,1)S(1)}, u32[]{:S(2)}, u32[]{:S(2)}) %collective-permute-start.15) | collective-permute-done | bytes 131104 | tf_op jit(solution)/shard_map/ppermute | solution.py:419
  50.0 1.3 %shard_map.135 = bf16[8,128,128]{2,1,0:T(8,128)(2,1)} custom-call(bf16[512,128]{1,0:T(8,128)(2,1)S(1)} %get-tuple-element.75.own_ref, bf16[1024,128]{1,0:T(8,128)(2,1)S(1)} %collective-permute-done.14.refs_4_.near_ref, bf16[512,128]{1,0:T(8,128)(2,1)S(1)} %collective-permute-done.15.got_ref, f32[8,512,128]{2,1,0:T(8,128)S(1)} %get-tuple-element.80.refs_6_.factor_ref, ...), custom_call_target="tpu_custom_call" | custom-call | flops 67108864 | bytes 262144 | tf_op jit(solution)/shard_map/pallas_call | solution.py:43
  (9 shorter events, 0.2 us)
Async XLA Ops:
  0.6 1.0 %copy-start = (bf16[8,128,128]{2,1,0:T(8,128)(2,1)S(1)}, bf16[8,128,128]{2,1,0:T(8,128)(2,1)}, u32[]{:S(2)}) copy-start(bf16[8,128,128]{2,1,0:T(8,128)(2,1)} %param.10) | copy-start | bytes 786436
  1.6 10.5 %collective-permute-start.4 = (bf16[512,128]{1,0:T(8,128)(2,1)S(1)}, bf16[512,128]{1,0:T(8,128)(2,1)S(1)}, u32[]{:S(2)}, u32[]{:S(2)}) collective-permute-start(bf16[512,128]{1,0:T(8,128)(2,1)S(1)} %get-tuple-element.45.refs_0_), channel_id=1, source_target_pairs={{0,8},{1,9},{2,10},{3,11},{4,12},{5,13},{6,14},{7,15},{8,0},{9,1},... | collective-permute-start | bytes 393224 | tf_op jit(solution)/shard_map/ppermute | solution.py:419
  5.7 13.9 %collective-permute-start.2 = (bf16[1024,128]{1,0:T(8,128)(2,1)S(1)}, bf16[1024,128]{1,0:T(8,128)(2,1)S(1)}, u32[]{:S(2)}, u32[]{:S(2)}) collective-permute-start(bf16[1024,128]{1,0:T(8,128)(2,1)S(1)} %shard_map.114.x_ref), channel_id=1, source_target_pairs={{0,4},{1,5},{2,6},{3,7},{4,0},{5,1},{6,2},{7,3},{8,12},{9,13},{10,... | collective-permute-start | bytes 786440 | tf_op jit(solution)/shard_map/ppermute | solution.py:419
  7.4 8.5 %collective-permute-start.1 = (bf16[1024,128]{1,0:T(8,128)(2,1)S(1)}, bf16[1024,128]{1,0:T(8,128)(2,1)S(1)}, u32[]{:S(2)}, u32[]{:S(2)}) collective-permute-start(bf16[1024,128]{1,0:T(8,128)(2,1)S(1)} %shard_map.114.x_ref), channel_id=1, source_target_pairs={{0,2},{1,3},{2,0},{3,1},{4,6},{5,7},{6,4},{7,5},{8,10},{9,11},{10,... | collective-permute-start | bytes 786440 | tf_op jit(solution)/shard_map/ppermute | solution.py:419
  8.9 12.4 %collective-permute-start = (bf16[1024,128]{1,0:T(8,128)(2,1)S(1)}, bf16[1024,128]{1,0:T(8,128)(2,1)S(1)}, u32[]{:S(2)}, u32[]{:S(2)}) collective-permute-start(bf16[1024,128]{1,0:T(8,128)(2,1)S(1)} %shard_map.114.x_ref), channel_id=1, source_target_pairs={{0,1},{1,0},{2,3},{3,2},{4,5},{5,4},{6,7},{7,6},{8,9},{9,8},{10,11... | collective-permute-start | bytes 786440 | tf_op jit(solution)/shard_map/ppermute | solution.py:419
  8.9 8.6 %collective-permute-start.3 = (bf16[512,128]{1,0:T(8,128)(2,1)S(1)}, bf16[512,128]{1,0:T(8,128)(2,1)S(1)}, u32[]{:S(2)}, u32[]{:S(2)}) collective-permute-start(bf16[512,128]{1,0:T(8,128)(2,1)S(1)} %get-tuple-element.49), channel_id=1, source_target_pairs={{0,8},{1,9},{2,10},{3,11},{4,12},{5,13},{6,14},{7,15},{8,0},{9,1},... | collective-permute-start | bytes 393224 | tf_op jit(solution)/shard_map/ppermute | solution.py:419
  12.1 5.5 %collective-permute-start.6 = (bf16[512,128]{1,0:T(8,128)(2,1)S(1)}, bf16[512,128]{1,0:T(8,128)(2,1)S(1)}, u32[]{:S(2)}, u32[]{:S(2)}) collective-permute-start(bf16[512,128]{1,0:T(8,128)(2,1)S(1)} %collective-permute-done.4.refs_1_), channel_id=1, source_target_pairs={{0,2},{1,3},{2,0},{3,1},{4,6},{5,7},{6,4},{7,5},{8,10},{9,11},{10,... | collective-permute-start | bytes 393224 | tf_op jit(solution)/shard_map/ppermute | solution.py:419
  13.7 2.1 %copy-start.1 = (bf16[8,128,128]{2,1,0:T(8,128)(2,1)S(1)}, bf16[8,128,128]{2,1,0:T(8,128)(2,1)}, u32[]{:S(2)}) copy-start(bf16[8,128,128]{2,1,0:T(8,128)(2,1)} %cot_ref.3) | copy-start | bytes 786436
  13.7 2.1 %copy-start.2 = (s32[8,128]{1,0:T(8,128)S(1)}, s32[8,128]{1,0:T(8,128)}, u32[]{:S(2)}) copy-start(s32[8,128]{1,0:T(8,128)} %mask_ref.3) | copy-start | bytes 12292
  16.0 7.0 %collective-permute-start.8 = (bf16[544,128]{1,0:T(8,128)(2,1)S(1)}, bf16[544,128]{1,0:T(8,128)(2,1)S(1)}, u32[]{:S(2)}, u32[]{:S(2)}) collective-permute-start(bf16[544,128]{1,0:T(8,128)(2,1)S(1)} %get-tuple-element.62), channel_id=1, source_target_pairs={{0,4},{1,5},{2,6},{3,7},{4,0},{5,1},{6,2},{7,3},{8,12},{9,13},{10,... | collective-permute-start | bytes 417800 | tf_op jit(solution)/shard_map/ppermute | solution.py:419
  17.7 5.9 %collective-permute-start.7 = (bf16[512,128]{1,0:T(8,128)(2,1)S(1)}, bf16[512,128]{1,0:T(8,128)(2,1)S(1)}, u32[]{:S(2)}, u32[]{:S(2)}) collective-permute-start(bf16[512,128]{1,0:T(8,128)(2,1)S(1)} %shard_map.118), channel_id=1, source_target_pairs={{0,2},{1,3},{2,0},{3,1},{4,6},{5,7},{6,4},{7,5},{8,10},{9,11},{10,... | collective-permute-start | bytes 393224 | tf_op jit(solution)/shard_map/ppermute | solution.py:419
  19.6 4.0 %collective-permute-start.5 = (bf16[1024,128]{1,0:T(8,128)(2,1)S(1)}, bf16[1024,128]{1,0:T(8,128)(2,1)S(1)}, u32[]{:S(2)}, u32[]{:S(2)}) collective-permute-start(bf16[1024,128]{1,0:T(8,128)(2,1)S(1)} %collective-permute-done.2.left_in), channel_id=1, source_target_pairs={{0,1},{1,0},{2,3},{3,2},{4,5},{5,4},{6,7},{7,6},{8,9},{9,8},{10,11... | collective-permute-start | bytes 786440 | tf_op jit(solution)/shard_map/ppermute | solution.py:419
  23.0 2.3 %collective-permute-start.9 = (bf16[544,128]{1,0:T(8,128)(2,1)S(1)}, bf16[544,128]{1,0:T(8,128)(2,1)S(1)}, u32[]{:S(2)}, u32[]{:S(2)}) collective-permute-start(bf16[544,128]{1,0:T(8,128)(2,1)S(1)} %shard_map.121), channel_id=1, source_target_pairs={{0,1},{1,0},{2,3},{3,2},{4,5},{5,4},{6,7},{7,6},{8,9},{9,8},{10,11... | collective-permute-start | bytes 417800 | tf_op jit(solution)/shard_map/ppermute | solution.py:419
  28.3 5.5 %collective-permute-start.17 = (bf16[512,128]{1,0:T(8,128)(2,1)S(1)}, bf16[512,128]{1,0:T(8,128)(2,1)S(1)}, u32[]{:S(2)}, u32[]{:S(2)}) collective-permute-start(bf16[512,128]{1,0:T(8,128)(2,1)S(1)} %get-tuple-element.67.refs_4_), channel_id=1, source_target_pairs={{0,2},{1,3},{2,0},{3,1},{4,6},{5,7},{6,4},{7,5},{8,10},{9,11},{10,... | collective-permute-start | bytes 393224 | tf_op jit(solution)/shard_map/ppermute | solution.py:419
  29.8 1.5 %collective-permute-start.11 = (bf16[1024,128]{1,0:T(8,128)(2,1)S(1)}, bf16[1024,128]{1,0:T(8,128)(2,1)S(1)}, u32[]{:S(2)}, u32[]{:S(2)}) collective-permute-start(bf16[1024,128]{1,0:T(8,128)(2,1)S(1)} %get-tuple-element.72), channel_id=1, source_target_pairs={{0,1},{1,0},{2,3},{3,2},{4,5},{5,4},{6,7},{7,6},{8,9},{9,8},{10,11... | collective-permute-start | bytes 786440 | tf_op jit(solution)/shard_map/ppermute | solution.py:419
  30.1 7.2 %collective-permute-start.10 = (bf16[512,128]{1,0:T(8,128)(2,1)S(1)}, bf16[512,128]{1,0:T(8,128)(2,1)S(1)}, u32[]{:S(2)}, u32[]{:S(2)}) collective-permute-start(bf16[512,128]{1,0:T(8,128)(2,1)S(1)} %get-tuple-element.70), channel_id=1, source_target_pairs={{0,4},{1,5},{2,6},{3,7},{4,0},{5,1},{6,2},{7,3},{8,12},{9,13},{10,... | collective-permute-start | bytes 393224 | tf_op jit(solution)/shard_map/ppermute | solution.py:419
  31.4 6.0 %collective-permute-start.13 = (bf16[512,128]{1,0:T(8,128)(2,1)S(1)}, bf16[512,128]{1,0:T(8,128)(2,1)S(1)}, u32[]{:S(2)}, u32[]{:S(2)}) collective-permute-start(bf16[512,128]{1,0:T(8,128)(2,1)S(1)} %shard_map.130), channel_id=1, source_target_pairs={{0,2},{1,3},{2,0},{3,1},{4,6},{5,7},{6,4},{7,5},{8,10},{9,11},{10,... | collective-permute-start | bytes 393224 | tf_op jit(solution)/shard_map/ppermute | solution.py:419
  32.3 14.9 %collective-permute-start.16 = (bf16[1024,128]{1,0:T(8,128)(2,1)S(1)}, bf16[1024,128]{1,0:T(8,128)(2,1)S(1)}, u32[]{:S(2)}, u32[]{:S(2)}) collective-permute-start(bf16[1024,128]{1,0:T(8,128)(2,1)S(1)} %shard_map.125.after_ref.refs_0_), channel_id=1, source_target_pairs={{0,4},{1,5},{2,6},{3,7},{4,0},{5,1},{6,2},{7,3},{8,12},{9,13},{10,... | collective-permute-start | bytes 786440 | tf_op jit(solution)/shard_map/ppermute | solution.py:419
  33.9 9.5 %collective-permute-start.18 = (bf16[512,128]{1,0:T(8,128)(2,1)S(1)}, bf16[512,128]{1,0:T(8,128)(2,1)S(1)}, u32[]{:S(2)}, u32[]{:S(2)}) collective-permute-start(bf16[512,128]{1,0:T(8,128)(2,1)S(1)} %shard_map.133), channel_id=1, source_target_pairs={{0,8},{1,9},{2,10},{3,11},{4,12},{5,13},{6,14},{7,15},{8,0},{9,1},... | collective-permute-start | bytes 393224 | tf_op jit(solution)/shard_map/ppermute | solution.py:419
  37.3 5.0 %collective-permute-start.12 = (bf16[1536,128]{1,0:T(8,128)(2,1)S(1)}, bf16[1536,128]{1,0:T(8,128)(2,1)S(1)}, u32[]{:S(2)}, u32[]{:S(2)}) collective-permute-start(bf16[1536,128]{1,0:T(8,128)(2,1)S(1)} %shard_map.126), channel_id=1, source_target_pairs={{0,1},{1,0},{2,3},{3,2},{4,5},{5,4},{6,7},{7,6},{8,9},{9,8},{10,11... | collective-permute-start | bytes 1179656 | tf_op jit(solution)/shard_map/ppermute | solution.py:419
  37.5 12.5 %collective-permute-start.15 = (bf16[512,128]{1,0:T(8,128)(2,1)S(1)}, bf16[512,128]{1,0:T(8,128)(2,1)S(1)}, u32[]{:S(2)}, u32[]{:S(2)}) collective-permute-start(bf16[512,128]{1,0:T(8,128)(2,1)S(1)} %shard_map.131.after_ref), channel_id=1, source_target_pairs={{0,8},{1,9},{2,10},{3,11},{4,12},{5,13},{6,14},{7,15},{8,0},{9,1},... | collective-permute-start | bytes 393224 | tf_op jit(solution)/shard_map/ppermute | solution.py:419
  40.1 8.0 %collective-permute-start.14 = (bf16[1024,128]{1,0:T(8,128)(2,1)S(1)}, bf16[1024,128]{1,0:T(8,128)(2,1)S(1)}, u32[]{:S(2)}, u32[]{:S(2)}) collective-permute-start(bf16[1024,128]{1,0:T(8,128)(2,1)S(1)} %shard_map.132), channel_id=1, source_target_pairs={{0,2},{1,3},{2,0},{3,1},{4,6},{5,7},{6,4},{7,5},{8,10},{9,11},{10,... | collective-permute-start | bytes 786440 | tf_op jit(solution)/shard_map/ppermute | solution.py:419

commit v12 on v11

--- a/solution.py
+++ b/solution.py
@@ -510,13 +510,13 @@
     (left_sum,) = call(add_kernel, [side], vmem=[left_parts[2], both_got])
     x_got.append(swap(after(right_b[3], left_sum), CHIP_X))
     left_got = swap(left_sum, Z_LOW)
+    (right_back,) = call(near_kernel, [side], vmem=[right_a[1], right_b[1], x_got[1]])
     z_got = []
-    for mine, got in zip((right_a[2], right_b[2]), x_got):
-        (total,) = call(add_kernel, [halves], vmem=[mine, got, left_sum])
+    for mine, got, late in zip((right_a[2], right_b[2]), x_got, (left_sum, right_back)):
+        (total,) = call(add_kernel, [halves], vmem=[mine, got, late])
         z_got.append(swap(total, Z_HIGH))
     (near_back,) = call(back_kernel, [core], vmem=[left_parts[1], out_1, out_far, left_sum])
     near_got = swap(near_back, CORE)
-    (right_back,) = call(near_kernel, [side], vmem=[right_a[1], right_b[1], total])
     right_near = swap(right_back, CHIP_X)
 
     factors, normed, inverse, open_part, gain_t = call(

time: 51.5 us -> 51.9 us (level)
  transfers between devices with their start and end apart: 19 -> 19, of which waited for: 10 -> 9; matrix products, arithmetic and copies ran while one was open for 3% -> 3% of each run, Pallas kernels for 21% -> 20%
where the time goes in v12:
time: 51.9 us; the launch traced here: 51.7 us
  starting transfers between devices  23.8 us (46%)
  Pallas kernels  14.9 us (29%)
  waiting for transfers between devices  9.5 us (18%)
  other arithmetic  1.67 us (3%)
  local copies, waits for them, and re-layouts  0.95 us (2%)
  between operations  0.83 us (2%)
    ppermute x19, starting transfers between devices, swap(): return lax.ppermute(values, 'row', [(s, s ^ offset) for s in range(16)])  23.8 us
    pallas_call x23, Pallas kernels, call(): pl.pallas_call(kernel, out_shape=[jax.ShapeDtypeStruct(s, d) for s, d in...  14.9 us
    ppermute x19, waiting for transfers between devices, swap(): return lax.ppermute(values, 'row', [(s, s ^ offset) for s in range(16)])  9.5 us
  transfers between devices with their start and end apart: 19, of which 9 were waited for; matrix products, arithmetic and copies ran while one was open for 3% of the time, Pallas kernels for 20%

profile of v12, /device:TPU:0, one launch (start us, length us, event | category | flops | bytes accessed | tf_op | source)
XLA Modules:
  0.0 51.7 jit_solution(1858631510288754395)
XLA Ops:
  0.6 0.0 copy-start
  0.6 0.9 %copy-done = bf16[8,128,128]{2,1,0:T(8,128)(2,1)S(1)} copy-done((bf16[8,128,128]{2,1,0:T(8,128)(2,1)S(1)}, bf16[8,128,128]{2,1,0:T(8,128)(2,1)}, u32[]{:S(2)}) %copy-start) | copy-done | bytes 262168
  1.6 4.1 %collective-permute-start.4 = (bf16[512,128]{1,0:T(8,128)(2,1)S(1)}, bf16[512,128]{1,0:T(8,128)(2,1)S(1)}, u32[]{:S(2)}, u32[]{:S(2)}) collective-permute-start(bf16[512,128]{1,0:T(8,128)(2,1)S(1)} %get-tuple-element.45.refs_0_), channel_id=1, source_target_pairs={{0,8},{1,9},{2,10},{3,11},{4,12},{5,13},{6,14},{7,15},{8,0},{9,1},... | collective-permute-start | bytes 393224 | tf_op jit(solution)/shard_map/ppermute | solution.py:419
  5.7 1.6 %collective-permute-start.2 = (bf16[1024,128]{1,0:T(8,128)(2,1)S(1)}, bf16[1024,128]{1,0:T(8,128)(2,1)S(1)}, u32[]{:S(2)}, u32[]{:S(2)}) collective-permute-start(bf16[1024,128]{1,0:T(8,128)(2,1)S(1)} %shard_map.114.x_ref), channel_id=1, source_target_pairs={{0,4},{1,5},{2,6},{3,7},{4,0},{5,1},{6,2},{7,3},{8,12},{9,13},{10,... | collective-permute-start | bytes 786440 | tf_op jit(solution)/shard_map/ppermute | solution.py:419
  7.4 1.5 %collective-permute-start.1 = (bf16[1024,128]{1,0:T(8,128)(2,1)S(1)}, bf16[1024,128]{1,0:T(8,128)(2,1)S(1)}, u32[]{:S(2)}, u32[]{:S(2)}) collective-permute-start(bf16[1024,128]{1,0:T(8,128)(2,1)S(1)} %shard_map.114.x_ref), channel_id=1, source_target_pairs={{0,2},{1,3},{2,0},{3,1},{4,6},{5,7},{6,4},{7,5},{8,10},{9,11},{10,... | collective-permute-start | bytes 786440 | tf_op jit(solution)/shard_map/ppermute | solution.py:419
  8.9 0.0 collective-permute-start
  8.9 0.3 collective-permute-start.3
  9.2 0.7 %pad_maximum_fusion.params_ref.refs_3_.refs_4_ = f32[4,128]{1,0:T(4,128)S(1)} fusion(f32[1,128]{1,0:T(1,128)} %bitcast.8, f32[1,128]{1,0:T(1,128)} %bitcast.9, f32[1,128]{1,0:T(1,128)} %bitcast.10, f32[1,128]{1,0:T(1,128)} %bitcast.11), kind=kLoop, calls=%fused_computation.1 | loop fusion | flops 1536 | bytes 4096 | tf_op jit(solution)/shard_map/stack | solution.py:450
  9.9 1.0 %pad_add_fusion.weight_ref.refs_2_.refs_3_.refs_8_ = bf16[128,768]{1,0:T(8,128)(2,1)S(1)} fusion(bf16[128,128]{1,0:T(8,128)(2,1)} %param.19, bf16[128,128]{1,0:T(8,128)(2,1)} %param.16, bf16[128,512]{1,0:T(8,128)(2,1)} %param.15), kind=kLoop, calls=%fused_computation | loop fusion | flops 589824 | bytes 393216 | tf_op jit(solution)/shard_map/add | solution.py:449
  10.9 1.2 %collective-permute-done.4.refs_1_ = bf16[512,128]{1,0:T(8,128)(2,1)S(1)} collective-permute-done((bf16[512,128]{1,0:T(8,128)(2,1)S(1)}, bf16[512,128]{1,0:T(8,128)(2,1)S(1)}, u32[]{:S(2)}, u32[]{:S(2)}) %collective-permute-start.4) | collective-permute-done | bytes 131104 | tf_op jit(solution)/shard_map/ppermute | solution.py:419
  12.1 1.6 %collective-permute-start.6 = (bf16[512,128]{1,0:T(8,128)(2,1)S(1)}, bf16[512,128]{1,0:T(8,128)(2,1)S(1)}, u32[]{:S(2)}, u32[]{:S(2)}) collective-permute-start(bf16[512,128]{1,0:T(8,128)(2,1)S(1)} %collective-permute-done.4.refs_1_), channel_id=1, source_target_pairs={{0,2},{1,3},{2,0},{3,1},{4,6},{5,7},{6,4},{7,5},{8,10},{9,11},{10,... | collective-permute-start | bytes 393224 | tf_op jit(solution)/shard_map/ppermute | solution.py:419
  13.7 0.0 copy-start.1
  13.7 0.0 copy-start.2
  13.7 1.9 %shard_map.115 = (bf16[1024,128]{1,0:T(8,128)(2,1)S(1)}, bf16[1024,128]{1,0:T(8,128)(2,1)S(1)}, f32[256,128]{1,0:T(8,128)S(1)}, bf16[512,128]{1,0:T(8,128)(2,1)S...) custom-call(s32[1]{0:T(128)} %bitcast.me_ref.refs_0_, bf16[1024,128]{1,0:T(8,128)(2,1)S(1)} %shard_map.114.x_ref, ...), custom_call_target="tpu_custom_call" | custom-call | flops 5000000000 | bytes 262144 | tf_op jit(solution)/shard_map/pallas_call | solution.py:43
  15.7 0.2 collective-permute-done.1.refs_0_.after_ref
  15.9 0.0 copy-done.1
  15.9 0.0 copy-done.2
  15.9 0.1 shard_map.120
  16.0 0.5 collective-permute-start.8
  16.5 1.0 %collective-permute-done.3.refs_0_.message_ref = bf16[512,128]{1,0:T(8,128)(2,1)S(1)} collective-permute-done((bf16[512,128]{1,0:T(8,128)(2,1)S(1)}, bf16[512,128]{1,0:T(8,128)(2,1)S(1)}, u32[]{:S(2)}, u32[]{:S(2)}) %collective-permute-start.3) | collective-permute-done | bytes 131104 | tf_op jit(solution)/shard_map/ppermute | solution.py:419
  17.5 0.2 collective-permute-done.6.refs_0_.refs_1_
  17.7 1.9 %collective-permute-start.7 = (bf16[512,128]{1,0:T(8,128)(2,1)S(1)}, bf16[512,128]{1,0:T(8,128)(2,1)S(1)}, u32[]{:S(2)}, u32[]{:S(2)}) collective-permute-start(bf16[512,128]{1,0:T(8,128)(2,1)S(1)} %shard_map.118), channel_id=1, source_target_pairs={{0,2},{1,3},{2,0},{3,1},{4,6},{5,7},{6,4},{7,5},{8,10},{9,11},{10,... | collective-permute-start | bytes 393224 | tf_op jit(solution)/shard_map/ppermute | solution.py:419
  19.6 0.0 collective-permute-done.2.left_in
  19.6 0.0 collective-permute-start.5
  19.6 1.7 %shard_map.117 = (bf16[1024,128]{1,0:T(8,128)(2,1)S(1)}, bf16[1024,128]{1,0:T(8,128)(2,1)S(1)}, f32[256,128]{1,0:T(8,128)S(1)}) custom-call(s32[1]{0:T(128)} %bitcast.me_ref.refs_0_, bf16[1024,128]{1,0:T(8,128)(2,1)S(1)} %collective-permute-done.2.left_in, bf16[512,128]{1,0:T(8,128)(2,1)S(1)} %collective-permute-done.3.refs_0_.message_ref, ...), custom_call_target="tpu_custom_call" | custom-call | flops 5000000000 | bytes 262144 | tf_op jit(solution)/shard_map/pallas_call | solution.py:43
  21.3 0.0 collective-permute-done.left_in
  21.3 1.7 %shard_map.116 = (bf16[1024,128]{1,0:T(8,128)(2,1)S(1)}, bf16[1024,128]{1,0:T(8,128)(2,1)S(1)}, f32[256,128]{1,0:T(8,128)S(1)}) custom-call(s32[1]{0:T(128)} %bitcast.me_ref.refs_0_, bf16[1024,128]{1,0:T(8,128)(2,1)S(1)} %collective-permute-done.left_in, bf16[1024,128]{1,0:T(8,128)(2,1)S(1)} %collective-permute-done.1.refs_0_.after_ref, ...), custom_call_target="tpu_custom_call" | custom-call | flops 5000000000 | bytes 262144 | tf_op jit(solution)/shard_map/pallas_call | solution.py:43
  23.0 0.0 collective-permute-done.8.got_ref.refs_15_
  23.0 0.6 %collective-permute-start.9 = (bf16[544,128]{1,0:T(8,128)(2,1)S(1)}, bf16[544,128]{1,0:T(8,128)(2,1)S(1)}, u32[]{:S(2)}, u32[]{:S(2)}) collective-permute-start(bf16[544,128]{1,0:T(8,128)(2,1)S(1)} %shard_map.121), channel_id=1, source_target_pairs={{0,1},{1,0},{2,3},{3,2},{4,5},{5,4},{6,7},{7,6},{8,9},{9,8},{10,11... | collective-permute-start | bytes 417800 | tf_op jit(solution)/shard_map/ppermute | solution.py:419
  23.6 0.0 collective-permute-done.7.refs_0_
  23.6 0.0 collective-permute-done.5.left_in
  23.6 1.7 %shard_map.119 = (bf16[1024,128]{1,0:T(8,128)(2,1)S(1)}, bf16[1024,128]{1,0:T(8,128)(2,1)S(1)}, f32[256,128]{1,0:T(8,128)S(1)}) custom-call(s32[1]{0:T(128)} %bitcast.me_ref.refs_0_, bf16[1024,128]{1,0:T(8,128)(2,1)S(1)} %collective-permute-done.5.left_in, bf16[512,128]{1,0:T(8,128)(2,1)S(1)} %collective-permute-done.7.refs_0_, ...), custom_call_target="tpu_custom_call" | custom-call | flops 5000000000 | bytes 262144 | tf_op jit(solution)/shard_map/pallas_call | solution.py:43
  25.3 0.0 collective-permute-done.9.refs_14_
  25.3 2.2 %shard_map.122 = (bf16[256,128]{1,0:T(8,128)(2,1)S(1)}, bf16[256,128]{1,0:T(8,128)(2,1)S(1)}, bf16[512,128]{1,0:T(8,128)(2,1)S(1)}, f32[1024,128]{1,0:T(8,128)S(1)}) custom-call(s32[1]{0:T(128)} %bitcast.me_ref.refs_0_, bf16[1024,128]{1,0:T(8,128)(2,1)S(1)} %get-tuple-element.46.refs_1_.refs_0_, bf16[1024,128]{1,0:T(8,128)(2,1)S(1)} %get-tuple-element.48.refs_2_.refs_1_, ...), custom_call_target="tpu_custom_call" | custom-call | flops 67108864 | bytes 262144 | tf_op jit(solution)/shard_map/pallas_call | solution.py:43
  27.5 0.3 shard_map.123
  27.9 0.4 shard_map.124
  28.3 1.4 %collective-permute-start.17 = (bf16[512,128]{1,0:T(8,128)(2,1)S(1)}, bf16[512,128]{1,0:T(8,128)(2,1)S(1)}, u32[]{:S(2)}, u32[]{:S(2)}) collective-permute-start(bf16[512,128]{1,0:T(8,128)(2,1)S(1)} %get-tuple-element.67.refs_4_), channel_id=1, source_target_pairs={{0,2},{1,3},{2,0},{3,1},{4,6},{5,7},{6,4},{7,5},{8,10},{9,11},{10,... | collective-permute-start | bytes 393224 | tf_op jit(solution)/shard_map/ppermute | solution.py:419
  29.8 0.0 collective-permute-start.11
  29.8 0.3 shard_map.129
  30.1 0.9 %collective-permute-start.10 = (bf16[512,128]{1,0:T(8,128)(2,1)S(1)}, bf16[512,128]{1,0:T(8,128)(2,1)S(1)}, u32[]{:S(2)}, u32[]{:S(2)}) collective-permute-start(bf16[512,128]{1,0:T(8,128)(2,1)S(1)} %get-tuple-element.70), channel_id=1, source_target_pairs={{0,4},{1,5},{2,6},{3,7},{4,0},{5,1},{6,2},{7,3},{8,12},{9,13},{10,... | collective-permute-start | bytes 393224 | tf_op jit(solution)/shard_map/ppermute | solution.py:419
  31.0 0.3 collective-permute-done.11.got_ref
  31.3 0.1 shard_map.125.after_ref.refs_0_
  31.4 0.9 %collective-permute-start.13 = (bf16[512,128]{1,0:T(8,128)(2,1)S(1)}, bf16[512,128]{1,0:T(8,128)(2,1)S(1)}, u32[]{:S(2)}, u32[]{:S(2)}) collective-permute-start(bf16[512,128]{1,0:T(8,128)(2,1)S(1)} %shard_map.130), channel_id=1, source_target_pairs={{0,2},{1,3},{2,0},{3,1},{4,6},{5,7},{6,4},{7,5},{8,10},{9,11},{10,... | collective-permute-start | bytes 393224 | tf_op jit(solution)/shard_map/ppermute | solution.py:419
  32.3 1.1 %collective-permute-start.16 = (bf16[1024,128]{1,0:T(8,128)(2,1)S(1)}, bf16[1024,128]{1,0:T(8,128)(2,1)S(1)}, u32[]{:S(2)}, u32[]{:S(2)}) collective-permute-start(bf16[1024,128]{1,0:T(8,128)(2,1)S(1)} %shard_map.125.after_ref.refs_0_), channel_id=1, source_target_pairs={{0,4},{1,5},{2,6},{3,7},{4,0},{5,1},{6,2},{7,3},{8,12},{9,13},{10,... | collective-permute-start | bytes 786440 | tf_op jit(solution)/shard_map/ppermute | solution.py:419
  33.4 0.4 collective-permute-done.17.got_ref
  33.9 3.4 %collective-permute-start.18 = (bf16[512,128]{1,0:T(8,128)(2,1)S(1)}, bf16[512,128]{1,0:T(8,128)(2,1)S(1)}, u32[]{:S(2)}, u32[]{:S(2)}) collective-permute-start(bf16[512,128]{1,0:T(8,128)(2,1)S(1)} %shard_map.133), channel_id=1, source_target_pairs={{0,8},{1,9},{2,10},{3,11},{4,12},{5,13},{6,14},{7,15},{8,0},{9,1},... | collective-permute-start | bytes 393224 | tf_op jit(solution)/shard_map/ppermute | solution.py:419
  37.3 0.0 collective-permute-done.10.far_ref
  37.3 0.1 collective-permute-start.12
  37.4 0.0 collective-permute-done.13.after_ref.got_ref
  37.5 0.7 %collective-permute-start.14 = (bf16[1024,128]{1,0:T(8,128)(2,1)S(1)}, bf16[1024,128]{1,0:T(8,128)(2,1)S(1)}, u32[]{:S(2)}, u32[]{:S(2)}) collective-permute-start(bf16[1024,128]{1,0:T(8,128)(2,1)S(1)} %shard_map.131.refs_0_), channel_id=1, source_target_pairs={{0,2},{1,3},{2,0},{3,1},{4,6},{5,7},{6,4},{7,5},{8,10},{9,11},{10,... | collective-permute-start | bytes 786440 | tf_op jit(solution)/shard_map/ppermute | solution.py:419
  38.2 3.0 %collective-permute-start.15 = (bf16[512,128]{1,0:T(8,128)(2,1)S(1)}, bf16[512,128]{1,0:T(8,128)(2,1)S(1)}, u32[]{:S(2)}, u32[]{:S(2)}) collective-permute-start(bf16[512,128]{1,0:T(8,128)(2,1)S(1)} %shard_map.132), channel_id=1, source_target_pairs={{0,8},{1,9},{2,10},{3,11},{4,12},{5,13},{6,14},{7,15},{8,0},{9,1},... | collective-permute-start | bytes 393224 | tf_op jit(solution)/shard_map/ppermute | solution.py:419
  41.2 1.1 %shard_map.127 = (f32[8,512,128]{2,1,0:T(8,128)S(1)}, f32[8,128,128]{2,1,0:T(8,128)S(1)}, f32[8,128]{1,0:T(8,128)S(1)}, f32[8,128,128]{2,1,0:T(8,128)S(1)}, f32[128,128]{1,0:T(8,128)S(1)}) custom-call(bf16[1024,128]{1,0:T(8,128)(2,1)S(1)} %shard_map.114.x_ref, bf16[8,128,128]{2,1,0:T(8,128)(2,1)S(1)} %copy-done.1, s32[8,128]{1,0:T(8,128)S(1)} %copy-done.2, ...), custom_call_target="tpu_custom_call" | custom-call | flops 5000000000 | bytes 262144 | tf_op jit(solution)/shard_map/pallas_call | solution.py:43
  42.3 0.0 collective-permute-done.12.near_ref.refs_1_
  42.3 0.9 %shard_map.128 = (bf16[8,128,128]{2,1,0:T(8,128)(2,1)}, f32[8,128,128]{2,1,0:T(8,128)S(1)}) custom-call(s32[1]{0:T(128)} %bitcast.me_ref.refs_0_, bf16[256,128]{1,0:T(8,128)(2,1)S(1)} %get-tuple-element.65.own_ref, bf16[1536,128]{1,0:T(8,128)(2,1)S(1)} %collective-permute-done.12.near_ref.refs_1_, bf16[512,128]{1,0:T(8,128)(2,1)S(1)} %collective-permute-done.10.far_ref, ...), custom_call_target="tpu_custom_call" | custom-call | flops 67108864 | bytes 262144 | tf_op jit(solution)/shard_map/pallas_call | solution.py:43
  43.2 0.1 collective-permute-done.18.refs_5_
  43.3 3.5 %collective-permute-done.16.refs_2_ = bf16[1024,128]{1,0:T(8,128)(2,1)S(1)} collective-permute-done((bf16[1024,128]{1,0:T(8,128)(2,1)S(1)}, bf16[1024,128]{1,0:T(8,128)(2,1)S(1)}, u32[]{:S(2)}, u32[]{:S(2)}) %collective-permute-start.16) | collective-permute-done | bytes 262176 | tf_op jit(solution)/shard_map/ppermute | solution.py:419
  46.8 0.0 collective-permute-done.14.refs_4_.near_ref
  46.8 1.0 %shard_map.134.sum_ref = f32[8,128,128]{2,1,0:T(8,128)S(1)} custom-call(bf16[1024,128]{1,0:T(8,128)(2,1)S(1)} %get-tuple-element.81.refs_0_, bf16[1536,128]{1,0:T(8,128)(2,1)S(1)} %collective-permute-done.12.near_ref.refs_1_, bf16[1024,128]{1,0:T(8,128)(2,1)S(1)} %collective-permute-done.16.refs_2_, bf16[512,128]{1,0:T(8,128)(2,1)S(1)} %get-tuple-element.82.refs_3_, ...), custom_call_target="tpu_custom_call" | custom-call | flops 1250000000 | bytes 262144 | tf_op jit(solution)/shard_map/pallas_call | solution.py:43
  47.8 2.5 %collective-permute-done.15.got_ref = bf16[512,128]{1,0:T(8,128)(2,1)S(1)} collective-permute-done((bf16[512,128]{1,0:T(8,128)(2,1)S(1)}, bf16[512,128]{1,0:T(8,128)(2,1)S(1)}, u32[]{:S(2)}, u32[]{:S(2)}) %collective-permute-start.15) | collective-permute-done | bytes 131104 | tf_op jit(solution)/shard_map/ppermute | solution.py:419
  50.4 1.3 %shard_map.135 = bf16[8,128,128]{2,1,0:T(8,128)(2,1)} custom-call(bf16[512,128]{1,0:T(8,128)(2,1)S(1)} %get-tuple-element.75.own_ref, bf16[1024,128]{1,0:T(8,128)(2,1)S(1)} %collective-permute-done.14.refs_4_.near_ref, bf16[512,128]{1,0:T(8,128)(2,1)S(1)} %collective-permute-done.15.got_ref, f32[8,512,128]{2,1,0:T(8,128)S(1)} %get-tuple-element.80.refs_6_.factor_ref, ...), custom_call_target="tpu_custom_call" | custom-call | flops 67108864 | bytes 262144 | tf_op jit(solution)/shard_map/pallas_call | solution.py:43
  (9 shorter events, 0.2 us)
Async XLA Ops:
  0.6 1.0 %copy-start = (bf16[8,128,128]{2,1,0:T(8,128)(2,1)S(1)}, bf16[8,128,128]{2,1,0:T(8,128)(2,1)}, u32[]{:S(2)}) copy-start(bf16[8,128,128]{2,1,0:T(8,128)(2,1)} %param.10) | copy-start | bytes 786436
  1.6 10.5 %collective-permute-start.4 = (bf16[512,128]{1,0:T(8,128)(2,1)S(1)}, bf16[512,128]{1,0:T(8,128)(2,1)S(1)}, u32[]{:S(2)}, u32[]{:S(2)}) collective-permute-start(bf16[512,128]{1,0:T(8,128)(2,1)S(1)} %get-tuple-element.45.refs_0_), channel_id=1, source_target_pairs={{0,8},{1,9},{2,10},{3,11},{4,12},{5,13},{6,14},{7,15},{8,0},{9,1},... | collective-permute-start | bytes 393224 | tf_op jit(solution)/shard_map/ppermute | solution.py:419
  5.7 13.9 %collective-permute-start.2 = (bf16[1024,128]{1,0:T(8,128)(2,1)S(1)}, bf16[1024,128]{1,0:T(8,128)(2,1)S(1)}, u32[]{:S(2)}, u32[]{:S(2)}) collective-permute-start(bf16[1024,128]{1,0:T(8,128)(2,1)S(1)} %shard_map.114.x_ref), channel_id=1, source_target_pairs={{0,4},{1,5},{2,6},{3,7},{4,0},{5,1},{6,2},{7,3},{8,12},{9,13},{10,... | collective-permute-start | bytes 786440 | tf_op jit(solution)/shard_map/ppermute | solution.py:419
  7.4 8.5 %collective-permute-start.1 = (bf16[1024,128]{1,0:T(8,128)(2,1)S(1)}, bf16[1024,128]{1,0:T(8,128)(2,1)S(1)}, u32[]{:S(2)}, u32[]{:S(2)}) collective-permute-start(bf16[1024,128]{1,0:T(8,128)(2,1)S(1)} %shard_map.114.x_ref), channel_id=1, source_target_pairs={{0,2},{1,3},{2,0},{3,1},{4,6},{5,7},{6,4},{7,5},{8,10},{9,11},{10,... | collective-permute-start | bytes 786440 | tf_op jit(solution)/shard_map/ppermute | solution.py:419
  8.9 12.4 %collective-permute-start = (bf16[1024,128]{1,0:T(8,128)(2,1)S(1)}, bf16[1024,128]{1,0:T(8,128)(2,1)S(1)}, u32[]{:S(2)}, u32[]{:S(2)}) collective-permute-start(bf16[1024,128]{1,0:T(8,128)(2,1)S(1)} %shard_map.114.x_ref), channel_id=1, source_target_pairs={{0,1},{1,0},{2,3},{3,2},{4,5},{5,4},{6,7},{7,6},{8,9},{9,8},{10,11... | collective-permute-start | bytes 786440 | tf_op jit(solution)/shard_map/ppermute | solution.py:419
  8.9 8.6 %collective-permute-start.3 = (bf16[512,128]{1,0:T(8,128)(2,1)S(1)}, bf16[512,128]{1,0:T(8,128)(2,1)S(1)}, u32[]{:S(2)}, u32[]{:S(2)}) collective-permute-start(bf16[512,128]{1,0:T(8,128)(2,1)S(1)} %get-tuple-element.49), channel_id=1, source_target_pairs={{0,8},{1,9},{2,10},{3,11},{4,12},{5,13},{6,14},{7,15},{8,0},{9,1},... | collective-permute-start | bytes 393224 | tf_op jit(solution)/shard_map/ppermute | solution.py:419
  12.1 5.5 %collective-permute-start.6 = (bf16[512,128]{1,0:T(8,128)(2,1)S(1)}, bf16[512,128]{1,0:T(8,128)(2,1)S(1)}, u32[]{:S(2)}, u32[]{:S(2)}) collective-permute-start(bf16[512,128]{1,0:T(8,128)(2,1)S(1)} %collective-permute-done.4.refs_1_), channel_id=1, source_target_pairs={{0,2},{1,3},{2,0},{3,1},{4,6},{5,7},{6,4},{7,5},{8,10},{9,11},{10,... | collective-permute-start | bytes 393224 | tf_op jit(solution)/shard_map/ppermute | solution.py:419
  13.7 2.1 %copy-start.1 = (bf16[8,128,128]{2,1,0:T(8,128)(2,1)S(1)}, bf16[8,128,128]{2,1,0:T(8,128)(2,1)}, u32[]{:S(2)}) copy-start(bf16[8,128,128]{2,1,0:T(8,128)(2,1)} %cot_ref.3) | copy-start | bytes 786436
  13.7 2.1 %copy-start.2 = (s32[8,128]{1,0:T(8,128)S(1)}, s32[8,128]{1,0:T(8,128)}, u32[]{:S(2)}) copy-start(s32[8,128]{1,0:T(8,128)} %mask_ref.3) | copy-start | bytes 12292
  16.0 7.0 %collective-permute-start.8 = (bf16[544,128]{1,0:T(8,128)(2,1)S(1)}, bf16[544,128]{1,0:T(8,128)(2,1)S(1)}, u32[]{:S(2)}, u32[]{:S(2)}) collective-permute-start(bf16[544,128]{1,0:T(8,128)(2,1)S(1)} %get-tuple-element.62), channel_id=1, source_target_pairs={{0,4},{1,5},{2,6},{3,7},{4,0},{5,1},{6,2},{7,3},{8,12},{9,13},{10,... | collective-permute-start | bytes 417800 | tf_op jit(solution)/shard_map/ppermute | solution.py:419
  17.7 5.9 %collective-permute-start.7 = (bf16[512,128]{1,0:T(8,128)(2,1)S(1)}, bf16[512,128]{1,0:T(8,128)(2,1)S(1)}, u32[]{:S(2)}, u32[]{:S(2)}) collective-permute-start(bf16[512,128]{1,0:T(8,128)(2,1)S(1)} %shard_map.118), channel_id=1, source_target_pairs={{0,2},{1,3},{2,0},{3,1},{4,6},{5,7},{6,4},{7,5},{8,10},{9,11},{10,... | collective-permute-start | bytes 393224 | tf_op jit(solution)/shard_map/ppermute | solution.py:419
  19.6 4.0 %collective-permute-start.5 = (bf16[1024,128]{1,0:T(8,128)(2,1)S(1)}, bf16[1024,128]{1,0:T(8,128)(2,1)S(1)}, u32[]{:S(2)}, u32[]{:S(2)}) collective-permute-start(bf16[1024,128]{1,0:T(8,128)(2,1)S(1)} %collective-permute-done.2.left_in), channel_id=1, source_target_pairs={{0,1},{1,0},{2,3},{3,2},{4,5},{5,4},{6,7},{7,6},{8,9},{9,8},{10,11... | collective-permute-start | bytes 786440 | tf_op jit(solution)/shard_map/ppermute | solution.py:419
  23.0 2.3 %collective-permute-start.9 = (bf16[544,128]{1,0:T(8,128)(2,1)S(1)}, bf16[544,128]{1,0:T(8,128)(2,1)S(1)}, u32[]{:S(2)}, u32[]{:S(2)}) collective-permute-start(bf16[544,128]{1,0:T(8,128)(2,1)S(1)} %shard_map.121), channel_id=1, source_target_pairs={{0,1},{1,0},{2,3},{3,2},{4,5},{5,4},{6,7},{7,6},{8,9},{9,8},{10,11... | collective-permute-start | bytes 417800 | tf_op jit(solution)/shard_map/ppermute | solution.py:419
  28.3 5.5 %collective-permute-start.17 = (bf16[512,128]{1,0:T(8,128)(2,1)S(1)}, bf16[512,128]{1,0:T(8,128)(2,1)S(1)}, u32[]{:S(2)}, u32[]{:S(2)}) collective-permute-start(bf16[512,128]{1,0:T(8,128)(2,1)S(1)} %get-tuple-element.67.refs_4_), channel_id=1, source_target_pairs={{0,2},{1,3},{2,0},{3,1},{4,6},{5,7},{6,4},{7,5},{8,10},{9,11},{10,... | collective-permute-start | bytes 393224 | tf_op jit(solution)/shard_map/ppermute | solution.py:419
  29.8 1.5 %collective-permute-start.11 = (bf16[1024,128]{1,0:T(8,128)(2,1)S(1)}, bf16[1024,128]{1,0:T(8,128)(2,1)S(1)}, u32[]{:S(2)}, u32[]{:S(2)}) collective-permute-start(bf16[1024,128]{1,0:T(8,128)(2,1)S(1)} %get-tuple-element.72), channel_id=1, source_target_pairs={{0,1},{1,0},{2,3},{3,2},{4,5},{5,4},{6,7},{7,6},{8,9},{9,8},{10,11... | collective-permute-start | bytes 786440 | tf_op jit(solution)/shard_map/ppermute | solution.py:419
  30.1 7.2 %collective-permute-start.10 = (bf16[512,128]{1,0:T(8,128)(2,1)S(1)}, bf16[512,128]{1,0:T(8,128)(2,1)S(1)}, u32[]{:S(2)}, u32[]{:S(2)}) collective-permute-start(bf16[512,128]{1,0:T(8,128)(2,1)S(1)} %get-tuple-element.70), channel_id=1, source_target_pairs={{0,4},{1,5},{2,6},{3,7},{4,0},{5,1},{6,2},{7,3},{8,12},{9,13},{10,... | collective-permute-start | bytes 393224 | tf_op jit(solution)/shard_map/ppermute | solution.py:419
  31.4 6.0 %collective-permute-start.13 = (bf16[512,128]{1,0:T(8,128)(2,1)S(1)}, bf16[512,128]{1,0:T(8,128)(2,1)S(1)}, u32[]{:S(2)}, u32[]{:S(2)}) collective-permute-start(bf16[512,128]{1,0:T(8,128)(2,1)S(1)} %shard_map.130), channel_id=1, source_target_pairs={{0,2},{1,3},{2,0},{3,1},{4,6},{5,7},{6,4},{7,5},{8,10},{9,11},{10,... | collective-permute-start | bytes 393224 | tf_op jit(solution)/shard_map/ppermute | solution.py:419
  32.3 14.5 %collective-permute-start.16 = (bf16[1024,128]{1,0:T(8,128)(2,1)S(1)}, bf16[1024,128]{1,0:T(8,128)(2,1)S(1)}, u32[]{:S(2)}, u32[]{:S(2)}) collective-permute-start(bf16[1024,128]{1,0:T(8,128)(2,1)S(1)} %shard_map.125.after_ref.refs_0_), channel_id=1, source_target_pairs={{0,4},{1,5},{2,6},{3,7},{4,0},{5,1},{6,2},{7,3},{8,12},{9,13},{10,... | collective-permute-start | bytes 786440 | tf_op jit(solution)/shard_map/ppermute | solution.py:419
  33.9 9.5 %collective-permute-start.18 = (bf16[512,128]{1,0:T(8,128)(2,1)S(1)}, bf16[512,128]{1,0:T(8,128)(2,1)S(1)}, u32[]{:S(2)}, u32[]{:S(2)}) collective-permute-start(bf16[512,128]{1,0:T(8,128)(2,1)S(1)} %shard_map.133), channel_id=1, source_target_pairs={{0,8},{1,9},{2,10},{3,11},{4,12},{5,13},{6,14},{7,15},{8,0},{9,1},... | collective-permute-start | bytes 393224 | tf_op jit(solution)/shard_map/ppermute | solution.py:419
  37.3 5.0 %collective-permute-start.12 = (bf16[1536,128]{1,0:T(8,128)(2,1)S(1)}, bf16[1536,128]{1,0:T(8,128)(2,1)S(1)}, u32[]{:S(2)}, u32[]{:S(2)}) collective-permute-start(bf16[1536,128]{1,0:T(8,128)(2,1)S(1)} %shard_map.126), channel_id=1, source_target_pairs={{0,1},{1,0},{2,3},{3,2},{4,5},{5,4},{6,7},{7,6},{8,9},{9,8},{10,11... | collective-permute-start | bytes 1179656 | tf_op jit(solution)/shard_map/ppermute | solution.py:419
  37.5 9.3 %collective-permute-start.14 = (bf16[1024,128]{1,0:T(8,128)(2,1)S(1)}, bf16[1024,128]{1,0:T(8,128)(2,1)S(1)}, u32[]{:S(2)}, u32[]{:S(2)}) collective-permute-start(bf16[1024,128]{1,0:T(8,128)(2,1)S(1)} %shard_map.131.refs_0_), channel_id=1, source_target_pairs={{0,2},{1,3},{2,0},{3,1},{4,6},{5,7},{6,4},{7,5},{8,10},{9,11},{10,... | collective-permute-start | bytes 786440 | tf_op jit(solution)/shard_map/ppermute | solution.py:419
  38.2 12.2 %collective-permute-start.15 = (bf16[512,128]{1,0:T(8,128)(2,1)S(1)}, bf16[512,128]{1,0:T(8,128)(2,1)S(1)}, u32[]{:S(2)}, u32[]{:S(2)}) collective-permute-start(bf16[512,128]{1,0:T(8,128)(2,1)S(1)} %shard_map.132), channel_id=1, source_target_pairs={{0,8},{1,9},{2,10},{3,11},{4,12},{5,13},{6,14},{7,15},{8,0},{9,1},... | collective-permute-start | bytes 393224 | tf_op jit(solution)/shard_map/ppermute | solution.py:419
